TPU v7x, 32 devices: a whole 2x2x4 slice. The times are simulated.
32 devices in a mesh: grp: 1, seq: 32 (over z, y, x, core).
Axes of the slice: x: 2, y: 2, z: 4, core: 2. Of those that a mesh axis runs over, the one named last changes fastest.
Arguments:
- queries: bfloat16 [256, 1792], P(('grp', 'seq')), may hold values from -6 to 6
- stretch_keys: bfloat16 [256, 256], P(('grp', 'seq')), may hold values from -6 to 6
- stretch_values: bfloat16 [256, 256], P(('grp', 'seq')), may hold values from -6 to 6
- cache_keys: bfloat16 [32768, 256], P(('grp', 'seq')), may hold values from -6 to 6
- cache_values: bfloat16 [32768, 256], P(('grp', 'seq')), may hold values from -6 to 6
- chosen: int32 [32, 14, 3], P(('grp', 'seq')), may hold values from 0 to 7, all different within a row; in each aligned block of 7 rows (0 to 6, 7 to 13, ..., all dimensions but the last counted through in order) at most 4 rows name the same one
- out_weight: bfloat16 [1792, 1792], replicated, may hold values from -0.5 to 0.5
Outputs:
- attended: bfloat16 [256, 1792], P(('grp', 'seq'))
Inputs may be any that keep to these rules, and one draw needn't show every extreme that they name: Each head's 3 chosen blocks differ. Among the 7 heads that share one key-value head, in one query block, no key block is chosen by more than 4 heads.
All inputs are finite; a program needn't handle non-finite values.
Results may differ from a plain program's by a relative error of at most 0.005.
Values may be sent and summed in bfloat16 or wider, within the bound.
No kernel may reach another device: no remote copies, remote signals or barrier semaphores. Data moves between devices by JAX's collectives and lax.ppermute only.
A program may use at most 64 MiB of HBM per device.

v0:
```python
import math

import jax
import jax.numpy as jnp
from jax import lax
from jax.sharding import PartitionSpec as P

H = 14
KVH = 2
HD = 128
BLK = 4096
TOPK = 3


LOW_SCORE = -1e30


def block_slots(selection, block_ids, kv_heads, capacity):
    source_count, head_count, pick_count = selection.shape
    chosen_mask = jnp.any(selection[:, None, :, :] == block_ids[None, :, None, None], axis=-1)
    chosen_mask = chosen_mask.reshape(
        source_count, block_ids.shape[0], kv_heads, head_count // kv_heads
    )
    slot_rank = jnp.cumsum(chosen_mask.astype(jnp.int32), axis=-1) - 1
    slot_index = jnp.arange(capacity, dtype=jnp.int32)
    return chosen_mask[:, :, :, None, :] & (
        slot_rank[:, :, :, None, :] == slot_index[None, None, None, :, None]
    )


def slot_stats(slots_in, cache_heads, value_heads, score_scale):
    source_count = slots_in.shape[0]
    stride = math.gcd(source_count, 16)
    grouped = slots_in.reshape((source_count // stride, stride) + slots_in.shape[1:])

    def segment_stats(pieces):
        scores = (
            jnp.einsum("sgkqd,cgd->sgkqc", pieces, cache_heads, preferred_element_type=jnp.float32)
            * score_scale
        )
        seg_max = jnp.max(scores, axis=-1)
        seg_weights = jnp.exp(scores - seg_max[..., None]).astype(jnp.bfloat16)
        seg_sum = jnp.sum(seg_weights, axis=-1, dtype=jnp.float32)
        seg_out = jnp.einsum(
            "sgkqc,cgd->sgkqd", seg_weights, value_heads, preferred_element_type=jnp.float32
        )
        return (seg_max, seg_sum, seg_out)

    results = lax.map(segment_stats, grouped)
    return tuple(
        (stacked_part.reshape((source_count,) + stacked_part.shape[2:]) for stacked_part in results)
    )


def body(queries, stretch_keys, stretch_values, cache_keys, cache_values, chosen, out_weight):
    devices = lax.axis_size("seq")
    device_index = lax.axis_index("seq")
    rows_here = queries.shape[0]
    cache_rows = cache_keys.shape[0]
    group = H // KVH
    span = BLK // cache_rows
    key_blocks = cache_rows * devices // BLK
    capacity = (group * TOPK + key_blocks - 1) // key_blocks + 1
    score_scale = HD ** (-0.5)
    highest = lax.Precision.HIGHEST
    cache_heads = cache_keys.reshape(cache_rows, KVH, HD)
    value_heads = cache_values.reshape(cache_rows, KVH, HD)
    query_heads = queries.reshape(rows_here, KVH, group, HD)
    all_blocks = jnp.arange(key_blocks, dtype=jnp.int32)
    own_match = block_slots(chosen, all_blocks, KVH, capacity)
    all_rows, all_sel = (
        lax.all_gather(queries, "seq", axis=0, tiled=True),
        lax.all_gather(chosen, "seq", axis=0, tiled=True),
    )
    home_block = jnp.reshape(device_index // span, (1,))
    src_match = block_slots(all_sel, home_block, KVH, capacity)
    src_queries = all_rows.reshape(devices, rows_here, KVH, group, HD)
    built = jnp.einsum(
        "sbgkr,sqgrd->sbgkqd",
        src_match.astype(jnp.bfloat16),
        src_queries,
        preferred_element_type=jnp.float32,
    ).astype(jnp.bfloat16)[:, 0]
    hist_max, hist_sum, hist_out = lax.all_to_all(
        slot_stats(built, cache_heads, value_heads, score_scale),
        "seq",
        split_axis=0,
        concat_axis=0,
        tiled=True,
    )
    keys_part = lax.all_gather(stretch_keys, "seq", axis=0, tiled=True)
    values_part = lax.all_gather(stretch_values, "seq", axis=0, tiled=True)
    part_rows = keys_part.shape[0]
    segments = part_rows // rows_here
    key_heads = keys_part.reshape(segments, rows_here, KVH, HD)
    val_heads = values_part.reshape(segments, rows_here, KVH, HD)
    scores = (
        jnp.einsum("qgrd,skgd->qgrsk", query_heads, key_heads, preferred_element_type=jnp.float32)
        * score_scale
    )
    key_pos = jnp.arange(part_rows, dtype=jnp.int32).reshape(segments, rows_here)
    query_pos = device_index * rows_here + jnp.arange(rows_here, dtype=jnp.int32)
    visible = (
        (key_pos[None] >= 0)
        & (key_pos[None] <= query_pos[:, None, None])
        & (key_pos[None] // BLK == query_pos[:, None, None] // BLK)
    )
    visible = visible[:, None, None, :, :]
    masked = jnp.where(visible, scores, LOW_SCORE)
    seg_max = jnp.max(masked, axis=-1)
    seg_weights = jnp.where(visible, jnp.exp(masked - seg_max[..., None]), 0.0).astype(jnp.bfloat16)
    seg_sum = jnp.sum(seg_weights, axis=-1, dtype=jnp.float32)
    seg_out = jnp.einsum(
        "qgrsk,skgd->qgrsd", seg_weights, val_heads, preferred_element_type=jnp.float32
    )
    run_max = jnp.full((rows_here, KVH, group), LOW_SCORE, jnp.float32)
    new_max = jnp.maximum(run_max, jnp.max(seg_max, axis=-1))
    seg_scale = jnp.exp(seg_max - new_max[..., None])
    new_sum = jnp.sum(seg_sum * seg_scale, axis=-1)
    new_out = jnp.sum(seg_out * seg_scale[..., None], axis=-2)
    slot_mask = jnp.repeat(own_match[0], span, axis=0)[..., None]
    masked_max = jnp.where(slot_mask, hist_max[:, :, :, None, :], LOW_SCORE)
    row_max = jnp.maximum(jnp.max(masked_max, axis=(0, 2)), new_max.transpose(1, 2, 0))
    weights_hist = jnp.where(slot_mask, jnp.exp(masked_max - row_max[None, :, None]), 0.0)
    own_scale = jnp.exp(new_max - row_max.transpose(2, 0, 1))
    denominator = new_sum * own_scale + jnp.einsum(
        "jgkrq,jgkq->qgr", weights_hist, hist_sum, precision=highest
    )
    numerator = new_out * own_scale[..., None] + jnp.einsum(
        "jgkrq,jgkqd->qgrd", weights_hist, hist_out, precision=highest
    )
    attention = (numerator / denominator[..., None]).reshape(rows_here, H * HD).astype(jnp.bfloat16)
    return jnp.dot(attention, out_weight, preferred_element_type=jnp.float32).astype(jnp.bfloat16)


def solution(mesh):
    return jax.shard_map(
        body,
        mesh=mesh,
        in_specs=(
            P(("grp", "seq"), None),
            P(("grp", "seq"), None),
            P(("grp", "seq"), None),
            P(("grp", "seq"), None),
            P(("grp", "seq"), None),
            P(("grp", "seq"), None, None),
            P(),
        ),
        out_specs=P(("grp", "seq"), None),
        check_vma=False,
    )
```

profile of v0, /device:TPU:0, one launch (start us, length us, event | category | flops | bytes accessed | tf_op | source)
XLA Modules:
  0.0 215.5 jit_solution(11162538486643171020)
XLA Ops:
  0.0 0.7 copy.244
  0.7 43.4 %all_gather.14 = s32[32,14,3]{1,2,0:T(4,128)S(1)} all-gather(s32[1,14,3]{1,2,0:T(4,128)S(1)} %copy.244), channel_id=1, replica_groups=mesh['grp'=1,'seq'=32] {'seq'}, dimensions={0}, use_global_device_ids=true | all-gather | bytes 5544 | tf_op jit(solution)/shard_map/all_gather | solution.py:73
  44.1 0.1 copy.161
  44.2 0.1 copy.164
  44.4 0.1 copy.165
  44.5 39.4 %all_gather.15 = bf16[256,1792]{1,0:T(8,128)(2,1)S(1)} all-gather(bf16[8,1792]{1,0:T(8,128)(2,1)} %param.9), channel_id=1, replica_groups=mesh['grp'=1,'seq'=32] {'seq'}, dimensions={0}, use_global_device_ids=true | all-gather | bytes 946176 | tf_op jit(solution)/shard_map/all_gather | solution.py:72
  83.9 1.2 copy.167
  85.1 0.3 copy.170
  85.4 1.3 copy.168
  86.6 0.3 copy.171
  86.9 0.4 convolution_convert_fusion.1
  87.4 0.0 copy-start.1
  87.4 0.0 copy-start
  87.4 8.9 %while.14 = (s32[]{:T(128)}, f32[2,16,2,4,8]{4,3,2,1,0:T(4,128)}, f32[2,16,2,4,8]{4,3,2,1,0:T(4,128)}, f32[2,16,2,4,8,128]{5,3,2,4,1,0:T(4,128)}, bf16[2,16,2,4,...) while((s32[]{:T(128)}, f32[2,16,2,4,8]{4,3,2,1,0:T(4,128)}, ...), condition=%wide.region_10.11_spmd, body=%wide.region_7.10_spmd.sunk | while | flops 547354624 | bytes 16147545 | solution.py:49
  87.4 0.1 constant_dynamic-slice_fusion.2
  87.5 0.8 bitcast_reduce_fusion.2
  88.4 0.9 convert_reduce_fusion.3
  89.3 0.7 copy_dynamic-update-slice_fusion.5
  90.0 0.9 convolution_bitcast_fusion.3
  90.9 0.9 copy_dynamic-update-slice_fusion.6
  91.8 0.1 constant_dynamic-slice_fusion.2
  92.0 0.8 bitcast_reduce_fusion.2
  92.8 0.9 convert_reduce_fusion.3
  93.7 0.7 copy_dynamic-update-slice_fusion.5
  94.4 0.9 convolution_bitcast_fusion.3
  95.4 1.0 copy_dynamic-update-slice_fusion.6
  96.3 2.6 %all-to-all-start = ((f32[32,2,4,8]{3,2,1,0:T(4,128)}), f32[32,2,4,8]{3,2,1,0:T(4,128)S(1)}, u32[]{:S(2)}, u32[]{:S(2)}) async-start(f32[32,2,4,8]{3,2,1,0:T(4,128)} %bitcast.30), calls=%async_computation | async-start | bytes 262144 | tf_op jit(solution)/shard_map/all_to_all | solution.py:84
  98.9 0.1 copy.158
  99.1 0.0 copy-done.1
  99.1 42.1 %all_gather.12 = bf16[256,256]{1,0:T(8,128)(2,1)S(1)} all-gather(bf16[8,256]{1,0:T(8,128)(2,1)S(1)} %copy-done.1), channel_id=1, replica_groups=mesh['grp'=1,'seq'=32] {'seq'}, dimensions={0}, use_global_device_ids=true | all-gather | bytes 135168 | tf_op jit(solution)/shard_map/all_gather | solution.py:91
  141.2 0.4 fusion.22
  141.6 0.0 copy-start.2
  141.7 0.0 all-to-all-done
  141.7 2.6 %all-to-all-start.2 = ((f32[32,2,4,8]{3,2,1,0:T(4,128)}), f32[32,2,4,8]{3,2,1,0:T(4,128)S(1)}, u32[]{:S(2)}, u32[]{:S(2)}) async-start(f32[32,2,4,8]{3,2,1,0:T(4,128)} %bitcast.36), calls=%async_computation.2 | async-start | bytes 262144 | tf_op jit(solution)/shard_map/all_to_all | solution.py:84
  144.3 0.1 broadcast_in_dim.92
  144.4 0.1 broadcast_in_dim.93
  144.6 0.6 copy.152
  145.2 7.3 %all-to-all-done.2 = f32[32,2,4,8]{3,2,1,0:T(4,128)S(1)} async-done(((f32[32,2,4,8]{3,2,1,0:T(4,128)}), f32[32,2,4,8]{3,2,1,0:T(4,128)S(1)}, u32[]{:S(2)}, u32[]{:S(2)}) %all-to-all-start.2) | async-done | bytes 8224 | tf_op jit(solution)/shard_map/all_to_all | solution.py:84
  152.5 2.6 %all-to-all-start.1 = ((f32[32,2,4,8,128]{4,2,1,3,0:T(4,128)}), f32[32,2,4,8,128]{4,2,1,3,0:T(4,128)S(1)}, u32[]{:S(2)}, u32[]{:S(2)}) async-start(f32[32,2,4,8,128]{4,2,1,3,0:T(4,128)} %bitcast.33), calls=%async_computation.1 | async-start | bytes 2097152 | tf_op jit(solution)/shard_map/all_to_all | solution.py:84
  155.1 0.1 compare_and_fusion
  155.2 0.3 fusion.14
  155.5 0.1 copy.216
  155.6 0.1 copy.156
  155.7 0.2 convert_reduce_fusion.1
  156.0 0.2 multiply_reduce_fusion
  156.2 0.1 copy.218
  156.3 0.2 copy.157
  156.4 0.6 copy.153
  157.0 0.0 copy-done.2
  157.0 50.7 %all_gather.13 = bf16[256,256]{1,0:T(8,128)(2,1)S(1)} all-gather(bf16[8,256]{1,0:T(8,128)(2,1)S(1)} %copy-done.2), channel_id=1, replica_groups=mesh['grp'=1,'seq'=32] {'seq'}, dimensions={0}, use_global_device_ids=true | all-gather | bytes 135168 | tf_op jit(solution)/shard_map/all_gather | solution.py:92
  207.7 0.6 fusion.7
  208.3 0.1 copy.174
  208.4 0.1 select_reduce_fusion
  208.6 0.1 copy.175
  208.7 0.1 copy.179
  208.8 0.1 copy.222
  208.9 0.2 fusion.20
  209.1 0.1 copy.199
  209.2 0.1 copy.176
  209.3 0.1 copy.185
  209.4 0.0 all-to-all-done.1
  209.4 1.6 fusion.10
  211.0 0.1 convert_element_type.65
  211.1 4.4 %convolution_convert_fusion = bf16[8,1792]{1,0:T(8,128)(2,1)} fusion(bf16[8,1792]{1,0:T(8,128)(2,1)S(1)} %convert_element_type.65, bf16[1792,1792]{1,0:T(8,128)(2,1)} %param.15), kind=kOutput, calls=%fused_computation.15 | convolution fusion | flops 51394560 | bytes 6479872 | tf_op jit(solution)/shard_map/dot_general | solution.py:133
  (22 shorter events, 0.2 us)
Async XLA Ops:
  87.4 11.7 %copy-start.1 = (bf16[8,256]{1,0:T(8,128)(2,1)S(1)}, bf16[8,256]{1,0:T(8,128)(2,1)}, u32[]{:S(2)}) copy-start(bf16[8,256]{1,0:T(8,128)(2,1)} %param.10) | copy-start | bytes 12292
  87.4 53.9 %copy-start = (bf16[8,1792]{1,0:T(8,128)(2,1)S(1)}, bf16[8,1792]{1,0:T(8,128)(2,1)}, u32[]{:S(2)}) copy-start(bf16[8,1792]{1,0:T(8,128)(2,1)} %param.9) | copy-start | bytes 86020
  96.3 45.4 %all-to-all-start = ((f32[32,2,4,8]{3,2,1,0:T(4,128)}), f32[32,2,4,8]{3,2,1,0:T(4,128)S(1)}, u32[]{:S(2)}, u32[]{:S(2)}) async-start(f32[32,2,4,8]{3,2,1,0:T(4,128)} %bitcast.30), calls=%async_computation | async-start | bytes 262144 | tf_op jit(solution)/shard_map/all_to_all | solution.py:84
  141.6 15.4 %copy-start.2 = (bf16[8,256]{1,0:T(8,128)(2,1)S(1)}, bf16[8,256]{1,0:T(8,128)(2,1)}, u32[]{:S(2)}) copy-start(bf16[8,256]{1,0:T(8,128)(2,1)} %param.11) | copy-start | bytes 12292
  141.7 10.8 %all-to-all-start.2 = ((f32[32,2,4,8]{3,2,1,0:T(4,128)}), f32[32,2,4,8]{3,2,1,0:T(4,128)S(1)}, u32[]{:S(2)}, u32[]{:S(2)}) async-start(f32[32,2,4,8]{3,2,1,0:T(4,128)} %bitcast.36), calls=%async_computation.2 | async-start | bytes 262144 | tf_op jit(solution)/shard_map/all_to_all | solution.py:84
  152.5 56.9 %all-to-all-start.1 = ((f32[32,2,4,8,128]{4,2,1,3,0:T(4,128)}), f32[32,2,4,8,128]{4,2,1,3,0:T(4,128)S(1)}, u32[]{:S(2)}, u32[]{:S(2)}) async-start(f32[32,2,4,8,128]{4,2,1,3,0:T(4,128)} %bitcast.33), calls=%async_computation.1 | async-start | bytes 2097152 | tf_op jit(solution)/shard_map/all_to_all | solution.py:84
where the time goes:
time: 216 us; the launch traced here: 215 us
  blocking collectives  176 us (81%)
  matrix products  11 us (5%)
  local copies, waits for them, and re-layouts  10.3 us (5%)
  starting transfers between devices  7.78 us (4%)
  waiting for transfers between devices  7.3 us (3%)
  other arithmetic  3.26 us (2%)
    all_gather x1, blocking collectives, body(): values_part = lax.all_gather(stretch_values, 'seq', axis=0, tiled=True)  50.7 us
    all_gather x1, blocking collectives, body(): lax.all_gather(chosen, 'seq', axis=0, tiled=True)  43.4 us
    all_gather x1, blocking collectives, body(): keys_part = lax.all_gather(stretch_keys, 'seq', axis=0, tiled=True)  42.1 us
    all_gather x1, blocking collectives, body(): lax.all_gather(queries, 'seq', axis=0, tiled=True)  39.4 us
    all_to_all x3, starting transfers between devices, body(): lax.all_to_all(slot_stats(built, cache_heads, value_heads, score_scale),...  7.78 us
    all_to_all x3, waiting for transfers between devices, body(): lax.all_to_all(slot_stats(built, cache_heads, value_heads, score_scale),...  7.3 us
    dot_general x1, matrix products, body(): jnp.dot(attention, out_weight, preferred_element_type=jnp.float32)  4.39 us
  transfers between devices with their start and end apart: 3, of which 1 were waited for; matrix products, arithmetic and copies ran while one was open for 2% of the time, Pallas kernels for 0%

commit v1 on v0

v1 whole, which is shorter than its diff:
```python
import functools
import math

import jax
import jax.numpy as jnp
from jax import lax
from jax.experimental import pallas as pl
from jax.experimental.pallas import tpu as pltpu
from jax.sharding import PartitionSpec as P

H = 14
KVH = 2
HD = 128
BLK = 4096
TOPK = 3
GROUP = H // KVH

LOW_SCORE = -1e30
LOG2E = math.log2(math.e)
LANES = 128


def head_rows(q_ref, g):
    q = q_ref[...].astype(jnp.float32)
    return [q[:, h * HD : (h + 1) * HD] for h in range(g * GROUP, (g + 1) * GROUP)]


def slot_match(chosen_ref, g, block, slot, token):
    rows = lax.broadcasted_iota(jnp.int32, block.shape, 0)
    same_token = token == rows
    seen = jnp.zeros(block.shape, jnp.int32)
    found = []
    for h in range(g * GROUP, (g + 1) * GROUP):
        picked = block == chosen_ref[0, h, 0]
        for t in range(1, TOPK):
            picked = picked | (block == chosen_ref[0, h, t])
        found.append(jnp.where(picked & same_token & (seen == slot), 1.0, 0.0))
        seen = seen + picked.astype(jnp.int32)
    return found


def pack_kernel(chips, capacity, chosen_ref, q_ref, k_ref, v_ref, send_ref):
    tokens = q_ref.shape[0]
    per = capacity * tokens
    span = chips * KVH
    key_blocks = send_ref.shape[0] // span
    lane = lax.broadcasted_iota(jnp.int32, (tokens, key_blocks * per), 1)
    block, slot, token = lane // per, lane % per // tokens, lane % tokens
    for g in range(KVH):
        spread = jnp.concatenate(
            slot_match(chosen_ref, g, block, slot, token) + [jnp.zeros(lane.shape, jnp.float32)], axis=0
        )
        rows = head_rows(q_ref, g)
        rows = jnp.concatenate(rows + [jnp.zeros_like(rows[0])], axis=0)
        slots = jnp.dot(
            spread.T.astype(jnp.bfloat16), rows.astype(jnp.bfloat16), preferred_element_type=jnp.float32
        ).astype(jnp.bfloat16)
        cols = slice(g * HD, (g + 1) * HD)
        fresh = jnp.concatenate(
            [k_ref[:, cols].astype(jnp.float32), v_ref[:, cols].astype(jnp.float32)], axis=0
        ).astype(jnp.bfloat16)
        for b in range(key_blocks):
            for chip in range(chips):
                to = b * span + chip * KVH + g
                send_ref[to, :per, :] = slots[b * per : (b + 1) * per]
                send_ref[to, per:, :] = fresh


def attend_kernel(per, core_ref, q_ref, k_ref, v_ref, peer_ref, out_ref, va_ref, vb_ref):
    cols = pl.ds(pl.multiple_of(core_ref[0] * HD, HD), HD)
    ones = jnp.ones((k_ref.shape[0], HD), jnp.bfloat16)
    va_ref[:, :HD] = v_ref[:, cols]
    va_ref[:, HD:] = ones
    vb_ref[:, :HD] = peer_ref[1]
    vb_ref[:, HD:] = ones
    sources = q_ref.shape[0]
    step = 256 // per
    scale = LOG2E * HD**-0.5
    nt = (((1,), (1,)), ((), ()))
    row = lax.broadcasted_iota(jnp.int32, (per, LANES), 0)
    lane = lax.broadcasted_iota(jnp.int32, (per, LANES), 1)
    diagonal = row == lane % per
    piece = lax.broadcasted_iota(jnp.int32, (16, LANES), 0)
    for first in range(0, sources, step):
        q = q_ref[first : first + step, :per, :].reshape(step * per, HD)
        sa = lax.dot_general(q, k_ref[:, cols], nt, preferred_element_type=jnp.float32)
        sb = lax.dot_general(q, peer_ref[0], nt, preferred_element_type=jnp.float32)
        top = jnp.maximum(jnp.max(sa, axis=1, keepdims=True), jnp.max(sb, axis=1, keepdims=True)) * scale
        wa = jnp.exp2(sa * scale - top).astype(jnp.bfloat16)
        wb = jnp.exp2(sb * scale - top).astype(jnp.bfloat16)
        both = jnp.dot(wa, va_ref[...], preferred_element_type=jnp.float32) + jnp.dot(
            wb, vb_ref[...], preferred_element_type=jnp.float32
        )
        total = both[:, HD:]
        out = (both[:, :HD] / total).astype(jnp.bfloat16)
        lse = top + jnp.log(total) * LOG2E
        for s in range(step):
            part = slice(s * per, (s + 1) * per)
            out_ref[first + s, :per, :] = out[part]
            flat = jnp.sum(jnp.where(diagonal, lse[part], 0.0), axis=0, keepdims=True)
            hi = flat.astype(jnp.bfloat16).astype(jnp.float32)
            mid = (flat - hi).astype(jnp.bfloat16).astype(jnp.float32)
            low = flat - hi - mid
            out_ref[first + s, per:, :] = jnp.where(
                piece == 0, hi, jnp.where(piece == 1, mid, jnp.where(piece == 2, low, 0.0))
            ).astype(jnp.bfloat16)


def fresh_kernel(chips, capacity, place_ref, chosen_ref, q_ref, mine_ref, peer_ref, out_ref, lse_ref, match_ref):
    tokens = q_ref.shape[0]
    sources = mine_ref.shape[0]
    per = capacity * tokens
    core, first = place_ref[0], place_ref[1]
    scale = LOG2E * HD**-0.5
    nt = (((1,), (1,)), ((), ()))
    shape = (GROUP * tokens, sources * tokens)
    key_pos = lax.broadcasted_iota(jnp.int32, shape, 1)
    query_pos = first + lax.broadcasted_iota(jnp.int32, shape, 0) % tokens
    visible = (key_pos <= query_pos) & (key_pos // BLK == query_pos // BLK)
    lane = lax.broadcasted_iota(jnp.int32, (tokens, match_ref.shape[2]), 1)
    block, slot, token = lane // (per * chips), lane % per // tokens, lane % tokens
    mine = mine_ref[...].astype(jnp.float32).reshape(sources, 2, tokens, HD)
    peer = peer_ref[...].astype(jnp.float32).reshape(sources, 2, tokens, HD)
    ones = jnp.ones((sources * tokens, HD), jnp.bfloat16)
    for g in range(KVH):
        match_ref[g] = jnp.concatenate(slot_match(chosen_ref, g, block, slot, token), axis=0)
        kv = jnp.where(core == g, mine, peer)
        keys = kv[:, 0].reshape(sources * tokens, HD).astype(jnp.bfloat16)
        values = kv[:, 1].reshape(sources * tokens, HD).astype(jnp.bfloat16)
        q = jnp.concatenate(head_rows(q_ref, g), axis=0).astype(jnp.bfloat16)
        s = lax.dot_general(q, keys, nt, preferred_element_type=jnp.float32) * scale
        s = jnp.where(visible, s, LOW_SCORE)
        top = jnp.max(s, axis=1, keepdims=True)
        w = jnp.where(visible, jnp.exp2(s - top), 0.0).astype(jnp.bfloat16)
        both = jnp.dot(w, jnp.concatenate([values, ones], axis=1), preferred_element_type=jnp.float32)
        total = both[:, HD:]
        out_ref[g] = both[:, :HD] / total
        lse_ref[g] = top + jnp.log(total) * LOG2E


def project_kernel(per, hist_ref, out_ref, lse_ref, match_ref, w_ref, y_ref, att_ref):
    tokens = y_ref.shape[0]
    holders = hist_ref.shape[0]
    fold = LANES // per
    row = lax.broadcasted_iota(jnp.int32, (holders, LANES), 0)
    lane = lax.broadcasted_iota(jnp.int32, (holders, LANES), 1)
    for g in range(KVH):
        outs = hist_ref[:, g, :per, :].reshape(holders * per, HD)
        stats = jnp.sum(hist_ref[:, g, per:, :].astype(jnp.float32), axis=1)
        stats = jnp.where(row % fold == lane // per, stats, 0.0)
        lse = jnp.concatenate(
            [
                jnp.sum(jnp.where(row // fold == m, stats, 0.0), axis=0, keepdims=True)
                for m in range(holders // fold)
            ],
            axis=1,
        )
        match = match_ref[g] > 0.5
        lse = jnp.where(match, lse, LOW_SCORE)
        own = lse_ref[g]
        top = jnp.maximum(jnp.max(lse, axis=1, keepdims=True), own)
        w = jnp.where(match, jnp.exp2(lse - top[:, :1]), 0.0)
        own_w = jnp.exp2(own - top)
        hi = w.astype(jnp.bfloat16)
        low = (w - hi.astype(jnp.float32)).astype(jnp.bfloat16)
        num = (
            jnp.dot(hi, outs, preferred_element_type=jnp.float32)
            + jnp.dot(low, outs, preferred_element_type=jnp.float32)
            + own_w * out_ref[g]
        )
        att = num / (jnp.sum(w, axis=1, keepdims=True) + own_w)
        for r in range(GROUP):
            h = g * GROUP + r
            att_ref[:, h * HD : (h + 1) * HD] = att[r * tokens : (r + 1) * tokens]
    y_ref[...] = jnp.dot(
        att_ref[...].astype(jnp.bfloat16), w_ref[...], preferred_element_type=jnp.float32
    ).astype(jnp.bfloat16)


VMEM = pl.BlockSpec(memory_space=pltpu.VMEM)
SMEM = pl.BlockSpec(memory_space=pltpu.SMEM)


def call(kernel, name, out_shape, specs, *operands, scratch=(), flops=0, moved=0, limit=16):
    outs = jax.tree.map(lambda _: VMEM, out_shape)
    return pl.pallas_call(
        kernel,
        name=name,
        out_shape=out_shape,
        in_specs=specs,
        out_specs=outs,
        scratch_shapes=scratch,
        cost_estimate=pl.CostEstimate(flops=flops, bytes_accessed=moved, transcendentals=0),
        compiler_params=pltpu.CompilerParams(vmem_limit_bytes=limit << 20),
    )(*operands)


def body(queries, stretch_keys, stretch_values, cache_keys, cache_values, chosen, out_weight):
    devices = lax.axis_size("seq")
    device_index = lax.axis_index("seq")
    tokens = queries.shape[0]
    cache_rows = cache_keys.shape[0]
    span = BLK // cache_rows
    chips = span // KVH
    key_blocks = cache_rows * devices // BLK
    capacity = (GROUP * TOPK + key_blocks - 1) // key_blocks + 1
    per = capacity * tokens
    core = device_index % KVH
    swap = [(i, i ^ 1) for i in range(devices)]
    f32, bf16 = jnp.float32, jnp.bfloat16

    send = call(
        functools.partial(pack_kernel, chips, capacity),
        "pack",
        jax.ShapeDtypeStruct((devices, per + 2 * tokens, HD), bf16),
        [SMEM, VMEM, VMEM, VMEM],
        chosen, queries, stretch_keys, stretch_values,
    )
    got = lax.all_to_all(send, "seq", split_axis=0, concat_axis=0, tiled=True)

    away = (1 - core) * HD
    peer_cache = lax.ppermute(
        jnp.stack(
            [
                lax.dynamic_slice_in_dim(cache_keys, away, HD, axis=1),
                lax.dynamic_slice_in_dim(cache_values, away, HD, axis=1),
            ]
        ),
        "seq",
        swap,
    )
    place = jnp.stack([core, device_index * tokens]).astype(jnp.int32)
    rows = devices * per
    back = call(
        functools.partial(attend_kernel, per),
        "attend",
        jax.ShapeDtypeStruct((devices, per + 16, HD), bf16),
        [SMEM, VMEM, VMEM, VMEM, VMEM],
        place, got, cache_keys, cache_values, peer_cache,
        scratch=[pltpu.VMEM((cache_rows, 2 * HD), bf16)] * 2,
        flops=8 * rows * cache_rows * HD,
        moved=4 << 20,
        limit=32,
    )
    hist = lax.all_to_all(back, "seq", split_axis=0, concat_axis=0, tiled=True)

    fresh = got[:, per:, :]
    peer_fresh = lax.ppermute(fresh, "seq", swap)
    holders = devices // KVH
    out, lse, match = call(
        functools.partial(fresh_kernel, chips, capacity),
        "fresh",
        (
            jax.ShapeDtypeStruct((KVH, GROUP * tokens, HD), f32),
            jax.ShapeDtypeStruct((KVH, GROUP * tokens, HD), f32),
            jax.ShapeDtypeStruct((KVH, GROUP * tokens, holders * per), f32),
        ),
        [SMEM, SMEM, VMEM, VMEM, VMEM],
        place, chosen, queries, fresh, peer_fresh,
        flops=8 * H * tokens * devices * tokens * HD,
        moved=2 << 20,
    )
    return call(
        functools.partial(project_kernel, per),
        "project",
        jax.ShapeDtypeStruct((tokens, out_weight.shape[1]), bf16),
        [VMEM] * 5,
        hist.reshape(holders, KVH, per + 16, HD), out, lse, match, out_weight,
        scratch=[pltpu.VMEM((tokens, H * HD), f32)],
        flops=2 * tokens * out_weight.size,
        moved=out_weight.size * 2,
        limit=24,
    )


def solution(mesh):
    seq = ("grp", "seq")
    return jax.shard_map(
        body,
        mesh=mesh,
        in_specs=(
            P(seq, None),
            P(seq, None),
            P(seq, None),
            P(seq, None),
            P(seq, None),
            P(seq, None, None),
            P(),
        ),
        out_specs=P(seq, None),
        check_vma=False,
    )
```

time: 216 us -> 53 us (0.25)
  blocking collectives: 176 us -> 0 us
  waiting for transfers between devices: 7.3 us -> 23.4 us
  matrix products: 11 us -> 0 us
  Pallas kernels: 0 us -> 9.41 us
  other arithmetic: 3.26 us -> 0.13 us
  starting transfers between devices: 7.78 us -> 10.6 us
    all_gather x4 -> x0, blocking collectives: 176 us -> none  [the longest x1 50.7 us: body(): values_part = lax.all_gather(stretch_values, 'seq', axis=0, tiled=True)]
    all_to_all x3 -> x2, waiting for transfers between devices: 7.3 us -> 20.7 us  [the longest x1 10.6 us: body(): hist = lax.all_to_all(back, 'seq', split_axis=0, concat_axis=0, tiled=True)]
    dot_general x9 -> x0, matrix products: 11 us -> none  [the longest x1 4.39 us: body(): jnp.dot(attention, out_weight, preferred_element_type=jnp.float32)]
    pallas_call x0 -> x4, Pallas kernels: none -> 9.41 us  [call(): pl.pallas_call(kernel, name=name, out_shape=out_shape, in_specs=specs, ou...]
    unnamed x12 -> x15, local copies, waits for them, and re-layouts: 3.49 us -> 7.8 us
    dynamic_update_slice x4 -> x0, local copies, waits for them, and re-layouts: 3.24 us -> none  [slot_stats(): results = lax.map(segment_stats, grouped)]
    ppermute x0 -> x2, waiting for transfers between devices: none -> 2.68 us  [the longest x1 1.58 us: body(): lax.ppermute(jnp.stack([lax.dynamic_slice_in_dim(cache_keys, away, HD, ax...]
    reduce_sum x4 -> x0, other arithmetic: 2.31 us -> none  [the longest x2 1.88 us: segment_stats(): seg_sum = jnp.sum(seg_weights, axis=-1, dtype=jnp.float32)]
  transfers between devices with their start and end apart: 3 -> 4, of which waited for: 1 -> 4; matrix products, arithmetic and copies ran while one was open for 2% -> 2% of each run, Pallas kernels for 0% -> 2%
where the time goes in v1:
time: 53 us; the launch traced here: 52.4 us
  waiting for transfers between devices  23.4 us (44%)
  starting transfers between devices  10.6 us (20%)
  Pallas kernels  9.41 us (18%)
  local copies, waits for them, and re-layouts  8.88 us (17%)
    all_to_all x1, waiting for transfers between devices, body(): hist = lax.all_to_all(back, 'seq', split_axis=0, concat_axis=0, tiled=True)  10.6 us
    all_to_all x1, waiting for transfers between devices, body(): got = lax.all_to_all(send, 'seq', split_axis=0, concat_axis=0, tiled=True)  10.1 us
    pallas_call x4, Pallas kernels, call(): pl.pallas_call(kernel, name=name, out_shape=out_shape, in_specs=specs, ou...  9.41 us
    unnamed x15, local copies, waits for them, and re-layouts  7.8 us
    all_to_all x1, starting transfers between devices, body(): got = lax.all_to_all(send, 'seq', split_axis=0, concat_axis=0, tiled=True)  7.3 us
    all_to_all x1, starting transfers between devices, body(): hist = lax.all_to_all(back, 'seq', split_axis=0, concat_axis=0, tiled=True)  2.63 us
    ppermute x1, waiting for transfers between devices, body(): lax.ppermute(jnp.stack([lax.dynamic_slice_in_dim(cache_keys, away, HD, ax...  1.58 us
    ppermute x1, waiting for transfers between devices, body(): peer_fresh = lax.ppermute(fresh, 'seq', swap)  1.1 us
  transfers between devices with their start and end apart: 4, of which 4 were waited for; matrix products, arithmetic and copies ran while one was open for 2% of the time, Pallas kernels for 2%

profile of v1, /device:TPU:0, one launch (start us, length us, event | category | flops | bytes accessed | tf_op | source)
XLA Modules:
  0.0 52.4 jit_solution(599025845011503011)
XLA Ops:
  0.0 0.8 %copy.8.chosen_ref = s32[1,14,3]{2,1,0:T(8,128)S(1)} copy(s32[1,14,3]{1,0,2:T(1,128)} %param.12) | data formatting | bytes 336 | tf_op args[5]
  0.8 0.0 copy-start.3
  0.8 0.7 %copy-done.3 = bf16[8,1792]{1,0:T(8,128)(2,1)S(1)} copy-done((bf16[8,1792]{1,0:T(8,128)(2,1)S(1)}, bf16[8,1792]{1,0:T(8,128)(2,1)}, u32[]{:S(2)}) %copy-start.3) | copy-done | bytes 28696
  1.5 0.0 copy-start.5
  1.5 0.7 %copy-done.5 = bf16[8,256]{1,0:T(8,128)(2,1)S(1)} copy-done((bf16[8,256]{1,0:T(8,128)(2,1)S(1)}, bf16[8,256]{1,0:T(8,128)(2,1)}, u32[]{:S(2)}) %copy-start.5) | copy-done | bytes 4120
  2.2 0.0 copy-start.6
  2.2 0.7 %copy-done.6 = bf16[8,256]{1,0:T(8,128)(2,1)S(1)} copy-done((bf16[8,256]{1,0:T(8,128)(2,1)S(1)}, bf16[8,256]{1,0:T(8,128)(2,1)}, u32[]{:S(2)}) %copy-start.6) | copy-done | bytes 4120
  2.9 0.0 copy-start.4
  2.9 1.7 %pack.1 = bf16[32,48,128]{2,1,0:T(8,128)(2,1)} custom-call(s32[1,14,3]{2,1,0:T(8,128)S(1)} %copy.8.chosen_ref, bf16[8,1792]{1,0:T(8,128)(2,1)S(1)} %copy-done.3, bf16[8,256]{1,0:T(8,128)(2,1)S(1)} %copy-done.5, bf16[8,256]{1,0:T(8,128)(2,1)S(1)} %copy-done.6), custom_call_target="tpu_custom_call" | custom-call | tf_op jit(solution)/shard_map/pack/pallas_call | solution.py:186
  4.6 7.3 %all-to-all-start = ((bf16[32,48,128]{2,1,0:T(8,128)(2,1)}), bf16[32,48,128]{2,1,0:T(8,128)(2,1)S(1)}, u32[]{:S(2)}, u32[]{:S(2)}) async-start(bf16[32,48,128]{2,1,0:T(8,128)(2,1)} %pack.1), calls=%async_computation | async-start | bytes 786432 | tf_op jit(solution)/shard_map/all_to_all | solution.py:219
  11.9 1.1 %dynamic-slice_bitcast_fusion = (bf16[1,1024,128]{2,1,0:T(8,128)(2,1)S(1)}, bf16[1,1024,128]{2,1,0:T(8,128)(2,1)S(1)}) fusion(bf16[1024,256]{1,0:T(8,128)(2,1)} %v_ref.3, s32[]{:T(128)S(6)} %select_n.12, bf16[1024,256]{1,0:T(8,128)(2,1)} %k_ref.3), kind=kLoop, calls=%fused_computation.1 | loop fusion | bytes 1048580 | tf_op jit(solution)/shard_map/stack | solution.py:223
  13.0 0.1 pad_maximum_fusion
  13.0 0.3 collective-permute-start
  13.3 0.1 pad_add_fusion.core_ref.place_ref
  13.4 1.6 %collective-permute-done.peer_ref = bf16[2,1024,128]{2,1,0:T(8,128)(2,1)S(1)} collective-permute-done((bf16[2,1024,128]{2,1,0:T(8,128)(2,1)S(1)}, bf16[2,1024,128]{2,1,0:T(8,128)(2,1)S(1)}, u32[]{:S(2)}, u32[]{:S(2)}) %collective-permute-start) | collective-permute-done | bytes 524320 | tf_op jit(solution)/shard_map/ppermute | solution.py:222
  15.0 10.1 %all-to-all-done.q_ref = bf16[32,48,128]{2,1,0:T(8,128)(2,1)S(1)} async-done(((bf16[32,48,128]{2,1,0:T(8,128)(2,1)}), bf16[32,48,128]{2,1,0:T(8,128)(2,1)S(1)}, u32[]{:S(2)}, u32[]{:S(2)}) %all-to-all-start) | async-done | bytes 393248 | tf_op jit(solution)/shard_map/all_to_all | solution.py:219
  25.1 0.0 copy-start.1
  25.1 1.0 %copy-done.1 = bf16[1024,256]{1,0:T(8,128)(2,1)S(1)} copy-done((bf16[1024,256]{1,0:T(8,128)(2,1)S(1)}, bf16[1024,256]{1,0:T(8,128)(2,1)}, u32[]{:S(2)}) %copy-start.1) | copy-done | bytes 524312
  26.1 0.0 copy-start.2
  26.1 1.0 %copy-done.2 = bf16[1024,256]{1,0:T(8,128)(2,1)S(1)} copy-done((bf16[1024,256]{1,0:T(8,128)(2,1)S(1)}, bf16[1024,256]{1,0:T(8,128)(2,1)}, u32[]{:S(2)}) %copy-start.2) | copy-done | bytes 524312
  27.1 4.6 %attend.1 = bf16[32,48,128]{2,1,0:T(8,128)(2,1)} custom-call(s32[2]{0:T(128)S(1)} %pad_add_fusion.core_ref.place_ref, bf16[32,48,128]{2,1,0:T(8,128)(2,1)S(1)} %all-to-all-done.q_ref, bf16[1024,256]{1,0:T(8,128)(2,1)S(1)} %copy-done.1, bf16[1024,256]{1,0:T(8,128)(2,1)S(1)} %copy-done.2, bf16[2,1024,128]{2,1,0:T(8,128)(2,1)S(1)} %collective-permute-done.peer_ref), custom_call_target="tpu_custom_call" | custom-call | flops 1073741824 | bytes 4194304 | tf_op jit(solution)/shard_map/attend/pallas_call | solution.py:186
  31.8 2.6 %all-to-all-start.1 = ((bf16[32,48,128]{2,1,0:T(8,128)(2,1)}), bf16[32,48,128]{2,1,0:T(8,128)(2,1)S(1)}, u32[]{:S(2)}, u32[]{:S(2)}) async-start(bf16[32,48,128]{2,1,0:T(8,128)(2,1)} %attend.1), calls=%async_computation.1 | async-start | bytes 786432 | tf_op jit(solution)/shard_map/all_to_all | solution.py:245
  34.4 0.3 collective-permute-start.1
  34.8 1.1 %collective-permute-done.1.peer_ref = bf16[32,16,128]{2,1,0:T(8,128)(2,1)S(1)} collective-permute-done((bf16[32,16,128]{2,1,0:T(8,128)(2,1)S(1)}, bf16[32,16,128]{2,1,0:T(8,128)(2,1)S(1)}, u32[]{:S(2)}, u32[]{:S(2)}) %collective-permute-start.1) | collective-permute-done | bytes 131104 | tf_op jit(solution)/shard_map/ppermute | solution.py:248
  35.8 0.0 copy-done.4
  35.9 1.1 %fresh.1 = (f32[2,56,128]{2,1,0:T(8,128)S(1)}, f32[2,56,128]{2,1,0:T(8,128)S(1)}, f32[2,56,512]{2,1,0:T(8,128)S(1)}) custom-call(s32[2]{0:T(128)S(1)} %pad_add_fusion.core_ref.place_ref, s32[1,14,3]{2,1,0:T(8,128)S(1)} %copy.8.chosen_ref, bf16[8,1792]{1,0:T(8,128)(2,1)S(1)} %copy-done.4, bf16[32,16,128]{2,1,0:T(8,128)(2,1)S(1)} %slice.4.mine_ref, ...), custom_call_target="tpu_custom_call" | custom-call | flops 29360128 | bytes 2097152 | tf_op jit(solution)/shard_map/fresh/pallas_call | solution.py:186
  37.0 10.6 %all-to-all-done.1 = bf16[32,48,128]{2,1,0:T(8,128)(2,1)S(1)} async-done(((bf16[32,48,128]{2,1,0:T(8,128)(2,1)}), bf16[32,48,128]{2,1,0:T(8,128)(2,1)S(1)}, u32[]{:S(2)}, u32[]{:S(2)}) %all-to-all-start.1) | async-done | bytes 393248 | tf_op jit(solution)/shard_map/all_to_all | solution.py:245
  47.6 0.0 copy-start
  47.6 2.8 %copy-done = bf16[1792,1792]{1,0:T(8,128)(2,1)S(1)} copy-done((bf16[1792,1792]{1,0:T(8,128)(2,1)S(1)}, bf16[1792,1792]{1,0:T(8,128)(2,1)}, u32[]{:S(2)}) %copy-start) | copy-done | bytes 6422552
  50.4 2.0 %project.1 = bf16[8,1792]{1,0:T(8,128)(2,1)} custom-call(bf16[16,2,48,128]{3,2,1,0:T(8,128)(2,1)S(1)} %bitcast.7, f32[2,56,128]{2,1,0:T(8,128)S(1)} %get-tuple-element.8.out_ref, f32[2,56,128]{2,1,0:T(8,128)S(1)} %get-tuple-element.9.lse_ref, f32[2,56,512]{2,1,0:T(8,128)S(1)} %get-tuple-element.10.match_ref, bf16[1792,1792]{1,0:T(8,128)(2,1)S(1)} %copy-done), custom_call_target="tpu_custom_call" | custom-call | flops 51380224 | bytes 6422528 | tf_op jit(solution)/shard_map/project/pallas_call | solution.py:186
  (1 shorter events, 0.0 us)
Async XLA Ops:
  0.8 0.7 %copy-start.3 = (bf16[8,1792]{1,0:T(8,128)(2,1)S(1)}, bf16[8,1792]{1,0:T(8,128)(2,1)}, u32[]{:S(2)}) copy-start(bf16[8,1792]{1,0:T(8,128)(2,1)} %q_ref.3) | copy-start | bytes 86020
  1.5 0.7 %copy-start.5 = (bf16[8,256]{1,0:T(8,128)(2,1)S(1)}, bf16[8,256]{1,0:T(8,128)(2,1)}, u32[]{:S(2)}) copy-start(bf16[8,256]{1,0:T(8,128)(2,1)} %k_ref.2) | copy-start | bytes 12292
  2.2 0.7 %copy-start.6 = (bf16[8,256]{1,0:T(8,128)(2,1)S(1)}, bf16[8,256]{1,0:T(8,128)(2,1)}, u32[]{:S(2)}) copy-start(bf16[8,256]{1,0:T(8,128)(2,1)} %v_ref.2) | copy-start | bytes 12292
  2.9 33.0 %copy-start.4 = (bf16[8,1792]{1,0:T(8,128)(2,1)S(1)}, bf16[8,1792]{1,0:T(8,128)(2,1)}, u32[]{:S(2)}) copy-start(bf16[8,1792]{1,0:T(8,128)(2,1)} %q_ref.3) | copy-start | bytes 86020
  4.6 20.5 %all-to-all-start = ((bf16[32,48,128]{2,1,0:T(8,128)(2,1)}), bf16[32,48,128]{2,1,0:T(8,128)(2,1)S(1)}, u32[]{:S(2)}, u32[]{:S(2)}) async-start(bf16[32,48,128]{2,1,0:T(8,128)(2,1)} %pack.1), calls=%async_computation | async-start | bytes 786432 | tf_op jit(solution)/shard_map/all_to_all | solution.py:219
  13.0 2.0 %collective-permute-start = (bf16[2,1024,128]{2,1,0:T(8,128)(2,1)S(1)}, bf16[2,1024,128]{2,1,0:T(8,128)(2,1)S(1)}, u32[]{:S(2)}, u32[]{:S(2)}) collective-permute-start(bf16[2,1024,128]{2,1,0:T(8,128)(2,1)S(1)} %pad_maximum_fusion), channel_id=1, source_target_pairs={{0,1},{1,0},{2,3},{3,2},{4,5},{5,4},{6,7},{7,6},{8,9},{9,8},{10,11... | collective-permute-start | bytes 1572872 | tf_op jit(solution)/shard_map/ppermute | solution.py:222
  25.1 1.0 %copy-start.1 = (bf16[1024,256]{1,0:T(8,128)(2,1)S(1)}, bf16[1024,256]{1,0:T(8,128)(2,1)}, u32[]{:S(2)}) copy-start(bf16[1024,256]{1,0:T(8,128)(2,1)} %k_ref.3) | copy-start | bytes 1572868
  26.1 1.0 %copy-start.2 = (bf16[1024,256]{1,0:T(8,128)(2,1)S(1)}, bf16[1024,256]{1,0:T(8,128)(2,1)}, u32[]{:S(2)}) copy-start(bf16[1024,256]{1,0:T(8,128)(2,1)} %v_ref.3) | copy-start | bytes 1572868
  31.8 15.8 %all-to-all-start.1 = ((bf16[32,48,128]{2,1,0:T(8,128)(2,1)}), bf16[32,48,128]{2,1,0:T(8,128)(2,1)S(1)}, u32[]{:S(2)}, u32[]{:S(2)}) async-start(bf16[32,48,128]{2,1,0:T(8,128)(2,1)} %attend.1), calls=%async_computation.1 | async-start | bytes 786432 | tf_op jit(solution)/shard_map/all_to_all | solution.py:245
  34.4 1.4 %collective-permute-start.1 = (bf16[32,16,128]{2,1,0:T(8,128)(2,1)S(1)}, bf16[32,16,128]{2,1,0:T(8,128)(2,1)S(1)}, u32[]{:S(2)}, u32[]{:S(2)}) collective-permute-start(bf16[32,16,128]{2,1,0:T(8,128)(2,1)S(1)} %slice.4.mine_ref), channel_id=1, source_target_pairs={{0,1},{1,0},{2,3},{3,2},{4,5},{5,4},{6,7},{7,6},{8,9},{9,8},{10,11... | collective-permute-start | bytes 393224 | tf_op jit(solution)/shard_map/ppermute | solution.py:248
  47.6 2.8 %copy-start = (bf16[1792,1792]{1,0:T(8,128)(2,1)S(1)}, bf16[1792,1792]{1,0:T(8,128)(2,1)}, u32[]{:S(2)}) copy-start(bf16[1792,1792]{1,0:T(8,128)(2,1)} %w_ref.1) | copy-start | bytes 19267588

commit v2 on v1

--- a/solution.py
+++ b/solution.py
@@ -31,21 +31,33 @@
     seen = jnp.zeros(block.shape, jnp.int32)
     found = []
     for h in range(g * GROUP, (g + 1) * GROUP):
-        picked = block == chosen_ref[0, h, 0]
+        picked = block == chosen_ref[0, :, h : h + 1]
         for t in range(1, TOPK):
-            picked = picked | (block == chosen_ref[0, h, t])
+            picked = picked | (block == chosen_ref[t, :, h : h + 1])
         found.append(jnp.where(picked & same_token & (seen == slot), 1.0, 0.0))
         seen = seen + picked.astype(jnp.int32)
     return found
 
 
-def pack_kernel(chips, capacity, chosen_ref, q_ref, k_ref, v_ref, send_ref):
+def fetch(pairs, sems):
+    copies = [pltpu.make_async_copy(src, dst, sems.at[i]) for i, (src, dst) in enumerate(pairs)]
+    for copy in copies:
+        copy.start()
+    return copies
+
+
+def pack_kernel(chips, capacity, chosen_hbm, q_hbm, k_hbm, v_hbm, send_ref, fresh_ref, chosen_ref, q_ref, sems):
+    copies = fetch(
+        [(chosen_hbm, chosen_ref), (q_hbm, q_ref), (k_hbm, fresh_ref.at[0]), (v_hbm, fresh_ref.at[1])], sems
+    )
     tokens = q_ref.shape[0]
     per = capacity * tokens
     span = chips * KVH
     key_blocks = send_ref.shape[0] // span
     lane = lax.broadcasted_iota(jnp.int32, (tokens, key_blocks * per), 1)
     block, slot, token = lane // per, lane % per // tokens, lane % tokens
+    for copy in copies:
+        copy.wait()
     for g in range(KVH):
         spread = jnp.concatenate(
             slot_match(chosen_ref, g, block, slot, token) + [jnp.zeros(lane.shape, jnp.float32)], axis=0
@@ -55,41 +67,49 @@
         slots = jnp.dot(
             spread.T.astype(jnp.bfloat16), rows.astype(jnp.bfloat16), preferred_element_type=jnp.float32
         ).astype(jnp.bfloat16)
-        cols = slice(g * HD, (g + 1) * HD)
-        fresh = jnp.concatenate(
-            [k_ref[:, cols].astype(jnp.float32), v_ref[:, cols].astype(jnp.float32)], axis=0
-        ).astype(jnp.bfloat16)
         for b in range(key_blocks):
             for chip in range(chips):
-                to = b * span + chip * KVH + g
-                send_ref[to, :per, :] = slots[b * per : (b + 1) * per]
-                send_ref[to, per:, :] = fresh
-
-
-def attend_kernel(per, core_ref, q_ref, k_ref, v_ref, peer_ref, out_ref, va_ref, vb_ref):
-    cols = pl.ds(pl.multiple_of(core_ref[0] * HD, HD), HD)
-    ones = jnp.ones((k_ref.shape[0], HD), jnp.bfloat16)
-    va_ref[:, :HD] = v_ref[:, cols]
-    va_ref[:, HD:] = ones
-    vb_ref[:, :HD] = peer_ref[1]
-    vb_ref[:, HD:] = ones
-    sources = q_ref.shape[0]
+                send_ref[b * span + chip * KVH + g] = slots[b * per : (b + 1) * per]
+
+
+def split_kernel(after_ref, k_hbm, v_hbm, own_ref, away_ref, sems):
+    core = lax.axis_index("seq") % KVH
+    own = pl.ds(pl.multiple_of(core * HD, HD), HD)
+    away = pl.ds(pl.multiple_of((1 - core) * HD, HD), HD)
+    copies = fetch(
+        [
+            (k_hbm.at[:, away], away_ref.at[:, :HD]),
+            (v_hbm.at[:, away], away_ref.at[:, HD : 2 * HD]),
+            (k_hbm.at[:, own], own_ref.at[:, :HD]),
+            (v_hbm.at[:, own], own_ref.at[:, HD : 2 * HD]),
+        ],
+        sems,
+    )
+    ones = jnp.ones((own_ref.shape[0], HD), jnp.bfloat16)
+    own_ref[:, 2 * HD :] = ones
+    away_ref[:, 2 * HD :] = ones
+    for copy in copies:
+        copy.wait()
+
+
+def attend_kernel(q_ref, own_ref, peer_ref, out_ref):
+    sources, per = q_ref.shape[:2]
     step = 256 // per
     scale = LOG2E * HD**-0.5
     nt = (((1,), (1,)), ((), ()))
     row = lax.broadcasted_iota(jnp.int32, (per, LANES), 0)
     lane = lax.broadcasted_iota(jnp.int32, (per, LANES), 1)
     diagonal = row == lane % per
-    piece = lax.broadcasted_iota(jnp.int32, (16, LANES), 0)
+    piece = lax.broadcasted_iota(jnp.int32, (8, LANES), 0)
     for first in range(0, sources, step):
-        q = q_ref[first : first + step, :per, :].reshape(step * per, HD)
-        sa = lax.dot_general(q, k_ref[:, cols], nt, preferred_element_type=jnp.float32)
-        sb = lax.dot_general(q, peer_ref[0], nt, preferred_element_type=jnp.float32)
+        q = q_ref[first : first + step].reshape(step * per, HD)
+        sa = lax.dot_general(q, own_ref[:, :HD], nt, preferred_element_type=jnp.float32)
+        sb = lax.dot_general(q, peer_ref[:, :HD], nt, preferred_element_type=jnp.float32)
         top = jnp.maximum(jnp.max(sa, axis=1, keepdims=True), jnp.max(sb, axis=1, keepdims=True)) * scale
         wa = jnp.exp2(sa * scale - top).astype(jnp.bfloat16)
         wb = jnp.exp2(sb * scale - top).astype(jnp.bfloat16)
-        both = jnp.dot(wa, va_ref[...], preferred_element_type=jnp.float32) + jnp.dot(
-            wb, vb_ref[...], preferred_element_type=jnp.float32
+        both = jnp.dot(wa, own_ref[:, HD:], preferred_element_type=jnp.float32) + jnp.dot(
+            wb, peer_ref[:, HD:], preferred_element_type=jnp.float32
         )
         total = both[:, HD:]
         out = (both[:, :HD] / total).astype(jnp.bfloat16)
@@ -106,27 +126,36 @@
             ).astype(jnp.bfloat16)
 
 
-def fresh_kernel(chips, capacity, place_ref, chosen_ref, q_ref, mine_ref, peer_ref, out_ref, lse_ref, match_ref):
+def fresh_kernel(chips, capacity, after_ref, chosen_hbm, q_hbm, w_hbm, kv_ref, out_ref, lse_ref, match_ref, w_ref, chosen_ref, q_ref, sems):
+    copies = fetch([(chosen_hbm, chosen_ref), (q_hbm, q_ref), (w_hbm, w_ref)], sems)
     tokens = q_ref.shape[0]
-    sources = mine_ref.shape[0]
+    sources = kv_ref.shape[0]
     per = capacity * tokens
-    core, first = place_ref[0], place_ref[1]
+    place = lax.axis_index("seq")
     scale = LOG2E * HD**-0.5
     nt = (((1,), (1,)), ((), ()))
-    shape = (GROUP * tokens, sources * tokens)
-    key_pos = lax.broadcasted_iota(jnp.int32, shape, 1)
-    query_pos = first + lax.broadcasted_iota(jnp.int32, shape, 0) % tokens
+    column = lax.broadcasted_iota(jnp.int32, (tokens, sources * tokens), 1)
+    source, bits = place, sources.bit_length() - 1
+    for i in range(bits):
+        source = source ^ ((column // (tokens << i) & 1) << (bits - 1 - i))
+    key_pos = source * tokens + column % tokens
+    query_pos = place * tokens + lax.broadcasted_iota(jnp.int32, column.shape, 0)
     visible = (key_pos <= query_pos) & (key_pos // BLK == query_pos // BLK)
+    visible = jnp.concatenate([visible.astype(jnp.int32)] * GROUP, axis=0) > 0
     lane = lax.broadcasted_iota(jnp.int32, (tokens, match_ref.shape[2]), 1)
     block, slot, token = lane // (per * chips), lane % per // tokens, lane % tokens
-    mine = mine_ref[...].astype(jnp.float32).reshape(sources, 2, tokens, HD)
-    peer = peer_ref[...].astype(jnp.float32).reshape(sources, 2, tokens, HD)
     ones = jnp.ones((sources * tokens, HD), jnp.bfloat16)
+    copies[0].wait()
+    copies[1].wait()
     for g in range(KVH):
         match_ref[g] = jnp.concatenate(slot_match(chosen_ref, g, block, slot, token), axis=0)
-        kv = jnp.where(core == g, mine, peer)
-        keys = kv[:, 0].reshape(sources * tokens, HD).astype(jnp.bfloat16)
-        values = kv[:, 1].reshape(sources * tokens, HD).astype(jnp.bfloat16)
+        keys, values = [
+            kv_ref[:, i, :, g * HD : (g + 1) * HD]
+            .astype(jnp.float32)
+            .reshape(sources * tokens, HD)
+            .astype(jnp.bfloat16)
+            for i in range(2)
+        ]
         q = jnp.concatenate(head_rows(q_ref, g), axis=0).astype(jnp.bfloat16)
         s = lax.dot_general(q, keys, nt, preferred_element_type=jnp.float32) * scale
         s = jnp.where(visible, s, LOW_SCORE)
@@ -136,6 +165,7 @@
         total = both[:, HD:]
         out_ref[g] = both[:, :HD] / total
         lse_ref[g] = top + jnp.log(total) * LOG2E
+    copies[2].wait()
 
 
 def project_kernel(per, hist_ref, out_ref, lse_ref, match_ref, w_ref, y_ref, att_ref):
@@ -178,7 +208,8 @@
 
 
 VMEM = pl.BlockSpec(memory_space=pltpu.VMEM)
-SMEM = pl.BlockSpec(memory_space=pltpu.SMEM)
+HBM = pl.BlockSpec(memory_space=pltpu.HBM)
+ANY = pl.BlockSpec(memory_space=pl.ANY)
 
 
 def call(kernel, name, out_shape, specs, *operands, scratch=(), flops=0, moved=0, limit=16):
@@ -197,7 +228,6 @@
 
 def body(queries, stretch_keys, stretch_values, cache_keys, cache_values, chosen, out_weight):
     devices = lax.axis_size("seq")
-    device_index = lax.axis_index("seq")
     tokens = queries.shape[0]
     cache_rows = cache_keys.shape[0]
     span = BLK // cache_rows
@@ -205,71 +235,91 @@
     key_blocks = cache_rows * devices // BLK
     capacity = (GROUP * TOPK + key_blocks - 1) // key_blocks + 1
     per = capacity * tokens
-    core = device_index % KVH
-    swap = [(i, i ^ 1) for i in range(devices)]
     f32, bf16 = jnp.float32, jnp.bfloat16
-
-    send = call(
+    picks = chosen.transpose(2, 0, 1)
+
+    def partner(bit):
+        return [(i, i ^ bit) for i in range(devices)]
+
+    send, fresh = call(
         functools.partial(pack_kernel, chips, capacity),
         "pack",
-        jax.ShapeDtypeStruct((devices, per + 2 * tokens, HD), bf16),
-        [SMEM, VMEM, VMEM, VMEM],
-        chosen, queries, stretch_keys, stretch_values,
+        (
+            jax.ShapeDtypeStruct((devices, per, HD), bf16),
+            jax.ShapeDtypeStruct((2, tokens, KVH * HD), bf16),
+        ),
+        [HBM] * 4,
+        picks, queries, stretch_keys, stretch_values,
+        scratch=[
+            pltpu.VMEM(picks.shape, jnp.int32),
+            pltpu.VMEM(queries.shape, bf16),
+            pltpu.SemaphoreType.DMA((4,)),
+        ],
+        limit=60,
     )
     got = lax.all_to_all(send, "seq", split_axis=0, concat_axis=0, tiled=True)
 
-    away = (1 - core) * HD
-    peer_cache = lax.ppermute(
-        jnp.stack(
-            [
-                lax.dynamic_slice_in_dim(cache_keys, away, HD, axis=1),
-                lax.dynamic_slice_in_dim(cache_values, away, HD, axis=1),
-            ]
-        ),
-        "seq",
-        swap,
-    )
-    place = jnp.stack([core, device_index * tokens]).astype(jnp.int32)
+    side = jax.ShapeDtypeStruct((cache_rows, 3 * HD), bf16)
+    own, away = call(
+        split_kernel,
+        "split",
+        (side, side),
+        [ANY, HBM, HBM],
+        fresh, cache_keys, cache_values,
+        scratch=[pltpu.SemaphoreType.DMA((4,))],
+        moved=4 << 20,
+    )
+    peer = lax.ppermute(away, "seq", partner(1))
+
+    gathered = fresh[None]
+    bit = devices // 2
+    while bit:
+        gathered = jnp.concatenate([gathered, lax.ppermute(gathered, "seq", partner(bit))], axis=0)
+        bit //= 2
     rows = devices * per
     back = call(
-        functools.partial(attend_kernel, per),
+        attend_kernel,
         "attend",
-        jax.ShapeDtypeStruct((devices, per + 16, HD), bf16),
-        [SMEM, VMEM, VMEM, VMEM, VMEM],
-        place, got, cache_keys, cache_values, peer_cache,
-        scratch=[pltpu.VMEM((cache_rows, 2 * HD), bf16)] * 2,
+        jax.ShapeDtypeStruct((devices, per + 8, HD), bf16),
+        [VMEM] * 3,
+        got, own, peer,
         flops=8 * rows * cache_rows * HD,
         moved=4 << 20,
         limit=32,
     )
     hist = lax.all_to_all(back, "seq", split_axis=0, concat_axis=0, tiled=True)
 
-    fresh = got[:, per:, :]
-    peer_fresh = lax.ppermute(fresh, "seq", swap)
     holders = devices // KVH
-    out, lse, match = call(
+    out, lse, match, weight = call(
         functools.partial(fresh_kernel, chips, capacity),
         "fresh",
         (
             jax.ShapeDtypeStruct((KVH, GROUP * tokens, HD), f32),
             jax.ShapeDtypeStruct((KVH, GROUP * tokens, HD), f32),
             jax.ShapeDtypeStruct((KVH, GROUP * tokens, holders * per), f32),
+            jax.ShapeDtypeStruct(out_weight.shape, bf16),
         ),
-        [SMEM, SMEM, VMEM, VMEM, VMEM],
-        place, chosen, queries, fresh, peer_fresh,
+        [ANY, HBM, HBM, HBM, VMEM],
+        back, picks, queries, out_weight, gathered,
+        scratch=[
+            pltpu.VMEM(picks.shape, jnp.int32),
+            pltpu.VMEM(queries.shape, bf16),
+            pltpu.SemaphoreType.DMA((3,)),
+        ],
         flops=8 * H * tokens * devices * tokens * HD,
-        moved=2 << 20,
+        moved=8 << 20,
+        limit=20,
     )
     return call(
         functools.partial(project_kernel, per),
         "project",
         jax.ShapeDtypeStruct((tokens, out_weight.shape[1]), bf16),
         [VMEM] * 5,
-        hist.reshape(holders, KVH, per + 16, HD), out, lse, match, out_weight,
+        hist.reshape(holders, KVH, per + 8, HD), out, lse, match, weight,
         scratch=[pltpu.VMEM((tokens, H * HD), f32)],
         flops=2 * tokens * out_weight.size,
         moved=out_weight.size * 2,
-        limit=24,
+        limit=20,
     )
 
 

time: 53 us -> 50.1 us (0.945)
  waiting for transfers between devices: 23.4 us -> 10.7 us
  starting transfers between devices: 10.6 us -> 16.2 us
  local copies, waits for them, and re-layouts: 8.88 us -> 11.1 us
  other arithmetic: 0.13 us -> 2.11 us
    all_to_all x1, waiting for transfers between devices: 10.6 us -> 0.01 us  [body(): hist = lax.all_to_all(back, 'seq', split_axis=0, concat_axis=0, tiled=True)]
    ppermute x2 -> x6, starting transfers between devices: 0.63 us -> 9.53 us  [the longest x5 9.01 us: body(): lax.ppermute(gathered, 'seq', partner(bit))]
    all_to_all x1, waiting for transfers between devices: 10.1 us -> 2.52 us  [body(): got = lax.all_to_all(send, 'seq', split_axis=0, concat_axis=0, tiled=True)]
    ppermute x2 -> x6, waiting for transfers between devices: 2.68 us -> 8.17 us  [the longest x5 8.16 us: body(): lax.ppermute(gathered, 'seq', partner(bit))]
    all_to_all x1, starting transfers between devices: 7.3 us -> 3.83 us  [body(): got = lax.all_to_all(send, 'seq', split_axis=0, concat_axis=0, tiled=True)]
    unnamed x15 -> x18, local copies, waits for them, and re-layouts: 7.8 us -> 11.1 us
    concatenate x0 -> x3, other arithmetic: none -> 2.11 us  [body(): jnp.concatenate([gathered, lax.ppermute(gathered, 'seq', partner(bit))],...]
    another operation x1 -> x0, local copies, waits for them, and re-layouts: 1.07 us -> none  [body(): jnp.stack([lax.dynamic_slice_in_dim(cache_keys, away, HD, axis=1), lax.dy...]
  transfers between devices with their start and end apart: 4 -> 8, of which waited for: 4 -> 4; matrix products, arithmetic and copies ran while one was open for 2% -> 6% of each run, Pallas kernels for 2% -> 10%
where the time goes in v2:
time: 50.1 us; the launch traced here: 49.5 us
  starting transfers between devices  16.2 us (32%)
  local copies, waits for them, and re-layouts  11.1 us (22%)
  waiting for transfers between devices  10.7 us (21%)
  Pallas kernels  9.21 us (18%)
  other arithmetic  2.11 us (4%)
    unnamed x18, local copies, waits for them, and re-layouts  11.1 us
    pallas_call x5, Pallas kernels, call(): pl.pallas_call(kernel, name=name, out_shape=out_shape, in_specs=specs, ou...  9.21 us
    ppermute x5, starting transfers between devices, body(): lax.ppermute(gathered, 'seq', partner(bit))  9.01 us
    ppermute x5, waiting for transfers between devices, body(): lax.ppermute(gathered, 'seq', partner(bit))  8.16 us
    all_to_all x1, starting transfers between devices, body(): got = lax.all_to_all(send, 'seq', split_axis=0, concat_axis=0, tiled=True)  3.83 us
    all_to_all x1, starting transfers between devices, body(): hist = lax.all_to_all(back, 'seq', split_axis=0, concat_axis=0, tiled=True)  2.86 us
    all_to_all x1, waiting for transfers between devices, body(): got = lax.all_to_all(send, 'seq', split_axis=0, concat_axis=0, tiled=True)  2.52 us
    concatenate x3, other arithmetic, body(): jnp.concatenate([gathered, lax.ppermute(gathered, 'seq', partner(bit))],...  2.11 us
  transfers between devices with their start and end apart: 8, of which 4 were waited for; matrix products, arithmetic and copies ran while one was open for 6% of the time, Pallas kernels for 10%

profile of v2, /device:TPU:0, one launch (start us, length us, event | category | flops | bytes accessed | tf_op | source)
XLA Modules:
  0.0 49.5 jit_solution(14834857317100567520)
XLA Ops:
  0.0 0.0 copy-start.6
  0.0 0.0 copy-start.5
  0.0 1.9 %pack.1 = (bf16[32,32,128]{2,1,0:T(8,128)(2,1)}, bf16[2,8,256]{2,1,0:T(8,128)(2,1)}) custom-call(s32[3,1,14]{2,1,0:T(1,128)} %bitcast.6, bf16[8,1792]{1,0:T(8,128)(2,1)} %q_hbm.3, bf16[8,256]{1,0:T(8,128)(2,1)} %k_hbm.2, bf16[8,256]{1,0:T(8,128)(2,1)} %v_hbm.2), custom_call_target="tpu_custom_call" | custom-call | tf_op jit(solution)/shard_map/pack/pallas_call | solution.py:217
  2.0 0.0 copy-start.3
  2.0 1.0 %copy-done.3 = bf16[1024,256]{1,0:T(8,128)(2,1)S(1)} copy-done((bf16[1024,256]{1,0:T(8,128)(2,1)S(1)}, bf16[1024,256]{1,0:T(8,128)(2,1)}, u32[]{:S(2)}) %copy-start.3) | copy-done | bytes 524312
  3.0 0.0 copy-start.4
  3.0 1.0 %copy-done.4 = bf16[1024,256]{1,0:T(8,128)(2,1)S(1)} copy-done((bf16[1024,256]{1,0:T(8,128)(2,1)S(1)}, bf16[1024,256]{1,0:T(8,128)(2,1)}, u32[]{:S(2)}) %copy-start.4) | copy-done | bytes 524312
  4.0 0.3 split.1
  4.3 0.5 %collective-permute-start = (bf16[1024,384]{1,0:T(8,128)(2,1)S(1)}, bf16[1024,384]{1,0:T(8,128)(2,1)S(1)}, u32[]{:S(2)}, u32[]{:S(2)}) collective-permute-start(bf16[1024,384]{1,0:T(8,128)(2,1)S(1)} %get-tuple-element.16), channel_id=1, source_target_pairs={{0,1},{1,0},{2,3},{3,2},{4,5},{5,4},{6,7},{7,6},{8,9},{9,8},{10,11... | collective-permute-start | bytes 2359304 | tf_op jit(solution)/shard_map/ppermute | solution.py:272
  4.9 3.7 %collective-permute-start.1 = (bf16[1,2,8,256]{3,2,1,0:T(8,128)(2,1)}, bf16[1,2,8,256]{3,2,1,0:T(8,128)(2,1)S(1)}, u32[]{:S(2)}, u32[]{:S(2)}) collective-permute-start(bf16[1,2,8,256]{3,2,1,0:T(8,128)(2,1)} %bitcast.2), channel_id=1, source_target_pairs={{0,16},{1,17},{2,18},{3,19},{4,20},{5,21},{6,22},{7,23},{8,24},{9,... | collective-permute-start | bytes 24584 | tf_op jit(solution)/shard_map/ppermute | solution.py:277
  8.5 3.8 %all-to-all-start = ((bf16[32,32,128]{2,1,0:T(8,128)(2,1)}), bf16[32,32,128]{2,1,0:T(8,128)(2,1)S(1)}, u32[]{:S(2)}, u32[]{:S(2)}) async-start(bf16[32,32,128]{2,1,0:T(8,128)(2,1)} %get-tuple-element.13), calls=%async_computation | async-start | bytes 524288 | tf_op jit(solution)/shard_map/all_to_all | solution.py:260
  12.4 0.7 %constant_dynamic-update-slice_fusion.4 = (bf16[16,2,8,256]{3,2,1,0:T(8,128)(2,1)S(1)}, bf16[32,2,8,256]{3,2,1,0:T(8,128)(2,1)S(1)}) fusion(bf16[2,8,256]{2,1,0:T(8,128)(2,1)} %get-tuple-element.14.after_ref), kind=kLoop, calls=%fused_computation.6 | loop fusion | bytes 24576
  13.1 0.0 collective-permute-done.1
  13.1 0.7 %pad_maximum_fusion.2 = bf16[2,2,8,256]{3,2,1,0:T(8,128)(2,1)S(1)} fusion(bf16[1,2,8,256]{3,2,1,0:T(8,128)(2,1)S(1)} %collective-permute-done.1, bf16[1,2,8,256]{3,2,1,0:T(8,128)(2,1)} %bitcast.2), kind=kLoop, calls=%fused_computation.13 | loop fusion | flops 8192 | bytes 32768 | tf_op jit(solution)/shard_map/concatenate | solution.py:277
  13.8 1.8 %collective-permute-start.2 = (bf16[2,2,8,256]{3,2,1,0:T(8,128)(2,1)S(1)}, bf16[2,2,8,256]{3,2,1,0:T(8,128)(2,1)S(1)}, u32[]{:S(2)}, u32[]{:S(2)}) collective-permute-start(bf16[2,2,8,256]{3,2,1,0:T(8,128)(2,1)S(1)} %pad_maximum_fusion.2), channel_id=1, source_target_pairs={{0,8},{1,9},{2,10},{3,11},{4,12},{5,13},{6,14},{7,15},{8,0},{9,1},... | collective-permute-start | bytes 49160 | tf_op jit(solution)/shard_map/ppermute | solution.py:277
  15.5 2.4 %collective-permute-done.2 = bf16[2,2,8,256]{3,2,1,0:T(8,128)(2,1)S(1)} collective-permute-done((bf16[2,2,8,256]{3,2,1,0:T(8,128)(2,1)S(1)}, bf16[2,2,8,256]{3,2,1,0:T(8,128)(2,1)S(1)}, u32[]{:S(2)}, u32[]{:S(2)}) %collective-permute-start.2) | collective-permute-done | bytes 16416 | tf_op jit(solution)/shard_map/ppermute | solution.py:277
  17.9 0.7 %pad_maximum_fusion.1 = bf16[4,2,8,256]{3,2,1,0:T(8,128)(2,1)S(1)} fusion(bf16[2,2,8,256]{3,2,1,0:T(8,128)(2,1)S(1)} %collective-permute-done.2, bf16[1,2,8,256]{3,2,1,0:T(8,128)(2,1)S(1)} %collective-permute-done.1, bf16[1,2,8,256]{3,2,1,0:T(8,128)(2,1)} %bitcast.2), kind=kLoop, calls=%fused_computation.1 | loop fusion | flops 32768 | bytes 65536 | tf_op jit(solution)/shard_map/concatenate | solution.py:277
  18.6 1.7 %collective-permute-start.3 = (bf16[4,2,8,256]{3,2,1,0:T(8,128)(2,1)S(1)}, bf16[4,2,8,256]{3,2,1,0:T(8,128)(2,1)S(1)}, u32[]{:S(2)}, u32[]{:S(2)}) collective-permute-start(bf16[4,2,8,256]{3,2,1,0:T(8,128)(2,1)S(1)} %pad_maximum_fusion.1), channel_id=1, source_target_pairs={{0,4},{1,5},{2,6},{3,7},{4,0},{5,1},{6,2},{7,3},{8,12},{9,13},{10,... | collective-permute-start | bytes 98312 | tf_op jit(solution)/shard_map/ppermute | solution.py:277
  20.3 2.5 %all-to-all-done.q_ref = bf16[32,32,128]{2,1,0:T(8,128)(2,1)S(1)} async-done(((bf16[32,32,128]{2,1,0:T(8,128)(2,1)}), bf16[32,32,128]{2,1,0:T(8,128)(2,1)S(1)}, u32[]{:S(2)}, u32[]{:S(2)}) %all-to-all-start) | async-done | bytes 262176 | tf_op jit(solution)/shard_map/all_to_all | solution.py:260
  22.8 0.0 collective-permute-done.peer_ref
  22.8 3.9 %attend.1.after_ref = bf16[32,40,128]{2,1,0:T(8,128)(2,1)} custom-call(bf16[32,32,128]{2,1,0:T(8,128)(2,1)S(1)} %all-to-all-done.q_ref, bf16[1024,384]{1,0:T(8,128)(2,1)S(1)} %get-tuple-element.15.own_ref, bf16[1024,384]{1,0:T(8,128)(2,1)S(1)} %collective-permute-done.peer_ref), custom_call_target="tpu_custom_call" | custom-call | flops 1073741824 | bytes 4194304 | tf_op jit(solution)/shard_map/attend/pallas_call | solution.py:217
  26.7 2.9 %all-to-all-start.1 = ((bf16[32,40,128]{2,1,0:T(8,128)(2,1)}), bf16[32,40,128]{2,1,0:T(8,128)(2,1)S(1)}, u32[]{:S(2)}, u32[]{:S(2)}) async-start(bf16[32,40,128]{2,1,0:T(8,128)(2,1)} %attend.1.after_ref), calls=%async_computation.1 | async-start | bytes 655360 | tf_op jit(solution)/shard_map/all_to_all | solution.py:290
  29.6 0.0 collective-permute-done.3
  29.6 0.7 %pad_maximum_fusion = bf16[8,2,8,256]{3,2,1,0:T(8,128)(2,1)S(1)} fusion(bf16[4,2,8,256]{3,2,1,0:T(8,128)(2,1)S(1)} %collective-permute-done.3, bf16[2,2,8,256]{3,2,1,0:T(8,128)(2,1)S(1)} %collective-permute-done.2, bf16[1,2,8,256]{3,2,1,0:T(8,128)(2,1)S(1)} %collective-permute-done.1, bf16[1,2,8,256]{3,2,1,0:T(8,128)(2,1)} %bitcast.2), kind=kLoop, calls=%fused_computation | loop fusion | flops 98304 | bytes 131072 | tf_op jit(solution)/shard_map/concatenate | solution.py:277
  30.3 1.8 %collective-permute-start.4 = (bf16[8,2,8,256]{3,2,1,0:T(8,128)(2,1)S(1)}, bf16[8,2,8,256]{3,2,1,0:T(8,128)(2,1)S(1)}, u32[]{:S(2)}, u32[]{:S(2)}) collective-permute-start(bf16[8,2,8,256]{3,2,1,0:T(8,128)(2,1)S(1)} %pad_maximum_fusion), channel_id=1, source_target_pairs={{0,2},{1,3},{2,0},{3,1},{4,6},{5,7},{6,4},{7,5},{8,10},{9,11},{10,... | collective-permute-start | bytes 196616 | tf_op jit(solution)/shard_map/ppermute | solution.py:277
  32.2 4.4 %collective-permute-done.4 = bf16[8,2,8,256]{3,2,1,0:T(8,128)(2,1)S(1)} collective-permute-done((bf16[8,2,8,256]{3,2,1,0:T(8,128)(2,1)S(1)}, bf16[8,2,8,256]{3,2,1,0:T(8,128)(2,1)S(1)}, u32[]{:S(2)}, u32[]{:S(2)}) %collective-permute-start.4) | collective-permute-done | bytes 65568 | tf_op jit(solution)/shard_map/ppermute | solution.py:277
  36.6 0.1 collective-permute-start.5
  36.7 1.3 %collective-permute-done.5 = bf16[16,2,8,256]{3,2,1,0:T(8,128)(2,1)S(1)} collective-permute-done((bf16[16,2,8,256]{3,2,1,0:T(8,128)(2,1)S(1)}, bf16[16,2,8,256]{3,2,1,0:T(8,128)(2,1)S(1)}, u32[]{:S(2)}, u32[]{:S(2)}) %collective-permute-start.5) | collective-permute-done | bytes 131104 | tf_op jit(solution)/shard_map/ppermute | solution.py:277
  38.0 0.0 copy-done.6
  38.0 0.0 copy-done.5
  38.1 0.0 copy-start
  38.1 2.8 %copy-done = bf16[1792,1792]{1,0:T(8,128)(2,1)S(1)} copy-done((bf16[1792,1792]{1,0:T(8,128)(2,1)S(1)}, bf16[1792,1792]{1,0:T(8,128)(2,1)}, u32[]{:S(2)}) %copy-start) | copy-done | bytes 6422552
  40.9 1.1 %fresh.1 = (f32[2,56,128]{2,1,0:T(8,128)S(1)}, f32[2,56,128]{2,1,0:T(8,128)S(1)}, f32[2,56,512]{2,1,0:T(8,128)S(1)}, bf16[1792,1792]{1,0:T(8,128)(2,1)S(1)}) custom-call(bf16[32,40,128]{2,1,0:T(8,128)(2,1)} %attend.1.after_ref, s32[3,1,14]{2,1,0:T(1,128)S(1)} %bitcast.7, bf16[8,1792]{1,0:T(8,128)(2,1)S(1)} %copy-done.5, bf16[1792,1792]{1,0:T(8,128)(2,1)S(1)} %copy-done, ...), custom_call_target="tpu_custom_call" | custom-call | flops 29360128 | bytes 8388608 | tf_op jit(solution)/shard_map/fresh/pallas_call | solution.py:217
  42.0 0.0 copy-start.1
  42.0 2.7 %copy-done.1 = bf16[1792,1792]{1,0:T(8,128)(2,1)} copy-done((bf16[1792,1792]{1,0:T(8,128)(2,1)}, bf16[1792,1792]{1,0:T(8,128)(2,1)S(1)}, u32[]{:S(2)}) %copy-start.1) | copy-done | bytes 6422552
  44.6 0.0 all-to-all-done.1
  44.6 0.0 copy-start.2
  44.6 2.8 %copy-done.2 = bf16[1792,1792]{1,0:T(8,128)(2,1)S(1)} copy-done((bf16[1792,1792]{1,0:T(8,128)(2,1)S(1)}, bf16[1792,1792]{1,0:T(8,128)(2,1)}, u32[]{:S(2)}) %copy-start.2) | copy-done | bytes 6422552
  47.5 2.0 %project.1 = bf16[8,1792]{1,0:T(8,128)(2,1)} custom-call(bf16[16,2,40,128]{3,2,1,0:T(8,128)(2,1)S(1)} %bitcast.5, f32[2,56,128]{2,1,0:T(8,128)S(1)} %get-tuple-element.17.out_ref, f32[2,56,128]{2,1,0:T(8,128)S(1)} %get-tuple-element.18.lse_ref, f32[2,56,512]{2,1,0:T(8,128)S(1)} %get-tuple-element.19.match_ref, bf16[1792,1792]{1,0:T(8,128)(2,1)S(1)} %copy-done.2), custom_call_target="tpu_custom_call" | custom-call | flops 51380224 | bytes 6422528 | tf_op jit(solution)/shard_map/project/pallas_call | solution.py:217
  (5 shorter events, 0.0 us)
Async XLA Ops:
  0.0 38.0 %copy-start.6 = (s32[1,14,3]{1,0,2:T(1,128)S(1)}, s32[1,14,3]{1,0,2:T(1,128)}, u32[]{:S(2)}) copy-start(s32[1,14,3]{1,0,2:T(1,128)} %param.12) | copy-start | bytes 508
  0.0 38.0 %copy-start.5 = (bf16[8,1792]{1,0:T(8,128)(2,1)S(1)}, bf16[8,1792]{1,0:T(8,128)(2,1)}, u32[]{:S(2)}) copy-start(bf16[8,1792]{1,0:T(8,128)(2,1)} %q_hbm.3) | copy-start | bytes 86020
  2.0 1.0 %copy-start.3 = (bf16[1024,256]{1,0:T(8,128)(2,1)S(1)}, bf16[1024,256]{1,0:T(8,128)(2,1)}, u32[]{:S(2)}) copy-start(bf16[1024,256]{1,0:T(8,128)(2,1)} %k_hbm.3) | copy-start | bytes 1572868
  3.0 1.0 %copy-start.4 = (bf16[1024,256]{1,0:T(8,128)(2,1)S(1)}, bf16[1024,256]{1,0:T(8,128)(2,1)}, u32[]{:S(2)}) copy-start(bf16[1024,256]{1,0:T(8,128)(2,1)} %v_hbm.3) | copy-start | bytes 1572868
  4.3 18.5 %collective-permute-start = (bf16[1024,384]{1,0:T(8,128)(2,1)S(1)}, bf16[1024,384]{1,0:T(8,128)(2,1)S(1)}, u32[]{:S(2)}, u32[]{:S(2)}) collective-permute-start(bf16[1024,384]{1,0:T(8,128)(2,1)S(1)} %get-tuple-element.16), channel_id=1, source_target_pairs={{0,1},{1,0},{2,3},{3,2},{4,5},{5,4},{6,7},{7,6},{8,9},{9,8},{10,11... | collective-permute-start | bytes 2359304 | tf_op jit(solution)/shard_map/ppermute | solution.py:272
  4.9 8.2 %collective-permute-start.1 = (bf16[1,2,8,256]{3,2,1,0:T(8,128)(2,1)}, bf16[1,2,8,256]{3,2,1,0:T(8,128)(2,1)S(1)}, u32[]{:S(2)}, u32[]{:S(2)}) collective-permute-start(bf16[1,2,8,256]{3,2,1,0:T(8,128)(2,1)} %bitcast.2), channel_id=1, source_target_pairs={{0,16},{1,17},{2,18},{3,19},{4,20},{5,21},{6,22},{7,23},{8,24},{9,... | collective-permute-start | bytes 24584 | tf_op jit(solution)/shard_map/ppermute | solution.py:277
  8.5 14.3 %all-to-all-start = ((bf16[32,32,128]{2,1,0:T(8,128)(2,1)}), bf16[32,32,128]{2,1,0:T(8,128)(2,1)S(1)}, u32[]{:S(2)}, u32[]{:S(2)}) async-start(bf16[32,32,128]{2,1,0:T(8,128)(2,1)} %get-tuple-element.13), calls=%async_computation | async-start | bytes 524288 | tf_op jit(solution)/shard_map/all_to_all | solution.py:260
  13.8 4.2 %collective-permute-start.2 = (bf16[2,2,8,256]{3,2,1,0:T(8,128)(2,1)S(1)}, bf16[2,2,8,256]{3,2,1,0:T(8,128)(2,1)S(1)}, u32[]{:S(2)}, u32[]{:S(2)}) collective-permute-start(bf16[2,2,8,256]{3,2,1,0:T(8,128)(2,1)S(1)} %pad_maximum_fusion.2), channel_id=1, source_target_pairs={{0,8},{1,9},{2,10},{3,11},{4,12},{5,13},{6,14},{7,15},{8,0},{9,1},... | collective-permute-start | bytes 49160 | tf_op jit(solution)/shard_map/ppermute | solution.py:277
  18.6 11.0 %collective-permute-start.3 = (bf16[4,2,8,256]{3,2,1,0:T(8,128)(2,1)S(1)}, bf16[4,2,8,256]{3,2,1,0:T(8,128)(2,1)S(1)}, u32[]{:S(2)}, u32[]{:S(2)}) collective-permute-start(bf16[4,2,8,256]{3,2,1,0:T(8,128)(2,1)S(1)} %pad_maximum_fusion.1), channel_id=1, source_target_pairs={{0,4},{1,5},{2,6},{3,7},{4,0},{5,1},{6,2},{7,3},{8,12},{9,13},{10,... | collective-permute-start | bytes 98312 | tf_op jit(solution)/shard_map/ppermute | solution.py:277
  26.7 17.9 %all-to-all-start.1 = ((bf16[32,40,128]{2,1,0:T(8,128)(2,1)}), bf16[32,40,128]{2,1,0:T(8,128)(2,1)S(1)}, u32[]{:S(2)}, u32[]{:S(2)}) async-start(bf16[32,40,128]{2,1,0:T(8,128)(2,1)} %attend.1.after_ref), calls=%async_computation.1 | async-start | bytes 655360 | tf_op jit(solution)/shard_map/all_to_all | solution.py:290
  30.3 6.3 %collective-permute-start.4 = (bf16[8,2,8,256]{3,2,1,0:T(8,128)(2,1)S(1)}, bf16[8,2,8,256]{3,2,1,0:T(8,128)(2,1)S(1)}, u32[]{:S(2)}, u32[]{:S(2)}) collective-permute-start(bf16[8,2,8,256]{3,2,1,0:T(8,128)(2,1)S(1)} %pad_maximum_fusion), channel_id=1, source_target_pairs={{0,2},{1,3},{2,0},{3,1},{4,6},{5,7},{6,4},{7,5},{8,10},{9,11},{10,... | collective-permute-start | bytes 196616 | tf_op jit(solution)/shard_map/ppermute | solution.py:277
  36.6 1.4 %collective-permute-start.5 = (bf16[16,2,8,256]{3,2,1,0:T(8,128)(2,1)S(1)}, bf16[16,2,8,256]{3,2,1,0:T(8,128)(2,1)S(1)}, u32[]{:S(2)}, u32[]{:S(2)}) collective-permute-start(bf16[16,2,8,256]{3,2,1,0:T(8,128)(2,1)S(1)} %get-tuple-element.21), channel_id=1, source_target_pairs={{0,1},{1,0},{2,3},{3,2},{4,5},{5,4},{6,7},{7,6},{8,9},{9,8},{10,11... | collective-permute-start | bytes 393224 | tf_op jit(solution)/shard_map/ppermute | solution.py:277
  38.1 2.8 %copy-start = (bf16[1792,1792]{1,0:T(8,128)(2,1)S(1)}, bf16[1792,1792]{1,0:T(8,128)(2,1)}, u32[]{:S(2)}) copy-start(bf16[1792,1792]{1,0:T(8,128)(2,1)} %w_hbm.1) | copy-start | bytes 19267588
  42.0 2.7 %copy-start.1 = (bf16[1792,1792]{1,0:T(8,128)(2,1)}, bf16[1792,1792]{1,0:T(8,128)(2,1)S(1)}, u32[]{:S(2)}) copy-start(bf16[1792,1792]{1,0:T(8,128)(2,1)S(1)} %get-tuple-element.20.w_ref) | copy-start | bytes 19267588
  44.6 2.8 %copy-start.2 = (bf16[1792,1792]{1,0:T(8,128)(2,1)S(1)}, bf16[1792,1792]{1,0:T(8,128)(2,1)}, u32[]{:S(2)}) copy-start(bf16[1792,1792]{1,0:T(8,128)(2,1)} %copy-done.1) | copy-start | bytes 19267588

commit v3 on v2

--- a/solution.py
+++ b/solution.py
@@ -46,10 +46,8 @@
     return copies
 
 
-def pack_kernel(chips, capacity, chosen_hbm, q_hbm, k_hbm, v_hbm, send_ref, fresh_ref, chosen_ref, q_ref, sems):
-    copies = fetch(
-        [(chosen_hbm, chosen_ref), (q_hbm, q_ref), (k_hbm, fresh_ref.at[0]), (v_hbm, fresh_ref.at[1])], sems
-    )
+def pack_kernel(chips, capacity, chosen_hbm, q_hbm, k_hbm, v_hbm, send_ref, chosen_ref, q_ref, k_ref, v_ref, sems):
+    copies = fetch([(chosen_hbm, chosen_ref), (q_hbm, q_ref), (k_hbm, k_ref), (v_hbm, v_ref)], sems)
     tokens = q_ref.shape[0]
     per = capacity * tokens
     span = chips * KVH
@@ -67,33 +65,18 @@
         slots = jnp.dot(
             spread.T.astype(jnp.bfloat16), rows.astype(jnp.bfloat16), preferred_element_type=jnp.float32
         ).astype(jnp.bfloat16)
+        cols = slice(g * HD, (g + 1) * HD)
+        fresh = [k_ref[:, cols], v_ref[:, cols]]
         for b in range(key_blocks):
             for chip in range(chips):
-                send_ref[b * span + chip * KVH + g] = slots[b * per : (b + 1) * per]
-
-
-def split_kernel(after_ref, k_hbm, v_hbm, own_ref, away_ref, sems):
-    core = lax.axis_index("seq") % KVH
-    own = pl.ds(pl.multiple_of(core * HD, HD), HD)
-    away = pl.ds(pl.multiple_of((1 - core) * HD, HD), HD)
-    copies = fetch(
-        [
-            (k_hbm.at[:, away], away_ref.at[:, :HD]),
-            (v_hbm.at[:, away], away_ref.at[:, HD : 2 * HD]),
-            (k_hbm.at[:, own], own_ref.at[:, :HD]),
-            (v_hbm.at[:, own], own_ref.at[:, HD : 2 * HD]),
-        ],
-        sems,
-    )
-    ones = jnp.ones((own_ref.shape[0], HD), jnp.bfloat16)
-    own_ref[:, 2 * HD :] = ones
-    away_ref[:, 2 * HD :] = ones
-    for copy in copies:
-        copy.wait()
-
-
-def attend_kernel(q_ref, own_ref, peer_ref, out_ref):
-    sources, per = q_ref.shape[:2]
+                to = b * span + chip * KVH + g
+                send_ref[to, :per, :] = slots[b * per : (b + 1) * per]
+                send_ref[to, per:, :] = fresh[chip % 2]
+
+
+def attend_kernel(per, q_ref, own_ref, peer_ref, out_ref, fresh_ref):
+    sources = q_ref.shape[0]
+    fresh_ref[...] = q_ref[:, per:, :]
     step = 256 // per
     scale = LOG2E * HD**-0.5
     nt = (((1,), (1,)), ((), ()))
@@ -102,7 +85,7 @@
     diagonal = row == lane % per
     piece = lax.broadcasted_iota(jnp.int32, (8, LANES), 0)
     for first in range(0, sources, step):
-        q = q_ref[first : first + step].reshape(step * per, HD)
+        q = q_ref[first : first + step, :per, :].reshape(step * per, HD)
         sa = lax.dot_general(q, own_ref[:, :HD], nt, preferred_element_type=jnp.float32)
         sb = lax.dot_general(q, peer_ref[:, :HD], nt, preferred_element_type=jnp.float32)
         top = jnp.maximum(jnp.max(sa, axis=1, keepdims=True), jnp.max(sb, axis=1, keepdims=True)) * scale
@@ -126,49 +109,48 @@
             ).astype(jnp.bfloat16)
 
 
-def fresh_kernel(chips, capacity, after_ref, chosen_hbm, q_hbm, w_hbm, kv_ref, out_ref, lse_ref, match_ref, w_ref, chosen_ref, q_ref, sems):
-    copies = fetch([(chosen_hbm, chosen_ref), (q_hbm, q_ref), (w_hbm, w_ref)], sems)
+def fresh_kernel(chips, capacity, chosen_hbm, q_hbm, kv_ref, kv1_ref, kv2_ref, kv3_ref, out_ref, lse_ref, match_ref, chosen_ref, q_ref, sems):
+    copies = fetch([(chosen_hbm, chosen_ref), (q_hbm, q_ref)], sems)
     tokens = q_ref.shape[0]
     sources = kv_ref.shape[0]
     per = capacity * tokens
     place = lax.axis_index("seq")
+    core, odd = place % KVH, place // KVH % 2
     scale = LOG2E * HD**-0.5
     nt = (((1,), (1,)), ((), ()))
     column = lax.broadcasted_iota(jnp.int32, (tokens, sources * tokens), 1)
-    source, bits = place, sources.bit_length() - 1
-    for i in range(bits):
-        source = source ^ ((column // (tokens << i) & 1) << (bits - 1 - i))
-    key_pos = source * tokens + column % tokens
     query_pos = place * tokens + lax.broadcasted_iota(jnp.int32, column.shape, 0)
-    visible = (key_pos <= query_pos) & (key_pos // BLK == query_pos // BLK)
+    visible = (column <= query_pos) & (column // BLK == query_pos // BLK)
     visible = jnp.concatenate([visible.astype(jnp.int32)] * GROUP, axis=0) > 0
     lane = lax.broadcasted_iota(jnp.int32, (tokens, match_ref.shape[2]), 1)
     block, slot, token = lane // (per * chips), lane % per // tokens, lane % tokens
     ones = jnp.ones((sources * tokens, HD), jnp.bfloat16)
-    copies[0].wait()
-    copies[1].wait()
+    here, near, far, both = [
+        ref[...].astype(jnp.float32).reshape(sources * tokens, HD) for ref in (kv_ref, kv1_ref, kv2_ref, kv3_ref)
+    ]
+    keys = [jnp.where(odd == 0, here, far), jnp.where(odd == 0, near, both)]
+    values = [jnp.where(odd == 0, far, here), jnp.where(odd == 0, both, near)]
+    for copy in copies:
+        copy.wait()
     for g in range(KVH):
         match_ref[g] = jnp.concatenate(slot_match(chosen_ref, g, block, slot, token), axis=0)
-        keys, values = [
-            kv_ref[:, i, :, g * HD : (g + 1) * HD]
-            .astype(jnp.float32)
-            .reshape(sources * tokens, HD)
-            .astype(jnp.bfloat16)
-            for i in range(2)
-        ]
+        k = jnp.where(core == g, keys[0], keys[1]).astype(jnp.bfloat16)
+        v = jnp.where(core == g, values[0], values[1]).astype(jnp.bfloat16)
         q = jnp.concatenate(head_rows(q_ref, g), axis=0).astype(jnp.bfloat16)
-        s = lax.dot_general(q, keys, nt, preferred_element_type=jnp.float32) * scale
+        s = lax.dot_general(q, k, nt, preferred_element_type=jnp.float32) * scale
         s = jnp.where(visible, s, LOW_SCORE)
         top = jnp.max(s, axis=1, keepdims=True)
         w = jnp.where(visible, jnp.exp2(s - top), 0.0).astype(jnp.bfloat16)
-        both = jnp.dot(w, jnp.concatenate([values, ones], axis=1), preferred_element_type=jnp.float32)
-        total = both[:, HD:]
-        out_ref[g] = both[:, :HD] / total
+        total_out = jnp.dot(w, jnp.concatenate([v, ones], axis=1), preferred_element_type=jnp.float32)
+        total = total_out[:, HD:]
+        out_ref[g] = total_out[:, :HD] / total
         lse_ref[g] = top + jnp.log(total) * LOG2E
-    copies[2].wait()
-
-
-def project_kernel(per, hist_ref, out_ref, lse_ref, match_ref, w_ref, y_ref, att_ref):
+
+
+def project_kernel(per, hist_ref, out_ref, lse_ref, match_ref, w_hbm, y_ref, att_ref, w_ref, sems):
+    depth = w_ref.shape[0] // GROUP
+    chunks = [pl.ds(i * depth, depth) for i in range(GROUP)]
+    copies = fetch([(w_hbm.at[chunk], w_ref.at[chunk]) for chunk in chunks], sems)
     tokens = y_ref.shape[0]
     holders = hist_ref.shape[0]
     fold = LANES // per
@@ -202,14 +184,16 @@
         for r in range(GROUP):
             h = g * GROUP + r
             att_ref[:, h * HD : (h + 1) * HD] = att[r * tokens : (r + 1) * tokens]
-    y_ref[...] = jnp.dot(
-        att_ref[...].astype(jnp.bfloat16), w_ref[...], preferred_element_type=jnp.float32
-    ).astype(jnp.bfloat16)
+    y = jnp.zeros(y_ref.shape, jnp.float32)
+    for chunk, copy in zip(chunks, copies):
+        att = att_ref[:, chunk].astype(jnp.bfloat16)
+        copy.wait()
+        y = y + jnp.dot(att, w_ref[chunk, :], preferred_element_type=jnp.float32)
+    y_ref[...] = y.astype(jnp.bfloat16)
 
 
 VMEM = pl.BlockSpec(memory_space=pltpu.VMEM)
 HBM = pl.BlockSpec(memory_space=pltpu.HBM)
-ANY = pl.BlockSpec(memory_space=pl.ANY)
 
 
 def call(kernel, name, out_shape, specs, *operands, scratch=(), flops=0, moved=0, limit=16):
@@ -241,46 +225,41 @@
     def partner(bit):
         return [(i, i ^ bit) for i in range(devices)]
 
-    send, fresh = call(
+    send = call(
         functools.partial(pack_kernel, chips, capacity),
         "pack",
-        (
-            jax.ShapeDtypeStruct((devices, per, HD), bf16),
-            jax.ShapeDtypeStruct((2, tokens, KVH * HD), bf16),
-        ),
+        jax.ShapeDtypeStruct((devices, per + tokens, HD), bf16),
         [HBM] * 4,
         picks, queries, stretch_keys, stretch_values,
         scratch=[
             pltpu.VMEM(picks.shape, jnp.int32),
             pltpu.VMEM(queries.shape, bf16),
+            pltpu.VMEM(stretch_keys.shape, bf16),
+            pltpu.VMEM(stretch_values.shape, bf16),
             pltpu.SemaphoreType.DMA((4,)),
         ],
         limit=60,
     )
     got = lax.all_to_all(send, "seq", split_axis=0, concat_axis=0, tiled=True)
 
-    side = jax.ShapeDtypeStruct((cache_rows, 3 * HD), bf16)
-    own, away = call(
-        split_kernel,
-        "split",
-        (side, side),
-        [ANY, HBM, HBM],
-        fresh, cache_keys, cache_values,
-        scratch=[pltpu.SemaphoreType.DMA((4,))],
-        moved=4 << 20,
-    )
-    peer = lax.ppermute(away, "seq", partner(1))
-
-    gathered = fresh[None]
-    bit = devices // 2
-    while bit:
-        gathered = jnp.concatenate([gathered, lax.ppermute(gathered, "seq", partner(bit))], axis=0)
-        bit //= 2
+    core = lax.axis_index("seq") % KVH
+    ones = jnp.ones((cache_rows, HD), bf16)
+
+    def side(head):
+        columns = [lax.dynamic_slice_in_dim(x, head * HD, HD, axis=1) for x in (cache_keys, cache_values)]
+        return jnp.concatenate(columns + [ones], axis=1)
+
+    own = side(core)
+    peer = lax.ppermute(side(1 - core), "seq", partner(1))
+
     rows = devices * per
-    back = call(
-        attend_kernel,
+    back, fresh = call(
+        functools.partial(attend_kernel, per),
         "attend",
-        jax.ShapeDtypeStruct((devices, per + 8, HD), bf16),
+        (
+            jax.ShapeDtypeStruct((devices, per + 8, HD), bf16),
+            jax.ShapeDtypeStruct((devices, tokens, HD), bf16),
+        ),
         [VMEM] * 3,
         got, own, peer,
         flops=8 * rows * cache_rows * HD,
@@ -290,36 +269,39 @@
     hist = lax.all_to_all(back, "seq", split_axis=0, concat_axis=0, tiled=True)
 
     holders = devices // KVH
-    out, lse, match, weight = call(
+    out, lse, match = call(
         functools.partial(fresh_kernel, chips, capacity),
         "fresh",
         (
             jax.ShapeDtypeStruct((KVH, GROUP * tokens, HD), f32),
             jax.ShapeDtypeStruct((KVH, GROUP * tokens, HD), f32),
             jax.ShapeDtypeStruct((KVH, GROUP * tokens, holders * per), f32),
-            jax.ShapeDtypeStruct(out_weight.shape, bf16),
         ),
-        [ANY, HBM, HBM, HBM, VMEM],
-        back, picks, queries, out_weight, gathered,
+        [HBM, HBM, VMEM, VMEM, VMEM, VMEM],
+        picks, queries, fresh, *[lax.ppermute(fresh, "seq", partner(bit)) for bit in (1, 2, 3)],
         scratch=[
             pltpu.VMEM(picks.shape, jnp.int32),
             pltpu.VMEM(queries.shape, bf16),
-            pltpu.SemaphoreType.DMA((3,)),
+            pltpu.SemaphoreType.DMA((2,)),
         ],
         flops=8 * H * tokens * devices * tokens * HD,
-        moved=8 << 20,
+        moved=2 << 20,
         limit=20,
     )
     return call(
         functools.partial(project_kernel, per),
         "project",
         jax.ShapeDtypeStruct((tokens, out_weight.shape[1]), bf16),
-        [VMEM] * 5,
-        hist.reshape(holders, KVH, per + 8, HD), out, lse, match, weight,
-        scratch=[pltpu.VMEM((tokens, H * HD), f32)],
+        [VMEM] * 4 + [HBM],
+        hist.reshape(holders, KVH, per + 8, HD), out, lse, match, out_weight,
+        scratch=[
+            pltpu.VMEM((tokens, H * HD), f32),
+            pltpu.VMEM(out_weight.shape, bf16),
+            pltpu.SemaphoreType.DMA((GROUP,)),
+        ],
         flops=2 * tokens * out_weight.size,
         moved=out_weight.size * 2,
-        limit=20,
+        limit=58,
     )
 
 

time: 50.1 us -> 47.4 us (0.946)
  blocking collectives: 0 us -> 19 us
  starting transfers between devices: 16.2 us -> 5.06 us
  local copies, waits for them, and re-layouts: 11.1 us -> 3.91 us
  waiting for transfers between devices: 10.7 us -> 7.56 us
  Pallas kernels: 9.21 us -> 11.2 us
  other arithmetic: 2.11 us -> 0.3 us
    all_to_all x0 -> x1, blocking collectives: none -> 19 us  [body(): got = lax.all_to_all(send, 'seq', split_axis=0, concat_axis=0, tiled=True)]
    unnamed x18 -> x12, local copies, waits for them, and re-layouts: 11.1 us -> 2.63 us
    ppermute x6 -> x4, starting transfers between devices: 9.53 us -> 2.47 us  [the longest x3 1.96 us: body(): lax.ppermute(fresh, 'seq', partner(bit))]
    all_to_all x1 -> x0, starting transfers between devices: 3.83 us -> none  [body(): got = lax.all_to_all(send, 'seq', split_axis=0, concat_axis=0, tiled=True)]
    all_to_all x1 -> x0, waiting for transfers between devices: 2.52 us -> none  [body(): got = lax.all_to_all(send, 'seq', split_axis=0, concat_axis=0, tiled=True)]
    ppermute x6 -> x4, waiting for transfers between devices: 8.17 us -> 5.73 us  [the longest x3 5.73 us: body(): lax.ppermute(fresh, 'seq', partner(bit))]
    pallas_call x5 -> x4, Pallas kernels: 9.21 us -> 11.2 us  [call(): pl.pallas_call(kernel, name=name, out_shape=out_shape, in_specs=specs, ou...]
    all_to_all x1, waiting for transfers between devices: 0.01 us -> 1.83 us  [body(): hist = lax.all_to_all(back, 'seq', split_axis=0, concat_axis=0, tiled=True)]
  transfers between devices with their start and end apart: 8 -> 5, of which waited for: 4 -> 3; matrix products, arithmetic and copies ran while one was open for 6% -> 0% of each run, Pallas kernels for 10% -> 5%
where the time goes in v3:
time: 47.4 us; the launch traced here: 47 us
  blocking collectives  19 us (40%)
  Pallas kernels  11.2 us (24%)
  waiting for transfers between devices  7.56 us (16%)
  starting transfers between devices  5.06 us (11%)
  local copies, waits for them, and re-layouts  3.91 us (8%)
    all_to_all x1, blocking collectives, body(): got = lax.all_to_all(send, 'seq', split_axis=0, concat_axis=0, tiled=True)  19 us
    pallas_call x4, Pallas kernels, call(): pl.pallas_call(kernel, name=name, out_shape=out_shape, in_specs=specs, ou...  11.2 us
    ppermute x3, waiting for transfers between devices, body(): lax.ppermute(fresh, 'seq', partner(bit))  5.73 us
    unnamed x12, local copies, waits for them, and re-layouts  2.63 us
    all_to_all x1, starting transfers between devices, body(): hist = lax.all_to_all(back, 'seq', split_axis=0, concat_axis=0, tiled=True)  2.59 us
    ppermute x3, starting transfers between devices, body(): lax.ppermute(fresh, 'seq', partner(bit))  1.96 us
    all_to_all x1, waiting for transfers between devices, body(): hist = lax.all_to_all(back, 'seq', split_axis=0, concat_axis=0, tiled=True)  1.83 us
    dynamic_slice x1, local copies, waits for them, and re-layouts, side(): lax.dynamic_slice_in_dim(x, head * HD, HD, axis=1)  1.26 us
  transfers between devices with their start and end apart: 5, of which 3 were waited for; matrix products, arithmetic and copies ran while one was open for 0% of the time, Pallas kernels for 5%

profile of v3, /device:TPU:0, one launch (start us, length us, event | category | flops | bytes accessed | tf_op | source)
XLA Modules:
  0.0 47.0 jit_solution(15221219799476567641)
XLA Ops:
  0.0 1.3 %constant_dynamic-slice_fusion = (bf16[1024,128]{1,0:T(8,128)(2,1)S(1)}, bf16[1024,128]{1,0:T(8,128)(2,1)S(1)}, bf16[1024,128]{1,0:T(8,128)(2,1)S(1)}, bf16[1024,128]{1,0:T(8,128)(2,1)S(1)}) fusion(bf16[1024,256]{1,0:T(8,128)(2,1)} %param.11, s32[]{:T(128)S(6)} %select_n.17, s32[]{:T(128)S(6)} %select_n.16, bf16[1024,256]{1,0:T(8,128)(2,1)} %param.10), kind=kLoop, calls=%fused_computation.2 | loop fusion | bytes 2097160 | tf_op jit(solution)/shard_map/dynamic_slice | solution.py:249
  1.3 0.3 maximum_maximum_fusion.1
  1.6 0.5 %collective-permute-start = (bf16[1024,384]{1,0:T(8,128)(2,1)S(1)}, bf16[1024,384]{1,0:T(8,128)(2,1)S(1)}, u32[]{:S(2)}, u32[]{:S(2)}) collective-permute-start(bf16[1024,384]{1,0:T(8,128)(2,1)S(1)} %get-tuple-element.19), channel_id=1, source_target_pairs={{0,1},{1,0},{2,3},{3,2},{4,5},{5,4},{6,7},{7,6},{8,9},{9,8},{10,11... | collective-permute-start | bytes 2359304 | tf_op jit(solution)/shard_map/ppermute | solution.py:253
  2.1 1.9 %pack.1 = bf16[32,40,128]{2,1,0:T(8,128)(2,1)} custom-call(s32[3,1,14]{2,1,0:T(1,128)} %bitcast.2, bf16[8,1792]{1,0:T(8,128)(2,1)} %q_hbm.3, bf16[8,256]{1,0:T(8,128)(2,1)} %k_hbm.1, bf16[8,256]{1,0:T(8,128)(2,1)} %v_hbm.1), custom_call_target="tpu_custom_call" | custom-call | tf_op jit(solution)/shard_map/pack/pallas_call | solution.py:201
  4.0 19.0 %all_to_all.10.q_ref = bf16[32,40,128]{2,1,0:T(8,128)(2,1)S(1)} all-to-all(bf16[32,40,128]{2,1,0:T(8,128)(2,1)} %pack.1), channel_id=1, replica_groups=mesh['grp'=1,'seq'=32] {'seq'}, dimensions={0} | all-to-all | bytes 655360 | tf_op jit(solution)/shard_map/all_to_all | solution.py:243
  23.0 0.0 collective-permute-done.peer_ref
  23.0 0.0 copy-start.1
  23.0 0.0 copy-start.4
  23.0 3.9 %attend.1 = (bf16[32,40,128]{2,1,0:T(8,128)(2,1)}, bf16[32,8,128]{2,1,0:T(8,128)(2,1)S(1)}) custom-call(bf16[32,40,128]{2,1,0:T(8,128)(2,1)S(1)} %all_to_all.10.q_ref, bf16[1024,384]{1,0:T(8,128)(2,1)S(1)} %get-tuple-element.20.own_ref, bf16[1024,384]{1,0:T(8,128)(2,1)S(1)} %collective-permute-done.peer_ref), custom_call_target="tpu_custom_call" | custom-call | flops 1073741824 | bytes 4194304 | tf_op jit(solution)/shard_map/attend/pallas_call | solution.py:201
  26.9 2.6 %all-to-all-start.1 = ((bf16[32,40,128]{2,1,0:T(8,128)(2,1)}), bf16[32,40,128]{2,1,0:T(8,128)(2,1)S(1)}, u32[]{:S(2)}, u32[]{:S(2)}) async-start(bf16[32,40,128]{2,1,0:T(8,128)(2,1)} %get-tuple-element.10), calls=%async_computation.1 | async-start | bytes 655360 | tf_op jit(solution)/shard_map/all_to_all | solution.py:269
  29.5 0.2 collective-permute-start.1
  29.6 1.7 %collective-permute-start.2 = (bf16[32,8,128]{2,1,0:T(8,128)(2,1)S(1)}, bf16[32,8,128]{2,1,0:T(8,128)(2,1)S(1)}, u32[]{:S(2)}, u32[]{:S(2)}) collective-permute-start(bf16[32,8,128]{2,1,0:T(8,128)(2,1)S(1)} %get-tuple-element.11.kv_ref), channel_id=1, source_target_pairs={{0,2},{1,3},{2,0},{3,1},{4,6},{5,7},{6,4},{7,5},{8,10},{9,11},{10,... | collective-permute-start | bytes 196616 | tf_op jit(solution)/shard_map/ppermute | solution.py:281
  31.3 0.1 collective-permute-start.3
  31.4 0.0 collective-permute-done.1.kv1_ref
  31.4 5.3 %collective-permute-done.2.kv2_ref = bf16[32,8,128]{2,1,0:T(8,128)(2,1)S(1)} collective-permute-done((bf16[32,8,128]{2,1,0:T(8,128)(2,1)S(1)}, bf16[32,8,128]{2,1,0:T(8,128)(2,1)S(1)}, u32[]{:S(2)}, u32[]{:S(2)}) %collective-permute-start.2) | collective-permute-done | bytes 65568 | tf_op jit(solution)/shard_map/ppermute | solution.py:281
  36.8 0.4 collective-permute-done.3.kv3_ref
  37.2 0.0 copy-done.1
  37.2 0.0 copy-done.4
  37.2 0.5 %fresh.1 = (f32[2,56,128]{2,1,0:T(8,128)S(1)}, f32[2,56,128]{2,1,0:T(8,128)S(1)}, f32[2,56,512]{2,1,0:T(8,128)S(1)}) custom-call(s32[3,1,14]{2,1,0:T(1,128)S(1)} %bitcast.3, bf16[8,1792]{1,0:T(8,128)(2,1)S(1)} %copy-done.1, bf16[32,8,128]{2,1,0:T(8,128)(2,1)S(1)} %get-tuple-element.11.kv_ref, bf16[32,8,128]{2,1,0:T(8,128)(2,1)S(1)} %collective-permute-done.1.kv1_ref, ...), custom_call_target="tpu_custom_call" | custom-call | flops 29360128 | bytes 2097152 | tf_op jit(solution)/shard_map/fresh/pallas_call | solution.py:201
  37.7 0.0 copy-start
  37.7 0.7 %copy-done = f32[2,56,512]{2,1,0:T(8,128)} copy-done((f32[2,56,512]{2,1,0:T(8,128)}, f32[2,56,512]{2,1,0:T(8,128)S(1)}, u32[]{:S(2)}) %copy-start) | copy-done | bytes 229400
  38.4 0.0 copy-start.2
  38.4 0.6 %copy-done.2 = f32[2,56,128]{2,1,0:T(8,128)} copy-done((f32[2,56,128]{2,1,0:T(8,128)}, f32[2,56,128]{2,1,0:T(8,128)S(1)}, u32[]{:S(2)}) %copy-start.2) | copy-done | bytes 57368
  39.0 0.0 copy-start.3
  39.0 0.6 %copy-done.3 = f32[2,56,128]{2,1,0:T(8,128)} copy-done((f32[2,56,128]{2,1,0:T(8,128)}, f32[2,56,128]{2,1,0:T(8,128)S(1)}, u32[]{:S(2)}) %copy-start.3) | copy-done | bytes 57368
  39.6 1.8 %all-to-all-done.1 = bf16[32,40,128]{2,1,0:T(8,128)(2,1)S(1)} async-done(((bf16[32,40,128]{2,1,0:T(8,128)(2,1)}), bf16[32,40,128]{2,1,0:T(8,128)(2,1)S(1)}, u32[]{:S(2)}, u32[]{:S(2)}) %all-to-all-start.1) | async-done | bytes 327712 | tf_op jit(solution)/shard_map/all_to_all | solution.py:269
  41.5 0.0 copy-start.5
  41.5 0.7 %copy-done.5 = bf16[32,40,128]{2,1,0:T(8,128)(2,1)} copy-done((bf16[32,40,128]{2,1,0:T(8,128)(2,1)}, bf16[32,40,128]{2,1,0:T(8,128)(2,1)S(1)}, u32[]{:S(2)}) %copy-start.5) | copy-done | bytes 327704
  42.2 4.9 %project.1 = bf16[8,1792]{1,0:T(8,128)(2,1)} custom-call(bf16[16,2,40,128]{3,2,1,0:T(8,128)(2,1)} %bitcast.4, f32[2,56,128]{2,1,0:T(8,128)} %copy-done.2, f32[2,56,128]{2,1,0:T(8,128)} %copy-done.3, f32[2,56,512]{2,1,0:T(8,128)} %copy-done, bf16[1792,1792]{1,0:T(8,128)(2,1)} %w_hbm.1), custom_call_target="tpu_custom_call" | custom-call | flops 51380224 | bytes 6422528 | tf_op jit(solution)/shard_map/project/pallas_call | solution.py:201
  (2 shorter events, 0.0 us)
Async XLA Ops:
  1.6 21.4 %collective-permute-start = (bf16[1024,384]{1,0:T(8,128)(2,1)S(1)}, bf16[1024,384]{1,0:T(8,128)(2,1)S(1)}, u32[]{:S(2)}, u32[]{:S(2)}) collective-permute-start(bf16[1024,384]{1,0:T(8,128)(2,1)S(1)} %get-tuple-element.19), channel_id=1, source_target_pairs={{0,1},{1,0},{2,3},{3,2},{4,5},{5,4},{6,7},{7,6},{8,9},{9,8},{10,11... | collective-permute-start | bytes 2359304 | tf_op jit(solution)/shard_map/ppermute | solution.py:253
  23.0 14.2 %copy-start.1 = (bf16[8,1792]{1,0:T(8,128)(2,1)S(1)}, bf16[8,1792]{1,0:T(8,128)(2,1)}, u32[]{:S(2)}) copy-start(bf16[8,1792]{1,0:T(8,128)(2,1)} %q_hbm.3) | copy-start | bytes 86020
  23.0 14.2 %copy-start.4 = (s32[1,14,3]{1,0,2:T(1,128)S(1)}, s32[1,14,3]{1,0,2:T(1,128)}, u32[]{:S(2)}) copy-start(s32[1,14,3]{1,0,2:T(1,128)} %param.12) | copy-start | bytes 508
  26.9 14.6 %all-to-all-start.1 = ((bf16[32,40,128]{2,1,0:T(8,128)(2,1)}), bf16[32,40,128]{2,1,0:T(8,128)(2,1)S(1)}, u32[]{:S(2)}, u32[]{:S(2)}) async-start(bf16[32,40,128]{2,1,0:T(8,128)(2,1)} %get-tuple-element.10), calls=%async_computation.1 | async-start | bytes 655360 | tf_op jit(solution)/shard_map/all_to_all | solution.py:269
  29.5 2.0 %collective-permute-start.1 = (bf16[32,8,128]{2,1,0:T(8,128)(2,1)S(1)}, bf16[32,8,128]{2,1,0:T(8,128)(2,1)S(1)}, u32[]{:S(2)}, u32[]{:S(2)}) collective-permute-start(bf16[32,8,128]{2,1,0:T(8,128)(2,1)S(1)} %get-tuple-element.11.kv_ref), channel_id=1, source_target_pairs={{0,1},{1,0},{2,3},{3,2},{4,5},{5,4},{6,7},{7,6},{8,9},{9,8},{10,11... | collective-permute-start | bytes 196616 | tf_op jit(solution)/shard_map/ppermute | solution.py:281
  29.6 7.1 %collective-permute-start.2 = (bf16[32,8,128]{2,1,0:T(8,128)(2,1)S(1)}, bf16[32,8,128]{2,1,0:T(8,128)(2,1)S(1)}, u32[]{:S(2)}, u32[]{:S(2)}) collective-permute-start(bf16[32,8,128]{2,1,0:T(8,128)(2,1)S(1)} %get-tuple-element.11.kv_ref), channel_id=1, source_target_pairs={{0,2},{1,3},{2,0},{3,1},{4,6},{5,7},{6,4},{7,5},{8,10},{9,11},{10,... | collective-permute-start | bytes 196616 | tf_op jit(solution)/shard_map/ppermute | solution.py:281
  31.3 5.8 %collective-permute-start.3 = (bf16[32,8,128]{2,1,0:T(8,128)(2,1)S(1)}, bf16[32,8,128]{2,1,0:T(8,128)(2,1)S(1)}, u32[]{:S(2)}, u32[]{:S(2)}) collective-permute-start(bf16[32,8,128]{2,1,0:T(8,128)(2,1)S(1)} %get-tuple-element.11.kv_ref), channel_id=1, source_target_pairs={{0,3},{1,2},{2,1},{3,0},{4,7},{5,6},{6,5},{7,4},{8,11},{9,10},{10,... | collective-permute-start | bytes 196616 | tf_op jit(solution)/shard_map/ppermute | solution.py:281
  37.7 0.7 %copy-start = (f32[2,56,512]{2,1,0:T(8,128)}, f32[2,56,512]{2,1,0:T(8,128)S(1)}, u32[]{:S(2)}) copy-start(f32[2,56,512]{2,1,0:T(8,128)S(1)} %get-tuple-element.14.match_ref) | copy-start | bytes 688132
  38.4 0.6 %copy-start.2 = (f32[2,56,128]{2,1,0:T(8,128)}, f32[2,56,128]{2,1,0:T(8,128)S(1)}, u32[]{:S(2)}) copy-start(f32[2,56,128]{2,1,0:T(8,128)S(1)} %get-tuple-element.12.out_ref) | copy-start | bytes 172036
  39.0 0.6 %copy-start.3 = (f32[2,56,128]{2,1,0:T(8,128)}, f32[2,56,128]{2,1,0:T(8,128)S(1)}, u32[]{:S(2)}) copy-start(f32[2,56,128]{2,1,0:T(8,128)S(1)} %get-tuple-element.13.lse_ref) | copy-start | bytes 172036
  41.5 0.7 %copy-start.5 = (bf16[32,40,128]{2,1,0:T(8,128)(2,1)}, bf16[32,40,128]{2,1,0:T(8,128)(2,1)S(1)}, u32[]{:S(2)}) copy-start(bf16[32,40,128]{2,1,0:T(8,128)(2,1)S(1)} %all-to-all-done.1) | copy-start | bytes 983044

commit v4 on v3

--- a/solution.py
+++ b/solution.py
@@ -46,7 +46,7 @@
     return copies
 
 
-def pack_kernel(chips, capacity, chosen_hbm, q_hbm, k_hbm, v_hbm, send_ref, chosen_ref, q_ref, k_ref, v_ref, sems):
+def pack_kernel(chips, capacity, chosen_hbm, q_hbm, k_hbm, v_hbm, send_ref, after_ref, chosen_ref, q_ref, k_ref, v_ref, sems):
     copies = fetch([(chosen_hbm, chosen_ref), (q_hbm, q_ref), (k_hbm, k_ref), (v_hbm, v_ref)], sems)
     tokens = q_ref.shape[0]
     per = capacity * tokens
@@ -72,6 +72,27 @@
                 to = b * span + chip * KVH + g
                 send_ref[to, :per, :] = slots[b * per : (b + 1) * per]
                 send_ref[to, per:, :] = fresh[chip % 2]
+    after_ref[...] = jnp.zeros_like(after_ref)
+
+
+def split_kernel(after_ref, k_hbm, v_hbm, own_ref, away_ref, sems):
+    core = lax.axis_index("seq") % KVH
+    own = pl.ds(pl.multiple_of(core * HD, HD), HD)
+    away = pl.ds(pl.multiple_of((1 - core) * HD, HD), HD)
+    copies = fetch(
+        [
+            (k_hbm.at[:, away], away_ref.at[:, :HD]),
+            (v_hbm.at[:, away], away_ref.at[:, HD : 2 * HD]),
+            (k_hbm.at[:, own], own_ref.at[:, :HD]),
+            (v_hbm.at[:, own], own_ref.at[:, HD : 2 * HD]),
+        ],
+        sems,
+    )
+    ones = jnp.ones((own_ref.shape[0], HD), jnp.bfloat16)
+    own_ref[:, 2 * HD :] = ones
+    away_ref[:, 2 * HD :] = ones
+    for copy in copies:
+        copy.wait()
 
 
 def attend_kernel(per, q_ref, own_ref, peer_ref, out_ref, fresh_ref):
@@ -225,10 +246,13 @@
     def partner(bit):
         return [(i, i ^ bit) for i in range(devices)]
 
-    send = call(
+    send, after = call(
         functools.partial(pack_kernel, chips, capacity),
         "pack",
-        jax.ShapeDtypeStruct((devices, per + tokens, HD), bf16),
+        (
+            jax.ShapeDtypeStruct((devices, per + tokens, HD), bf16),
+            jax.ShapeDtypeStruct((8, LANES), f32),
+        ),
         [HBM] * 4,
         picks, queries, stretch_keys, stretch_values,
         scratch=[
@@ -242,15 +266,16 @@
     )
     got = lax.all_to_all(send, "seq", split_axis=0, concat_axis=0, tiled=True)
 
-    core = lax.axis_index("seq") % KVH
-    ones = jnp.ones((cache_rows, HD), bf16)
-
-    def side(head):
-        columns = [lax.dynamic_slice_in_dim(x, head * HD, HD, axis=1) for x in (cache_keys, cache_values)]
-        return jnp.concatenate(columns + [ones], axis=1)
-
-    own = side(core)
-    peer = lax.ppermute(side(1 - core), "seq", partner(1))
+    side = jax.ShapeDtypeStruct((cache_rows, 3 * HD), bf16)
+    own, away = call(
+        split_kernel,
+        "split",
+        (side, side),
+        [VMEM, HBM, HBM],
+        after, cache_keys, cache_values,
+        scratch=[pltpu.SemaphoreType.DMA((4,))],
+    )
+    peer = lax.ppermute(away, "seq", partner(1))
 
     rows = devices * per
     back, fresh = call(
@@ -301,7 +326,7 @@
         ],
         flops=2 * tokens * out_weight.size,
         moved=out_weight.size * 2,
-        limit=58,
+        limit=50,
     )
 
 

time: 47.4 us -> 47.3 us (level)
  Pallas kernels: 11.2 us -> 10.5 us
  waiting for transfers between devices: 7.56 us -> 8.07 us
    unnamed x12 -> x10, local copies, waits for them, and re-layouts: 2.63 us -> 4.19 us
    dynamic_slice x1 -> x0, local copies, waits for them, and re-layouts: 1.26 us -> none  [side(): lax.dynamic_slice_in_dim(x, head * HD, HD, axis=1)]
    pallas_call x4 -> x5, Pallas kernels: 11.2 us -> 10.5 us  [call(): pl.pallas_call(kernel, name=name, out_shape=out_shape, in_specs=specs, ou...]
    ppermute x3, waiting for transfers between devices: 5.73 us -> 6.21 us  [body(): lax.ppermute(fresh, 'seq', partner(bit))]
  transfers between devices with their start and end apart: 5 -> 5, of which waited for: 3 -> 3; matrix products, arithmetic and copies ran while one was open for 0% -> 0% of each run, Pallas kernels for 5% -> 1%
where the time goes in v4:
time: 47.3 us; the launch traced here: 46.8 us
  blocking collectives  19 us (40%)
  Pallas kernels  10.5 us (22%)
  waiting for transfers between devices  8.07 us (17%)
  starting transfers between devices  5.06 us (11%)
  local copies, waits for them, and re-layouts  4.19 us (9%)
    all_to_all x1, blocking collectives, body(): got = lax.all_to_all(send, 'seq', split_axis=0, concat_axis=0, tiled=True)  19 us
    pallas_call x5, Pallas kernels, call(): pl.pallas_call(kernel, name=name, out_shape=out_shape, in_specs=specs, ou...  10.5 us
    ppermute x3, waiting for transfers between devices, body(): lax.ppermute(fresh, 'seq', partner(bit))  6.21 us
    unnamed x10, local copies, waits for them, and re-layouts  4.19 us
    all_to_all x1, starting transfers between devices, body(): hist = lax.all_to_all(back, 'seq', split_axis=0, concat_axis=0, tiled=True)  2.59 us
    ppermute x3, starting transfers between devices, body(): lax.ppermute(fresh, 'seq', partner(bit))  1.96 us
    all_to_all x1, waiting for transfers between devices, body(): hist = lax.all_to_all(back, 'seq', split_axis=0, concat_axis=0, tiled=True)  1.85 us
  transfers between devices with their start and end apart: 5, of which 3 were waited for; matrix products, arithmetic and copies ran while one was open for 0% of the time, Pallas kernels for 1%

profile of v4, /device:TPU:0, one launch (start us, length us, event | category | flops | bytes accessed | tf_op | source)
XLA Modules:
  0.0 46.8 jit_solution(17805863847031433410)
XLA Ops:
  0.0 1.9 %pack.1 = (bf16[32,40,128]{2,1,0:T(8,128)(2,1)}, f32[8,128]{1,0:T(8,128)}) custom-call(s32[3,1,14]{2,1,0:T(1,128)} %bitcast.3, bf16[8,1792]{1,0:T(8,128)(2,1)} %q_hbm.3, bf16[8,256]{1,0:T(8,128)(2,1)} %k_hbm.2, bf16[8,256]{1,0:T(8,128)(2,1)} %v_hbm.2), custom_call_target="tpu_custom_call" | custom-call | tf_op jit(solution)/shard_map/pack/pallas_call | solution.py:222
  1.9 0.0 copy-start
  1.9 1.0 %copy-done = bf16[1024,256]{1,0:T(8,128)(2,1)S(1)} copy-done((bf16[1024,256]{1,0:T(8,128)(2,1)S(1)}, bf16[1024,256]{1,0:T(8,128)(2,1)}, u32[]{:S(2)}) %copy-start) | copy-done | bytes 524312
  3.0 0.0 copy-start.1
  3.0 1.0 %copy-done.1 = bf16[1024,256]{1,0:T(8,128)(2,1)S(1)} copy-done((bf16[1024,256]{1,0:T(8,128)(2,1)S(1)}, bf16[1024,256]{1,0:T(8,128)(2,1)}, u32[]{:S(2)}) %copy-start.1) | copy-done | bytes 524312
  4.0 0.0 copy-start.4
  4.0 0.7 %copy-done.4 = f32[8,128]{1,0:T(8,128)S(1)} copy-done((f32[8,128]{1,0:T(8,128)S(1)}, f32[8,128]{1,0:T(8,128)}, u32[]{:S(2)}) %copy-start.4) | copy-done | bytes 4120
  4.7 0.3 split.1
  5.0 0.5 %collective-permute-start = (bf16[1024,384]{1,0:T(8,128)(2,1)S(1)}, bf16[1024,384]{1,0:T(8,128)(2,1)S(1)}, u32[]{:S(2)}, u32[]{:S(2)}) collective-permute-start(bf16[1024,384]{1,0:T(8,128)(2,1)S(1)} %get-tuple-element.17), channel_id=1, source_target_pairs={{0,1},{1,0},{2,3},{3,2},{4,5},{5,4},{6,7},{7,6},{8,9},{9,8},{10,11... | collective-permute-start | bytes 2359304 | tf_op jit(solution)/shard_map/ppermute | solution.py:278
  5.5 19.0 %all_to_all.10.q_ref = bf16[32,40,128]{2,1,0:T(8,128)(2,1)S(1)} all-to-all(bf16[32,40,128]{2,1,0:T(8,128)(2,1)} %get-tuple-element.14), channel_id=1, replica_groups=mesh['grp'=1,'seq'=32] {'seq'}, dimensions={0} | all-to-all | bytes 655360 | tf_op jit(solution)/shard_map/all_to_all | solution.py:267
  24.5 0.0 collective-permute-done.peer_ref
  24.5 3.9 %attend.1 = (bf16[32,40,128]{2,1,0:T(8,128)(2,1)}, bf16[32,8,128]{2,1,0:T(8,128)(2,1)S(1)}) custom-call(bf16[32,40,128]{2,1,0:T(8,128)(2,1)S(1)} %all_to_all.10.q_ref, bf16[1024,384]{1,0:T(8,128)(2,1)S(1)} %get-tuple-element.16.own_ref, bf16[1024,384]{1,0:T(8,128)(2,1)S(1)} %collective-permute-done.peer_ref), custom_call_target="tpu_custom_call" | custom-call | flops 1073741824 | bytes 4194304 | tf_op jit(solution)/shard_map/attend/pallas_call | solution.py:222
  28.4 2.6 %all-to-all-start.1 = ((bf16[32,40,128]{2,1,0:T(8,128)(2,1)}), bf16[32,40,128]{2,1,0:T(8,128)(2,1)S(1)}, u32[]{:S(2)}, u32[]{:S(2)}) async-start(bf16[32,40,128]{2,1,0:T(8,128)(2,1)} %get-tuple-element.18), calls=%async_computation.1 | async-start | bytes 655360 | tf_op jit(solution)/shard_map/all_to_all | solution.py:294
  30.9 1.5 %collective-permute-start.3 = (bf16[32,8,128]{2,1,0:T(8,128)(2,1)S(1)}, bf16[32,8,128]{2,1,0:T(8,128)(2,1)S(1)}, u32[]{:S(2)}, u32[]{:S(2)}) collective-permute-start(bf16[32,8,128]{2,1,0:T(8,128)(2,1)S(1)} %get-tuple-element.19.kv_ref), channel_id=1, source_target_pairs={{0,3},{1,2},{2,1},{3,0},{4,7},{5,6},{6,5},{7,4},{8,11},{9,10},{10,... | collective-permute-start | bytes 196616 | tf_op jit(solution)/shard_map/ppermute | solution.py:306
  32.4 0.4 collective-permute-start.2
  32.8 0.1 collective-permute-start.1
  32.9 3.3 %collective-permute-done.3.kv3_ref = bf16[32,8,128]{2,1,0:T(8,128)(2,1)S(1)} collective-permute-done((bf16[32,8,128]{2,1,0:T(8,128)(2,1)S(1)}, bf16[32,8,128]{2,1,0:T(8,128)(2,1)S(1)}, u32[]{:S(2)}, u32[]{:S(2)}) %collective-permute-start.3) | collective-permute-done | bytes 65568 | tf_op jit(solution)/shard_map/ppermute | solution.py:306
  36.2 2.9 %collective-permute-done.2.kv2_ref = bf16[32,8,128]{2,1,0:T(8,128)(2,1)S(1)} collective-permute-done((bf16[32,8,128]{2,1,0:T(8,128)(2,1)S(1)}, bf16[32,8,128]{2,1,0:T(8,128)(2,1)S(1)}, u32[]{:S(2)}, u32[]{:S(2)}) %collective-permute-start.2) | collective-permute-done | bytes 65568 | tf_op jit(solution)/shard_map/ppermute | solution.py:306
  39.1 0.0 collective-permute-done.1.kv1_ref
  39.1 0.0 copy-start.2
  39.1 0.7 %copy-done.2 = bf16[8,1792]{1,0:T(8,128)(2,1)S(1)} copy-done((bf16[8,1792]{1,0:T(8,128)(2,1)S(1)}, bf16[8,1792]{1,0:T(8,128)(2,1)}, u32[]{:S(2)}) %copy-start.2) | copy-done | bytes 28696
  39.9 0.0 copy-start.3
  39.9 0.7 %copy-done.3 = s32[1,14,3]{1,0,2:T(1,128)S(1)} copy-done((s32[1,14,3]{1,0,2:T(1,128)S(1)}, s32[1,14,3]{1,0,2:T(1,128)}, u32[]{:S(2)}) %copy-start.3) | copy-done | bytes 192
  40.6 0.5 %fresh.1 = (f32[2,56,128]{2,1,0:T(8,128)S(1)}, f32[2,56,128]{2,1,0:T(8,128)S(1)}, f32[2,56,512]{2,1,0:T(8,128)S(1)}) custom-call(s32[3,1,14]{2,1,0:T(1,128)S(1)} %bitcast.4, bf16[8,1792]{1,0:T(8,128)(2,1)S(1)} %copy-done.2, bf16[32,8,128]{2,1,0:T(8,128)(2,1)S(1)} %get-tuple-element.19.kv_ref, bf16[32,8,128]{2,1,0:T(8,128)(2,1)S(1)} %collective-permute-done.1.kv1_ref, ...), custom_call_target="tpu_custom_call" | custom-call | flops 29360128 | bytes 2097152 | tf_op jit(solution)/shard_map/fresh/pallas_call | solution.py:222
  41.1 1.9 %all-to-all-done.1 = bf16[32,40,128]{2,1,0:T(8,128)(2,1)S(1)} async-done(((bf16[32,40,128]{2,1,0:T(8,128)(2,1)}), bf16[32,40,128]{2,1,0:T(8,128)(2,1)S(1)}, u32[]{:S(2)}, u32[]{:S(2)}) %all-to-all-start.1) | async-done | bytes 327712 | tf_op jit(solution)/shard_map/all_to_all | solution.py:294
  42.9 3.9 %project.1 = bf16[8,1792]{1,0:T(8,128)(2,1)} custom-call(bf16[16,2,40,128]{3,2,1,0:T(8,128)(2,1)S(1)} %bitcast.2, f32[2,56,128]{2,1,0:T(8,128)S(1)} %get-tuple-element.20.out_ref, f32[2,56,128]{2,1,0:T(8,128)S(1)} %get-tuple-element.21.lse_ref, f32[2,56,512]{2,1,0:T(8,128)S(1)} %get-tuple-element.22.match_ref, bf16[1792,1792]{1,0:T(8,128)(2,1)} %w_hbm.1), custom_call_target="tpu_custom_call" | custom-call | flops 51380224 | bytes 6422528 | tf_op jit(solution)/shard_map/project/pallas_call | solution.py:222
Async XLA Ops:
  1.9 1.0 %copy-start = (bf16[1024,256]{1,0:T(8,128)(2,1)S(1)}, bf16[1024,256]{1,0:T(8,128)(2,1)}, u32[]{:S(2)}) copy-start(bf16[1024,256]{1,0:T(8,128)(2,1)} %k_hbm.3) | copy-start | bytes 1572868
  3.0 1.0 %copy-start.1 = (bf16[1024,256]{1,0:T(8,128)(2,1)S(1)}, bf16[1024,256]{1,0:T(8,128)(2,1)}, u32[]{:S(2)}) copy-start(bf16[1024,256]{1,0:T(8,128)(2,1)} %v_hbm.3) | copy-start | bytes 1572868
  4.0 0.7 %copy-start.4 = (f32[8,128]{1,0:T(8,128)S(1)}, f32[8,128]{1,0:T(8,128)}, u32[]{:S(2)}) copy-start(f32[8,128]{1,0:T(8,128)} %get-tuple-element.15.after_ref) | copy-start | bytes 12292
  5.0 19.5 %collective-permute-start = (bf16[1024,384]{1,0:T(8,128)(2,1)S(1)}, bf16[1024,384]{1,0:T(8,128)(2,1)S(1)}, u32[]{:S(2)}, u32[]{:S(2)}) collective-permute-start(bf16[1024,384]{1,0:T(8,128)(2,1)S(1)} %get-tuple-element.17), channel_id=1, source_target_pairs={{0,1},{1,0},{2,3},{3,2},{4,5},{5,4},{6,7},{7,6},{8,9},{9,8},{10,11... | collective-permute-start | bytes 2359304 | tf_op jit(solution)/shard_map/ppermute | solution.py:278
  28.4 14.6 %all-to-all-start.1 = ((bf16[32,40,128]{2,1,0:T(8,128)(2,1)}), bf16[32,40,128]{2,1,0:T(8,128)(2,1)S(1)}, u32[]{:S(2)}, u32[]{:S(2)}) async-start(bf16[32,40,128]{2,1,0:T(8,128)(2,1)} %get-tuple-element.18), calls=%async_computation.1 | async-start | bytes 655360 | tf_op jit(solution)/shard_map/all_to_all | solution.py:294
  30.9 5.3 %collective-permute-start.3 = (bf16[32,8,128]{2,1,0:T(8,128)(2,1)S(1)}, bf16[32,8,128]{2,1,0:T(8,128)(2,1)S(1)}, u32[]{:S(2)}, u32[]{:S(2)}) collective-permute-start(bf16[32,8,128]{2,1,0:T(8,128)(2,1)S(1)} %get-tuple-element.19.kv_ref), channel_id=1, source_target_pairs={{0,3},{1,2},{2,1},{3,0},{4,7},{5,6},{6,5},{7,4},{8,11},{9,10},{10,... | collective-permute-start | bytes 196616 | tf_op jit(solution)/shard_map/ppermute | solution.py:306
  32.4 6.7 %collective-permute-start.2 = (bf16[32,8,128]{2,1,0:T(8,128)(2,1)S(1)}, bf16[32,8,128]{2,1,0:T(8,128)(2,1)S(1)}, u32[]{:S(2)}, u32[]{:S(2)}) collective-permute-start(bf16[32,8,128]{2,1,0:T(8,128)(2,1)S(1)} %get-tuple-element.19.kv_ref), channel_id=1, source_target_pairs={{0,2},{1,3},{2,0},{3,1},{4,6},{5,7},{6,4},{7,5},{8,10},{9,11},{10,... | collective-permute-start | bytes 196616 | tf_op jit(solution)/shard_map/ppermute | solution.py:306
  32.8 6.4 %collective-permute-start.1 = (bf16[32,8,128]{2,1,0:T(8,128)(2,1)S(1)}, bf16[32,8,128]{2,1,0:T(8,128)(2,1)S(1)}, u32[]{:S(2)}, u32[]{:S(2)}) collective-permute-start(bf16[32,8,128]{2,1,0:T(8,128)(2,1)S(1)} %get-tuple-element.19.kv_ref), channel_id=1, source_target_pairs={{0,1},{1,0},{2,3},{3,2},{4,5},{5,4},{6,7},{7,6},{8,9},{9,8},{10,11... | collective-permute-start | bytes 196616 | tf_op jit(solution)/shard_map/ppermute | solution.py:306
  39.1 0.7 %copy-start.2 = (bf16[8,1792]{1,0:T(8,128)(2,1)S(1)}, bf16[8,1792]{1,0:T(8,128)(2,1)}, u32[]{:S(2)}) copy-start(bf16[8,1792]{1,0:T(8,128)(2,1)} %q_hbm.3) | copy-start | bytes 86020
  39.9 0.7 %copy-start.3 = (s32[1,14,3]{1,0,2:T(1,128)S(1)}, s32[1,14,3]{1,0,2:T(1,128)}, u32[]{:S(2)}) copy-start(s32[1,14,3]{1,0,2:T(1,128)} %param.12) | copy-start | bytes 508

commit v5 on v4

--- a/solution.py
+++ b/solution.py
@@ -18,6 +18,7 @@
 LOW_SCORE = -1e30
 LOG2E = math.log2(math.e)
 LANES = 128
+EARLY = 3
 
 
 def head_rows(q_ref, g):
@@ -75,27 +76,39 @@
     after_ref[...] = jnp.zeros_like(after_ref)
 
 
-def split_kernel(after_ref, k_hbm, v_hbm, own_ref, away_ref, sems):
+def split_kernel(
+    chips, capacity, after_ref, k_hbm, v_hbm, chosen_hbm, q_hbm, w_hbm,
+    k_own, v_own, k_away, v_away, match_ref, rows_ref, w_ref, chosen_ref, q_ref, sems,
+):
     core = lax.axis_index("seq") % KVH
     own = pl.ds(pl.multiple_of(core * HD, HD), HD)
     away = pl.ds(pl.multiple_of((1 - core) * HD, HD), HD)
     copies = fetch(
         [
-            (k_hbm.at[:, away], away_ref.at[:, :HD]),
-            (v_hbm.at[:, away], away_ref.at[:, HD : 2 * HD]),
-            (k_hbm.at[:, own], own_ref.at[:, :HD]),
-            (v_hbm.at[:, own], own_ref.at[:, HD : 2 * HD]),
+            (k_hbm.at[:, away], k_away),
+            (v_hbm.at[:, away], v_away),
+            (chosen_hbm, chosen_ref),
+            (q_hbm, q_ref),
+            (k_hbm.at[:, own], k_own),
+            (v_hbm.at[:, own], v_own),
+            (w_hbm.at[: w_ref.shape[0]], w_ref),
         ],
         sems,
     )
-    ones = jnp.ones((own_ref.shape[0], HD), jnp.bfloat16)
-    own_ref[:, 2 * HD :] = ones
-    away_ref[:, 2 * HD :] = ones
-    for copy in copies:
-        copy.wait()
-
-
-def attend_kernel(per, q_ref, own_ref, peer_ref, out_ref, fresh_ref):
+    tokens = q_ref.shape[0]
+    per = capacity * tokens
+    lane = lax.broadcasted_iota(jnp.int32, (tokens, match_ref.shape[2]), 1)
+    block, slot, token = lane // (per * chips), lane % per // tokens, lane % tokens
+    copies[2].wait()
+    copies[3].wait()
+    for g in range(KVH):
+        match_ref[g] = jnp.concatenate(slot_match(chosen_ref, g, block, slot, token), axis=0)
+        rows_ref[g] = jnp.concatenate(head_rows(q_ref, g), axis=0)
+    for i in (0, 1, 4, 5, 6):
+        copies[i].wait()
+
+
+def attend_kernel(per, q_ref, ka_ref, va_ref, kb_ref, vb_ref, out_ref, fresh_ref):
     sources = q_ref.shape[0]
     fresh_ref[...] = q_ref[:, per:, :]
     step = 256 // per
@@ -105,16 +118,17 @@
     lane = lax.broadcasted_iota(jnp.int32, (per, LANES), 1)
     diagonal = row == lane % per
     piece = lax.broadcasted_iota(jnp.int32, (8, LANES), 0)
+    ones = jnp.ones(va_ref.shape, jnp.bfloat16)
     for first in range(0, sources, step):
         q = q_ref[first : first + step, :per, :].reshape(step * per, HD)
-        sa = lax.dot_general(q, own_ref[:, :HD], nt, preferred_element_type=jnp.float32)
-        sb = lax.dot_general(q, peer_ref[:, :HD], nt, preferred_element_type=jnp.float32)
+        sa = lax.dot_general(q, ka_ref[...], nt, preferred_element_type=jnp.float32)
+        sb = lax.dot_general(q, kb_ref[...], nt, preferred_element_type=jnp.float32)
         top = jnp.maximum(jnp.max(sa, axis=1, keepdims=True), jnp.max(sb, axis=1, keepdims=True)) * scale
         wa = jnp.exp2(sa * scale - top).astype(jnp.bfloat16)
         wb = jnp.exp2(sb * scale - top).astype(jnp.bfloat16)
-        both = jnp.dot(wa, own_ref[:, HD:], preferred_element_type=jnp.float32) + jnp.dot(
-            wb, peer_ref[:, HD:], preferred_element_type=jnp.float32
-        )
+        both = jnp.dot(
+            wa, jnp.concatenate([va_ref[...], ones], axis=1), preferred_element_type=jnp.float32
+        ) + jnp.dot(wb, jnp.concatenate([vb_ref[...], ones], axis=1), preferred_element_type=jnp.float32)
         total = both[:, HD:]
         out = (both[:, :HD] / total).astype(jnp.bfloat16)
         lse = top + jnp.log(total) * LOG2E
@@ -130,11 +144,8 @@
             ).astype(jnp.bfloat16)
 
 
-def fresh_kernel(chips, capacity, chosen_hbm, q_hbm, kv_ref, kv1_ref, kv2_ref, kv3_ref, out_ref, lse_ref, match_ref, chosen_ref, q_ref, sems):
-    copies = fetch([(chosen_hbm, chosen_ref), (q_hbm, q_ref)], sems)
-    tokens = q_ref.shape[0]
+def fresh_kernel(tokens, rows_ref, kv_ref, kv1_ref, kv2_ref, kv3_ref, out_ref, lse_ref):
     sources = kv_ref.shape[0]
-    per = capacity * tokens
     place = lax.axis_index("seq")
     core, odd = place % KVH, place // KVH % 2
     scale = LOG2E * HD**-0.5
@@ -143,21 +154,16 @@
     query_pos = place * tokens + lax.broadcasted_iota(jnp.int32, column.shape, 0)
     visible = (column <= query_pos) & (column // BLK == query_pos // BLK)
     visible = jnp.concatenate([visible.astype(jnp.int32)] * GROUP, axis=0) > 0
-    lane = lax.broadcasted_iota(jnp.int32, (tokens, match_ref.shape[2]), 1)
-    block, slot, token = lane // (per * chips), lane % per // tokens, lane % tokens
     ones = jnp.ones((sources * tokens, HD), jnp.bfloat16)
     here, near, far, both = [
         ref[...].astype(jnp.float32).reshape(sources * tokens, HD) for ref in (kv_ref, kv1_ref, kv2_ref, kv3_ref)
     ]
     keys = [jnp.where(odd == 0, here, far), jnp.where(odd == 0, near, both)]
     values = [jnp.where(odd == 0, far, here), jnp.where(odd == 0, both, near)]
-    for copy in copies:
-        copy.wait()
     for g in range(KVH):
-        match_ref[g] = jnp.concatenate(slot_match(chosen_ref, g, block, slot, token), axis=0)
         k = jnp.where(core == g, keys[0], keys[1]).astype(jnp.bfloat16)
         v = jnp.where(core == g, values[0], values[1]).astype(jnp.bfloat16)
-        q = jnp.concatenate(head_rows(q_ref, g), axis=0).astype(jnp.bfloat16)
+        q = rows_ref[g].astype(jnp.bfloat16)
         s = lax.dot_general(q, k, nt, preferred_element_type=jnp.float32) * scale
         s = jnp.where(visible, s, LOW_SCORE)
         top = jnp.max(s, axis=1, keepdims=True)
@@ -168,10 +174,16 @@
         lse_ref[g] = top + jnp.log(total) * LOG2E
 
 
-def project_kernel(per, hist_ref, out_ref, lse_ref, match_ref, w_hbm, y_ref, att_ref, w_ref, sems):
-    depth = w_ref.shape[0] // GROUP
-    chunks = [pl.ds(i * depth, depth) for i in range(GROUP)]
-    copies = fetch([(w_hbm.at[chunk], w_ref.at[chunk]) for chunk in chunks], sems)
+def project_kernel(per, hist_ref, out_ref, lse_ref, match_ref, first_ref, w_hbm, y_ref, att_ref, w_ref, sems):
+    depth = KVH * HD
+    ready = first_ref.shape[0] // depth
+    copies = fetch(
+        [
+            (w_hbm.at[pl.ds((ready + i) * depth, depth)], w_ref.at[pl.ds(i * depth, depth)])
+            for i in range(w_ref.shape[0] // depth)
+        ],
+        sems,
+    )
     tokens = y_ref.shape[0]
     holders = hist_ref.shape[0]
     fold = LANES // per
@@ -205,11 +217,15 @@
         for r in range(GROUP):
             h = g * GROUP + r
             att_ref[:, h * HD : (h + 1) * HD] = att[r * tokens : (r + 1) * tokens]
-    y = jnp.zeros(y_ref.shape, jnp.float32)
-    for chunk, copy in zip(chunks, copies):
-        att = att_ref[:, chunk].astype(jnp.bfloat16)
+    att = att_ref[...].astype(jnp.bfloat16)
+    y = jnp.dot(att[:, : ready * depth], first_ref[...], preferred_element_type=jnp.float32)
+    for i, copy in enumerate(copies):
         copy.wait()
-        y = y + jnp.dot(att, w_ref[chunk, :], preferred_element_type=jnp.float32)
+        y = y + jnp.dot(
+            att[:, (ready + i) * depth : (ready + i + 1) * depth],
+            w_ref[i * depth : (i + 1) * depth, :],
+            preferred_element_type=jnp.float32,
+        )
     y_ref[...] = y.astype(jnp.bfloat16)
 
 
@@ -266,16 +282,31 @@
     )
     got = lax.all_to_all(send, "seq", split_axis=0, concat_axis=0, tiled=True)
 
-    side = jax.ShapeDtypeStruct((cache_rows, 3 * HD), bf16)
-    own, away = call(
-        split_kernel,
+    holders = devices // KVH
+    ready = EARLY * KVH * HD
+    side = jax.ShapeDtypeStruct((cache_rows, HD), bf16)
+    k_own, v_own, k_away, v_away, match, query_rows, first = call(
+        functools.partial(split_kernel, chips, capacity),
         "split",
-        (side, side),
-        [VMEM, HBM, HBM],
-        after, cache_keys, cache_values,
-        scratch=[pltpu.SemaphoreType.DMA((4,))],
-    )
-    peer = lax.ppermute(away, "seq", partner(1))
+        (
+            side,
+            side,
+            side,
+            side,
+            jax.ShapeDtypeStruct((KVH, GROUP * tokens, holders * per), f32),
+            jax.ShapeDtypeStruct((KVH, GROUP * tokens, HD), f32),
+            jax.ShapeDtypeStruct((ready, out_weight.shape[1]), bf16),
+        ),
+        [VMEM] + [HBM] * 5,
+        after, cache_keys, cache_values, picks, queries, out_weight,
+        scratch=[
+            pltpu.VMEM(picks.shape, jnp.int32),
+            pltpu.VMEM(queries.shape, bf16),
+            pltpu.SemaphoreType.DMA((7,)),
+        ],
+        limit=50,
+    )
+    k_peer, v_peer = [lax.ppermute(x, "seq", partner(1)) for x in (k_away, v_away)]
 
     rows = devices * per
     back, fresh = call(
@@ -285,44 +316,34 @@
             jax.ShapeDtypeStruct((devices, per + 8, HD), bf16),
             jax.ShapeDtypeStruct((devices, tokens, HD), bf16),
         ),
-        [VMEM] * 3,
-        got, own, peer,
+        [VMEM] * 5,
+        got, k_own, v_own, k_peer, v_peer,
         flops=8 * rows * cache_rows * HD,
         moved=4 << 20,
         limit=32,
     )
     hist = lax.all_to_all(back, "seq", split_axis=0, concat_axis=0, tiled=True)
 
-    holders = devices // KVH
-    out, lse, match = call(
-        functools.partial(fresh_kernel, chips, capacity),
+    part = jax.ShapeDtypeStruct((KVH, GROUP * tokens, HD), f32)
+    out, lse = call(
+        functools.partial(fresh_kernel, tokens),
         "fresh",
-        (
-            jax.ShapeDtypeStruct((KVH, GROUP * tokens, HD), f32),
-            jax.ShapeDtypeStruct((KVH, GROUP * tokens, HD), f32),
-            jax.ShapeDtypeStruct((KVH, GROUP * tokens, holders * per), f32),
-        ),
-        [HBM, HBM, VMEM, VMEM, VMEM, VMEM],
-        picks, queries, fresh, *[lax.ppermute(fresh, "seq", partner(bit)) for bit in (1, 2, 3)],
-        scratch=[
-            pltpu.VMEM(picks.shape, jnp.int32),
-            pltpu.VMEM(queries.shape, bf16),
-            pltpu.SemaphoreType.DMA((2,)),
-        ],
+        (part, part),
+        [VMEM] * 5,
+        query_rows, fresh, *[lax.ppermute(fresh, "seq", partner(bit)) for bit in (1, 2, 3)],
         flops=8 * H * tokens * devices * tokens * HD,
-        moved=2 << 20,
-        limit=20,
+        moved=1 << 20,
     )
     return call(
         functools.partial(project_kernel, per),
         "project",
         jax.ShapeDtypeStruct((tokens, out_weight.shape[1]), bf16),
-        [VMEM] * 4 + [HBM],
-        hist.reshape(holders, KVH, per + 8, HD), out, lse, match, out_weight,
+        [VMEM] * 5 + [HBM],
+        hist.reshape(holders, KVH, per + 8, HD), out, lse, match, first, out_weight,
         scratch=[
             pltpu.VMEM((tokens, H * HD), f32),
-            pltpu.VMEM(out_weight.shape, bf16),
-            pltpu.SemaphoreType.DMA((GROUP,)),
+            pltpu.VMEM((out_weight.shape[0] - ready, out_weight.shape[1]), bf16),
+            pltpu.SemaphoreType.DMA((GROUP - EARLY,)),
         ],
         flops=2 * tokens * out_weight.size,
         moved=out_weight.size * 2,

time: 47.3 us -> 50.6 us (1.070)
  blocking collectives: 19 us -> 0 us
  starting transfers between devices: 5.06 us -> 15.6 us
  local copies, waits for them, and re-layouts: 4.19 us -> 10.8 us
  waiting for transfers between devices: 8.07 us -> 10.6 us
  Pallas kernels: 10.5 us -> 12.8 us
    all_to_all x1 -> x0, blocking collectives: 19 us -> none  [body(): got = lax.all_to_all(send, 'seq', split_axis=0, concat_axis=0, tiled=True)]
    all_to_all x0 -> x1, starting transfers between devices: none -> 7.3 us  [body(): got = lax.all_to_all(send, 'seq', split_axis=0, concat_axis=0, tiled=True)]
    unnamed x10 -> x28, local copies, waits for them, and re-layouts: 4.19 us -> 10.8 us
    all_to_all x1, starting transfers between devices: 2.59 us -> 5.83 us  [body(): hist = lax.all_to_all(back, 'seq', split_axis=0, concat_axis=0, tiled=True)]
    pallas_call x5, Pallas kernels: 10.5 us -> 12.8 us  [call(): pl.pallas_call(kernel, name=name, out_shape=out_shape, in_specs=specs, ou...]
    all_to_all x1, waiting for transfers between devices: 1.85 us -> 3.24 us  [body(): hist = lax.all_to_all(back, 'seq', split_axis=0, concat_axis=0, tiled=True)]
    ppermute x1 -> x2, waiting for transfers between devices: 0.01 us -> 1.03 us  [body(): lax.ppermute(x, 'seq', partner(1))]
  transfers between devices with their start and end apart: 5 -> 7, of which waited for: 3 -> 4; matrix products, arithmetic and copies ran while one was open for 0% -> 0% of each run, Pallas kernels for 1% -> 8%
where the time goes in v5:
time: 50.6 us; the launch traced here: 49.9 us
  starting transfers between devices  15.6 us (31%)
  Pallas kernels  12.8 us (25%)
  local copies, waits for them, and re-layouts  10.8 us (21%)
  waiting for transfers between devices  10.6 us (21%)
    pallas_call x5, Pallas kernels, call(): pl.pallas_call(kernel, name=name, out_shape=out_shape, in_specs=specs, ou...  12.8 us
    unnamed x28, local copies, waits for them, and re-layouts  10.8 us
    all_to_all x1, starting transfers between devices, body(): got = lax.all_to_all(send, 'seq', split_axis=0, concat_axis=0, tiled=True)  7.3 us
    ppermute x3, waiting for transfers between devices, body(): lax.ppermute(fresh, 'seq', partner(bit))  6.34 us
    all_to_all x1, starting transfers between devices, body(): hist = lax.all_to_all(back, 'seq', split_axis=0, concat_axis=0, tiled=True)  5.83 us
    all_to_all x1, waiting for transfers between devices, body(): hist = lax.all_to_all(back, 'seq', split_axis=0, concat_axis=0, tiled=True)  3.24 us
    ppermute x3, starting transfers between devices, body(): lax.ppermute(fresh, 'seq', partner(bit))  1.96 us
    ppermute x2, waiting for transfers between devices, body(): lax.ppermute(x, 'seq', partner(1))  1.03 us
  transfers between devices with their start and end apart: 7, of which 4 were waited for; matrix products, arithmetic and copies ran while one was open for 0% of the time, Pallas kernels for 8%

profile of v5, /device:TPU:0, one launch (start us, length us, event | category | flops | bytes accessed | tf_op | source)
XLA Modules:
  0.0 49.9 jit_solution(14808991551323844097)
XLA Ops:
  0.0 1.9 %pack.1 = (bf16[32,40,128]{2,1,0:T(8,128)(2,1)}, f32[8,128]{1,0:T(8,128)}) custom-call(s32[3,1,14]{2,1,0:T(1,128)} %bitcast.3, bf16[8,1792]{1,0:T(8,128)(2,1)} %q_hbm.3, bf16[8,256]{1,0:T(8,128)(2,1)} %k_hbm.2, bf16[8,256]{1,0:T(8,128)(2,1)} %v_hbm.2), custom_call_target="tpu_custom_call" | custom-call | tf_op jit(solution)/shard_map/pack/pallas_call | solution.py:238
  1.9 7.3 %all-to-all-start = ((bf16[32,40,128]{2,1,0:T(8,128)(2,1)}), bf16[32,40,128]{2,1,0:T(8,128)(2,1)S(1)}, u32[]{:S(2)}, u32[]{:S(2)}) async-start(bf16[32,40,128]{2,1,0:T(8,128)(2,1)} %get-tuple-element.18), calls=%async_computation | async-start | bytes 655360 | tf_op jit(solution)/shard_map/all_to_all | solution.py:283
  9.2 0.0 copy-start.1
  9.2 1.0 %copy-done.1 = bf16[1024,256]{1,0:T(8,128)(2,1)S(1)} copy-done((bf16[1024,256]{1,0:T(8,128)(2,1)S(1)}, bf16[1024,256]{1,0:T(8,128)(2,1)}, u32[]{:S(2)}) %copy-start.1) | copy-done | bytes 524312
  10.3 0.0 copy-start.2
  10.3 1.0 %copy-done.2 = bf16[1024,256]{1,0:T(8,128)(2,1)S(1)} copy-done((bf16[1024,256]{1,0:T(8,128)(2,1)S(1)}, bf16[1024,256]{1,0:T(8,128)(2,1)}, u32[]{:S(2)}) %copy-start.2) | copy-done | bytes 524312
  11.3 0.0 copy-start.3
  11.3 0.7 %copy-done.3 = bf16[8,1792]{1,0:T(8,128)(2,1)S(1)} copy-done((bf16[8,1792]{1,0:T(8,128)(2,1)S(1)}, bf16[8,1792]{1,0:T(8,128)(2,1)}, u32[]{:S(2)}) %copy-start.3) | copy-done | bytes 28696
  12.1 0.0 copy-start.4
  12.1 0.7 %copy-done.4 = s32[1,14,3]{1,0,2:T(1,128)S(1)} copy-done((s32[1,14,3]{1,0,2:T(1,128)S(1)}, s32[1,14,3]{1,0,2:T(1,128)}, u32[]{:S(2)}) %copy-start.4) | copy-done | bytes 192
  12.7 0.0 copy-start.5
  12.7 0.7 %copy-done.5 = f32[8,128]{1,0:T(8,128)S(1)} copy-done((f32[8,128]{1,0:T(8,128)S(1)}, f32[8,128]{1,0:T(8,128)}, u32[]{:S(2)}) %copy-start.5) | copy-done | bytes 4120
  13.4 3.6 %split.1 = (bf16[1024,128]{1,0:T(8,128)(2,1)S(1)}, bf16[1024,128]{1,0:T(8,128)(2,1)S(1)}, bf16[1024,128]{1,0:T(8,128)(2,1)S(1)}, bf16[1024,128]{1,0:T(8,128)(2,1...) custom-call(f32[8,128]{1,0:T(8,128)S(1)} %copy-done.5, ...), custom_call_target="tpu_custom_call" | custom-call | tf_op jit(solution)/shard_map/split/pallas_call | solution.py:238
  17.0 0.0 copy-start.6
  17.0 0.7 %copy-done.6 = bf16[1024,128]{1,0:T(8,128)(2,1)} copy-done((bf16[1024,128]{1,0:T(8,128)(2,1)}, bf16[1024,128]{1,0:T(8,128)(2,1)S(1)}, u32[]{:S(2)}) %copy-start.6) | copy-done | bytes 262168
  17.7 0.0 copy-start.8
  17.7 0.7 %copy-done.8 = bf16[1024,128]{1,0:T(8,128)(2,1)} copy-done((bf16[1024,128]{1,0:T(8,128)(2,1)}, bf16[1024,128]{1,0:T(8,128)(2,1)S(1)}, u32[]{:S(2)}) %copy-start.8) | copy-done | bytes 262168
  18.4 0.0 copy-start
  18.4 0.3 collective-permute-start
  18.7 0.3 collective-permute-start.1
  18.9 1.0 %collective-permute-done.kb_ref = bf16[1024,128]{1,0:T(8,128)(2,1)S(1)} collective-permute-done((bf16[1024,128]{1,0:T(8,128)(2,1)S(1)}, bf16[1024,128]{1,0:T(8,128)(2,1)S(1)}, u32[]{:S(2)}, u32[]{:S(2)}) %collective-permute-start) | collective-permute-done | bytes 262176 | tf_op jit(solution)/shard_map/ppermute | solution.py:309
  19.9 0.0 copy-start.10
  20.0 0.7 %copy-done.10 = bf16[1024,128]{1,0:T(8,128)(2,1)} copy-done((bf16[1024,128]{1,0:T(8,128)(2,1)}, bf16[1024,128]{1,0:T(8,128)(2,1)S(1)}, u32[]{:S(2)}) %copy-start.10) | copy-done | bytes 262168
  20.6 0.0 collective-permute-done.1.vb_ref
  20.6 0.0 copy-start.12
  20.6 0.7 %copy-done.12 = bf16[1024,128]{1,0:T(8,128)(2,1)} copy-done((bf16[1024,128]{1,0:T(8,128)(2,1)}, bf16[1024,128]{1,0:T(8,128)(2,1)S(1)}, u32[]{:S(2)}) %copy-start.12) | copy-done | bytes 262168
  21.4 0.0 all-to-all-done.q_ref
  21.4 0.0 copy-start.7
  21.4 0.9 %copy-done.7 = bf16[1024,128]{1,0:T(8,128)(2,1)S(1)} copy-done((bf16[1024,128]{1,0:T(8,128)(2,1)S(1)}, bf16[1024,128]{1,0:T(8,128)(2,1)}, u32[]{:S(2)}) %copy-start.7) | copy-done | bytes 262168
  22.3 0.0 copy-start.9
  22.3 0.9 %copy-done.9 = bf16[1024,128]{1,0:T(8,128)(2,1)S(1)} copy-done((bf16[1024,128]{1,0:T(8,128)(2,1)S(1)}, bf16[1024,128]{1,0:T(8,128)(2,1)}, u32[]{:S(2)}) %copy-start.9) | copy-done | bytes 262168
  23.3 0.0 copy-start.11
  23.3 0.9 %copy-done.11 = bf16[1024,128]{1,0:T(8,128)(2,1)S(1)} copy-done((bf16[1024,128]{1,0:T(8,128)(2,1)S(1)}, bf16[1024,128]{1,0:T(8,128)(2,1)}, u32[]{:S(2)}) %copy-start.11) | copy-done | bytes 262168
  24.2 0.0 copy-start.13
  24.2 0.9 %copy-done.13 = bf16[1024,128]{1,0:T(8,128)(2,1)S(1)} copy-done((bf16[1024,128]{1,0:T(8,128)(2,1)S(1)}, bf16[1024,128]{1,0:T(8,128)(2,1)}, u32[]{:S(2)}) %copy-start.13) | copy-done | bytes 262168
  25.2 3.9 %attend.1 = (bf16[32,40,128]{2,1,0:T(8,128)(2,1)}, bf16[32,8,128]{2,1,0:T(8,128)(2,1)S(1)}) custom-call(bf16[32,40,128]{2,1,0:T(8,128)(2,1)S(1)} %all-to-all-done.q_ref, bf16[1024,128]{1,0:T(8,128)(2,1)S(1)} %copy-done.7, bf16[1024,128]{1,0:T(8,128)(2,1)S(1)} %copy-done.9, bf16[1024,128]{1,0:T(8,128)(2,1)S(1)} %copy-done.11, bf16[1024,128]{1,0:T(8,128)(2,1)S(1)} %copy-done.13), custom_call_target="tpu_custom_call" | custom-call | flops 1073741824 | bytes 4194304 | tf_op jit(solution)/shard_map/attend/pallas_call | solution.py:238
  29.1 5.8 %all-to-all-start.1 = ((bf16[32,40,128]{2,1,0:T(8,128)(2,1)}), bf16[32,40,128]{2,1,0:T(8,128)(2,1)S(1)}, u32[]{:S(2)}, u32[]{:S(2)}) async-start(bf16[32,40,128]{2,1,0:T(8,128)(2,1)} %get-tuple-element.24), calls=%async_computation.1 | async-start | bytes 655360 | tf_op jit(solution)/shard_map/all_to_all | solution.py:325
  34.9 1.6 %collective-permute-start.4 = (bf16[32,8,128]{2,1,0:T(8,128)(2,1)S(1)}, bf16[32,8,128]{2,1,0:T(8,128)(2,1)S(1)}, u32[]{:S(2)}, u32[]{:S(2)}) collective-permute-start(bf16[32,8,128]{2,1,0:T(8,128)(2,1)S(1)} %get-tuple-element.26.kv_ref), channel_id=1, source_target_pairs={{0,3},{1,2},{2,1},{3,0},{4,7},{5,6},{6,5},{7,4},{8,11},{9,10},{10,... | collective-permute-start | bytes 196616 | tf_op jit(solution)/shard_map/ppermute | solution.py:333
  36.5 0.4 collective-permute-start.3
  36.9 0.0 collective-permute-start.2
  36.9 3.6 %collective-permute-done.4.kv3_ref = bf16[32,8,128]{2,1,0:T(8,128)(2,1)S(1)} collective-permute-done((bf16[32,8,128]{2,1,0:T(8,128)(2,1)S(1)}, bf16[32,8,128]{2,1,0:T(8,128)(2,1)S(1)}, u32[]{:S(2)}, u32[]{:S(2)}) %collective-permute-start.4) | collective-permute-done | bytes 65568 | tf_op jit(solution)/shard_map/ppermute | solution.py:333
  40.4 2.8 %collective-permute-done.3.kv2_ref = bf16[32,8,128]{2,1,0:T(8,128)(2,1)S(1)} collective-permute-done((bf16[32,8,128]{2,1,0:T(8,128)(2,1)S(1)}, bf16[32,8,128]{2,1,0:T(8,128)(2,1)S(1)}, u32[]{:S(2)}, u32[]{:S(2)}) %collective-permute-start.3) | collective-permute-done | bytes 65568 | tf_op jit(solution)/shard_map/ppermute | solution.py:333
  43.2 0.0 collective-permute-done.2.kv1_ref
  43.2 0.4 fresh.1
  43.7 3.2 %all-to-all-done.1 = bf16[32,40,128]{2,1,0:T(8,128)(2,1)S(1)} async-done(((bf16[32,40,128]{2,1,0:T(8,128)(2,1)}), bf16[32,40,128]{2,1,0:T(8,128)(2,1)S(1)}, u32[]{:S(2)}, u32[]{:S(2)}) %all-to-all-start.1) | async-done | bytes 327712 | tf_op jit(solution)/shard_map/all_to_all | solution.py:325
  46.9 0.0 copy-done
  46.9 3.0 %project.1 = bf16[8,1792]{1,0:T(8,128)(2,1)} custom-call(bf16[16,2,40,128]{3,2,1,0:T(8,128)(2,1)S(1)} %bitcast.2, f32[2,56,128]{2,1,0:T(8,128)S(1)} %get-tuple-element.27.out_ref, f32[2,56,128]{2,1,0:T(8,128)S(1)} %get-tuple-element.28.lse_ref, f32[2,56,512]{2,1,0:T(8,128)S(1)} %get-tuple-element.29.match_ref, bf16[768,1792]{1,0:T(8,128)(2,1)S(1)} %copy-done, ...), custom_call_target="tpu_custom_call" | custom-call | flops 51380224 | bytes 6422528 | tf_op jit(solution)/shard_map/project/pallas_call | solution.py:238
Async XLA Ops:
  1.9 19.4 %all-to-all-start = ((bf16[32,40,128]{2,1,0:T(8,128)(2,1)}), bf16[32,40,128]{2,1,0:T(8,128)(2,1)S(1)}, u32[]{:S(2)}, u32[]{:S(2)}) async-start(bf16[32,40,128]{2,1,0:T(8,128)(2,1)} %get-tuple-element.18), calls=%async_computation | async-start | bytes 655360 | tf_op jit(solution)/shard_map/all_to_all | solution.py:283
  9.2 1.0 %copy-start.1 = (bf16[1024,256]{1,0:T(8,128)(2,1)S(1)}, bf16[1024,256]{1,0:T(8,128)(2,1)}, u32[]{:S(2)}) copy-start(bf16[1024,256]{1,0:T(8,128)(2,1)} %k_hbm.3) | copy-start | bytes 1572868
  10.3 1.0 %copy-start.2 = (bf16[1024,256]{1,0:T(8,128)(2,1)S(1)}, bf16[1024,256]{1,0:T(8,128)(2,1)}, u32[]{:S(2)}) copy-start(bf16[1024,256]{1,0:T(8,128)(2,1)} %v_hbm.3) | copy-start | bytes 1572868
  11.3 0.7 %copy-start.3 = (bf16[8,1792]{1,0:T(8,128)(2,1)S(1)}, bf16[8,1792]{1,0:T(8,128)(2,1)}, u32[]{:S(2)}) copy-start(bf16[8,1792]{1,0:T(8,128)(2,1)} %q_hbm.3) | copy-start | bytes 86020
  12.1 0.7 %copy-start.4 = (s32[1,14,3]{1,0,2:T(1,128)S(1)}, s32[1,14,3]{1,0,2:T(1,128)}, u32[]{:S(2)}) copy-start(s32[1,14,3]{1,0,2:T(1,128)} %param.12) | copy-start | bytes 508
  12.7 0.7 %copy-start.5 = (f32[8,128]{1,0:T(8,128)S(1)}, f32[8,128]{1,0:T(8,128)}, u32[]{:S(2)}) copy-start(f32[8,128]{1,0:T(8,128)} %get-tuple-element.19.after_ref) | copy-start | bytes 12292
  17.0 0.7 %copy-start.6 = (bf16[1024,128]{1,0:T(8,128)(2,1)}, bf16[1024,128]{1,0:T(8,128)(2,1)S(1)}, u32[]{:S(2)}) copy-start(bf16[1024,128]{1,0:T(8,128)(2,1)S(1)} %get-tuple-element.20.ka_ref) | copy-start | bytes 786436
  17.7 0.7 %copy-start.8 = (bf16[1024,128]{1,0:T(8,128)(2,1)}, bf16[1024,128]{1,0:T(8,128)(2,1)S(1)}, u32[]{:S(2)}) copy-start(bf16[1024,128]{1,0:T(8,128)(2,1)S(1)} %get-tuple-element.21.va_ref) | copy-start | bytes 786436
  18.4 28.5 %copy-start = (bf16[768,1792]{1,0:T(8,128)(2,1)S(1)}, bf16[768,1792]{1,0:T(8,128)(2,1)}, u32[]{:S(2)}) copy-start(bf16[768,1792]{1,0:T(8,128)(2,1)} %get-tuple-element.30.first_ref) | copy-start | bytes 8257540
  18.4 1.5 %collective-permute-start = (bf16[1024,128]{1,0:T(8,128)(2,1)S(1)}, bf16[1024,128]{1,0:T(8,128)(2,1)S(1)}, u32[]{:S(2)}, u32[]{:S(2)}) collective-permute-start(bf16[1024,128]{1,0:T(8,128)(2,1)S(1)} %get-tuple-element.22), channel_id=1, source_target_pairs={{0,1},{1,0},{2,3},{3,2},{4,5},{5,4},{6,7},{7,6},{8,9},{9,8},{10,11... | collective-permute-start | bytes 786440 | tf_op jit(solution)/shard_map/ppermute | solution.py:309
  18.7 2.0 %collective-permute-start.1 = (bf16[1024,128]{1,0:T(8,128)(2,1)S(1)}, bf16[1024,128]{1,0:T(8,128)(2,1)S(1)}, u32[]{:S(2)}, u32[]{:S(2)}) collective-permute-start(bf16[1024,128]{1,0:T(8,128)(2,1)S(1)} %get-tuple-element.23), channel_id=1, source_target_pairs={{0,1},{1,0},{2,3},{3,2},{4,5},{5,4},{6,7},{7,6},{8,9},{9,8},{10,11... | collective-permute-start | bytes 786440 | tf_op jit(solution)/shard_map/ppermute | solution.py:309
  19.9 0.7 %copy-start.10 = (bf16[1024,128]{1,0:T(8,128)(2,1)}, bf16[1024,128]{1,0:T(8,128)(2,1)S(1)}, u32[]{:S(2)}) copy-start(bf16[1024,128]{1,0:T(8,128)(2,1)S(1)} %collective-permute-done.kb_ref) | copy-start | bytes 786436
  20.6 0.7 %copy-start.12 = (bf16[1024,128]{1,0:T(8,128)(2,1)}, bf16[1024,128]{1,0:T(8,128)(2,1)S(1)}, u32[]{:S(2)}) copy-start(bf16[1024,128]{1,0:T(8,128)(2,1)S(1)} %collective-permute-done.1.vb_ref) | copy-start | bytes 786436
  21.4 1.0 %copy-start.7 = (bf16[1024,128]{1,0:T(8,128)(2,1)S(1)}, bf16[1024,128]{1,0:T(8,128)(2,1)}, u32[]{:S(2)}) copy-start(bf16[1024,128]{1,0:T(8,128)(2,1)} %copy-done.6) | copy-start | bytes 786436
  22.3 0.9 %copy-start.9 = (bf16[1024,128]{1,0:T(8,128)(2,1)S(1)}, bf16[1024,128]{1,0:T(8,128)(2,1)}, u32[]{:S(2)}) copy-start(bf16[1024,128]{1,0:T(8,128)(2,1)} %copy-done.8) | copy-start | bytes 786436
  23.3 0.9 %copy-start.11 = (bf16[1024,128]{1,0:T(8,128)(2,1)S(1)}, bf16[1024,128]{1,0:T(8,128)(2,1)}, u32[]{:S(2)}) copy-start(bf16[1024,128]{1,0:T(8,128)(2,1)} %copy-done.10) | copy-start | bytes 786436
  24.2 0.9 %copy-start.13 = (bf16[1024,128]{1,0:T(8,128)(2,1)S(1)}, bf16[1024,128]{1,0:T(8,128)(2,1)}, u32[]{:S(2)}) copy-start(bf16[1024,128]{1,0:T(8,128)(2,1)} %copy-done.12) | copy-start | bytes 786436
  29.1 17.8 %all-to-all-start.1 = ((bf16[32,40,128]{2,1,0:T(8,128)(2,1)}), bf16[32,40,128]{2,1,0:T(8,128)(2,1)S(1)}, u32[]{:S(2)}, u32[]{:S(2)}) async-start(bf16[32,40,128]{2,1,0:T(8,128)(2,1)} %get-tuple-element.24), calls=%async_computation.1 | async-start | bytes 655360 | tf_op jit(solution)/shard_map/all_to_all | solution.py:325
  34.9 5.5 %collective-permute-start.4 = (bf16[32,8,128]{2,1,0:T(8,128)(2,1)S(1)}, bf16[32,8,128]{2,1,0:T(8,128)(2,1)S(1)}, u32[]{:S(2)}, u32[]{:S(2)}) collective-permute-start(bf16[32,8,128]{2,1,0:T(8,128)(2,1)S(1)} %get-tuple-element.26.kv_ref), channel_id=1, source_target_pairs={{0,3},{1,2},{2,1},{3,0},{4,7},{5,6},{6,5},{7,4},{8,11},{9,10},{10,... | collective-permute-start | bytes 196616 | tf_op jit(solution)/shard_map/ppermute | solution.py:333
  36.5 6.7 %collective-permute-start.3 = (bf16[32,8,128]{2,1,0:T(8,128)(2,1)S(1)}, bf16[32,8,128]{2,1,0:T(8,128)(2,1)S(1)}, u32[]{:S(2)}, u32[]{:S(2)}) collective-permute-start(bf16[32,8,128]{2,1,0:T(8,128)(2,1)S(1)} %get-tuple-element.26.kv_ref), channel_id=1, source_target_pairs={{0,2},{1,3},{2,0},{3,1},{4,6},{5,7},{6,4},{7,5},{8,10},{9,11},{10,... | collective-permute-start | bytes 196616 | tf_op jit(solution)/shard_map/ppermute | solution.py:333
  36.9 6.4 %collective-permute-start.2 = (bf16[32,8,128]{2,1,0:T(8,128)(2,1)S(1)}, bf16[32,8,128]{2,1,0:T(8,128)(2,1)S(1)}, u32[]{:S(2)}, u32[]{:S(2)}) collective-permute-start(bf16[32,8,128]{2,1,0:T(8,128)(2,1)S(1)} %get-tuple-element.26.kv_ref), channel_id=1, source_target_pairs={{0,1},{1,0},{2,3},{3,2},{4,5},{5,4},{6,7},{7,6},{8,9},{9,8},{10,11... | collective-permute-start | bytes 196616 | tf_op jit(solution)/shard_map/ppermute | solution.py:333

commit v6 on v5

--- a/solution.py
+++ b/solution.py
@@ -47,7 +47,7 @@
     return copies
 
 
-def pack_kernel(chips, capacity, chosen_hbm, q_hbm, k_hbm, v_hbm, send_ref, after_ref, chosen_ref, q_ref, k_ref, v_ref, sems):
+def pack_kernel(chips, capacity, chosen_hbm, q_hbm, k_hbm, v_hbm, send_ref, chosen_ref, q_ref, k_ref, v_ref, sems):
     copies = fetch([(chosen_hbm, chosen_ref), (q_hbm, q_ref), (k_hbm, k_ref), (v_hbm, v_ref)], sems)
     tokens = q_ref.shape[0]
     per = capacity * tokens
@@ -73,39 +73,16 @@
                 to = b * span + chip * KVH + g
                 send_ref[to, :per, :] = slots[b * per : (b + 1) * per]
                 send_ref[to, per:, :] = fresh[chip % 2]
-    after_ref[...] = jnp.zeros_like(after_ref)
-
-
-def split_kernel(
-    chips, capacity, after_ref, k_hbm, v_hbm, chosen_hbm, q_hbm, w_hbm,
-    k_own, v_own, k_away, v_away, match_ref, rows_ref, w_ref, chosen_ref, q_ref, sems,
-):
-    core = lax.axis_index("seq") % KVH
-    own = pl.ds(pl.multiple_of(core * HD, HD), HD)
-    away = pl.ds(pl.multiple_of((1 - core) * HD, HD), HD)
-    copies = fetch(
-        [
-            (k_hbm.at[:, away], k_away),
-            (v_hbm.at[:, away], v_away),
-            (chosen_hbm, chosen_ref),
-            (q_hbm, q_ref),
-            (k_hbm.at[:, own], k_own),
-            (v_hbm.at[:, own], v_own),
-            (w_hbm.at[: w_ref.shape[0]], w_ref),
-        ],
-        sems,
-    )
+
+
+def masks_kernel(chips, capacity, chosen_ref, q_ref, match_ref, rows_ref):
     tokens = q_ref.shape[0]
     per = capacity * tokens
     lane = lax.broadcasted_iota(jnp.int32, (tokens, match_ref.shape[2]), 1)
     block, slot, token = lane // (per * chips), lane % per // tokens, lane % tokens
-    copies[2].wait()
-    copies[3].wait()
     for g in range(KVH):
         match_ref[g] = jnp.concatenate(slot_match(chosen_ref, g, block, slot, token), axis=0)
         rows_ref[g] = jnp.concatenate(head_rows(q_ref, g), axis=0)
-    for i in (0, 1, 4, 5, 6):
-        copies[i].wait()
 
 
 def attend_kernel(per, q_ref, ka_ref, va_ref, kb_ref, vb_ref, out_ref, fresh_ref):
@@ -144,7 +121,8 @@
             ).astype(jnp.bfloat16)
 
 
-def fresh_kernel(tokens, rows_ref, kv_ref, kv1_ref, kv2_ref, kv3_ref, out_ref, lse_ref):
+def fresh_kernel(tokens, rows_ref, kv_ref, kv1_ref, kv2_ref, kv3_ref, w_hbm, out_ref, lse_ref, w_ref, sems):
+    copies = fetch([(w_hbm.at[: w_ref.shape[0]], w_ref)], sems)
     sources = kv_ref.shape[0]
     place = lax.axis_index("seq")
     core, odd = place % KVH, place // KVH % 2
@@ -172,6 +150,8 @@
         total = total_out[:, HD:]
         out_ref[g] = total_out[:, :HD] / total
         lse_ref[g] = top + jnp.log(total) * LOG2E
+    for copy in copies:
+        copy.wait()
 
 
 def project_kernel(per, hist_ref, out_ref, lse_ref, match_ref, first_ref, w_hbm, y_ref, att_ref, w_ref, sems):
@@ -262,13 +242,10 @@
     def partner(bit):
         return [(i, i ^ bit) for i in range(devices)]
 
-    send, after = call(
+    send = call(
         functools.partial(pack_kernel, chips, capacity),
         "pack",
-        (
-            jax.ShapeDtypeStruct((devices, per + tokens, HD), bf16),
-            jax.ShapeDtypeStruct((8, LANES), f32),
-        ),
+        jax.ShapeDtypeStruct((devices, per + tokens, HD), bf16),
         [HBM] * 4,
         picks, queries, stretch_keys, stretch_values,
         scratch=[
@@ -280,33 +257,29 @@
         ],
         limit=60,
     )
+    send, cache_keys, cache_values, picks, queries = lax.optimization_barrier(
+        (send, cache_keys, cache_values, picks, queries)
+    )
     got = lax.all_to_all(send, "seq", split_axis=0, concat_axis=0, tiled=True)
 
+    core = lax.axis_index("seq") % KVH
+
+    def halves(head):
+        return [lax.dynamic_slice_in_dim(x, head * HD, HD, axis=1) for x in (cache_keys, cache_values)]
+
+    k_own, v_own = halves(core)
+    k_peer, v_peer = [lax.ppermute(x, "seq", partner(1)) for x in halves(1 - core)]
     holders = devices // KVH
-    ready = EARLY * KVH * HD
-    side = jax.ShapeDtypeStruct((cache_rows, HD), bf16)
-    k_own, v_own, k_away, v_away, match, query_rows, first = call(
-        functools.partial(split_kernel, chips, capacity),
-        "split",
+    match, query_rows = call(
+        functools.partial(masks_kernel, chips, capacity),
+        "masks",
         (
-            side,
-            side,
-            side,
-            side,
             jax.ShapeDtypeStruct((KVH, GROUP * tokens, holders * per), f32),
             jax.ShapeDtypeStruct((KVH, GROUP * tokens, HD), f32),
-            jax.ShapeDtypeStruct((ready, out_weight.shape[1]), bf16),
         ),
-        [VMEM] + [HBM] * 5,
-        after, cache_keys, cache_values, picks, queries, out_weight,
-        scratch=[
-            pltpu.VMEM(picks.shape, jnp.int32),
-            pltpu.VMEM(queries.shape, bf16),
-            pltpu.SemaphoreType.DMA((7,)),
-        ],
-        limit=50,
-    )
-    k_peer, v_peer = [lax.ppermute(x, "seq", partner(1)) for x in (k_away, v_away)]
+        [VMEM] * 2,
+        picks, queries,
+    )
 
     rows = devices * per
     back, fresh = call(
@@ -324,15 +297,20 @@
     )
     hist = lax.all_to_all(back, "seq", split_axis=0, concat_axis=0, tiled=True)
 
+    far = lax.ppermute(fresh, "seq", partner(2))
+    near, both = [lax.ppermute(x, "seq", partner(1)) for x in (fresh, far)]
     part = jax.ShapeDtypeStruct((KVH, GROUP * tokens, HD), f32)
-    out, lse = call(
+    ready = EARLY * KVH * HD
+    out, lse, first = call(
         functools.partial(fresh_kernel, tokens),
         "fresh",
-        (part, part),
-        [VMEM] * 5,
-        query_rows, fresh, *[lax.ppermute(fresh, "seq", partner(bit)) for bit in (1, 2, 3)],
+        (part, part, jax.ShapeDtypeStruct((ready, out_weight.shape[1]), bf16)),
+        [VMEM] * 5 + [HBM],
+        query_rows, fresh, near, far, both, out_weight,
+        scratch=[pltpu.SemaphoreType.DMA((1,))],
         flops=8 * H * tokens * devices * tokens * HD,
         moved=1 << 20,
+        limit=50,
     )
     return call(
         functools.partial(project_kernel, per),

time: 50.6 us -> 43.1 us (0.85)
  local copies, waits for them, and re-layouts: 10.8 us -> 2.14 us
  waiting for transfers between devices: 10.6 us -> 17.5 us
  starting transfers between devices: 15.6 us -> 12.2 us
  Pallas kernels: 12.8 us -> 10.7 us
    unnamed x28 -> x4, local copies, waits for them, and re-layouts: 10.8 us -> 0.01 us
    all_to_all x1, waiting for transfers between devices: 0.01 us -> 7.91 us  [body(): got = lax.all_to_all(send, 'seq', split_axis=0, concat_axis=0, tiled=True)]
    all_to_all x1, starting transfers between devices: 5.83 us -> 2.59 us  [body(): hist = lax.all_to_all(back, 'seq', split_axis=0, concat_axis=0, tiled=True)]
    dynamic_slice x0 -> x2, local copies, waits for them, and re-layouts: none -> 2.13 us  [halves(): lax.dynamic_slice_in_dim(x, head * HD, HD, axis=1)]
    pallas_call x5, Pallas kernels: 12.8 us -> 10.7 us  [call(): pl.pallas_call(kernel, name=name, out_shape=out_shape, in_specs=specs, ou...]
    all_to_all x1, waiting for transfers between devices: 3.24 us -> 2.37 us  [body(): hist = lax.all_to_all(back, 'seq', split_axis=0, concat_axis=0, tiled=True)]
  transfers between devices with their start and end apart: 7 -> 7, of which waited for: 4 -> 5; matrix products, arithmetic and copies ran while one was open for 0% -> 5% of each run, Pallas kernels for 8% -> 5%
where the time goes in v6:
time: 43.1 us; the launch traced here: 42.7 us
  waiting for transfers between devices  17.5 us (41%)
  starting transfers between devices  12.2 us (28%)
  Pallas kernels  10.7 us (25%)
  local copies, waits for them, and re-layouts  2.14 us (5%)
    pallas_call x5, Pallas kernels, call(): pl.pallas_call(kernel, name=name, out_shape=out_shape, in_specs=specs, ou...  10.7 us
    all_to_all x1, waiting for transfers between devices, body(): got = lax.all_to_all(send, 'seq', split_axis=0, concat_axis=0, tiled=True)  7.91 us
    all_to_all x1, starting transfers between devices, body(): got = lax.all_to_all(send, 'seq', split_axis=0, concat_axis=0, tiled=True)  7.3 us
    ppermute x1, waiting for transfers between devices, body(): far = lax.ppermute(fresh, 'seq', partner(2))  4.83 us
    all_to_all x1, starting transfers between devices, body(): hist = lax.all_to_all(back, 'seq', split_axis=0, concat_axis=0, tiled=True)  2.59 us
    all_to_all x1, waiting for transfers between devices, body(): hist = lax.all_to_all(back, 'seq', split_axis=0, concat_axis=0, tiled=True)  2.37 us
    dynamic_slice x2, local copies, waits for them, and re-layouts, halves(): lax.dynamic_slice_in_dim(x, head * HD, HD, axis=1)  2.13 us
    ppermute x1, starting transfers between devices, body(): far = lax.ppermute(fresh, 'seq', partner(2))  1.7 us
  transfers between devices with their start and end apart: 7, of which 5 were waited for; matrix products, arithmetic and copies ran while one was open for 5% of the time, Pallas kernels for 5%

profile of v6, /device:TPU:0, one launch (start us, length us, event | category | flops | bytes accessed | tf_op | source)
XLA Modules:
  0.0 42.7 jit_solution(3321861703837759921)
XLA Ops:
  0.0 0.0 copy-start
  0.0 0.0 copy-start.1
  0.0 1.9 %pack.1 = bf16[32,40,128]{2,1,0:T(8,128)(2,1)} custom-call(s32[3,1,14]{2,1,0:T(1,128)} %bitcast.3, bf16[8,1792]{1,0:T(8,128)(2,1)} %q_ref, bf16[8,256]{1,0:T(8,128)(2,1)} %k_hbm.1, bf16[8,256]{1,0:T(8,128)(2,1)} %v_hbm.1), custom_call_target="tpu_custom_call" | custom-call | tf_op jit(solution)/shard_map/pack/pallas_call | solution.py:218
  2.0 7.3 %all-to-all-start = ((bf16[32,40,128]{2,1,0:T(8,128)(2,1)}), bf16[32,40,128]{2,1,0:T(8,128)(2,1)S(1)}, u32[]{:S(2)}, u32[]{:S(2)}) async-start(bf16[32,40,128]{2,1,0:T(8,128)(2,1)} %pack.1), calls=%async_computation | async-start | bytes 655360 | tf_op jit(solution)/shard_map/all_to_all | solution.py:263
  9.3 1.1 %constant_dynamic-slice_fusion.1 = (bf16[1024,128]{1,0:T(8,128)(2,1)S(1)}, bf16[1024,128]{1,0:T(8,128)(2,1)S(1)}) fusion(bf16[1024,256]{1,0:T(8,128)(2,1)} %param.10, s32[]{:T(128)S(6)} %select_n.17, s32[]{:T(128)S(6)} %select_n.16), kind=kLoop, calls=%fused_computation.1 | loop fusion | bytes 1048584 | tf_op jit(solution)/shard_map/dynamic_slice | solution.py:268
  10.4 0.3 collective-permute-start
  10.7 1.1 %constant_dynamic-slice_fusion = (bf16[1024,128]{1,0:T(8,128)(2,1)S(1)}, bf16[1024,128]{1,0:T(8,128)(2,1)S(1)}) fusion(bf16[1024,256]{1,0:T(8,128)(2,1)} %param.11, s32[]{:T(128)S(6)} %select_n.17, s32[]{:T(128)S(6)} %select_n.16), kind=kLoop, calls=%fused_computation | loop fusion | bytes 1048584 | tf_op jit(solution)/shard_map/dynamic_slice | solution.py:268
  11.7 0.3 collective-permute-start.1
  12.1 0.0 collective-permute-done.kb_ref
  12.1 1.3 %collective-permute-done.1.vb_ref = bf16[1024,128]{1,0:T(8,128)(2,1)S(1)} collective-permute-done((bf16[1024,128]{1,0:T(8,128)(2,1)S(1)}, bf16[1024,128]{1,0:T(8,128)(2,1)S(1)}, u32[]{:S(2)}, u32[]{:S(2)}) %collective-permute-start.1) | collective-permute-done | bytes 262176 | tf_op jit(solution)/shard_map/ppermute | solution.py:271
  13.3 7.9 %all-to-all-done.q_ref = bf16[32,40,128]{2,1,0:T(8,128)(2,1)S(1)} async-done(((bf16[32,40,128]{2,1,0:T(8,128)(2,1)}), bf16[32,40,128]{2,1,0:T(8,128)(2,1)S(1)}, u32[]{:S(2)}, u32[]{:S(2)}) %all-to-all-start) | async-done | bytes 327712 | tf_op jit(solution)/shard_map/all_to_all | solution.py:263
  21.3 3.8 %attend.1 = (bf16[32,40,128]{2,1,0:T(8,128)(2,1)}, bf16[32,8,128]{2,1,0:T(8,128)(2,1)S(1)}) custom-call(bf16[32,40,128]{2,1,0:T(8,128)(2,1)S(1)} %all-to-all-done.q_ref, bf16[1024,128]{1,0:T(8,128)(2,1)S(1)} %get-tuple-element.32.ka_ref, bf16[1024,128]{1,0:T(8,128)(2,1)S(1)} %get-tuple-element.30.va_ref, bf16[1024,128]{1,0:T(8,128)(2,1)S(1)} %collective-permute-done.kb_ref, ...), custom_call_target="tpu_custom_call" | custom-call | flops 1073741824 | bytes 4194304 | tf_op jit(solution)/shard_map/attend/pallas_call | solution.py:218
  25.1 2.6 %all-to-all-start.1 = ((bf16[32,40,128]{2,1,0:T(8,128)(2,1)}), bf16[32,40,128]{2,1,0:T(8,128)(2,1)S(1)}, u32[]{:S(2)}, u32[]{:S(2)}) async-start(bf16[32,40,128]{2,1,0:T(8,128)(2,1)} %get-tuple-element.20), calls=%async_computation.1 | async-start | bytes 655360 | tf_op jit(solution)/shard_map/all_to_all | solution.py:298
  27.7 1.7 %collective-permute-start.3 = (bf16[32,8,128]{2,1,0:T(8,128)(2,1)S(1)}, bf16[32,8,128]{2,1,0:T(8,128)(2,1)S(1)}, u32[]{:S(2)}, u32[]{:S(2)}) collective-permute-start(bf16[32,8,128]{2,1,0:T(8,128)(2,1)S(1)} %get-tuple-element.24.kv_ref), channel_id=1, source_target_pairs={{0,2},{1,3},{2,0},{3,1},{4,6},{5,7},{6,4},{7,5},{8,10},{9,11},{10,... | collective-permute-start | bytes 196616 | tf_op jit(solution)/shard_map/ppermute | solution.py:300
  29.4 0.0 collective-permute-start.2
  29.4 4.8 %collective-permute-done.3.kv2_ref = bf16[32,8,128]{2,1,0:T(8,128)(2,1)S(1)} collective-permute-done((bf16[32,8,128]{2,1,0:T(8,128)(2,1)S(1)}, bf16[32,8,128]{2,1,0:T(8,128)(2,1)S(1)}, u32[]{:S(2)}, u32[]{:S(2)}) %collective-permute-start.3) | collective-permute-done | bytes 65568 | tf_op jit(solution)/shard_map/ppermute | solution.py:300
  34.2 0.0 collective-permute-start.4
  34.2 0.0 copy-done
  34.2 0.0 copy-done.1
  34.2 0.1 masks.1
  34.4 0.0 collective-permute-done.2.kv1_ref
  34.4 1.1 %collective-permute-done.4.kv3_ref = bf16[32,8,128]{2,1,0:T(8,128)(2,1)S(1)} collective-permute-done((bf16[32,8,128]{2,1,0:T(8,128)(2,1)S(1)}, bf16[32,8,128]{2,1,0:T(8,128)(2,1)S(1)}, u32[]{:S(2)}, u32[]{:S(2)}) %collective-permute-start.4) | collective-permute-done | bytes 65568 | tf_op jit(solution)/shard_map/ppermute | solution.py:301
  35.5 1.8 %fresh.1 = (f32[2,56,128]{2,1,0:T(8,128)S(1)}, f32[2,56,128]{2,1,0:T(8,128)S(1)}, bf16[768,1792]{1,0:T(8,128)(2,1)S(1)}) custom-call(f32[2,56,128]{2,1,0:T(8,128)S(1)} %get-tuple-element.23.rows_ref, bf16[32,8,128]{2,1,0:T(8,128)(2,1)S(1)} %get-tuple-element.24.kv_ref, bf16[32,8,128]{2,1,0:T(8,128)(2,1)S(1)} %collective-permute-done.2.kv1_ref, ...), custom_call_target="tpu_custom_call" | custom-call | flops 29360128 | bytes 1048576 | tf_op jit(solution)/shard_map/fresh/pallas_call | solution.py:218
  37.3 2.4 %all-to-all-done.1 = bf16[32,40,128]{2,1,0:T(8,128)(2,1)S(1)} async-done(((bf16[32,40,128]{2,1,0:T(8,128)(2,1)}), bf16[32,40,128]{2,1,0:T(8,128)(2,1)S(1)}, u32[]{:S(2)}, u32[]{:S(2)}) %all-to-all-start.1) | async-done | bytes 327712 | tf_op jit(solution)/shard_map/all_to_all | solution.py:298
  39.7 3.0 %project.1 = bf16[8,1792]{1,0:T(8,128)(2,1)} custom-call(bf16[16,2,40,128]{3,2,1,0:T(8,128)(2,1)S(1)} %bitcast.2, f32[2,56,128]{2,1,0:T(8,128)S(1)} %get-tuple-element.25.out_ref, f32[2,56,128]{2,1,0:T(8,128)S(1)} %get-tuple-element.26.lse_ref, f32[2,56,512]{2,1,0:T(8,128)S(1)} %get-tuple-element.27.match_ref, ...), custom_call_target="tpu_custom_call" | custom-call | flops 51380224 | bytes 6422528 | tf_op jit(solution)/shard_map/project/pallas_call | solution.py:218
Async XLA Ops:
  0.0 34.2 %copy-start = (bf16[8,1792]{1,0:T(8,128)(2,1)S(1)}, bf16[8,1792]{1,0:T(8,128)(2,1)}, u32[]{:S(2)}) copy-start(bf16[8,1792]{1,0:T(8,128)(2,1)} %q_ref) | copy-start | bytes 86020
  0.0 34.2 %copy-start.1 = (s32[1,14,3]{1,0,2:T(1,128)S(1)}, s32[1,14,3]{1,0,2:T(1,128)}, u32[]{:S(2)}) copy-start(s32[1,14,3]{1,0,2:T(1,128)} %param.12) | copy-start | bytes 508
  2.0 19.3 %all-to-all-start = ((bf16[32,40,128]{2,1,0:T(8,128)(2,1)}), bf16[32,40,128]{2,1,0:T(8,128)(2,1)S(1)}, u32[]{:S(2)}, u32[]{:S(2)}) async-start(bf16[32,40,128]{2,1,0:T(8,128)(2,1)} %pack.1), calls=%async_computation | async-start | bytes 655360 | tf_op jit(solution)/shard_map/all_to_all | solution.py:263
  10.4 1.7 %collective-permute-start = (bf16[1024,128]{1,0:T(8,128)(2,1)S(1)}, bf16[1024,128]{1,0:T(8,128)(2,1)S(1)}, u32[]{:S(2)}, u32[]{:S(2)}) collective-permute-start(bf16[1024,128]{1,0:T(8,128)(2,1)S(1)} %get-tuple-element.31), channel_id=1, source_target_pairs={{0,1},{1,0},{2,3},{3,2},{4,5},{5,4},{6,7},{7,6},{8,9},{9,8},{10,11... | collective-permute-start | bytes 786440 | tf_op jit(solution)/shard_map/ppermute | solution.py:271
  11.7 1.6 %collective-permute-start.1 = (bf16[1024,128]{1,0:T(8,128)(2,1)S(1)}, bf16[1024,128]{1,0:T(8,128)(2,1)S(1)}, u32[]{:S(2)}, u32[]{:S(2)}) collective-permute-start(bf16[1024,128]{1,0:T(8,128)(2,1)S(1)} %get-tuple-element.29), channel_id=1, source_target_pairs={{0,1},{1,0},{2,3},{3,2},{4,5},{5,4},{6,7},{7,6},{8,9},{9,8},{10,11... | collective-permute-start | bytes 786440 | tf_op jit(solution)/shard_map/ppermute | solution.py:271
  25.1 14.6 %all-to-all-start.1 = ((bf16[32,40,128]{2,1,0:T(8,128)(2,1)}), bf16[32,40,128]{2,1,0:T(8,128)(2,1)S(1)}, u32[]{:S(2)}, u32[]{:S(2)}) async-start(bf16[32,40,128]{2,1,0:T(8,128)(2,1)} %get-tuple-element.20), calls=%async_computation.1 | async-start | bytes 655360 | tf_op jit(solution)/shard_map/all_to_all | solution.py:298
  27.7 6.5 %collective-permute-start.3 = (bf16[32,8,128]{2,1,0:T(8,128)(2,1)S(1)}, bf16[32,8,128]{2,1,0:T(8,128)(2,1)S(1)}, u32[]{:S(2)}, u32[]{:S(2)}) collective-permute-start(bf16[32,8,128]{2,1,0:T(8,128)(2,1)S(1)} %get-tuple-element.24.kv_ref), channel_id=1, source_target_pairs={{0,2},{1,3},{2,0},{3,1},{4,6},{5,7},{6,4},{7,5},{8,10},{9,11},{10,... | collective-permute-start | bytes 196616 | tf_op jit(solution)/shard_map/ppermute | solution.py:300
  29.4 5.0 %collective-permute-start.2 = (bf16[32,8,128]{2,1,0:T(8,128)(2,1)S(1)}, bf16[32,8,128]{2,1,0:T(8,128)(2,1)S(1)}, u32[]{:S(2)}, u32[]{:S(2)}) collective-permute-start(bf16[32,8,128]{2,1,0:T(8,128)(2,1)S(1)} %get-tuple-element.24.kv_ref), channel_id=1, source_target_pairs={{0,1},{1,0},{2,3},{3,2},{4,5},{5,4},{6,7},{7,6},{8,9},{9,8},{10,11... | collective-permute-start | bytes 196616 | tf_op jit(solution)/shard_map/ppermute | solution.py:301
  34.2 1.3 %collective-permute-start.4 = (bf16[32,8,128]{2,1,0:T(8,128)(2,1)S(1)}, bf16[32,8,128]{2,1,0:T(8,128)(2,1)S(1)}, u32[]{:S(2)}, u32[]{:S(2)}) collective-permute-start(bf16[32,8,128]{2,1,0:T(8,128)(2,1)S(1)} %collective-permute-done.3.kv2_ref), channel_id=1, source_target_pairs={{0,1},{1,0},{2,3},{3,2},{4,5},{5,4},{6,7},{7,6},{8,9},{9,8},{10,11... | collective-permute-start | bytes 196616 | tf_op jit(solution)/shard_map/ppermute | solution.py:301

commit v7 on v6

--- a/solution.py
+++ b/solution.py
@@ -19,6 +19,7 @@
 LOG2E = math.log2(math.e)
 LANES = 128
 EARLY = 3
+SPAN = 4
 
 
 def head_rows(q_ref, g):
@@ -47,32 +48,44 @@
     return copies
 
 
-def pack_kernel(chips, capacity, chosen_hbm, q_hbm, k_hbm, v_hbm, send_ref, chosen_ref, q_ref, k_ref, v_ref, sems):
+def pack_kernel(capacity, chosen_hbm, q_hbm, k_hbm, v_hbm, send_ref, chosen_ref, q_ref, k_ref, v_ref, sems):
     copies = fetch([(chosen_hbm, chosen_ref), (q_hbm, q_ref), (k_hbm, k_ref), (v_hbm, v_ref)], sems)
+    core = lax.axis_index("seq") % KVH
     tokens = q_ref.shape[0]
     per = capacity * tokens
-    span = chips * KVH
-    key_blocks = send_ref.shape[0] // span
+    key_blocks = send_ref.shape[0]
     lane = lax.broadcasted_iota(jnp.int32, (tokens, key_blocks * per), 1)
     block, slot, token = lane // per, lane % per // tokens, lane % tokens
     for copy in copies:
         copy.wait()
+    slots = []
     for g in range(KVH):
         spread = jnp.concatenate(
             slot_match(chosen_ref, g, block, slot, token) + [jnp.zeros(lane.shape, jnp.float32)], axis=0
         )
         rows = head_rows(q_ref, g)
         rows = jnp.concatenate(rows + [jnp.zeros_like(rows[0])], axis=0)
-        slots = jnp.dot(
-            spread.T.astype(jnp.bfloat16), rows.astype(jnp.bfloat16), preferred_element_type=jnp.float32
-        ).astype(jnp.bfloat16)
-        cols = slice(g * HD, (g + 1) * HD)
-        fresh = [k_ref[:, cols], v_ref[:, cols]]
-        for b in range(key_blocks):
-            for chip in range(chips):
-                to = b * span + chip * KVH + g
-                send_ref[to, :per, :] = slots[b * per : (b + 1) * per]
-                send_ref[to, per:, :] = fresh[chip % 2]
+        slots.append(
+            jnp.dot(
+                spread.T.astype(jnp.bfloat16), rows.astype(jnp.bfloat16), preferred_element_type=jnp.float32
+            )
+        )
+    ordered = [
+        jnp.where(core == 0, slots[0], slots[1]).astype(jnp.bfloat16),
+        jnp.where(core == 0, slots[1], slots[0]).astype(jnp.bfloat16),
+    ]
+    fresh = jnp.concatenate(
+        [
+            ref[:, g * HD : (g + 1) * HD].astype(jnp.float32)
+            for g in range(KVH)
+            for ref in (k_ref, v_ref)
+        ],
+        axis=0,
+    ).astype(jnp.bfloat16)
+    for b in range(key_blocks):
+        for i in range(KVH):
+            send_ref[b, i * per : (i + 1) * per, :] = ordered[i][b * per : (b + 1) * per]
+        send_ref[b, KVH * per :, :] = fresh
 
 
 def masks_kernel(chips, capacity, chosen_ref, q_ref, match_ref, rows_ref):
@@ -85,9 +98,9 @@
         rows_ref[g] = jnp.concatenate(head_rows(q_ref, g), axis=0)
 
 
-def attend_kernel(per, q_ref, ka_ref, va_ref, kb_ref, vb_ref, out_ref, fresh_ref):
-    sources = q_ref.shape[0]
-    fresh_ref[...] = q_ref[:, per:, :]
+def attend_kernel(q0_ref, q1_ref, q2_ref, q3_ref, ka_ref, va_ref, kb_ref, vb_ref, out_ref):
+    place = lax.axis_index("seq") % SPAN
+    sources, per = q0_ref.shape[:2]
     step = 256 // per
     scale = LOG2E * HD**-0.5
     nt = (((1,), (1,)), ((), ()))
@@ -96,51 +109,54 @@
     diagonal = row == lane % per
     piece = lax.broadcasted_iota(jnp.int32, (8, LANES), 0)
     ones = jnp.ones(va_ref.shape, jnp.bfloat16)
-    for first in range(0, sources, step):
-        q = q_ref[first : first + step, :per, :].reshape(step * per, HD)
-        sa = lax.dot_general(q, ka_ref[...], nt, preferred_element_type=jnp.float32)
-        sb = lax.dot_general(q, kb_ref[...], nt, preferred_element_type=jnp.float32)
-        top = jnp.maximum(jnp.max(sa, axis=1, keepdims=True), jnp.max(sb, axis=1, keepdims=True)) * scale
-        wa = jnp.exp2(sa * scale - top).astype(jnp.bfloat16)
-        wb = jnp.exp2(sb * scale - top).astype(jnp.bfloat16)
-        both = jnp.dot(
-            wa, jnp.concatenate([va_ref[...], ones], axis=1), preferred_element_type=jnp.float32
-        ) + jnp.dot(wb, jnp.concatenate([vb_ref[...], ones], axis=1), preferred_element_type=jnp.float32)
-        total = both[:, HD:]
-        out = (both[:, :HD] / total).astype(jnp.bfloat16)
-        lse = top + jnp.log(total) * LOG2E
-        for s in range(step):
-            part = slice(s * per, (s + 1) * per)
-            out_ref[first + s, :per, :] = out[part]
-            flat = jnp.sum(jnp.where(diagonal, lse[part], 0.0), axis=0, keepdims=True)
-            hi = flat.astype(jnp.bfloat16).astype(jnp.float32)
-            mid = (flat - hi).astype(jnp.bfloat16).astype(jnp.float32)
-            low = flat - hi - mid
-            out_ref[first + s, per:, :] = jnp.where(
-                piece == 0, hi, jnp.where(piece == 1, mid, jnp.where(piece == 2, low, 0.0))
-            ).astype(jnp.bfloat16)
-
-
-def fresh_kernel(tokens, rows_ref, kv_ref, kv1_ref, kv2_ref, kv3_ref, w_hbm, out_ref, lse_ref, w_ref, sems):
+    for apart, q_ref in enumerate((q0_ref, q1_ref, q2_ref, q3_ref)):
+        for first in range(0, sources, step):
+            q = q_ref[first : first + step].reshape(step * per, HD)
+            sa = lax.dot_general(q, ka_ref[...], nt, preferred_element_type=jnp.float32)
+            sb = lax.dot_general(q, kb_ref[...], nt, preferred_element_type=jnp.float32)
+            top = scale * jnp.maximum(jnp.max(sa, axis=1, keepdims=True), jnp.max(sb, axis=1, keepdims=True))
+            wa = jnp.exp2(sa * scale - top).astype(jnp.bfloat16)
+            wb = jnp.exp2(sb * scale - top).astype(jnp.bfloat16)
+            both = jnp.dot(
+                wa, jnp.concatenate([va_ref[...], ones], axis=1), preferred_element_type=jnp.float32
+            ) + jnp.dot(wb, jnp.concatenate([vb_ref[...], ones], axis=1), preferred_element_type=jnp.float32)
+            total = both[:, HD:]
+            out = (both[:, :HD] / total).astype(jnp.bfloat16)
+            lse = top + jnp.log(total) * LOG2E
+            for s in range(step):
+                part = slice(s * per, (s + 1) * per)
+                to = (first + s) * SPAN + (place ^ apart)
+                out_ref[to, :per, :] = out[part]
+                flat = jnp.sum(jnp.where(diagonal, lse[part], 0.0), axis=0, keepdims=True)
+                hi = flat.astype(jnp.bfloat16).astype(jnp.float32)
+                mid = (flat - hi).astype(jnp.bfloat16).astype(jnp.float32)
+                low = flat - hi - mid
+                out_ref[to, per:, :] = jnp.where(
+                    piece == 0, hi, jnp.where(piece == 1, mid, jnp.where(piece == 2, low, 0.0))
+                ).astype(jnp.bfloat16)
+
+
+def fresh_kernel(tokens, rows_ref, kv0_ref, kv1_ref, kv2_ref, kv3_ref, w_hbm, out_ref, lse_ref, w_ref, sems):
     copies = fetch([(w_hbm.at[: w_ref.shape[0]], w_ref)], sems)
-    sources = kv_ref.shape[0]
+    blocks = kv0_ref.shape[0]
     place = lax.axis_index("seq")
-    core, odd = place % KVH, place // KVH % 2
     scale = LOG2E * HD**-0.5
     nt = (((1,), (1,)), ((), ()))
-    column = lax.broadcasted_iota(jnp.int32, (tokens, sources * tokens), 1)
+    column = lax.broadcasted_iota(jnp.int32, (tokens, SPAN * blocks * tokens), 1)
+    source = column // tokens % blocks * SPAN + (place % SPAN ^ column // (blocks * tokens))
+    key_pos = source * tokens + column % tokens
     query_pos = place * tokens + lax.broadcasted_iota(jnp.int32, column.shape, 0)
-    visible = (column <= query_pos) & (column // BLK == query_pos // BLK)
+    visible = (key_pos <= query_pos) & (key_pos // BLK == query_pos // BLK)
     visible = jnp.concatenate([visible.astype(jnp.int32)] * GROUP, axis=0) > 0
-    ones = jnp.ones((sources * tokens, HD), jnp.bfloat16)
-    here, near, far, both = [
-        ref[...].astype(jnp.float32).reshape(sources * tokens, HD) for ref in (kv_ref, kv1_ref, kv2_ref, kv3_ref)
-    ]
-    keys = [jnp.where(odd == 0, here, far), jnp.where(odd == 0, near, both)]
-    values = [jnp.where(odd == 0, far, here), jnp.where(odd == 0, both, near)]
+    ones = jnp.ones((SPAN * blocks * tokens, HD), jnp.bfloat16)
+    kv = [ref[...].astype(jnp.float32) for ref in (kv0_ref, kv1_ref, kv2_ref, kv3_ref)]
     for g in range(KVH):
-        k = jnp.where(core == g, keys[0], keys[1]).astype(jnp.bfloat16)
-        v = jnp.where(core == g, values[0], values[1]).astype(jnp.bfloat16)
+        k, v = [
+            jnp.concatenate(
+                [x[:, i * tokens : (i + 1) * tokens].reshape(blocks * tokens, HD) for x in kv], axis=0
+            ).astype(jnp.bfloat16)
+            for i in (2 * g, 2 * g + 1)
+        ]
         q = rows_ref[g].astype(jnp.bfloat16)
         s = lax.dot_general(q, k, nt, preferred_element_type=jnp.float32) * scale
         s = jnp.where(visible, s, LOW_SCORE)
@@ -231,8 +247,7 @@
     devices = lax.axis_size("seq")
     tokens = queries.shape[0]
     cache_rows = cache_keys.shape[0]
-    span = BLK // cache_rows
-    chips = span // KVH
+    chips = SPAN // KVH
     key_blocks = cache_rows * devices // BLK
     capacity = (GROUP * TOPK + key_blocks - 1) // key_blocks + 1
     per = capacity * tokens
@@ -243,9 +258,9 @@
         return [(i, i ^ bit) for i in range(devices)]
 
     send = call(
-        functools.partial(pack_kernel, chips, capacity),
+        functools.partial(pack_kernel, capacity),
         "pack",
-        jax.ShapeDtypeStruct((devices, per + tokens, HD), bf16),
+        jax.ShapeDtypeStruct((key_blocks, KVH * per + 2 * KVH * tokens, HD), bf16),
         [HBM] * 4,
         picks, queries, stretch_keys, stretch_values,
         scratch=[
@@ -260,7 +275,12 @@
     send, cache_keys, cache_values, picks, queries = lax.optimization_barrier(
         (send, cache_keys, cache_values, picks, queries)
     )
-    got = lax.all_to_all(send, "seq", split_axis=0, concat_axis=0, tiled=True)
+    columns = [[b * SPAN + i for b in range(key_blocks)] for i in range(SPAN)]
+    got = lax.all_to_all(
+        send, "seq", split_axis=0, concat_axis=0, axis_index_groups=columns, tiled=True
+    )
+    same, other, fresh = got[:, :per], got[:, per : KVH * per], got[:, KVH * per :]
+    slots = [same] + [lax.ppermute(x, "seq", partner(i)) for i, x in ((1, other), (2, same), (3, other))]
 
     core = lax.axis_index("seq") % KVH
 
@@ -282,23 +302,20 @@
     )
 
     rows = devices * per
-    back, fresh = call(
-        functools.partial(attend_kernel, per),
+    back = call(
+        attend_kernel,
         "attend",
-        (
-            jax.ShapeDtypeStruct((devices, per + 8, HD), bf16),
-            jax.ShapeDtypeStruct((devices, tokens, HD), bf16),
-        ),
-        [VMEM] * 5,
-        got, k_own, v_own, k_peer, v_peer,
+        jax.ShapeDtypeStruct((devices, per + 8, HD), bf16),
+        [VMEM] * 8,
+        *slots, k_own, v_own, k_peer, v_peer,
         flops=8 * rows * cache_rows * HD,
         moved=4 << 20,
         limit=32,
     )
     hist = lax.all_to_all(back, "seq", split_axis=0, concat_axis=0, tiled=True)
 
-    far = lax.ppermute(fresh, "seq", partner(2))
-    near, both = [lax.ppermute(x, "seq", partner(1)) for x in (fresh, far)]
+    back, fresh = lax.optimization_barrier((back, fresh))
+    spread = [fresh] + [lax.ppermute(fresh, "seq", partner(i)) for i in (1, 2, 3)]
     part = jax.ShapeDtypeStruct((KVH, GROUP * tokens, HD), f32)
     ready = EARLY * KVH * HD
     out, lse, first = call(
@@ -306,7 +323,7 @@
         "fresh",
         (part, part, jax.ShapeDtypeStruct((ready, out_weight.shape[1]), bf16)),
         [VMEM] * 5 + [HBM],
-        query_rows, fresh, near, far, both, out_weight,
+        query_rows, *spread, out_weight,
         scratch=[pltpu.SemaphoreType.DMA((1,))],
         flops=8 * H * tokens * devices * tokens * HD,
         moved=1 << 20,

time: 43.1 us -> 45.2 us (1.049)
  starting transfers between devices: 12.2 us -> 14.9 us
  waiting for transfers between devices: 17.5 us -> 17 us
    ppermute x3 -> x6, waiting for transfers between devices: 5.92 us -> 9.91 us  [the longest x3 6.19 us: body(): lax.ppermute(fresh, 'seq', partner(i))]
    all_to_all x1, waiting for transfers between devices: 7.91 us -> 5.18 us  [body(): lax.all_to_all(send, 'seq', split_axis=0, concat_axis=0, axis_index_group...]
    ppermute x3 -> x6, starting transfers between devices: 1.71 us -> 4.16 us  [the longest x3 2.2 us: body(): lax.ppermute(x, 'seq', partner(i))]
    ppermute x2, waiting for transfers between devices: 1.28 us -> 0.01 us  [body(): lax.ppermute(x, 'seq', partner(1))]
    all_to_all x1, waiting for transfers between devices: 2.37 us -> 1.88 us  [body(): hist = lax.all_to_all(back, 'seq', split_axis=0, concat_axis=0, tiled=True)]
  transfers between devices with their start and end apart: 7 -> 10, of which waited for: 5 -> 6; matrix products, arithmetic and copies ran while one was open for 5% -> 5% of each run, Pallas kernels for 5% -> 4%
where the time goes in v7:
time: 45.2 us; the launch traced here: 44.8 us
  waiting for transfers between devices  17 us (38%)
  starting transfers between devices  14.9 us (33%)
  Pallas kernels  10.7 us (24%)
  local copies, waits for them, and re-layouts  2.16 us (5%)
    pallas_call x5, Pallas kernels, call(): pl.pallas_call(kernel, name=name, out_shape=out_shape, in_specs=specs, ou...  10.7 us
    all_to_all x1, starting transfers between devices, body(): lax.all_to_all(send, 'seq', split_axis=0, concat_axis=0, axis_index_group...  7.3 us
    ppermute x3, waiting for transfers between devices, body(): lax.ppermute(fresh, 'seq', partner(i))  6.19 us
    all_to_all x1, waiting for transfers between devices, body(): lax.all_to_all(send, 'seq', split_axis=0, concat_axis=0, axis_index_group...  5.18 us
    ppermute x3, waiting for transfers between devices, body(): lax.ppermute(x, 'seq', partner(i))  3.72 us
    all_to_all x1, starting transfers between devices, body(): hist = lax.all_to_all(back, 'seq', split_axis=0, concat_axis=0, tiled=True)  2.8 us
    ppermute x3, starting transfers between devices, body(): lax.ppermute(x, 'seq', partner(i))  2.2 us
    dynamic_slice x2, local copies, waits for them, and re-layouts, halves(): lax.dynamic_slice_in_dim(x, head * HD, HD, axis=1)  2.14 us
  transfers between devices with their start and end apart: 10, of which 6 were waited for; matrix products, arithmetic and copies ran while one was open for 5% of the time, Pallas kernels for 4%

profile of v7, /device:TPU:0, one launch (start us, length us, event | category | flops | bytes accessed | tf_op | source)
XLA Modules:
  0.0 44.8 jit_solution(7935493895964772519)
XLA Ops:
  0.0 0.0 copy-start
  0.0 0.0 copy-start.1
  0.0 1.9 %pack.1 = bf16[8,96,128]{2,1,0:T(8,128)(2,1)} custom-call(s32[3,1,14]{2,1,0:T(1,128)} %bitcast.3, bf16[8,1792]{1,0:T(8,128)(2,1)} %q_ref, bf16[8,256]{1,0:T(8,128)(2,1)} %k_hbm.1, bf16[8,256]{1,0:T(8,128)(2,1)} %v_hbm.1), custom_call_target="tpu_custom_call" | custom-call | tf_op jit(solution)/shard_map/pack/pallas_call | solution.py:234
  1.9 7.3 %all-to-all-start = ((bf16[8,96,128]{2,1,0:T(8,128)(2,1)}), bf16[8,96,128]{2,1,0:T(8,128)(2,1)S(1)}, u32[]{:S(2)}, u32[]{:S(2)}) async-start(bf16[8,96,128]{2,1,0:T(8,128)(2,1)} %pack.1), calls=%async_computation | async-start | bytes 393216 | tf_op jit(solution)/shard_map/all_to_all | solution.py:279
  9.2 1.1 %constant_dynamic-slice_fusion.1 = (bf16[1024,128]{1,0:T(8,128)(2,1)S(1)}, bf16[1024,128]{1,0:T(8,128)(2,1)S(1)}) fusion(bf16[1024,256]{1,0:T(8,128)(2,1)} %param.10, s32[]{:T(128)S(6)} %select_n.17, s32[]{:T(128)S(6)} %select_n.16), kind=kLoop, calls=%fused_computation.1 | loop fusion | bytes 1048584 | tf_op jit(solution)/shard_map/dynamic_slice | solution.py:288
  10.3 0.1 collective-permute-start.3
  10.4 1.1 %constant_dynamic-slice_fusion = (bf16[1024,128]{1,0:T(8,128)(2,1)S(1)}, bf16[1024,128]{1,0:T(8,128)(2,1)S(1)}) fusion(bf16[1024,256]{1,0:T(8,128)(2,1)} %param.11, s32[]{:T(128)S(6)} %select_n.17, s32[]{:T(128)S(6)} %select_n.16), kind=kLoop, calls=%fused_computation | loop fusion | bytes 1048584 | tf_op jit(solution)/shard_map/dynamic_slice | solution.py:288
  11.4 0.6 %collective-permute-start.4 = (bf16[1024,128]{1,0:T(8,128)(2,1)S(1)}, bf16[1024,128]{1,0:T(8,128)(2,1)S(1)}, u32[]{:S(2)}, u32[]{:S(2)}) collective-permute-start(bf16[1024,128]{1,0:T(8,128)(2,1)S(1)} %get-tuple-element.27), channel_id=1, source_target_pairs={{0,1},{1,0},{2,3},{3,2},{4,5},{5,4},{6,7},{7,6},{8,9},{9,8},{10,11... | collective-permute-start | bytes 786440 | tf_op jit(solution)/shard_map/ppermute | solution.py:291
  12.0 5.2 %all-to-all-done = bf16[8,96,128]{2,1,0:T(8,128)(2,1)S(1)} async-done(((bf16[8,96,128]{2,1,0:T(8,128)(2,1)}), bf16[8,96,128]{2,1,0:T(8,128)(2,1)S(1)}, u32[]{:S(2)}, u32[]{:S(2)}) %all-to-all-start) | async-done | bytes 196640 | tf_op jit(solution)/shard_map/all_to_all | solution.py:279
  17.2 0.1 collective-permute-start.2
  17.3 1.6 %collective-permute-start = (bf16[8,32,128]{2,1,0:T(8,128)(2,1)S(1)}, bf16[8,32,128]{2,1,0:T(8,128)(2,1)S(1)}, u32[]{:S(2)}, u32[]{:S(2)}) collective-permute-start(bf16[8,32,128]{2,1,0:T(8,128)(2,1)S(1)} %get-tuple-element.32), channel_id=1, source_target_pairs={{0,1},{1,0},{2,3},{3,2},{4,5},{5,4},{6,7},{7,6},{8,9},{9,8},{10,11... | collective-permute-start | bytes 196616 | tf_op jit(solution)/shard_map/ppermute | solution.py:283
  18.9 0.5 %collective-permute-start.1 = (bf16[8,32,128]{2,1,0:T(8,128)(2,1)S(1)}, bf16[8,32,128]{2,1,0:T(8,128)(2,1)S(1)}, u32[]{:S(2)}, u32[]{:S(2)}) collective-permute-start(bf16[8,32,128]{2,1,0:T(8,128)(2,1)S(1)} %get-tuple-element.33.q0_ref), channel_id=1, source_target_pairs={{0,2},{1,3},{2,0},{3,1},{4,6},{5,7},{6,4},{7,5},{8,10},{9,11},{10,... | collective-permute-start | bytes 196616 | tf_op jit(solution)/shard_map/ppermute | solution.py:283
  19.4 0.0 collective-permute-done.3.kb_ref
  19.4 0.0 collective-permute-done.4.vb_ref
  19.4 2.2 %collective-permute-done.2.q3_ref = bf16[8,32,128]{2,1,0:T(8,128)(2,1)S(1)} collective-permute-done((bf16[8,32,128]{2,1,0:T(8,128)(2,1)S(1)}, bf16[8,32,128]{2,1,0:T(8,128)(2,1)S(1)}, u32[]{:S(2)}, u32[]{:S(2)}) %collective-permute-start.2) | collective-permute-done | bytes 65568 | tf_op jit(solution)/shard_map/ppermute | solution.py:283
  21.6 0.0 collective-permute-done.q1_ref
  21.6 1.5 %collective-permute-done.1.q2_ref = bf16[8,32,128]{2,1,0:T(8,128)(2,1)S(1)} collective-permute-done((bf16[8,32,128]{2,1,0:T(8,128)(2,1)S(1)}, bf16[8,32,128]{2,1,0:T(8,128)(2,1)S(1)}, u32[]{:S(2)}, u32[]{:S(2)}) %collective-permute-start.1) | collective-permute-done | bytes 65568 | tf_op jit(solution)/shard_map/ppermute | solution.py:283
  23.1 3.8 %attend.1 = bf16[32,40,128]{2,1,0:T(8,128)(2,1)} custom-call(bf16[8,32,128]{2,1,0:T(8,128)(2,1)S(1)} %get-tuple-element.33.q0_ref, bf16[8,32,128]{2,1,0:T(8,128)(2,1)S(1)} %collective-permute-done.q1_ref, bf16[8,32,128]{2,1,0:T(8,128)(2,1)S(1)} %collective-permute-done.1.q2_ref, bf16[8,32,128]{2,1,0:T(8,128)(2,1)S(1)} %collective-permute-done.2.q3_ref, ...), custom_call_target="tpu_custom_call" | custom-call | flops 1073741824 | bytes 4194304 | tf_op jit(solution)/shard_map/attend/pallas_call | solution.py:234
  27.0 2.8 %all-to-all-start.1 = ((bf16[32,40,128]{2,1,0:T(8,128)(2,1)}), bf16[32,40,128]{2,1,0:T(8,128)(2,1)S(1)}, u32[]{:S(2)}, u32[]{:S(2)}) async-start(bf16[32,40,128]{2,1,0:T(8,128)(2,1)} %attend.1), calls=%async_computation.1 | async-start | bytes 655360 | tf_op jit(solution)/shard_map/all_to_all | solution.py:315
  29.8 1.6 %collective-permute-start.7 = (bf16[8,32,128]{2,1,0:T(8,128)(2,1)S(1)}, bf16[8,32,128]{2,1,0:T(8,128)(2,1)S(1)}, u32[]{:S(2)}, u32[]{:S(2)}) collective-permute-start(bf16[8,32,128]{2,1,0:T(8,128)(2,1)S(1)} %get-tuple-element.22.kv0_ref), channel_id=1, source_target_pairs={{0,3},{1,2},{2,1},{3,0},{4,7},{5,6},{6,5},{7,4},{8,11},{9,10},{10,... | collective-permute-start | bytes 196616 | tf_op jit(solution)/shard_map/ppermute | solution.py:318
  31.4 0.4 collective-permute-start.6
  31.7 0.0 collective-permute-start.5
  31.7 0.0 copy-done
  31.7 0.0 copy-done.1
  31.7 0.1 masks.1
  31.9 3.4 %collective-permute-done.7.kv3_ref = bf16[8,32,128]{2,1,0:T(8,128)(2,1)S(1)} collective-permute-done((bf16[8,32,128]{2,1,0:T(8,128)(2,1)S(1)}, bf16[8,32,128]{2,1,0:T(8,128)(2,1)S(1)}, u32[]{:S(2)}, u32[]{:S(2)}) %collective-permute-start.7) | collective-permute-done | bytes 65568 | tf_op jit(solution)/shard_map/ppermute | solution.py:318
  35.3 2.8 %collective-permute-done.6.kv2_ref = bf16[8,32,128]{2,1,0:T(8,128)(2,1)S(1)} collective-permute-done((bf16[8,32,128]{2,1,0:T(8,128)(2,1)S(1)}, bf16[8,32,128]{2,1,0:T(8,128)(2,1)S(1)}, u32[]{:S(2)}, u32[]{:S(2)}) %collective-permute-start.6) | collective-permute-done | bytes 65568 | tf_op jit(solution)/shard_map/ppermute | solution.py:318
  38.1 0.0 collective-permute-done.5.kv1_ref
  38.1 1.8 %fresh.1 = (f32[2,56,128]{2,1,0:T(8,128)S(1)}, f32[2,56,128]{2,1,0:T(8,128)S(1)}, bf16[768,1792]{1,0:T(8,128)(2,1)S(1)}) custom-call(f32[2,56,128]{2,1,0:T(8,128)S(1)} %get-tuple-element.21.rows_ref, bf16[8,32,128]{2,1,0:T(8,128)(2,1)S(1)} %get-tuple-element.22.kv0_ref, bf16[8,32,128]{2,1,0:T(8,128)(2,1)S(1)} %collective-permute-done.5.kv1_ref, ...), custom_call_target="tpu_custom_call" | custom-call | flops 29360128 | bytes 1048576 | tf_op jit(solution)/shard_map/fresh/pallas_call | solution.py:234
  39.9 1.9 %all-to-all-done.1 = bf16[32,40,128]{2,1,0:T(8,128)(2,1)S(1)} async-done(((bf16[32,40,128]{2,1,0:T(8,128)(2,1)}), bf16[32,40,128]{2,1,0:T(8,128)(2,1)S(1)}, u32[]{:S(2)}, u32[]{:S(2)}) %all-to-all-start.1) | async-done | bytes 327712 | tf_op jit(solution)/shard_map/all_to_all | solution.py:315
  41.8 3.0 %project.1 = bf16[8,1792]{1,0:T(8,128)(2,1)} custom-call(bf16[16,2,40,128]{3,2,1,0:T(8,128)(2,1)S(1)} %bitcast.2, f32[2,56,128]{2,1,0:T(8,128)S(1)} %get-tuple-element.23.out_ref, f32[2,56,128]{2,1,0:T(8,128)S(1)} %get-tuple-element.24.lse_ref, f32[2,56,512]{2,1,0:T(8,128)S(1)} %get-tuple-element.25.match_ref, ...), custom_call_target="tpu_custom_call" | custom-call | flops 51380224 | bytes 6422528 | tf_op jit(solution)/shard_map/project/pallas_call | solution.py:234
  (1 shorter events, 0.0 us)
Async XLA Ops:
  0.0 31.7 %copy-start = (bf16[8,1792]{1,0:T(8,128)(2,1)S(1)}, bf16[8,1792]{1,0:T(8,128)(2,1)}, u32[]{:S(2)}) copy-start(bf16[8,1792]{1,0:T(8,128)(2,1)} %q_ref) | copy-start | bytes 86020
  0.0 31.7 %copy-start.1 = (s32[1,14,3]{1,0,2:T(1,128)S(1)}, s32[1,14,3]{1,0,2:T(1,128)}, u32[]{:S(2)}) copy-start(s32[1,14,3]{1,0,2:T(1,128)} %param.12) | copy-start | bytes 508
  1.9 15.2 %all-to-all-start = ((bf16[8,96,128]{2,1,0:T(8,128)(2,1)}), bf16[8,96,128]{2,1,0:T(8,128)(2,1)S(1)}, u32[]{:S(2)}, u32[]{:S(2)}) async-start(bf16[8,96,128]{2,1,0:T(8,128)(2,1)} %pack.1), calls=%async_computation | async-start | bytes 393216 | tf_op jit(solution)/shard_map/all_to_all | solution.py:279
  10.3 9.1 %collective-permute-start.3 = (bf16[1024,128]{1,0:T(8,128)(2,1)S(1)}, bf16[1024,128]{1,0:T(8,128)(2,1)S(1)}, u32[]{:S(2)}, u32[]{:S(2)}) collective-permute-start(bf16[1024,128]{1,0:T(8,128)(2,1)S(1)} %get-tuple-element.29), channel_id=1, source_target_pairs={{0,1},{1,0},{2,3},{3,2},{4,5},{5,4},{6,7},{7,6},{8,9},{9,8},{10,11... | collective-permute-start | bytes 786440 | tf_op jit(solution)/shard_map/ppermute | solution.py:291
  11.4 8.0 %collective-permute-start.4 = (bf16[1024,128]{1,0:T(8,128)(2,1)S(1)}, bf16[1024,128]{1,0:T(8,128)(2,1)S(1)}, u32[]{:S(2)}, u32[]{:S(2)}) collective-permute-start(bf16[1024,128]{1,0:T(8,128)(2,1)S(1)} %get-tuple-element.27), channel_id=1, source_target_pairs={{0,1},{1,0},{2,3},{3,2},{4,5},{5,4},{6,7},{7,6},{8,9},{9,8},{10,11... | collective-permute-start | bytes 786440 | tf_op jit(solution)/shard_map/ppermute | solution.py:291
  17.2 4.4 %collective-permute-start.2 = (bf16[8,32,128]{2,1,0:T(8,128)(2,1)S(1)}, bf16[8,32,128]{2,1,0:T(8,128)(2,1)S(1)}, u32[]{:S(2)}, u32[]{:S(2)}) collective-permute-start(bf16[8,32,128]{2,1,0:T(8,128)(2,1)S(1)} %get-tuple-element.32), channel_id=1, source_target_pairs={{0,3},{1,2},{2,1},{3,0},{4,7},{5,6},{6,5},{7,4},{8,11},{9,10},{10,... | collective-permute-start | bytes 196616 | tf_op jit(solution)/shard_map/ppermute | solution.py:283
  17.3 4.3 %collective-permute-start = (bf16[8,32,128]{2,1,0:T(8,128)(2,1)S(1)}, bf16[8,32,128]{2,1,0:T(8,128)(2,1)S(1)}, u32[]{:S(2)}, u32[]{:S(2)}) collective-permute-start(bf16[8,32,128]{2,1,0:T(8,128)(2,1)S(1)} %get-tuple-element.32), channel_id=1, source_target_pairs={{0,1},{1,0},{2,3},{3,2},{4,5},{5,4},{6,7},{7,6},{8,9},{9,8},{10,11... | collective-permute-start | bytes 196616 | tf_op jit(solution)/shard_map/ppermute | solution.py:283
  18.9 4.3 %collective-permute-start.1 = (bf16[8,32,128]{2,1,0:T(8,128)(2,1)S(1)}, bf16[8,32,128]{2,1,0:T(8,128)(2,1)S(1)}, u32[]{:S(2)}, u32[]{:S(2)}) collective-permute-start(bf16[8,32,128]{2,1,0:T(8,128)(2,1)S(1)} %get-tuple-element.33.q0_ref), channel_id=1, source_target_pairs={{0,2},{1,3},{2,0},{3,1},{4,6},{5,7},{6,4},{7,5},{8,10},{9,11},{10,... | collective-permute-start | bytes 196616 | tf_op jit(solution)/shard_map/ppermute | solution.py:283
  27.0 14.8 %all-to-all-start.1 = ((bf16[32,40,128]{2,1,0:T(8,128)(2,1)}), bf16[32,40,128]{2,1,0:T(8,128)(2,1)S(1)}, u32[]{:S(2)}, u32[]{:S(2)}) async-start(bf16[32,40,128]{2,1,0:T(8,128)(2,1)} %attend.1), calls=%async_computation.1 | async-start | bytes 655360 | tf_op jit(solution)/shard_map/all_to_all | solution.py:315
  29.8 5.5 %collective-permute-start.7 = (bf16[8,32,128]{2,1,0:T(8,128)(2,1)S(1)}, bf16[8,32,128]{2,1,0:T(8,128)(2,1)S(1)}, u32[]{:S(2)}, u32[]{:S(2)}) collective-permute-start(bf16[8,32,128]{2,1,0:T(8,128)(2,1)S(1)} %get-tuple-element.22.kv0_ref), channel_id=1, source_target_pairs={{0,3},{1,2},{2,1},{3,0},{4,7},{5,6},{6,5},{7,4},{8,11},{9,10},{10,... | collective-permute-start | bytes 196616 | tf_op jit(solution)/shard_map/ppermute | solution.py:318
  31.4 6.7 %collective-permute-start.6 = (bf16[8,32,128]{2,1,0:T(8,128)(2,1)S(1)}, bf16[8,32,128]{2,1,0:T(8,128)(2,1)S(1)}, u32[]{:S(2)}, u32[]{:S(2)}) collective-permute-start(bf16[8,32,128]{2,1,0:T(8,128)(2,1)S(1)} %get-tuple-element.22.kv0_ref), channel_id=1, source_target_pairs={{0,2},{1,3},{2,0},{3,1},{4,6},{5,7},{6,4},{7,5},{8,10},{9,11},{10,... | collective-permute-start | bytes 196616 | tf_op jit(solution)/shard_map/ppermute | solution.py:318
  31.7 6.4 %collective-permute-start.5 = (bf16[8,32,128]{2,1,0:T(8,128)(2,1)S(1)}, bf16[8,32,128]{2,1,0:T(8,128)(2,1)S(1)}, u32[]{:S(2)}, u32[]{:S(2)}) collective-permute-start(bf16[8,32,128]{2,1,0:T(8,128)(2,1)S(1)} %get-tuple-element.22.kv0_ref), channel_id=1, source_target_pairs={{0,1},{1,0},{2,3},{3,2},{4,5},{5,4},{6,7},{7,6},{8,9},{9,8},{10,11... | collective-permute-start | bytes 196616 | tf_op jit(solution)/shard_map/ppermute | solution.py:318

commit v8 on v7

--- a/solution.py
+++ b/solution.py
@@ -48,32 +48,28 @@
     return copies
 
 
-def pack_kernel(capacity, chosen_hbm, q_hbm, k_hbm, v_hbm, send_ref, chosen_ref, q_ref, k_ref, v_ref, sems):
+def pack_kernel(capacity, chosen_hbm, q_hbm, k_hbm, v_hbm, *refs):
+    *send_refs, chosen_ref, q_ref, k_ref, v_ref, slots_ref, sems = refs
     copies = fetch([(chosen_hbm, chosen_ref), (q_hbm, q_ref), (k_hbm, k_ref), (v_hbm, v_ref)], sems)
-    core = lax.axis_index("seq") % KVH
+    place = lax.axis_index("seq")
+    core, home = place % KVH, place // SPAN
     tokens = q_ref.shape[0]
     per = capacity * tokens
-    key_blocks = send_ref.shape[0]
+    key_blocks = len(send_refs)
     lane = lax.broadcasted_iota(jnp.int32, (tokens, key_blocks * per), 1)
     block, slot, token = lane // per, lane % per // tokens, lane % tokens
     for copy in copies:
         copy.wait()
-    slots = []
     for g in range(KVH):
         spread = jnp.concatenate(
             slot_match(chosen_ref, g, block, slot, token) + [jnp.zeros(lane.shape, jnp.float32)], axis=0
         )
         rows = head_rows(q_ref, g)
         rows = jnp.concatenate(rows + [jnp.zeros_like(rows[0])], axis=0)
-        slots.append(
-            jnp.dot(
-                spread.T.astype(jnp.bfloat16), rows.astype(jnp.bfloat16), preferred_element_type=jnp.float32
-            )
-        )
-    ordered = [
-        jnp.where(core == 0, slots[0], slots[1]).astype(jnp.bfloat16),
-        jnp.where(core == 0, slots[1], slots[0]).astype(jnp.bfloat16),
-    ]
+        slots = jnp.dot(
+            spread.T.astype(jnp.bfloat16), rows.astype(jnp.bfloat16), preferred_element_type=jnp.float32
+        )
+        slots_ref[core ^ g] = slots.astype(jnp.bfloat16).reshape(key_blocks, per, HD)
     fresh = jnp.concatenate(
         [
             ref[:, g * HD : (g + 1) * HD].astype(jnp.float32)
@@ -82,10 +78,19 @@
         ],
         axis=0,
     ).astype(jnp.bfloat16)
-    for b in range(key_blocks):
+    for apart, send_ref in enumerate(send_refs):
         for i in range(KVH):
-            send_ref[b, i * per : (i + 1) * per, :] = ordered[i][b * per : (b + 1) * per]
-        send_ref[b, KVH * per :, :] = fresh
+            send_ref[i * per : (i + 1) * per, :] = slots_ref[i, home ^ apart]
+        send_ref[KVH * per :, :] = fresh
+
+
+def gather_kernel(*refs):
+    *got_refs, same_ref, other_ref, fresh_ref = refs
+    per = same_ref.shape[1]
+    for i, ref in enumerate(got_refs):
+        same_ref[i] = ref[:per, :]
+        other_ref[i] = ref[per : KVH * per, :]
+        fresh_ref[i] = ref[KVH * per :, :]
 
 
 def masks_kernel(chips, capacity, chosen_ref, q_ref, match_ref, rows_ref):
@@ -99,7 +104,7 @@
 
 
 def attend_kernel(q0_ref, q1_ref, q2_ref, q3_ref, ka_ref, va_ref, kb_ref, vb_ref, out_ref):
-    place = lax.axis_index("seq") % SPAN
+    place = lax.axis_index("seq")
     sources, per = q0_ref.shape[:2]
     step = 256 // per
     scale = LOG2E * HD**-0.5
@@ -125,7 +130,7 @@
             lse = top + jnp.log(total) * LOG2E
             for s in range(step):
                 part = slice(s * per, (s + 1) * per)
-                to = (first + s) * SPAN + (place ^ apart)
+                to = place ^ (apart + (first + s) * SPAN)
                 out_ref[to, :per, :] = out[part]
                 flat = jnp.sum(jnp.where(diagonal, lse[part], 0.0), axis=0, keepdims=True)
                 hi = flat.astype(jnp.bfloat16).astype(jnp.float32)
@@ -143,7 +148,7 @@
     scale = LOG2E * HD**-0.5
     nt = (((1,), (1,)), ((), ()))
     column = lax.broadcasted_iota(jnp.int32, (tokens, SPAN * blocks * tokens), 1)
-    source = column // tokens % blocks * SPAN + (place % SPAN ^ column // (blocks * tokens))
+    source = place ^ (column // tokens % blocks * SPAN + column // (blocks * tokens))
     key_pos = source * tokens + column % tokens
     query_pos = place * tokens + lax.broadcasted_iota(jnp.int32, column.shape, 0)
     visible = (key_pos <= query_pos) & (key_pos // BLK == query_pos // BLK)
@@ -260,7 +265,7 @@
     send = call(
         functools.partial(pack_kernel, capacity),
         "pack",
-        jax.ShapeDtypeStruct((key_blocks, KVH * per + 2 * KVH * tokens, HD), bf16),
+        (jax.ShapeDtypeStruct((KVH * per + 2 * KVH * tokens, HD), bf16),) * key_blocks,
         [HBM] * 4,
         picks, queries, stretch_keys, stretch_values,
         scratch=[
@@ -268,18 +273,26 @@
             pltpu.VMEM(queries.shape, bf16),
             pltpu.VMEM(stretch_keys.shape, bf16),
             pltpu.VMEM(stretch_values.shape, bf16),
+            pltpu.VMEM((KVH, key_blocks, per, HD), bf16),
             pltpu.SemaphoreType.DMA((4,)),
         ],
         limit=60,
     )
-    send, cache_keys, cache_values, picks, queries = lax.optimization_barrier(
-        (send, cache_keys, cache_values, picks, queries)
-    )
-    columns = [[b * SPAN + i for b in range(key_blocks)] for i in range(SPAN)]
-    got = lax.all_to_all(
-        send, "seq", split_axis=0, concat_axis=0, axis_index_groups=columns, tiled=True
-    )
-    same, other, fresh = got[:, :per], got[:, per : KVH * per], got[:, KVH * per :]
+    got = [send[0]] + [lax.ppermute(x, "seq", partner(SPAN * m)) for m, x in enumerate(send) if m]
+    got[1], cache_keys, cache_values, picks, queries = lax.optimization_barrier(
+        (got[1], cache_keys, cache_values, picks, queries)
+    )
+    same, other, fresh = call(
+        gather_kernel,
+        "gather",
+        (
+            jax.ShapeDtypeStruct((key_blocks, per, HD), bf16),
+            jax.ShapeDtypeStruct((key_blocks, per, HD), bf16),
+            jax.ShapeDtypeStruct((key_blocks, 2 * KVH * tokens, HD), bf16),
+        ),
+        [VMEM] * key_blocks,
+        *got,
+    )
     slots = [same] + [lax.ppermute(x, "seq", partner(i)) for i, x in ((1, other), (2, same), (3, other))]
 
     core = lax.axis_index("seq") % KVH

time: 45.2 us -> 55.6 us (1.23)
  starting transfers between devices: 14.9 us -> 23.8 us
  local copies, waits for them, and re-layouts: 2.16 us -> 2.88 us
  waiting for transfers between devices: 17 us -> 17.7 us
    ppermute x0 -> x7, starting transfers between devices: none -> 15.6 us  [body(): lax.ppermute(x, 'seq', partner(SPAN * m))]
    all_to_all x1 -> x0, starting transfers between devices: 7.3 us -> none  [body(): lax.all_to_all(send, 'seq', split_axis=0, concat_axis=0, axis_index_group...]
    ppermute x0 -> x7, waiting for transfers between devices: none -> 6.12 us  [body(): lax.ppermute(x, 'seq', partner(SPAN * m))]
    all_to_all x1 -> x0, waiting for transfers between devices: 5.18 us -> none  [body(): lax.all_to_all(send, 'seq', split_axis=0, concat_axis=0, axis_index_group...]
    unnamed x4 -> x6, local copies, waits for them, and re-layouts: 0.01 us -> 0.74 us
    all_to_all x1, starting transfers between devices: 2.8 us -> 3.37 us  [body(): hist = lax.all_to_all(back, 'seq', split_axis=0, concat_axis=0, tiled=True)]
    pallas_call x5 -> x6, Pallas kernels: 10.7 us -> 10.7 us  [call(): pl.pallas_call(kernel, name=name, out_shape=out_shape, in_specs=specs, ou...]
  transfers between devices with their start and end apart: 10 -> 16, of which waited for: 6 -> 8; matrix products, arithmetic and copies ran while one was open for 5% -> 2% of each run, Pallas kernels for 4% -> 4%
where the time goes in v8:
time: 55.6 us; the launch traced here: 55.2 us
  starting transfers between devices  23.8 us (43%)
  waiting for transfers between devices  17.7 us (32%)
  Pallas kernels  10.7 us (19%)
  local copies, waits for them, and re-layouts  2.88 us (5%)
    ppermute x7, starting transfers between devices, body(): lax.ppermute(x, 'seq', partner(SPAN * m))  15.6 us
    pallas_call x6, Pallas kernels, call(): pl.pallas_call(kernel, name=name, out_shape=out_shape, in_specs=specs, ou...  10.7 us
    ppermute x3, waiting for transfers between devices, body(): lax.ppermute(fresh, 'seq', partner(i))  6.19 us
    ppermute x7, waiting for transfers between devices, body(): lax.ppermute(x, 'seq', partner(SPAN * m))  6.12 us
    ppermute x3, waiting for transfers between devices, body(): lax.ppermute(x, 'seq', partner(i))  3.53 us
    all_to_all x1, starting transfers between devices, body(): hist = lax.all_to_all(back, 'seq', split_axis=0, concat_axis=0, tiled=True)  3.37 us
    ppermute x3, starting transfers between devices, body(): lax.ppermute(x, 'seq', partner(i))  2.21 us
    dynamic_slice x2, local copies, waits for them, and re-layouts, halves(): lax.dynamic_slice_in_dim(x, head * HD, HD, axis=1)  2.14 us
  transfers between devices with their start and end apart: 16, of which 8 were waited for; matrix products, arithmetic and copies ran while one was open for 2% of the time, Pallas kernels for 4%

profile of v8, /device:TPU:0, one launch (start us, length us, event | category | flops | bytes accessed | tf_op | source)
XLA Modules:
  0.0 55.2 jit_solution(10344852194370544991)
XLA Ops:
  0.0 0.0 copy-start
  0.0 0.0 copy-start.2
  0.0 1.9 %pack.1 = (bf16[96,128]{1,0:T(8,128)(2,1)}, bf16[96,128]{1,0:T(8,128)(2,1)}, bf16[96,128]{1,0:T(8,128)(2,1)}, bf16[96,128]{1,0:T(8,128)(2,1)}, bf16[96,128]{1,0:...) custom-call(s32[3,1,14]{2,1,0:T(1,128)} %bitcast.3, ...), custom_call_target="tpu_custom_call" | custom-call | tf_op jit(solution)/shard_map/pack/pallas_call | solution.py:239
  1.9 3.0 %collective-permute-start = (bf16[96,128]{1,0:T(8,128)(2,1)}, bf16[96,128]{1,0:T(8,128)(2,1)S(1)}, u32[]{:S(2)}, u32[]{:S(2)}) collective-permute-start(bf16[96,128]{1,0:T(8,128)(2,1)} %get-tuple-element.28), channel_id=1, source_target_pairs={{0,4},{1,5},{2,6},{3,7},{4,0},{5,1},{6,2},{7,3},{8,12},{9,13},{10,... | collective-permute-start | bytes 73736 | tf_op jit(solution)/shard_map/ppermute | solution.py:281
  4.9 2.0 %collective-permute-done.refs_1_ = bf16[96,128]{1,0:T(8,128)(2,1)S(1)} collective-permute-done((bf16[96,128]{1,0:T(8,128)(2,1)}, bf16[96,128]{1,0:T(8,128)(2,1)S(1)}, u32[]{:S(2)}, u32[]{:S(2)}) %collective-permute-start) | collective-permute-done | bytes 24608 | tf_op jit(solution)/shard_map/ppermute | solution.py:281
  7.0 1.1 %constant_dynamic-slice_fusion.1 = (bf16[1024,128]{1,0:T(8,128)(2,1)S(1)}, bf16[1024,128]{1,0:T(8,128)(2,1)S(1)}) fusion(bf16[1024,256]{1,0:T(8,128)(2,1)} %param.10, s32[]{:T(128)S(6)} %select_n.17, s32[]{:T(128)S(6)} %select_n.16), kind=kLoop, calls=%fused_computation.1 | loop fusion | bytes 1048584 | tf_op jit(solution)/shard_map/dynamic_slice | solution.py:301
  8.0 0.1 collective-permute-start.10
  8.1 1.1 %constant_dynamic-slice_fusion = (bf16[1024,128]{1,0:T(8,128)(2,1)S(1)}, bf16[1024,128]{1,0:T(8,128)(2,1)S(1)}) fusion(bf16[1024,256]{1,0:T(8,128)(2,1)} %param.11, s32[]{:T(128)S(6)} %select_n.17, s32[]{:T(128)S(6)} %select_n.16), kind=kLoop, calls=%fused_computation | loop fusion | bytes 1048584 | tf_op jit(solution)/shard_map/dynamic_slice | solution.py:301
  9.2 0.6 %collective-permute-start.11 = (bf16[1024,128]{1,0:T(8,128)(2,1)S(1)}, bf16[1024,128]{1,0:T(8,128)(2,1)S(1)}, u32[]{:S(2)}, u32[]{:S(2)}) collective-permute-start(bf16[1024,128]{1,0:T(8,128)(2,1)S(1)} %get-tuple-element.49), channel_id=1, source_target_pairs={{0,1},{1,0},{2,3},{3,2},{4,5},{5,4},{6,7},{7,6},{8,9},{9,8},{10,11... | collective-permute-start | bytes 786440 | tf_op jit(solution)/shard_map/ppermute | solution.py:304
  9.7 2.1 %collective-permute-start.1 = (bf16[96,128]{1,0:T(8,128)(2,1)}, bf16[96,128]{1,0:T(8,128)(2,1)S(1)}, u32[]{:S(2)}, u32[]{:S(2)}) collective-permute-start(bf16[96,128]{1,0:T(8,128)(2,1)} %get-tuple-element.30), channel_id=1, source_target_pairs={{0,8},{1,9},{2,10},{3,11},{4,12},{5,13},{6,14},{7,15},{8,0},{9,1},... | collective-permute-start | bytes 73736 | tf_op jit(solution)/shard_map/ppermute | solution.py:281
  11.8 1.4 %collective-permute-start.2 = (bf16[96,128]{1,0:T(8,128)(2,1)}, bf16[96,128]{1,0:T(8,128)(2,1)S(1)}, u32[]{:S(2)}, u32[]{:S(2)}) collective-permute-start(bf16[96,128]{1,0:T(8,128)(2,1)} %get-tuple-element.31), channel_id=1, source_target_pairs={{0,12},{1,13},{2,14},{3,15},{4,8},{5,9},{6,10},{7,11},{8,4},{9,5},... | collective-permute-start | bytes 73736 | tf_op jit(solution)/shard_map/ppermute | solution.py:281
  13.2 2.6 %collective-permute-start.3 = (bf16[96,128]{1,0:T(8,128)(2,1)}, bf16[96,128]{1,0:T(8,128)(2,1)S(1)}, u32[]{:S(2)}, u32[]{:S(2)}) collective-permute-start(bf16[96,128]{1,0:T(8,128)(2,1)} %get-tuple-element.32), channel_id=1, source_target_pairs={{0,16},{1,17},{2,18},{3,19},{4,20},{5,21},{6,22},{7,23},{8,24},{9,... | collective-permute-start | bytes 73736 | tf_op jit(solution)/shard_map/ppermute | solution.py:281
  15.8 0.0 collective-permute-done.1.refs_2_
  15.8 2.0 %collective-permute-start.4 = (bf16[96,128]{1,0:T(8,128)(2,1)}, bf16[96,128]{1,0:T(8,128)(2,1)S(1)}, u32[]{:S(2)}, u32[]{:S(2)}) collective-permute-start(bf16[96,128]{1,0:T(8,128)(2,1)} %get-tuple-element.33), channel_id=1, source_target_pairs={{0,20},{1,21},{2,22},{3,23},{4,16},{5,17},{6,18},{7,19},{8,28},{9,... | collective-permute-start | bytes 73736 | tf_op jit(solution)/shard_map/ppermute | solution.py:281
  17.8 0.0 collective-permute-done.2.refs_3_
  17.8 1.9 %collective-permute-start.5 = (bf16[96,128]{1,0:T(8,128)(2,1)}, bf16[96,128]{1,0:T(8,128)(2,1)S(1)}, u32[]{:S(2)}, u32[]{:S(2)}) collective-permute-start(bf16[96,128]{1,0:T(8,128)(2,1)} %get-tuple-element.34), channel_id=1, source_target_pairs={{0,24},{1,25},{2,26},{3,27},{4,28},{5,29},{6,30},{7,31},{8,16},{9,... | collective-permute-start | bytes 73736 | tf_op jit(solution)/shard_map/ppermute | solution.py:281
  19.7 0.0 collective-permute-done.3.refs_4_
  19.7 2.6 %collective-permute-start.6 = (bf16[96,128]{1,0:T(8,128)(2,1)}, bf16[96,128]{1,0:T(8,128)(2,1)S(1)}, u32[]{:S(2)}, u32[]{:S(2)}) collective-permute-start(bf16[96,128]{1,0:T(8,128)(2,1)} %get-tuple-element.35), channel_id=1, source_target_pairs={{0,28},{1,29},{2,30},{3,31},{4,24},{5,25},{6,26},{7,27},{8,20},{9,... | collective-permute-start | bytes 73736 | tf_op jit(solution)/shard_map/ppermute | solution.py:281
  22.3 0.0 collective-permute-done.4.refs_5_
  22.3 1.3 %collective-permute-done.5.refs_6_ = bf16[96,128]{1,0:T(8,128)(2,1)S(1)} collective-permute-done((bf16[96,128]{1,0:T(8,128)(2,1)}, bf16[96,128]{1,0:T(8,128)(2,1)S(1)}, u32[]{:S(2)}, u32[]{:S(2)}) %collective-permute-start.5) | collective-permute-done | bytes 24608 | tf_op jit(solution)/shard_map/ppermute | solution.py:281
  23.7 2.8 %collective-permute-done.6.refs_7_ = bf16[96,128]{1,0:T(8,128)(2,1)S(1)} collective-permute-done((bf16[96,128]{1,0:T(8,128)(2,1)}, bf16[96,128]{1,0:T(8,128)(2,1)S(1)}, u32[]{:S(2)}, u32[]{:S(2)}) %collective-permute-start.6) | collective-permute-done | bytes 24608 | tf_op jit(solution)/shard_map/ppermute | solution.py:281
  26.4 0.0 copy-start.1
  26.4 0.7 %copy-done.1 = bf16[96,128]{1,0:T(8,128)(2,1)S(1)} copy-done((bf16[96,128]{1,0:T(8,128)(2,1)S(1)}, bf16[96,128]{1,0:T(8,128)(2,1)}, u32[]{:S(2)}) %copy-start.1) | copy-done | bytes 24600
  27.2 1.6 %collective-permute-start.8 = (bf16[8,32,128]{2,1,0:T(8,128)(2,1)S(1)}, bf16[8,32,128]{2,1,0:T(8,128)(2,1)S(1)}, u32[]{:S(2)}, u32[]{:S(2)}) collective-permute-start(bf16[8,32,128]{2,1,0:T(8,128)(2,1)S(1)} %get-tuple-element.36.q0_ref), channel_id=1, source_target_pairs={{0,2},{1,3},{2,0},{3,1},{4,6},{5,7},{6,4},{7,5},{8,10},{9,11},{10,... | collective-permute-start | bytes 196616 | tf_op jit(solution)/shard_map/ppermute | solution.py:296
  28.8 0.0 collective-permute-start.9
  28.8 0.6 %collective-permute-start.7 = (bf16[8,32,128]{2,1,0:T(8,128)(2,1)S(1)}, bf16[8,32,128]{2,1,0:T(8,128)(2,1)S(1)}, u32[]{:S(2)}, u32[]{:S(2)}) collective-permute-start(bf16[8,32,128]{2,1,0:T(8,128)(2,1)S(1)} %get-tuple-element.37), channel_id=1, source_target_pairs={{0,1},{1,0},{2,3},{3,2},{4,5},{5,4},{6,7},{7,6},{8,9},{9,8},{10,11... | collective-permute-start | bytes 196616 | tf_op jit(solution)/shard_map/ppermute | solution.py:296
  29.4 2.1 %collective-permute-done.8.q2_ref = bf16[8,32,128]{2,1,0:T(8,128)(2,1)S(1)} collective-permute-done((bf16[8,32,128]{2,1,0:T(8,128)(2,1)S(1)}, bf16[8,32,128]{2,1,0:T(8,128)(2,1)S(1)}, u32[]{:S(2)}, u32[]{:S(2)}) %collective-permute-start.8) | collective-permute-done | bytes 65568 | tf_op jit(solution)/shard_map/ppermute | solution.py:296
  31.5 1.4 %collective-permute-done.9.q3_ref = bf16[8,32,128]{2,1,0:T(8,128)(2,1)S(1)} collective-permute-done((bf16[8,32,128]{2,1,0:T(8,128)(2,1)S(1)}, bf16[8,32,128]{2,1,0:T(8,128)(2,1)S(1)}, u32[]{:S(2)}, u32[]{:S(2)}) %collective-permute-start.9) | collective-permute-done | bytes 65568 | tf_op jit(solution)/shard_map/ppermute | solution.py:296
  32.9 0.0 collective-permute-done.7.q1_ref
  32.9 0.0 collective-permute-done.10.kb_ref
  32.9 0.0 collective-permute-done.11.vb_ref
  32.9 3.9 %attend.1 = bf16[32,40,128]{2,1,0:T(8,128)(2,1)} custom-call(bf16[8,32,128]{2,1,0:T(8,128)(2,1)S(1)} %get-tuple-element.36.q0_ref, bf16[8,32,128]{2,1,0:T(8,128)(2,1)S(1)} %collective-permute-done.7.q1_ref, bf16[8,32,128]{2,1,0:T(8,128)(2,1)S(1)} %collective-permute-done.8.q2_ref, bf16[8,32,128]{2,1,0:T(8,128)(2,1)S(1)} %collective-permute-done.9.q3_ref, ...), custom_call_target="tpu_custom_call" | custom-call | flops 1073741824 | bytes 4194304 | tf_op jit(solution)/shard_map/attend/pallas_call | solution.py:239
  36.8 3.4 %all-to-all-start = ((bf16[32,40,128]{2,1,0:T(8,128)(2,1)}), bf16[32,40,128]{2,1,0:T(8,128)(2,1)S(1)}, u32[]{:S(2)}, u32[]{:S(2)}) async-start(bf16[32,40,128]{2,1,0:T(8,128)(2,1)} %attend.1), calls=%async_computation | async-start | bytes 655360 | tf_op jit(solution)/shard_map/all_to_all | solution.py:328
  40.2 1.6 %collective-permute-start.14 = (bf16[8,32,128]{2,1,0:T(8,128)(2,1)S(1)}, bf16[8,32,128]{2,1,0:T(8,128)(2,1)S(1)}, u32[]{:S(2)}, u32[]{:S(2)}) collective-permute-start(bf16[8,32,128]{2,1,0:T(8,128)(2,1)S(1)} %get-tuple-element.44.kv0_ref), channel_id=1, source_target_pairs={{0,3},{1,2},{2,1},{3,0},{4,7},{5,6},{6,5},{7,4},{8,11},{9,10},{10,... | collective-permute-start | bytes 196616 | tf_op jit(solution)/shard_map/ppermute | solution.py:331
  41.8 0.4 collective-permute-start.13
  42.1 0.0 collective-permute-start.12
  42.1 0.0 copy-done
  42.1 0.0 copy-done.2
  42.2 0.1 masks.1
  42.3 3.4 %collective-permute-done.14.kv3_ref = bf16[8,32,128]{2,1,0:T(8,128)(2,1)S(1)} collective-permute-done((bf16[8,32,128]{2,1,0:T(8,128)(2,1)S(1)}, bf16[8,32,128]{2,1,0:T(8,128)(2,1)S(1)}, u32[]{:S(2)}, u32[]{:S(2)}) %collective-permute-start.14) | collective-permute-done | bytes 65568 | tf_op jit(solution)/shard_map/ppermute | solution.py:331
  45.7 2.8 %collective-permute-done.13.kv2_ref = bf16[8,32,128]{2,1,0:T(8,128)(2,1)S(1)} collective-permute-done((bf16[8,32,128]{2,1,0:T(8,128)(2,1)S(1)}, bf16[8,32,128]{2,1,0:T(8,128)(2,1)S(1)}, u32[]{:S(2)}, u32[]{:S(2)}) %collective-permute-start.13) | collective-permute-done | bytes 65568 | tf_op jit(solution)/shard_map/ppermute | solution.py:331
  48.5 0.0 collective-permute-done.12.kv1_ref
  48.5 1.8 %fresh.1 = (f32[2,56,128]{2,1,0:T(8,128)S(1)}, f32[2,56,128]{2,1,0:T(8,128)S(1)}, bf16[768,1792]{1,0:T(8,128)(2,1)S(1)}) custom-call(f32[2,56,128]{2,1,0:T(8,128)S(1)} %get-tuple-element.42.rows_ref, bf16[8,32,128]{2,1,0:T(8,128)(2,1)S(1)} %get-tuple-element.44.kv0_ref, bf16[8,32,128]{2,1,0:T(8,128)(2,1)S(1)} %collective-permute-done.12.kv1_ref, ...), custom_call_target="tpu_custom_call" | custom-call | flops 29360128 | bytes 1048576 | tf_op jit(solution)/shard_map/fresh/pallas_call | solution.py:239
  50.3 1.9 %all-to-all-done = bf16[32,40,128]{2,1,0:T(8,128)(2,1)S(1)} async-done(((bf16[32,40,128]{2,1,0:T(8,128)(2,1)}), bf16[32,40,128]{2,1,0:T(8,128)(2,1)S(1)}, u32[]{:S(2)}, u32[]{:S(2)}) %all-to-all-start) | async-done | bytes 327712 | tf_op jit(solution)/shard_map/all_to_all | solution.py:328
  52.2 3.0 %project.1 = bf16[8,1792]{1,0:T(8,128)(2,1)} custom-call(bf16[16,2,40,128]{3,2,1,0:T(8,128)(2,1)S(1)} %bitcast.2, f32[2,56,128]{2,1,0:T(8,128)S(1)} %get-tuple-element.45.out_ref, f32[2,56,128]{2,1,0:T(8,128)S(1)} %get-tuple-element.46.lse_ref, f32[2,56,512]{2,1,0:T(8,128)S(1)} %get-tuple-element.47.match_ref, ...), custom_call_target="tpu_custom_call" | custom-call | flops 51380224 | bytes 6422528 | tf_op jit(solution)/shard_map/project/pallas_call | solution.py:239
  (1 shorter events, 0.0 us)
Async XLA Ops:
  0.0 42.1 %copy-start = (bf16[8,1792]{1,0:T(8,128)(2,1)S(1)}, bf16[8,1792]{1,0:T(8,128)(2,1)}, u32[]{:S(2)}) copy-start(bf16[8,1792]{1,0:T(8,128)(2,1)} %q_ref) | copy-start | bytes 86020
  0.0 42.1 %copy-start.2 = (s32[1,14,3]{1,0,2:T(1,128)S(1)}, s32[1,14,3]{1,0,2:T(1,128)}, u32[]{:S(2)}) copy-start(s32[1,14,3]{1,0,2:T(1,128)} %param.12) | copy-start | bytes 508
  1.9 5.0 %collective-permute-start = (bf16[96,128]{1,0:T(8,128)(2,1)}, bf16[96,128]{1,0:T(8,128)(2,1)S(1)}, u32[]{:S(2)}, u32[]{:S(2)}) collective-permute-start(bf16[96,128]{1,0:T(8,128)(2,1)} %get-tuple-element.28), channel_id=1, source_target_pairs={{0,4},{1,5},{2,6},{3,7},{4,0},{5,1},{6,2},{7,3},{8,12},{9,13},{10,... | collective-permute-start | bytes 73736 | tf_op jit(solution)/shard_map/ppermute | solution.py:281
  8.0 24.9 %collective-permute-start.10 = (bf16[1024,128]{1,0:T(8,128)(2,1)S(1)}, bf16[1024,128]{1,0:T(8,128)(2,1)S(1)}, u32[]{:S(2)}, u32[]{:S(2)}) collective-permute-start(bf16[1024,128]{1,0:T(8,128)(2,1)S(1)} %get-tuple-element.51), channel_id=1, source_target_pairs={{0,1},{1,0},{2,3},{3,2},{4,5},{5,4},{6,7},{7,6},{8,9},{9,8},{10,11... | collective-permute-start | bytes 786440 | tf_op jit(solution)/shard_map/ppermute | solution.py:304
  9.2 23.8 %collective-permute-start.11 = (bf16[1024,128]{1,0:T(8,128)(2,1)S(1)}, bf16[1024,128]{1,0:T(8,128)(2,1)S(1)}, u32[]{:S(2)}, u32[]{:S(2)}) collective-permute-start(bf16[1024,128]{1,0:T(8,128)(2,1)S(1)} %get-tuple-element.49), channel_id=1, source_target_pairs={{0,1},{1,0},{2,3},{3,2},{4,5},{5,4},{6,7},{7,6},{8,9},{9,8},{10,11... | collective-permute-start | bytes 786440 | tf_op jit(solution)/shard_map/ppermute | solution.py:304
  9.7 6.1 %collective-permute-start.1 = (bf16[96,128]{1,0:T(8,128)(2,1)}, bf16[96,128]{1,0:T(8,128)(2,1)S(1)}, u32[]{:S(2)}, u32[]{:S(2)}) collective-permute-start(bf16[96,128]{1,0:T(8,128)(2,1)} %get-tuple-element.30), channel_id=1, source_target_pairs={{0,8},{1,9},{2,10},{3,11},{4,12},{5,13},{6,14},{7,15},{8,0},{9,1},... | collective-permute-start | bytes 73736 | tf_op jit(solution)/shard_map/ppermute | solution.py:281
  11.8 6.0 %collective-permute-start.2 = (bf16[96,128]{1,0:T(8,128)(2,1)}, bf16[96,128]{1,0:T(8,128)(2,1)S(1)}, u32[]{:S(2)}, u32[]{:S(2)}) collective-permute-start(bf16[96,128]{1,0:T(8,128)(2,1)} %get-tuple-element.31), channel_id=1, source_target_pairs={{0,12},{1,13},{2,14},{3,15},{4,8},{5,9},{6,10},{7,11},{8,4},{9,5},... | collective-permute-start | bytes 73736 | tf_op jit(solution)/shard_map/ppermute | solution.py:281
  13.2 6.5 %collective-permute-start.3 = (bf16[96,128]{1,0:T(8,128)(2,1)}, bf16[96,128]{1,0:T(8,128)(2,1)S(1)}, u32[]{:S(2)}, u32[]{:S(2)}) collective-permute-start(bf16[96,128]{1,0:T(8,128)(2,1)} %get-tuple-element.32), channel_id=1, source_target_pairs={{0,16},{1,17},{2,18},{3,19},{4,20},{5,21},{6,22},{7,23},{8,24},{9,... | collective-permute-start | bytes 73736 | tf_op jit(solution)/shard_map/ppermute | solution.py:281
  15.8 6.5 %collective-permute-start.4 = (bf16[96,128]{1,0:T(8,128)(2,1)}, bf16[96,128]{1,0:T(8,128)(2,1)S(1)}, u32[]{:S(2)}, u32[]{:S(2)}) collective-permute-start(bf16[96,128]{1,0:T(8,128)(2,1)} %get-tuple-element.33), channel_id=1, source_target_pairs={{0,20},{1,21},{2,22},{3,23},{4,16},{5,17},{6,18},{7,19},{8,28},{9,... | collective-permute-start | bytes 73736 | tf_op jit(solution)/shard_map/ppermute | solution.py:281
  17.8 5.8 %collective-permute-start.5 = (bf16[96,128]{1,0:T(8,128)(2,1)}, bf16[96,128]{1,0:T(8,128)(2,1)S(1)}, u32[]{:S(2)}, u32[]{:S(2)}) collective-permute-start(bf16[96,128]{1,0:T(8,128)(2,1)} %get-tuple-element.34), channel_id=1, source_target_pairs={{0,24},{1,25},{2,26},{3,27},{4,28},{5,29},{6,30},{7,31},{8,16},{9,... | collective-permute-start | bytes 73736 | tf_op jit(solution)/shard_map/ppermute | solution.py:281
  19.7 6.7 %collective-permute-start.6 = (bf16[96,128]{1,0:T(8,128)(2,1)}, bf16[96,128]{1,0:T(8,128)(2,1)S(1)}, u32[]{:S(2)}, u32[]{:S(2)}) collective-permute-start(bf16[96,128]{1,0:T(8,128)(2,1)} %get-tuple-element.35), channel_id=1, source_target_pairs={{0,28},{1,29},{2,30},{3,31},{4,24},{5,25},{6,26},{7,27},{8,20},{9,... | collective-permute-start | bytes 73736 | tf_op jit(solution)/shard_map/ppermute | solution.py:281
  26.4 0.7 %copy-start.1 = (bf16[96,128]{1,0:T(8,128)(2,1)S(1)}, bf16[96,128]{1,0:T(8,128)(2,1)}, u32[]{:S(2)}) copy-start(bf16[96,128]{1,0:T(8,128)(2,1)} %get-tuple-element.27.refs_0_) | copy-start | bytes 73732
  27.2 4.3 %collective-permute-start.8 = (bf16[8,32,128]{2,1,0:T(8,128)(2,1)S(1)}, bf16[8,32,128]{2,1,0:T(8,128)(2,1)S(1)}, u32[]{:S(2)}, u32[]{:S(2)}) collective-permute-start(bf16[8,32,128]{2,1,0:T(8,128)(2,1)S(1)} %get-tuple-element.36.q0_ref), channel_id=1, source_target_pairs={{0,2},{1,3},{2,0},{3,1},{4,6},{5,7},{6,4},{7,5},{8,10},{9,11},{10,... | collective-permute-start | bytes 196616 | tf_op jit(solution)/shard_map/ppermute | solution.py:296
  28.8 4.2 %collective-permute-start.9 = (bf16[8,32,128]{2,1,0:T(8,128)(2,1)S(1)}, bf16[8,32,128]{2,1,0:T(8,128)(2,1)S(1)}, u32[]{:S(2)}, u32[]{:S(2)}) collective-permute-start(bf16[8,32,128]{2,1,0:T(8,128)(2,1)S(1)} %get-tuple-element.37), channel_id=1, source_target_pairs={{0,3},{1,2},{2,1},{3,0},{4,7},{5,6},{6,5},{7,4},{8,11},{9,10},{10,... | collective-permute-start | bytes 196616 | tf_op jit(solution)/shard_map/ppermute | solution.py:296
  28.8 4.2 %collective-permute-start.7 = (bf16[8,32,128]{2,1,0:T(8,128)(2,1)S(1)}, bf16[8,32,128]{2,1,0:T(8,128)(2,1)S(1)}, u32[]{:S(2)}, u32[]{:S(2)}) collective-permute-start(bf16[8,32,128]{2,1,0:T(8,128)(2,1)S(1)} %get-tuple-element.37), channel_id=1, source_target_pairs={{0,1},{1,0},{2,3},{3,2},{4,5},{5,4},{6,7},{7,6},{8,9},{9,8},{10,11... | collective-permute-start | bytes 196616 | tf_op jit(solution)/shard_map/ppermute | solution.py:296
  36.8 15.4 %all-to-all-start = ((bf16[32,40,128]{2,1,0:T(8,128)(2,1)}), bf16[32,40,128]{2,1,0:T(8,128)(2,1)S(1)}, u32[]{:S(2)}, u32[]{:S(2)}) async-start(bf16[32,40,128]{2,1,0:T(8,128)(2,1)} %attend.1), calls=%async_computation | async-start | bytes 655360 | tf_op jit(solution)/shard_map/all_to_all | solution.py:328
  40.2 5.5 %collective-permute-start.14 = (bf16[8,32,128]{2,1,0:T(8,128)(2,1)S(1)}, bf16[8,32,128]{2,1,0:T(8,128)(2,1)S(1)}, u32[]{:S(2)}, u32[]{:S(2)}) collective-permute-start(bf16[8,32,128]{2,1,0:T(8,128)(2,1)S(1)} %get-tuple-element.44.kv0_ref), channel_id=1, source_target_pairs={{0,3},{1,2},{2,1},{3,0},{4,7},{5,6},{6,5},{7,4},{8,11},{9,10},{10,... | collective-permute-start | bytes 196616 | tf_op jit(solution)/shard_map/ppermute | solution.py:331
  41.8 6.7 %collective-permute-start.13 = (bf16[8,32,128]{2,1,0:T(8,128)(2,1)S(1)}, bf16[8,32,128]{2,1,0:T(8,128)(2,1)S(1)}, u32[]{:S(2)}, u32[]{:S(2)}) collective-permute-start(bf16[8,32,128]{2,1,0:T(8,128)(2,1)S(1)} %get-tuple-element.44.kv0_ref), channel_id=1, source_target_pairs={{0,2},{1,3},{2,0},{3,1},{4,6},{5,7},{6,4},{7,5},{8,10},{9,11},{10,... | collective-permute-start | bytes 196616 | tf_op jit(solution)/shard_map/ppermute | solution.py:331
  42.1 6.4 %collective-permute-start.12 = (bf16[8,32,128]{2,1,0:T(8,128)(2,1)S(1)}, bf16[8,32,128]{2,1,0:T(8,128)(2,1)S(1)}, u32[]{:S(2)}, u32[]{:S(2)}) collective-permute-start(bf16[8,32,128]{2,1,0:T(8,128)(2,1)S(1)} %get-tuple-element.44.kv0_ref), channel_id=1, source_target_pairs={{0,1},{1,0},{2,3},{3,2},{4,5},{5,4},{6,7},{7,6},{8,9},{9,8},{10,11... | collective-permute-start | bytes 196616 | tf_op jit(solution)/shard_map/ppermute | solution.py:331

commit v9 on v6

--- a/solution.py
+++ b/solution.py
@@ -47,35 +47,41 @@
     return copies
 
 
-def pack_kernel(chips, capacity, chosen_hbm, q_hbm, k_hbm, v_hbm, send_ref, chosen_ref, q_ref, k_ref, v_ref, sems):
+def pack_kernel(capacity, chosen_hbm, q_hbm, k_hbm, v_hbm, send_hbm, chosen_ref, q_ref, k_ref, v_ref, send_ref, sems):
     copies = fetch([(chosen_hbm, chosen_ref), (q_hbm, q_ref), (k_hbm, k_ref), (v_hbm, v_ref)], sems)
     tokens = q_ref.shape[0]
     per = capacity * tokens
-    span = chips * KVH
-    key_blocks = send_ref.shape[0] // span
+    key_blocks, chips = send_ref.shape[1:3]
     lane = lax.broadcasted_iota(jnp.int32, (tokens, key_blocks * per), 1)
     block, slot, token = lane // per, lane % per // tokens, lane % tokens
-    for copy in copies:
-        copy.wait()
+    copies[0].wait()
+    spread = [
+        jnp.concatenate(
+            slot_match(chosen_ref, g, block, slot, token) + [jnp.zeros(lane.shape, jnp.float32)], axis=0
+        ).T.astype(jnp.bfloat16)
+        for g in range(KVH)
+    ]
+    for copy in copies[1:]:
+        copy.wait()
+    sent = []
     for g in range(KVH):
-        spread = jnp.concatenate(
-            slot_match(chosen_ref, g, block, slot, token) + [jnp.zeros(lane.shape, jnp.float32)], axis=0
-        )
         rows = head_rows(q_ref, g)
-        rows = jnp.concatenate(rows + [jnp.zeros_like(rows[0])], axis=0)
-        slots = jnp.dot(
-            spread.T.astype(jnp.bfloat16), rows.astype(jnp.bfloat16), preferred_element_type=jnp.float32
-        ).astype(jnp.bfloat16)
+        rows = jnp.concatenate(rows + [jnp.zeros_like(rows[0])], axis=0).astype(jnp.bfloat16)
+        slots = jnp.dot(spread[g], rows, preferred_element_type=jnp.float32).astype(jnp.bfloat16)
         cols = slice(g * HD, (g + 1) * HD)
         fresh = [k_ref[:, cols], v_ref[:, cols]]
         for b in range(key_blocks):
             for chip in range(chips):
-                to = b * span + chip * KVH + g
-                send_ref[to, :per, :] = slots[b * per : (b + 1) * per]
-                send_ref[to, per:, :] = fresh[chip % 2]
-
-
-def masks_kernel(chips, capacity, chosen_ref, q_ref, match_ref, rows_ref):
+                send_ref[g, b, chip, :per, :] = slots[b * per : (b + 1) * per]
+                send_ref[g, b, chip, per:, :] = fresh[chip % 2]
+        sent.append(pltpu.make_async_copy(send_ref.at[g], send_hbm.at[:, :, g], sems.at[4 + g]))
+        sent[g].start()
+    for copy in sent:
+        copy.wait()
+
+
+def masks_kernel(chips, capacity, chosen_ref, q_ref, w_hbm, match_ref, rows_ref, w_ref, sems):
+    copies = fetch([(w_hbm.at[: w_ref.shape[0]], w_ref)], sems)
     tokens = q_ref.shape[0]
     per = capacity * tokens
     lane = lax.broadcasted_iota(jnp.int32, (tokens, match_ref.shape[2]), 1)
@@ -83,12 +89,15 @@
     for g in range(KVH):
         match_ref[g] = jnp.concatenate(slot_match(chosen_ref, g, block, slot, token), axis=0)
         rows_ref[g] = jnp.concatenate(head_rows(q_ref, g), axis=0)
-
-
-def attend_kernel(per, q_ref, ka_ref, va_ref, kb_ref, vb_ref, out_ref, fresh_ref):
+    for copy in copies:
+        copy.wait()
+
+
+def attend_kernel(per, q_ref, ka_ref, va_ref, kb_ref, vb_ref, out_hbm, fresh_ref, out_ref, sems):
     sources = q_ref.shape[0]
+    sent = []
     fresh_ref[...] = q_ref[:, per:, :]
-    step = 256 // per
+    step = 512 // per
     scale = LOG2E * HD**-0.5
     nt = (((1,), (1,)), ((), ()))
     row = lax.broadcasted_iota(jnp.int32, (per, LANES), 0)
@@ -119,10 +128,14 @@
             out_ref[first + s, per:, :] = jnp.where(
                 piece == 0, hi, jnp.where(piece == 1, mid, jnp.where(piece == 2, low, 0.0))
             ).astype(jnp.bfloat16)
-
-
-def fresh_kernel(tokens, rows_ref, kv_ref, kv1_ref, kv2_ref, kv3_ref, w_hbm, out_ref, lse_ref, w_ref, sems):
-    copies = fetch([(w_hbm.at[: w_ref.shape[0]], w_ref)], sems)
+        done = pl.ds(first, step)
+        sent.append(pltpu.make_async_copy(out_ref.at[done], out_hbm.at[done], sems.at[first // step]))
+        sent[-1].start()
+    for copy in sent:
+        copy.wait()
+
+
+def fresh_kernel(tokens, rows_ref, kv_ref, kv1_ref, kv2_ref, kv3_ref, out_ref, lse_ref):
     sources = kv_ref.shape[0]
     place = lax.axis_index("seq")
     core, odd = place % KVH, place // KVH % 2
@@ -150,11 +163,9 @@
         total = total_out[:, HD:]
         out_ref[g] = total_out[:, :HD] / total
         lse_ref[g] = top + jnp.log(total) * LOG2E
-    for copy in copies:
-        copy.wait()
-
-
-def project_kernel(per, hist_ref, out_ref, lse_ref, match_ref, first_ref, w_hbm, y_ref, att_ref, w_ref, sems):
+
+
+def project_kernel(per, hist_ref, out_ref, lse_ref, match_ref, first_ref, w_hbm, y_ref, w_ref, sems):
     depth = KVH * HD
     ready = first_ref.shape[0] // depth
     copies = fetch(
@@ -169,6 +180,12 @@
     fold = LANES // per
     row = lax.broadcasted_iota(jnp.int32, (holders, LANES), 0)
     lane = lax.broadcasted_iota(jnp.int32, (holders, LANES), 1)
+
+    def times(heads, weights):
+        lhs = jnp.concatenate(heads, axis=1).astype(jnp.bfloat16)
+        return jnp.dot(lhs, weights, preferred_element_type=jnp.float32)
+
+    heads = []
     for g in range(KVH):
         outs = hist_ref[:, g, :per, :].reshape(holders * per, HD)
         stats = jnp.sum(hist_ref[:, g, per:, :].astype(jnp.float32), axis=1)
@@ -194,27 +211,22 @@
             + own_w * out_ref[g]
         )
         att = num / (jnp.sum(w, axis=1, keepdims=True) + own_w)
-        for r in range(GROUP):
-            h = g * GROUP + r
-            att_ref[:, h * HD : (h + 1) * HD] = att[r * tokens : (r + 1) * tokens]
-    att = att_ref[...].astype(jnp.bfloat16)
-    y = jnp.dot(att[:, : ready * depth], first_ref[...], preferred_element_type=jnp.float32)
+        heads = heads + [att[r * tokens : (r + 1) * tokens] for r in range(GROUP)]
+        if g == 0:
+            y = times(heads[: ready * KVH], first_ref[...])
     for i, copy in enumerate(copies):
         copy.wait()
-        y = y + jnp.dot(
-            att[:, (ready + i) * depth : (ready + i + 1) * depth],
-            w_ref[i * depth : (i + 1) * depth, :],
-            preferred_element_type=jnp.float32,
-        )
+        y = y + times(heads[(ready + i) * KVH : (ready + i + 1) * KVH], w_ref[i * depth : (i + 1) * depth, :])
     y_ref[...] = y.astype(jnp.bfloat16)
 
 
 VMEM = pl.BlockSpec(memory_space=pltpu.VMEM)
 HBM = pl.BlockSpec(memory_space=pltpu.HBM)
-
-
-def call(kernel, name, out_shape, specs, *operands, scratch=(), flops=0, moved=0, limit=16):
-    outs = jax.tree.map(lambda _: VMEM, out_shape)
+ANY = pl.BlockSpec(memory_space=pl.ANY)
+
+
+def call(kernel, name, out_shape, specs, *operands, outs=None, scratch=(), flops=0, moved=0, limit=16):
+    outs = outs or jax.tree.map(lambda _: VMEM, out_shape)
     return pl.pallas_call(
         kernel,
         name=name,
@@ -243,23 +255,26 @@
         return [(i, i ^ bit) for i in range(devices)]
 
     send = call(
-        functools.partial(pack_kernel, chips, capacity),
+        functools.partial(pack_kernel, capacity),
         "pack",
-        jax.ShapeDtypeStruct((devices, per + tokens, HD), bf16),
+        jax.ShapeDtypeStruct((key_blocks, chips, KVH, per + tokens, HD), bf16),
         [HBM] * 4,
         picks, queries, stretch_keys, stretch_values,
+        outs=ANY,
         scratch=[
             pltpu.VMEM(picks.shape, jnp.int32),
             pltpu.VMEM(queries.shape, bf16),
             pltpu.VMEM(stretch_keys.shape, bf16),
             pltpu.VMEM(stretch_values.shape, bf16),
-            pltpu.SemaphoreType.DMA((4,)),
+            pltpu.VMEM((KVH, key_blocks, chips, per + tokens, HD), bf16),
+            pltpu.SemaphoreType.DMA((4 + KVH,)),
         ],
         limit=60,
     )
     send, cache_keys, cache_values, picks, queries = lax.optimization_barrier(
         (send, cache_keys, cache_values, picks, queries)
     )
+    send = send.reshape(devices, per + tokens, HD)
     got = lax.all_to_all(send, "seq", split_axis=0, concat_axis=0, tiled=True)
 
     core = lax.axis_index("seq") % KVH
@@ -270,17 +285,6 @@
     k_own, v_own = halves(core)
     k_peer, v_peer = [lax.ppermute(x, "seq", partner(1)) for x in halves(1 - core)]
     holders = devices // KVH
-    match, query_rows = call(
-        functools.partial(masks_kernel, chips, capacity),
-        "masks",
-        (
-            jax.ShapeDtypeStruct((KVH, GROUP * tokens, holders * per), f32),
-            jax.ShapeDtypeStruct((KVH, GROUP * tokens, HD), f32),
-        ),
-        [VMEM] * 2,
-        picks, queries,
-    )
-
     rows = devices * per
     back, fresh = call(
         functools.partial(attend_kernel, per),
@@ -291,26 +295,44 @@
         ),
         [VMEM] * 5,
         got, k_own, v_own, k_peer, v_peer,
+        outs=(ANY, VMEM),
+        scratch=[
+            pltpu.VMEM((devices, per + 8, HD), bf16),
+            pltpu.SemaphoreType.DMA((rows // 512,)),
+        ],
         flops=8 * rows * cache_rows * HD,
         moved=4 << 20,
         limit=32,
     )
+    back, picks, queries, out_weight = lax.optimization_barrier((back, picks, queries, out_weight))
     hist = lax.all_to_all(back, "seq", split_axis=0, concat_axis=0, tiled=True)
+
+    ready = EARLY * KVH * HD
+    match, query_rows, first = call(
+        functools.partial(masks_kernel, chips, capacity),
+        "masks",
+        (
+            jax.ShapeDtypeStruct((KVH, GROUP * tokens, holders * per), f32),
+            jax.ShapeDtypeStruct((KVH, GROUP * tokens, HD), f32),
+            jax.ShapeDtypeStruct((ready, out_weight.shape[1]), bf16),
+        ),
+        [VMEM, VMEM, HBM],
+        picks, queries, out_weight,
+        scratch=[pltpu.SemaphoreType.DMA((1,))],
+        limit=50,
+    )
 
     far = lax.ppermute(fresh, "seq", partner(2))
     near, both = [lax.ppermute(x, "seq", partner(1)) for x in (fresh, far)]
     part = jax.ShapeDtypeStruct((KVH, GROUP * tokens, HD), f32)
-    ready = EARLY * KVH * HD
-    out, lse, first = call(
+    out, lse = call(
         functools.partial(fresh_kernel, tokens),
         "fresh",
-        (part, part, jax.ShapeDtypeStruct((ready, out_weight.shape[1]), bf16)),
-        [VMEM] * 5 + [HBM],
-        query_rows, fresh, near, far, both, out_weight,
-        scratch=[pltpu.SemaphoreType.DMA((1,))],
+        (part, part),
+        [VMEM] * 5,
+        query_rows, fresh, near, far, both,
         flops=8 * H * tokens * devices * tokens * HD,
         moved=1 << 20,
-        limit=50,
     )
     return call(
         functools.partial(project_kernel, per),
@@ -319,7 +341,6 @@
         [VMEM] * 5 + [HBM],
         hist.reshape(holders, KVH, per + 8, HD), out, lse, match, first, out_weight,
         scratch=[
-            pltpu.VMEM((tokens, H * HD), f32),
             pltpu.VMEM((out_weight.shape[0] - ready, out_weight.shape[1]), bf16),
             pltpu.SemaphoreType.DMA((GROUP - EARLY,)),
         ],

time: 43.1 us -> 43.7 us (1.014)
  Pallas kernels: 10.7 us -> 11.6 us
    ppermute x2, waiting for transfers between devices: 1.1 us -> 0.01 us  [body(): near, both = [lax.ppermute(x, 'seq', partner(1)) for x in (fresh, far)]]
    pallas_call x5, Pallas kernels: 10.7 us -> 11.6 us  [call(): pl.pallas_call(kernel, name=name, out_shape=out_shape, in_specs=specs, ou...]
    all_to_all x1, waiting for transfers between devices: 2.37 us -> 3.18 us  [body(): hist = lax.all_to_all(back, 'seq', split_axis=0, concat_axis=0, tiled=True)]
  transfers between devices with their start and end apart: 7 -> 7, of which waited for: 5 -> 4; matrix products, arithmetic and copies ran while one was open for 5% -> 5% of each run, Pallas kernels for 5% -> 5%
where the time goes in v9:
time: 43.7 us; the launch traced here: 43.3 us
  waiting for transfers between devices  17.2 us (39%)
  starting transfers between devices  12.3 us (28%)
  Pallas kernels  11.6 us (27%)
  local copies, waits for them, and re-layouts  2.14 us (5%)
    pallas_call x5, Pallas kernels, call(): pl.pallas_call(kernel, name=name, out_shape=out_shape, in_specs=specs, ou...  11.6 us
    all_to_all x1, waiting for transfers between devices, body(): got = lax.all_to_all(send, 'seq', split_axis=0, concat_axis=0, tiled=True)  7.91 us
    all_to_all x1, starting transfers between devices, body(): got = lax.all_to_all(send, 'seq', split_axis=0, concat_axis=0, tiled=True)  7.3 us
    ppermute x1, waiting for transfers between devices, body(): far = lax.ppermute(fresh, 'seq', partner(2))  4.83 us
    all_to_all x1, waiting for transfers between devices, body(): hist = lax.all_to_all(back, 'seq', split_axis=0, concat_axis=0, tiled=True)  3.18 us
    all_to_all x1, starting transfers between devices, body(): hist = lax.all_to_all(back, 'seq', split_axis=0, concat_axis=0, tiled=True)  2.61 us
    dynamic_slice x2, local copies, waits for them, and re-layouts, halves(): lax.dynamic_slice_in_dim(x, head * HD, HD, axis=1)  2.13 us
    ppermute x1, starting transfers between devices, body(): far = lax.ppermute(fresh, 'seq', partner(2))  1.7 us
  transfers between devices with their start and end apart: 7, of which 4 were waited for; matrix products, arithmetic and copies ran while one was open for 5% of the time, Pallas kernels for 5%

profile of v9, /device:TPU:0, one launch (start us, length us, event | category | flops | bytes accessed | tf_op | source)
XLA Modules:
  0.0 43.3 jit_solution(1308425625606984384)
XLA Ops:
  0.0 0.0 copy-start
  0.0 0.0 copy-start.1
  0.0 2.0 %pack.1 = bf16[8,2,2,40,128]{4,3,2,1,0:T(8,128)(2,1)} custom-call(s32[3,1,14]{2,1,0:T(1,128)} %bitcast.4, bf16[8,1792]{1,0:T(8,128)(2,1)} %q_ref, bf16[8,256]{1,0:T(8,128)(2,1)} %k_hbm.1, bf16[8,256]{1,0:T(8,128)(2,1)} %v_hbm.1), custom_call_target="tpu_custom_call" | custom-call | tf_op jit(solution)/shard_map/pack/pallas_call | solution.py:230
  2.0 7.3 %all-to-all-start = ((bf16[32,40,128]{2,1,0:T(8,128)(2,1)}), bf16[32,40,128]{2,1,0:T(8,128)(2,1)S(1)}, u32[]{:S(2)}, u32[]{:S(2)}) async-start(bf16[32,40,128]{2,1,0:T(8,128)(2,1)} %bitcast.6), calls=%async_computation | async-start | bytes 655360 | tf_op jit(solution)/shard_map/all_to_all | solution.py:278
  9.4 1.1 %constant_dynamic-slice_fusion.1 = (bf16[1024,128]{1,0:T(8,128)(2,1)S(1)}, bf16[1024,128]{1,0:T(8,128)(2,1)S(1)}) fusion(bf16[1024,256]{1,0:T(8,128)(2,1)} %param.10, s32[]{:T(128)S(6)} %select_n.17, s32[]{:T(128)S(6)} %select_n.16), kind=kLoop, calls=%fused_computation.1 | loop fusion | bytes 1048584 | tf_op jit(solution)/shard_map/dynamic_slice | solution.py:283
  10.4 0.3 collective-permute-start
  10.7 1.1 %constant_dynamic-slice_fusion = (bf16[1024,128]{1,0:T(8,128)(2,1)S(1)}, bf16[1024,128]{1,0:T(8,128)(2,1)S(1)}) fusion(bf16[1024,256]{1,0:T(8,128)(2,1)} %param.11, s32[]{:T(128)S(6)} %select_n.17, s32[]{:T(128)S(6)} %select_n.16), kind=kLoop, calls=%fused_computation | loop fusion | bytes 1048584 | tf_op jit(solution)/shard_map/dynamic_slice | solution.py:283
  11.8 0.3 collective-permute-start.1
  12.1 0.0 collective-permute-done.kb_ref
  12.1 1.3 %collective-permute-done.1.vb_ref = bf16[1024,128]{1,0:T(8,128)(2,1)S(1)} collective-permute-done((bf16[1024,128]{1,0:T(8,128)(2,1)S(1)}, bf16[1024,128]{1,0:T(8,128)(2,1)S(1)}, u32[]{:S(2)}, u32[]{:S(2)}) %collective-permute-start.1) | collective-permute-done | bytes 262176 | tf_op jit(solution)/shard_map/ppermute | solution.py:286
  13.4 7.9 %all-to-all-done.q_ref = bf16[32,40,128]{2,1,0:T(8,128)(2,1)S(1)} async-done(((bf16[32,40,128]{2,1,0:T(8,128)(2,1)}), bf16[32,40,128]{2,1,0:T(8,128)(2,1)S(1)}, u32[]{:S(2)}, u32[]{:S(2)}) %all-to-all-start) | async-done | bytes 327712 | tf_op jit(solution)/shard_map/all_to_all | solution.py:278
  21.3 4.3 %attend.1 = (bf16[32,40,128]{2,1,0:T(8,128)(2,1)}, bf16[32,8,128]{2,1,0:T(8,128)(2,1)S(1)}) custom-call(bf16[32,40,128]{2,1,0:T(8,128)(2,1)S(1)} %all-to-all-done.q_ref, bf16[1024,128]{1,0:T(8,128)(2,1)S(1)} %get-tuple-element.40.ka_ref, bf16[1024,128]{1,0:T(8,128)(2,1)S(1)} %get-tuple-element.38.va_ref, bf16[1024,128]{1,0:T(8,128)(2,1)S(1)} %collective-permute-done.kb_ref, ...), custom_call_target="tpu_custom_call" | custom-call | flops 1073741824 | bytes 4194304 | tf_op jit(solution)/shard_map/attend/pallas_call | solution.py:230
  25.6 2.6 %all-to-all-start.1 = ((bf16[32,40,128]{2,1,0:T(8,128)(2,1)}), bf16[32,40,128]{2,1,0:T(8,128)(2,1)S(1)}, u32[]{:S(2)}, u32[]{:S(2)}) async-start(bf16[32,40,128]{2,1,0:T(8,128)(2,1)} %get-tuple-element.27), calls=%async_computation.1 | async-start | bytes 655360 | tf_op jit(solution)/shard_map/all_to_all | solution.py:308
  28.2 1.7 %collective-permute-start.3 = (bf16[32,8,128]{2,1,0:T(8,128)(2,1)S(1)}, bf16[32,8,128]{2,1,0:T(8,128)(2,1)S(1)}, u32[]{:S(2)}, u32[]{:S(2)}) collective-permute-start(bf16[32,8,128]{2,1,0:T(8,128)(2,1)S(1)} %get-tuple-element.32.kv_ref), channel_id=1, source_target_pairs={{0,2},{1,3},{2,0},{3,1},{4,6},{5,7},{6,4},{7,5},{8,10},{9,11},{10,... | collective-permute-start | bytes 196616 | tf_op jit(solution)/shard_map/ppermute | solution.py:325
  30.0 0.0 collective-permute-start.2
  30.0 4.8 %collective-permute-done.3.kv2_ref = bf16[32,8,128]{2,1,0:T(8,128)(2,1)S(1)} collective-permute-done((bf16[32,8,128]{2,1,0:T(8,128)(2,1)S(1)}, bf16[32,8,128]{2,1,0:T(8,128)(2,1)S(1)}, u32[]{:S(2)}, u32[]{:S(2)}) %collective-permute-start.3) | collective-permute-done | bytes 65568 | tf_op jit(solution)/shard_map/ppermute | solution.py:325
  34.8 0.0 collective-permute-start.4
  34.8 0.0 copy-done
  34.8 0.0 copy-done.1
  34.8 1.8 %masks.1 = (f32[2,56,512]{2,1,0:T(8,128)S(1)}, f32[2,56,128]{2,1,0:T(8,128)S(1)}, bf16[768,1792]{1,0:T(8,128)(2,1)S(1)}) custom-call(s32[3,1,14]{2,1,0:T(1,128)S(1)} %bitcast.5, bf16[8,1792]{1,0:T(8,128)(2,1)S(1)} %copy-done, bf16[1792,1792]{1,0:T(8,128)(2,1)} %w_hbm.1), custom_call_target="tpu_custom_call" | custom-call | tf_op jit(solution)/shard_map/masks/pallas_call | solution.py:230
  36.6 0.0 collective-permute-done.2.kv1_ref
  36.6 0.0 collective-permute-done.4.kv3_ref
  36.6 0.4 %fresh.1 = (f32[2,56,128]{2,1,0:T(8,128)S(1)}, f32[2,56,128]{2,1,0:T(8,128)S(1)}) custom-call(f32[2,56,128]{2,1,0:T(8,128)S(1)} %get-tuple-element.31.rows_ref, bf16[32,8,128]{2,1,0:T(8,128)(2,1)S(1)} %get-tuple-element.32.kv_ref, bf16[32,8,128]{2,1,0:T(8,128)(2,1)S(1)} %collective-permute-done.2.kv1_ref, ...), custom_call_target="tpu_custom_call" | custom-call | flops 29360128 | bytes 1048576 | tf_op jit(solution)/shard_map/fresh/pallas_call | solution.py:230
  37.1 3.2 %all-to-all-done.1 = bf16[32,40,128]{2,1,0:T(8,128)(2,1)S(1)} async-done(((bf16[32,40,128]{2,1,0:T(8,128)(2,1)}), bf16[32,40,128]{2,1,0:T(8,128)(2,1)S(1)}, u32[]{:S(2)}, u32[]{:S(2)}) %all-to-all-start.1) | async-done | bytes 327712 | tf_op jit(solution)/shard_map/all_to_all | solution.py:308
  40.2 3.1 %project.1 = bf16[8,1792]{1,0:T(8,128)(2,1)} custom-call(bf16[16,2,40,128]{3,2,1,0:T(8,128)(2,1)S(1)} %bitcast.3, f32[2,56,128]{2,1,0:T(8,128)S(1)} %get-tuple-element.33.out_ref, f32[2,56,128]{2,1,0:T(8,128)S(1)} %get-tuple-element.34.lse_ref, f32[2,56,512]{2,1,0:T(8,128)S(1)} %get-tuple-element.35.match_ref, ...), custom_call_target="tpu_custom_call" | custom-call | flops 51380224 | bytes 6422528 | tf_op jit(solution)/shard_map/project/pallas_call | solution.py:230
Async XLA Ops:
  0.0 34.8 %copy-start = (bf16[8,1792]{1,0:T(8,128)(2,1)S(1)}, bf16[8,1792]{1,0:T(8,128)(2,1)}, u32[]{:S(2)}) copy-start(bf16[8,1792]{1,0:T(8,128)(2,1)} %q_ref) | copy-start | bytes 86020
  0.0 34.8 %copy-start.1 = (s32[1,14,3]{1,0,2:T(1,128)S(1)}, s32[1,14,3]{1,0,2:T(1,128)}, u32[]{:S(2)}) copy-start(s32[1,14,3]{1,0,2:T(1,128)} %param.12) | copy-start | bytes 508
  2.0 19.3 %all-to-all-start = ((bf16[32,40,128]{2,1,0:T(8,128)(2,1)}), bf16[32,40,128]{2,1,0:T(8,128)(2,1)S(1)}, u32[]{:S(2)}, u32[]{:S(2)}) async-start(bf16[32,40,128]{2,1,0:T(8,128)(2,1)} %bitcast.6), calls=%async_computation | async-start | bytes 655360 | tf_op jit(solution)/shard_map/all_to_all | solution.py:278
  10.4 1.7 %collective-permute-start = (bf16[1024,128]{1,0:T(8,128)(2,1)S(1)}, bf16[1024,128]{1,0:T(8,128)(2,1)S(1)}, u32[]{:S(2)}, u32[]{:S(2)}) collective-permute-start(bf16[1024,128]{1,0:T(8,128)(2,1)S(1)} %get-tuple-element.39), channel_id=1, source_target_pairs={{0,1},{1,0},{2,3},{3,2},{4,5},{5,4},{6,7},{7,6},{8,9},{9,8},{10,11... | collective-permute-start | bytes 786440 | tf_op jit(solution)/shard_map/ppermute | solution.py:286
  11.8 1.6 %collective-permute-start.1 = (bf16[1024,128]{1,0:T(8,128)(2,1)S(1)}, bf16[1024,128]{1,0:T(8,128)(2,1)S(1)}, u32[]{:S(2)}, u32[]{:S(2)}) collective-permute-start(bf16[1024,128]{1,0:T(8,128)(2,1)S(1)} %get-tuple-element.37), channel_id=1, source_target_pairs={{0,1},{1,0},{2,3},{3,2},{4,5},{5,4},{6,7},{7,6},{8,9},{9,8},{10,11... | collective-permute-start | bytes 786440 | tf_op jit(solution)/shard_map/ppermute | solution.py:286
  25.6 14.6 %all-to-all-start.1 = ((bf16[32,40,128]{2,1,0:T(8,128)(2,1)}), bf16[32,40,128]{2,1,0:T(8,128)(2,1)S(1)}, u32[]{:S(2)}, u32[]{:S(2)}) async-start(bf16[32,40,128]{2,1,0:T(8,128)(2,1)} %get-tuple-element.27), calls=%async_computation.1 | async-start | bytes 655360 | tf_op jit(solution)/shard_map/all_to_all | solution.py:308
  28.2 6.5 %collective-permute-start.3 = (bf16[32,8,128]{2,1,0:T(8,128)(2,1)S(1)}, bf16[32,8,128]{2,1,0:T(8,128)(2,1)S(1)}, u32[]{:S(2)}, u32[]{:S(2)}) collective-permute-start(bf16[32,8,128]{2,1,0:T(8,128)(2,1)S(1)} %get-tuple-element.32.kv_ref), channel_id=1, source_target_pairs={{0,2},{1,3},{2,0},{3,1},{4,6},{5,7},{6,4},{7,5},{8,10},{9,11},{10,... | collective-permute-start | bytes 196616 | tf_op jit(solution)/shard_map/ppermute | solution.py:325
  30.0 6.6 %collective-permute-start.2 = (bf16[32,8,128]{2,1,0:T(8,128)(2,1)S(1)}, bf16[32,8,128]{2,1,0:T(8,128)(2,1)S(1)}, u32[]{:S(2)}, u32[]{:S(2)}) collective-permute-start(bf16[32,8,128]{2,1,0:T(8,128)(2,1)S(1)} %get-tuple-element.32.kv_ref), channel_id=1, source_target_pairs={{0,1},{1,0},{2,3},{3,2},{4,5},{5,4},{6,7},{7,6},{8,9},{9,8},{10,11... | collective-permute-start | bytes 196616 | tf_op jit(solution)/shard_map/ppermute | solution.py:326
  34.8 1.8 %collective-permute-start.4 = (bf16[32,8,128]{2,1,0:T(8,128)(2,1)S(1)}, bf16[32,8,128]{2,1,0:T(8,128)(2,1)S(1)}, u32[]{:S(2)}, u32[]{:S(2)}) collective-permute-start(bf16[32,8,128]{2,1,0:T(8,128)(2,1)S(1)} %collective-permute-done.3.kv2_ref), channel_id=1, source_target_pairs={{0,1},{1,0},{2,3},{3,2},{4,5},{5,4},{6,7},{7,6},{8,9},{9,8},{10,11... | collective-permute-start | bytes 196616 | tf_op jit(solution)/shard_map/ppermute | solution.py:326

commit v10 on v9

--- a/solution.py
+++ b/solution.py
@@ -19,6 +19,7 @@
 LOG2E = math.log2(math.e)
 LANES = 128
 EARLY = 3
+STEP = 128
 
 
 def head_rows(q_ref, g):
@@ -96,8 +97,7 @@
 def attend_kernel(per, q_ref, ka_ref, va_ref, kb_ref, vb_ref, out_hbm, fresh_ref, out_ref, sems):
     sources = q_ref.shape[0]
     sent = []
-    fresh_ref[...] = q_ref[:, per:, :]
-    step = 512 // per
+    step = STEP // per
     scale = LOG2E * HD**-0.5
     nt = (((1,), (1,)), ((), ()))
     row = lax.broadcasted_iota(jnp.int32, (per, LANES), 0)
@@ -105,11 +105,20 @@
     diagonal = row == lane % per
     piece = lax.broadcasted_iota(jnp.int32, (8, LANES), 0)
     ones = jnp.ones(va_ref.shape, jnp.bfloat16)
+    fresh_ref[...] = q_ref[:, per:, :]
+
+    def scores(first):
+        q = q_ref[first : first + step, :per, :].reshape(step * per, HD)
+        return [
+            lax.dot_general(q, k_ref[...], nt, preferred_element_type=jnp.float32) for k_ref in (ka_ref, kb_ref)
+        ]
+
+    ahead = scores(0)
     for first in range(0, sources, step):
-        q = q_ref[first : first + step, :per, :].reshape(step * per, HD)
-        sa = lax.dot_general(q, ka_ref[...], nt, preferred_element_type=jnp.float32)
-        sb = lax.dot_general(q, kb_ref[...], nt, preferred_element_type=jnp.float32)
-        top = jnp.maximum(jnp.max(sa, axis=1, keepdims=True), jnp.max(sb, axis=1, keepdims=True)) * scale
+        sa, sb = ahead
+        if first + step < sources:
+            ahead = scores(first + step)
+        top = scale * jnp.maximum(jnp.max(sa, axis=1, keepdims=True), jnp.max(sb, axis=1, keepdims=True))
         wa = jnp.exp2(sa * scale - top).astype(jnp.bfloat16)
         wb = jnp.exp2(sb * scale - top).astype(jnp.bfloat16)
         both = jnp.dot(
@@ -298,7 +307,7 @@
         outs=(ANY, VMEM),
         scratch=[
             pltpu.VMEM((devices, per + 8, HD), bf16),
-            pltpu.SemaphoreType.DMA((rows // 512,)),
+            pltpu.SemaphoreType.DMA((rows // STEP,)),
         ],
         flops=8 * rows * cache_rows * HD,
         moved=4 << 20,

time: 43.7 us -> 42.9 us (0.982)
  Pallas kernels: 11.6 us -> 10.8 us
    pallas_call x5, Pallas kernels: 11.6 us -> 10.8 us  [call(): pl.pallas_call(kernel, name=name, out_shape=out_shape, in_specs=specs, ou...]
where the time goes in v10:
time: 42.9 us; the launch traced here: 42.5 us
  waiting for transfers between devices  17.2 us (40%)
  starting transfers between devices  12.3 us (29%)
  Pallas kernels  10.8 us (25%)
  local copies, waits for them, and re-layouts  2.14 us (5%)
    pallas_call x5, Pallas kernels, call(): pl.pallas_call(kernel, name=name, out_shape=out_shape, in_specs=specs, ou...  10.8 us
    all_to_all x1, waiting for transfers between devices, body(): got = lax.all_to_all(send, 'seq', split_axis=0, concat_axis=0, tiled=True)  7.91 us
    all_to_all x1, starting transfers between devices, body(): got = lax.all_to_all(send, 'seq', split_axis=0, concat_axis=0, tiled=True)  7.3 us
    ppermute x1, waiting for transfers between devices, body(): far = lax.ppermute(fresh, 'seq', partner(2))  4.83 us
    all_to_all x1, waiting for transfers between devices, body(): hist = lax.all_to_all(back, 'seq', split_axis=0, concat_axis=0, tiled=True)  3.18 us
    all_to_all x1, starting transfers between devices, body(): hist = lax.all_to_all(back, 'seq', split_axis=0, concat_axis=0, tiled=True)  2.61 us
    dynamic_slice x2, local copies, waits for them, and re-layouts, halves(): lax.dynamic_slice_in_dim(x, head * HD, HD, axis=1)  2.13 us
    ppermute x1, starting transfers between devices, body(): far = lax.ppermute(fresh, 'seq', partner(2))  1.7 us
  transfers between devices with their start and end apart: 7, of which 4 were waited for; matrix products, arithmetic and copies ran while one was open for 5% of the time, Pallas kernels for 5%

profile of v10, /device:TPU:0, one launch (start us, length us, event | category | flops | bytes accessed | tf_op | source)
XLA Modules:
  0.0 42.5 jit_solution(538546890918138142)
XLA Ops:
  0.0 0.0 copy-start
  0.0 0.0 copy-start.1
  0.0 2.0 %pack.1 = bf16[8,2,2,40,128]{4,3,2,1,0:T(8,128)(2,1)} custom-call(s32[3,1,14]{2,1,0:T(1,128)} %bitcast.4, bf16[8,1792]{1,0:T(8,128)(2,1)} %q_ref, bf16[8,256]{1,0:T(8,128)(2,1)} %k_hbm.1, bf16[8,256]{1,0:T(8,128)(2,1)} %v_hbm.1), custom_call_target="tpu_custom_call" | custom-call | tf_op jit(solution)/shard_map/pack/pallas_call | solution.py:239
  2.0 7.3 %all-to-all-start = ((bf16[32,40,128]{2,1,0:T(8,128)(2,1)}), bf16[32,40,128]{2,1,0:T(8,128)(2,1)S(1)}, u32[]{:S(2)}, u32[]{:S(2)}) async-start(bf16[32,40,128]{2,1,0:T(8,128)(2,1)} %bitcast.6), calls=%async_computation | async-start | bytes 655360 | tf_op jit(solution)/shard_map/all_to_all | solution.py:287
  9.4 1.1 %constant_dynamic-slice_fusion.1 = (bf16[1024,128]{1,0:T(8,128)(2,1)S(1)}, bf16[1024,128]{1,0:T(8,128)(2,1)S(1)}) fusion(bf16[1024,256]{1,0:T(8,128)(2,1)} %param.10, s32[]{:T(128)S(6)} %select_n.17, s32[]{:T(128)S(6)} %select_n.16), kind=kLoop, calls=%fused_computation.1 | loop fusion | bytes 1048584 | tf_op jit(solution)/shard_map/dynamic_slice | solution.py:292
  10.4 0.3 collective-permute-start
  10.7 1.1 %constant_dynamic-slice_fusion = (bf16[1024,128]{1,0:T(8,128)(2,1)S(1)}, bf16[1024,128]{1,0:T(8,128)(2,1)S(1)}) fusion(bf16[1024,256]{1,0:T(8,128)(2,1)} %param.11, s32[]{:T(128)S(6)} %select_n.17, s32[]{:T(128)S(6)} %select_n.16), kind=kLoop, calls=%fused_computation | loop fusion | bytes 1048584 | tf_op jit(solution)/shard_map/dynamic_slice | solution.py:292
  11.8 0.3 collective-permute-start.1
  12.1 0.0 collective-permute-done.kb_ref
  12.1 1.3 %collective-permute-done.1.vb_ref = bf16[1024,128]{1,0:T(8,128)(2,1)S(1)} collective-permute-done((bf16[1024,128]{1,0:T(8,128)(2,1)S(1)}, bf16[1024,128]{1,0:T(8,128)(2,1)S(1)}, u32[]{:S(2)}, u32[]{:S(2)}) %collective-permute-start.1) | collective-permute-done | bytes 262176 | tf_op jit(solution)/shard_map/ppermute | solution.py:295
  13.4 7.9 %all-to-all-done.q_ref = bf16[32,40,128]{2,1,0:T(8,128)(2,1)S(1)} async-done(((bf16[32,40,128]{2,1,0:T(8,128)(2,1)}), bf16[32,40,128]{2,1,0:T(8,128)(2,1)S(1)}, u32[]{:S(2)}, u32[]{:S(2)}) %all-to-all-start) | async-done | bytes 327712 | tf_op jit(solution)/shard_map/all_to_all | solution.py:287
  21.3 3.4 %attend.1 = (bf16[32,40,128]{2,1,0:T(8,128)(2,1)}, bf16[32,8,128]{2,1,0:T(8,128)(2,1)S(1)}) custom-call(bf16[32,40,128]{2,1,0:T(8,128)(2,1)S(1)} %all-to-all-done.q_ref, bf16[1024,128]{1,0:T(8,128)(2,1)S(1)} %get-tuple-element.40.ka_ref, bf16[1024,128]{1,0:T(8,128)(2,1)S(1)} %get-tuple-element.38.va_ref, bf16[1024,128]{1,0:T(8,128)(2,1)S(1)} %collective-permute-done.kb_ref, ...), custom_call_target="tpu_custom_call" | custom-call | flops 1073741824 | bytes 4194304 | tf_op jit(solution)/shard_map/attend/pallas_call | solution.py:239
  24.8 2.6 %all-to-all-start.1 = ((bf16[32,40,128]{2,1,0:T(8,128)(2,1)}), bf16[32,40,128]{2,1,0:T(8,128)(2,1)S(1)}, u32[]{:S(2)}, u32[]{:S(2)}) async-start(bf16[32,40,128]{2,1,0:T(8,128)(2,1)} %get-tuple-element.27), calls=%async_computation.1 | async-start | bytes 655360 | tf_op jit(solution)/shard_map/all_to_all | solution.py:317
  27.4 1.7 %collective-permute-start.3 = (bf16[32,8,128]{2,1,0:T(8,128)(2,1)S(1)}, bf16[32,8,128]{2,1,0:T(8,128)(2,1)S(1)}, u32[]{:S(2)}, u32[]{:S(2)}) collective-permute-start(bf16[32,8,128]{2,1,0:T(8,128)(2,1)S(1)} %get-tuple-element.32.kv_ref), channel_id=1, source_target_pairs={{0,2},{1,3},{2,0},{3,1},{4,6},{5,7},{6,4},{7,5},{8,10},{9,11},{10,... | collective-permute-start | bytes 196616 | tf_op jit(solution)/shard_map/ppermute | solution.py:334
  29.1 0.0 collective-permute-start.2
  29.1 4.8 %collective-permute-done.3.kv2_ref = bf16[32,8,128]{2,1,0:T(8,128)(2,1)S(1)} collective-permute-done((bf16[32,8,128]{2,1,0:T(8,128)(2,1)S(1)}, bf16[32,8,128]{2,1,0:T(8,128)(2,1)S(1)}, u32[]{:S(2)}, u32[]{:S(2)}) %collective-permute-start.3) | collective-permute-done | bytes 65568 | tf_op jit(solution)/shard_map/ppermute | solution.py:334
  33.9 0.0 collective-permute-start.4
  33.9 0.0 copy-done
  33.9 0.0 copy-done.1
  33.9 1.8 %masks.1 = (f32[2,56,512]{2,1,0:T(8,128)S(1)}, f32[2,56,128]{2,1,0:T(8,128)S(1)}, bf16[768,1792]{1,0:T(8,128)(2,1)S(1)}) custom-call(s32[3,1,14]{2,1,0:T(1,128)S(1)} %bitcast.5, bf16[8,1792]{1,0:T(8,128)(2,1)S(1)} %copy-done, bf16[1792,1792]{1,0:T(8,128)(2,1)} %w_hbm.1), custom_call_target="tpu_custom_call" | custom-call | tf_op jit(solution)/shard_map/masks/pallas_call | solution.py:239
  35.7 0.0 collective-permute-done.2.kv1_ref
  35.7 0.0 collective-permute-done.4.kv3_ref
  35.8 0.4 %fresh.1 = (f32[2,56,128]{2,1,0:T(8,128)S(1)}, f32[2,56,128]{2,1,0:T(8,128)S(1)}) custom-call(f32[2,56,128]{2,1,0:T(8,128)S(1)} %get-tuple-element.31.rows_ref, bf16[32,8,128]{2,1,0:T(8,128)(2,1)S(1)} %get-tuple-element.32.kv_ref, bf16[32,8,128]{2,1,0:T(8,128)(2,1)S(1)} %collective-permute-done.2.kv1_ref, ...), custom_call_target="tpu_custom_call" | custom-call | flops 29360128 | bytes 1048576 | tf_op jit(solution)/shard_map/fresh/pallas_call | solution.py:239
  36.2 3.2 %all-to-all-done.1 = bf16[32,40,128]{2,1,0:T(8,128)(2,1)S(1)} async-done(((bf16[32,40,128]{2,1,0:T(8,128)(2,1)}), bf16[32,40,128]{2,1,0:T(8,128)(2,1)S(1)}, u32[]{:S(2)}, u32[]{:S(2)}) %all-to-all-start.1) | async-done | bytes 327712 | tf_op jit(solution)/shard_map/all_to_all | solution.py:317
  39.4 3.1 %project.1 = bf16[8,1792]{1,0:T(8,128)(2,1)} custom-call(bf16[16,2,40,128]{3,2,1,0:T(8,128)(2,1)S(1)} %bitcast.3, f32[2,56,128]{2,1,0:T(8,128)S(1)} %get-tuple-element.33.out_ref, f32[2,56,128]{2,1,0:T(8,128)S(1)} %get-tuple-element.34.lse_ref, f32[2,56,512]{2,1,0:T(8,128)S(1)} %get-tuple-element.35.match_ref, ...), custom_call_target="tpu_custom_call" | custom-call | flops 51380224 | bytes 6422528 | tf_op jit(solution)/shard_map/project/pallas_call | solution.py:239
Async XLA Ops:
  0.0 33.9 %copy-start = (bf16[8,1792]{1,0:T(8,128)(2,1)S(1)}, bf16[8,1792]{1,0:T(8,128)(2,1)}, u32[]{:S(2)}) copy-start(bf16[8,1792]{1,0:T(8,128)(2,1)} %q_ref) | copy-start | bytes 86020
  0.0 33.9 %copy-start.1 = (s32[1,14,3]{1,0,2:T(1,128)S(1)}, s32[1,14,3]{1,0,2:T(1,128)}, u32[]{:S(2)}) copy-start(s32[1,14,3]{1,0,2:T(1,128)} %param.12) | copy-start | bytes 508
  2.0 19.3 %all-to-all-start = ((bf16[32,40,128]{2,1,0:T(8,128)(2,1)}), bf16[32,40,128]{2,1,0:T(8,128)(2,1)S(1)}, u32[]{:S(2)}, u32[]{:S(2)}) async-start(bf16[32,40,128]{2,1,0:T(8,128)(2,1)} %bitcast.6), calls=%async_computation | async-start | bytes 655360 | tf_op jit(solution)/shard_map/all_to_all | solution.py:287
  10.4 1.7 %collective-permute-start = (bf16[1024,128]{1,0:T(8,128)(2,1)S(1)}, bf16[1024,128]{1,0:T(8,128)(2,1)S(1)}, u32[]{:S(2)}, u32[]{:S(2)}) collective-permute-start(bf16[1024,128]{1,0:T(8,128)(2,1)S(1)} %get-tuple-element.39), channel_id=1, source_target_pairs={{0,1},{1,0},{2,3},{3,2},{4,5},{5,4},{6,7},{7,6},{8,9},{9,8},{10,11... | collective-permute-start | bytes 786440 | tf_op jit(solution)/shard_map/ppermute | solution.py:295
  11.8 1.6 %collective-permute-start.1 = (bf16[1024,128]{1,0:T(8,128)(2,1)S(1)}, bf16[1024,128]{1,0:T(8,128)(2,1)S(1)}, u32[]{:S(2)}, u32[]{:S(2)}) collective-permute-start(bf16[1024,128]{1,0:T(8,128)(2,1)S(1)} %get-tuple-element.37), channel_id=1, source_target_pairs={{0,1},{1,0},{2,3},{3,2},{4,5},{5,4},{6,7},{7,6},{8,9},{9,8},{10,11... | collective-permute-start | bytes 786440 | tf_op jit(solution)/shard_map/ppermute | solution.py:295
  24.8 14.6 %all-to-all-start.1 = ((bf16[32,40,128]{2,1,0:T(8,128)(2,1)}), bf16[32,40,128]{2,1,0:T(8,128)(2,1)S(1)}, u32[]{:S(2)}, u32[]{:S(2)}) async-start(bf16[32,40,128]{2,1,0:T(8,128)(2,1)} %get-tuple-element.27), calls=%async_computation.1 | async-start | bytes 655360 | tf_op jit(solution)/shard_map/all_to_all | solution.py:317
  27.4 6.5 %collective-permute-start.3 = (bf16[32,8,128]{2,1,0:T(8,128)(2,1)S(1)}, bf16[32,8,128]{2,1,0:T(8,128)(2,1)S(1)}, u32[]{:S(2)}, u32[]{:S(2)}) collective-permute-start(bf16[32,8,128]{2,1,0:T(8,128)(2,1)S(1)} %get-tuple-element.32.kv_ref), channel_id=1, source_target_pairs={{0,2},{1,3},{2,0},{3,1},{4,6},{5,7},{6,4},{7,5},{8,10},{9,11},{10,... | collective-permute-start | bytes 196616 | tf_op jit(solution)/shard_map/ppermute | solution.py:334
  29.1 6.6 %collective-permute-start.2 = (bf16[32,8,128]{2,1,0:T(8,128)(2,1)S(1)}, bf16[32,8,128]{2,1,0:T(8,128)(2,1)S(1)}, u32[]{:S(2)}, u32[]{:S(2)}) collective-permute-start(bf16[32,8,128]{2,1,0:T(8,128)(2,1)S(1)} %get-tuple-element.32.kv_ref), channel_id=1, source_target_pairs={{0,1},{1,0},{2,3},{3,2},{4,5},{5,4},{6,7},{7,6},{8,9},{9,8},{10,11... | collective-permute-start | bytes 196616 | tf_op jit(solution)/shard_map/ppermute | solution.py:335
  33.9 1.8 %collective-permute-start.4 = (bf16[32,8,128]{2,1,0:T(8,128)(2,1)S(1)}, bf16[32,8,128]{2,1,0:T(8,128)(2,1)S(1)}, u32[]{:S(2)}, u32[]{:S(2)}) collective-permute-start(bf16[32,8,128]{2,1,0:T(8,128)(2,1)S(1)} %collective-permute-done.3.kv2_ref), channel_id=1, source_target_pairs={{0,1},{1,0},{2,3},{3,2},{4,5},{5,4},{6,7},{7,6},{8,9},{9,8},{10,11... | collective-permute-start | bytes 196616 | tf_op jit(solution)/shard_map/ppermute | solution.py:335

commit v11 on v10

--- a/solution.py
+++ b/solution.py
@@ -19,7 +19,8 @@
 LOG2E = math.log2(math.e)
 LANES = 128
 EARLY = 3
-STEP = 128
+PIECES = 4
+STEP = 256
 
 
 def head_rows(q_ref, g):
@@ -177,10 +178,11 @@
 def project_kernel(per, hist_ref, out_ref, lse_ref, match_ref, first_ref, w_hbm, y_ref, w_ref, sems):
     depth = KVH * HD
     ready = first_ref.shape[0] // depth
+    piece = depth // PIECES
     copies = fetch(
         [
-            (w_hbm.at[pl.ds((ready + i) * depth, depth)], w_ref.at[pl.ds(i * depth, depth)])
-            for i in range(w_ref.shape[0] // depth)
+            (w_hbm.at[pl.ds(first_ref.shape[0] + i * piece, piece)], w_ref.at[pl.ds(i * piece, piece)])
+            for i in range(w_ref.shape[0] // piece)
         ],
         sems,
     )
@@ -223,8 +225,9 @@
         heads = heads + [att[r * tokens : (r + 1) * tokens] for r in range(GROUP)]
         if g == 0:
             y = times(heads[: ready * KVH], first_ref[...])
-    for i, copy in enumerate(copies):
-        copy.wait()
+    for i in range(w_ref.shape[0] // depth):
+        for copy in copies[i * PIECES : (i + 1) * PIECES]:
+            copy.wait()
         y = y + times(heads[(ready + i) * KVH : (ready + i + 1) * KVH], w_ref[i * depth : (i + 1) * depth, :])
     y_ref[...] = y.astype(jnp.bfloat16)
 
@@ -351,7 +354,7 @@
         hist.reshape(holders, KVH, per + 8, HD), out, lse, match, first, out_weight,
         scratch=[
             pltpu.VMEM((out_weight.shape[0] - ready, out_weight.shape[1]), bf16),
-            pltpu.SemaphoreType.DMA((GROUP - EARLY,)),
+            pltpu.SemaphoreType.DMA(((GROUP - EARLY) * PIECES,)),
         ],
         flops=2 * tokens * out_weight.size,
         moved=out_weight.size * 2,

time: 42.9 us -> 43 us (level)
  no operation moved by 1% of the time
where the time goes in v11:
time: 43 us; the launch traced here: 42.6 us
  waiting for transfers between devices  17.2 us (40%)
  starting transfers between devices  12.3 us (29%)
  Pallas kernels  10.9 us (25%)
  local copies, waits for them, and re-layouts  2.14 us (5%)
    pallas_call x5, Pallas kernels, call(): pl.pallas_call(kernel, name=name, out_shape=out_shape, in_specs=specs, ou...  10.9 us
    all_to_all x1, waiting for transfers between devices, body(): got = lax.all_to_all(send, 'seq', split_axis=0, concat_axis=0, tiled=True)  7.91 us
    all_to_all x1, starting transfers between devices, body(): got = lax.all_to_all(send, 'seq', split_axis=0, concat_axis=0, tiled=True)  7.3 us
    ppermute x1, waiting for transfers between devices, body(): far = lax.ppermute(fresh, 'seq', partner(2))  4.83 us
    all_to_all x1, waiting for transfers between devices, body(): hist = lax.all_to_all(back, 'seq', split_axis=0, concat_axis=0, tiled=True)  3.18 us
    all_to_all x1, starting transfers between devices, body(): hist = lax.all_to_all(back, 'seq', split_axis=0, concat_axis=0, tiled=True)  2.61 us
    dynamic_slice x2, local copies, waits for them, and re-layouts, halves(): lax.dynamic_slice_in_dim(x, head * HD, HD, axis=1)  2.13 us
    ppermute x1, starting transfers between devices, body(): far = lax.ppermute(fresh, 'seq', partner(2))  1.7 us
  transfers between devices with their start and end apart: 7, of which 4 were waited for; matrix products, arithmetic and copies ran while one was open for 5% of the time, Pallas kernels for 5%

profile of v11, /device:TPU:0, one launch (start us, length us, event | category | flops | bytes accessed | tf_op | source)
XLA Modules:
  0.0 42.6 jit_solution(18230690732231482109)
XLA Ops:
  0.0 0.0 copy-start
  0.0 0.0 copy-start.1
  0.0 2.0 %pack.1 = bf16[8,2,2,40,128]{4,3,2,1,0:T(8,128)(2,1)} custom-call(s32[3,1,14]{2,1,0:T(1,128)} %bitcast.4, bf16[8,1792]{1,0:T(8,128)(2,1)} %q_ref, bf16[8,256]{1,0:T(8,128)(2,1)} %k_hbm.1, bf16[8,256]{1,0:T(8,128)(2,1)} %v_hbm.1), custom_call_target="tpu_custom_call" | custom-call | tf_op jit(solution)/shard_map/pack/pallas_call | solution.py:242
  2.0 7.3 %all-to-all-start = ((bf16[32,40,128]{2,1,0:T(8,128)(2,1)}), bf16[32,40,128]{2,1,0:T(8,128)(2,1)S(1)}, u32[]{:S(2)}, u32[]{:S(2)}) async-start(bf16[32,40,128]{2,1,0:T(8,128)(2,1)} %bitcast.6), calls=%async_computation | async-start | bytes 655360 | tf_op jit(solution)/shard_map/all_to_all | solution.py:290
  9.4 1.1 %constant_dynamic-slice_fusion.1 = (bf16[1024,128]{1,0:T(8,128)(2,1)S(1)}, bf16[1024,128]{1,0:T(8,128)(2,1)S(1)}) fusion(bf16[1024,256]{1,0:T(8,128)(2,1)} %param.10, s32[]{:T(128)S(6)} %select_n.17, s32[]{:T(128)S(6)} %select_n.16), kind=kLoop, calls=%fused_computation.1 | loop fusion | bytes 1048584 | tf_op jit(solution)/shard_map/dynamic_slice | solution.py:295
  10.4 0.3 collective-permute-start
  10.7 1.1 %constant_dynamic-slice_fusion = (bf16[1024,128]{1,0:T(8,128)(2,1)S(1)}, bf16[1024,128]{1,0:T(8,128)(2,1)S(1)}) fusion(bf16[1024,256]{1,0:T(8,128)(2,1)} %param.11, s32[]{:T(128)S(6)} %select_n.17, s32[]{:T(128)S(6)} %select_n.16), kind=kLoop, calls=%fused_computation | loop fusion | bytes 1048584 | tf_op jit(solution)/shard_map/dynamic_slice | solution.py:295
  11.8 0.3 collective-permute-start.1
  12.1 0.0 collective-permute-done.kb_ref
  12.1 1.3 %collective-permute-done.1.vb_ref = bf16[1024,128]{1,0:T(8,128)(2,1)S(1)} collective-permute-done((bf16[1024,128]{1,0:T(8,128)(2,1)S(1)}, bf16[1024,128]{1,0:T(8,128)(2,1)S(1)}, u32[]{:S(2)}, u32[]{:S(2)}) %collective-permute-start.1) | collective-permute-done | bytes 262176 | tf_op jit(solution)/shard_map/ppermute | solution.py:298
  13.4 7.9 %all-to-all-done.q_ref = bf16[32,40,128]{2,1,0:T(8,128)(2,1)S(1)} async-done(((bf16[32,40,128]{2,1,0:T(8,128)(2,1)}), bf16[32,40,128]{2,1,0:T(8,128)(2,1)S(1)}, u32[]{:S(2)}, u32[]{:S(2)}) %all-to-all-start) | async-done | bytes 327712 | tf_op jit(solution)/shard_map/all_to_all | solution.py:290
  21.3 3.3 %attend.1 = (bf16[32,40,128]{2,1,0:T(8,128)(2,1)}, bf16[32,8,128]{2,1,0:T(8,128)(2,1)S(1)}) custom-call(bf16[32,40,128]{2,1,0:T(8,128)(2,1)S(1)} %all-to-all-done.q_ref, bf16[1024,128]{1,0:T(8,128)(2,1)S(1)} %get-tuple-element.40.ka_ref, bf16[1024,128]{1,0:T(8,128)(2,1)S(1)} %get-tuple-element.38.va_ref, bf16[1024,128]{1,0:T(8,128)(2,1)S(1)} %collective-permute-done.kb_ref, ...), custom_call_target="tpu_custom_call" | custom-call | flops 1073741824 | bytes 4194304 | tf_op jit(solution)/shard_map/attend/pallas_call | solution.py:242
  24.7 2.6 %all-to-all-start.1 = ((bf16[32,40,128]{2,1,0:T(8,128)(2,1)}), bf16[32,40,128]{2,1,0:T(8,128)(2,1)S(1)}, u32[]{:S(2)}, u32[]{:S(2)}) async-start(bf16[32,40,128]{2,1,0:T(8,128)(2,1)} %get-tuple-element.27), calls=%async_computation.1 | async-start | bytes 655360 | tf_op jit(solution)/shard_map/all_to_all | solution.py:320
  27.3 1.7 %collective-permute-start.3 = (bf16[32,8,128]{2,1,0:T(8,128)(2,1)S(1)}, bf16[32,8,128]{2,1,0:T(8,128)(2,1)S(1)}, u32[]{:S(2)}, u32[]{:S(2)}) collective-permute-start(bf16[32,8,128]{2,1,0:T(8,128)(2,1)S(1)} %get-tuple-element.32.kv_ref), channel_id=1, source_target_pairs={{0,2},{1,3},{2,0},{3,1},{4,6},{5,7},{6,4},{7,5},{8,10},{9,11},{10,... | collective-permute-start | bytes 196616 | tf_op jit(solution)/shard_map/ppermute | solution.py:337
  29.0 0.0 collective-permute-start.2
  29.0 4.8 %collective-permute-done.3.kv2_ref = bf16[32,8,128]{2,1,0:T(8,128)(2,1)S(1)} collective-permute-done((bf16[32,8,128]{2,1,0:T(8,128)(2,1)S(1)}, bf16[32,8,128]{2,1,0:T(8,128)(2,1)S(1)}, u32[]{:S(2)}, u32[]{:S(2)}) %collective-permute-start.3) | collective-permute-done | bytes 65568 | tf_op jit(solution)/shard_map/ppermute | solution.py:337
  33.8 0.0 collective-permute-start.4
  33.8 0.0 copy-done
  33.8 0.0 copy-done.1
  33.8 1.8 %masks.1 = (f32[2,56,512]{2,1,0:T(8,128)S(1)}, f32[2,56,128]{2,1,0:T(8,128)S(1)}, bf16[768,1792]{1,0:T(8,128)(2,1)S(1)}) custom-call(s32[3,1,14]{2,1,0:T(1,128)S(1)} %bitcast.5, bf16[8,1792]{1,0:T(8,128)(2,1)S(1)} %copy-done, bf16[1792,1792]{1,0:T(8,128)(2,1)} %w_hbm.1), custom_call_target="tpu_custom_call" | custom-call | tf_op jit(solution)/shard_map/masks/pallas_call | solution.py:242
  35.6 0.0 collective-permute-done.2.kv1_ref
  35.6 0.0 collective-permute-done.4.kv3_ref
  35.6 0.4 %fresh.1 = (f32[2,56,128]{2,1,0:T(8,128)S(1)}, f32[2,56,128]{2,1,0:T(8,128)S(1)}) custom-call(f32[2,56,128]{2,1,0:T(8,128)S(1)} %get-tuple-element.31.rows_ref, bf16[32,8,128]{2,1,0:T(8,128)(2,1)S(1)} %get-tuple-element.32.kv_ref, bf16[32,8,128]{2,1,0:T(8,128)(2,1)S(1)} %collective-permute-done.2.kv1_ref, ...), custom_call_target="tpu_custom_call" | custom-call | flops 29360128 | bytes 1048576 | tf_op jit(solution)/shard_map/fresh/pallas_call | solution.py:242
  36.1 3.2 %all-to-all-done.1 = bf16[32,40,128]{2,1,0:T(8,128)(2,1)S(1)} async-done(((bf16[32,40,128]{2,1,0:T(8,128)(2,1)}), bf16[32,40,128]{2,1,0:T(8,128)(2,1)S(1)}, u32[]{:S(2)}, u32[]{:S(2)}) %all-to-all-start.1) | async-done | bytes 327712 | tf_op jit(solution)/shard_map/all_to_all | solution.py:320
  39.3 3.3 %project.1 = bf16[8,1792]{1,0:T(8,128)(2,1)} custom-call(bf16[16,2,40,128]{3,2,1,0:T(8,128)(2,1)S(1)} %bitcast.3, f32[2,56,128]{2,1,0:T(8,128)S(1)} %get-tuple-element.33.out_ref, f32[2,56,128]{2,1,0:T(8,128)S(1)} %get-tuple-element.34.lse_ref, f32[2,56,512]{2,1,0:T(8,128)S(1)} %get-tuple-element.35.match_ref, ...), custom_call_target="tpu_custom_call" | custom-call | flops 51380224 | bytes 6422528 | tf_op jit(solution)/shard_map/project/pallas_call | solution.py:242
Async XLA Ops:
  0.0 33.8 %copy-start = (bf16[8,1792]{1,0:T(8,128)(2,1)S(1)}, bf16[8,1792]{1,0:T(8,128)(2,1)}, u32[]{:S(2)}) copy-start(bf16[8,1792]{1,0:T(8,128)(2,1)} %q_ref) | copy-start | bytes 86020
  0.0 33.8 %copy-start.1 = (s32[1,14,3]{1,0,2:T(1,128)S(1)}, s32[1,14,3]{1,0,2:T(1,128)}, u32[]{:S(2)}) copy-start(s32[1,14,3]{1,0,2:T(1,128)} %param.12) | copy-start | bytes 508
  2.0 19.3 %all-to-all-start = ((bf16[32,40,128]{2,1,0:T(8,128)(2,1)}), bf16[32,40,128]{2,1,0:T(8,128)(2,1)S(1)}, u32[]{:S(2)}, u32[]{:S(2)}) async-start(bf16[32,40,128]{2,1,0:T(8,128)(2,1)} %bitcast.6), calls=%async_computation | async-start | bytes 655360 | tf_op jit(solution)/shard_map/all_to_all | solution.py:290
  10.4 1.7 %collective-permute-start = (bf16[1024,128]{1,0:T(8,128)(2,1)S(1)}, bf16[1024,128]{1,0:T(8,128)(2,1)S(1)}, u32[]{:S(2)}, u32[]{:S(2)}) collective-permute-start(bf16[1024,128]{1,0:T(8,128)(2,1)S(1)} %get-tuple-element.39), channel_id=1, source_target_pairs={{0,1},{1,0},{2,3},{3,2},{4,5},{5,4},{6,7},{7,6},{8,9},{9,8},{10,11... | collective-permute-start | bytes 786440 | tf_op jit(solution)/shard_map/ppermute | solution.py:298
  11.8 1.6 %collective-permute-start.1 = (bf16[1024,128]{1,0:T(8,128)(2,1)S(1)}, bf16[1024,128]{1,0:T(8,128)(2,1)S(1)}, u32[]{:S(2)}, u32[]{:S(2)}) collective-permute-start(bf16[1024,128]{1,0:T(8,128)(2,1)S(1)} %get-tuple-element.37), channel_id=1, source_target_pairs={{0,1},{1,0},{2,3},{3,2},{4,5},{5,4},{6,7},{7,6},{8,9},{9,8},{10,11... | collective-permute-start | bytes 786440 | tf_op jit(solution)/shard_map/ppermute | solution.py:298
  24.7 14.6 %all-to-all-start.1 = ((bf16[32,40,128]{2,1,0:T(8,128)(2,1)}), bf16[32,40,128]{2,1,0:T(8,128)(2,1)S(1)}, u32[]{:S(2)}, u32[]{:S(2)}) async-start(bf16[32,40,128]{2,1,0:T(8,128)(2,1)} %get-tuple-element.27), calls=%async_computation.1 | async-start | bytes 655360 | tf_op jit(solution)/shard_map/all_to_all | solution.py:320
  27.3 6.5 %collective-permute-start.3 = (bf16[32,8,128]{2,1,0:T(8,128)(2,1)S(1)}, bf16[32,8,128]{2,1,0:T(8,128)(2,1)S(1)}, u32[]{:S(2)}, u32[]{:S(2)}) collective-permute-start(bf16[32,8,128]{2,1,0:T(8,128)(2,1)S(1)} %get-tuple-element.32.kv_ref), channel_id=1, source_target_pairs={{0,2},{1,3},{2,0},{3,1},{4,6},{5,7},{6,4},{7,5},{8,10},{9,11},{10,... | collective-permute-start | bytes 196616 | tf_op jit(solution)/shard_map/ppermute | solution.py:337
  29.0 6.6 %collective-permute-start.2 = (bf16[32,8,128]{2,1,0:T(8,128)(2,1)S(1)}, bf16[32,8,128]{2,1,0:T(8,128)(2,1)S(1)}, u32[]{:S(2)}, u32[]{:S(2)}) collective-permute-start(bf16[32,8,128]{2,1,0:T(8,128)(2,1)S(1)} %get-tuple-element.32.kv_ref), channel_id=1, source_target_pairs={{0,1},{1,0},{2,3},{3,2},{4,5},{5,4},{6,7},{7,6},{8,9},{9,8},{10,11... | collective-permute-start | bytes 196616 | tf_op jit(solution)/shard_map/ppermute | solution.py:338
  33.8 1.8 %collective-permute-start.4 = (bf16[32,8,128]{2,1,0:T(8,128)(2,1)S(1)}, bf16[32,8,128]{2,1,0:T(8,128)(2,1)S(1)}, u32[]{:S(2)}, u32[]{:S(2)}) collective-permute-start(bf16[32,8,128]{2,1,0:T(8,128)(2,1)S(1)} %collective-permute-done.3.kv2_ref), channel_id=1, source_target_pairs={{0,1},{1,0},{2,3},{3,2},{4,5},{5,4},{6,7},{7,6},{8,9},{9,8},{10,11... | collective-permute-start | bytes 196616 | tf_op jit(solution)/shard_map/ppermute | solution.py:338

commit v12 on v10

--- a/solution.py
+++ b/solution.py
@@ -19,7 +19,7 @@
 LOG2E = math.log2(math.e)
 LANES = 128
 EARLY = 3
-STEP = 128
+STEP = 256
 
 
 def head_rows(q_ref, g):
@@ -96,21 +96,20 @@
 
 def attend_kernel(per, q_ref, ka_ref, va_ref, kb_ref, vb_ref, out_hbm, fresh_ref, out_ref, sems):
     sources = q_ref.shape[0]
-    sent = []
     step = STEP // per
+    fold = LANES // per
+    group = lax.axis_index("seq") // KVH % fold
     scale = LOG2E * HD**-0.5
     nt = (((1,), (1,)), ((), ()))
-    row = lax.broadcasted_iota(jnp.int32, (per, LANES), 0)
-    lane = lax.broadcasted_iota(jnp.int32, (per, LANES), 1)
-    diagonal = row == lane % per
     piece = lax.broadcasted_iota(jnp.int32, (8, LANES), 0)
-    ones = jnp.ones(va_ref.shape, jnp.bfloat16)
+    ones = jnp.ones((16, va_ref.shape[1]), jnp.bfloat16)
     fresh_ref[...] = q_ref[:, per:, :]
+    sent = []
 
     def scores(first):
-        q = q_ref[first : first + step, :per, :].reshape(step * per, HD)
+        q = q_ref[first : first + step, :per, :].reshape(STEP, HD)
         return [
-            lax.dot_general(q, k_ref[...], nt, preferred_element_type=jnp.float32) for k_ref in (ka_ref, kb_ref)
+            lax.dot_general(k_ref[...], q, nt, preferred_element_type=jnp.float32) for k_ref in (ka_ref, kb_ref)
         ]
 
     ahead = scores(0)
@@ -118,25 +117,28 @@
         sa, sb = ahead
         if first + step < sources:
             ahead = scores(first + step)
-        top = scale * jnp.maximum(jnp.max(sa, axis=1, keepdims=True), jnp.max(sb, axis=1, keepdims=True))
+        top = scale * jnp.maximum(jnp.max(sa, axis=0, keepdims=True), jnp.max(sb, axis=0, keepdims=True))
         wa = jnp.exp2(sa * scale - top).astype(jnp.bfloat16)
         wb = jnp.exp2(sb * scale - top).astype(jnp.bfloat16)
         both = jnp.dot(
-            wa, jnp.concatenate([va_ref[...], ones], axis=1), preferred_element_type=jnp.float32
-        ) + jnp.dot(wb, jnp.concatenate([vb_ref[...], ones], axis=1), preferred_element_type=jnp.float32)
-        total = both[:, HD:]
-        out = (both[:, :HD] / total).astype(jnp.bfloat16)
+            jnp.concatenate([va_ref[...], ones], axis=0), wa, preferred_element_type=jnp.float32
+        ) + jnp.dot(jnp.concatenate([vb_ref[...], ones], axis=0), wb, preferred_element_type=jnp.float32)
+        total = both[HD : HD + 1]
+        out = (both[:HD] / total).T.astype(jnp.bfloat16)
         lse = top + jnp.log(total) * LOG2E
+        hi = lse.astype(jnp.bfloat16).astype(jnp.float32)
+        mid = (lse - hi).astype(jnp.bfloat16).astype(jnp.float32)
+        low = lse - hi - mid
         for s in range(step):
-            part = slice(s * per, (s + 1) * per)
-            out_ref[first + s, :per, :] = out[part]
-            flat = jnp.sum(jnp.where(diagonal, lse[part], 0.0), axis=0, keepdims=True)
-            hi = flat.astype(jnp.bfloat16).astype(jnp.float32)
-            mid = (flat - hi).astype(jnp.bfloat16).astype(jnp.float32)
-            low = flat - hi - mid
-            out_ref[first + s, per:, :] = jnp.where(
-                piece == 0, hi, jnp.where(piece == 1, mid, jnp.where(piece == 2, low, 0.0))
-            ).astype(jnp.bfloat16)
+            out_ref[first + s, :per, :] = out[s * per : (s + 1) * per]
+        for t in range(step // fold):
+            lanes = slice(t * LANES, (t + 1) * LANES)
+            parts = jnp.where(
+                piece == 0, hi[:, lanes], jnp.where(piece == 1, mid[:, lanes], jnp.where(piece == 2, low[:, lanes], 0.0))
+            )
+            for i in range(fold):
+                turned = pltpu.roll(parts, lax.rem(group - i + fold, fold) * per, 1)
+                out_ref[first + t * fold + i, per:, :] = turned.astype(jnp.bfloat16)
         done = pl.ds(first, step)
         sent.append(pltpu.make_async_copy(out_ref.at[done], out_hbm.at[done], sems.at[first // step]))
         sent[-1].start()
@@ -289,7 +291,8 @@
     core = lax.axis_index("seq") % KVH
 
     def halves(head):
-        return [lax.dynamic_slice_in_dim(x, head * HD, HD, axis=1) for x in (cache_keys, cache_values)]
+        keys, values = [lax.dynamic_slice_in_dim(x, head * HD, HD, axis=1) for x in (cache_keys, cache_values)]
+        return keys, values.T
 
     k_own, v_own = halves(core)
     k_peer, v_peer = [lax.ppermute(x, "seq", partner(1)) for x in halves(1 - core)]

time: 42.9 us -> 43.3 us (level)
    optimization_barrier x0 -> x1, local copies, waits for them, and re-layouts: none -> 1.25 us  [body(): lax.optimization_barrier((send, cache_keys, cache_values, picks, queries))]
    dynamic_slice x2 -> x1, local copies, waits for them, and re-layouts: 2.13 us -> 1.06 us  [halves(): lax.dynamic_slice_in_dim(x, head * HD, HD, axis=1)]
  transfers between devices with their start and end apart: 7 -> 7, of which waited for: 4 -> 4; matrix products, arithmetic and copies ran while one was open for 5% -> 6% of each run, Pallas kernels for 5% -> 5%
where the time goes in v12:
time: 43.3 us; the launch traced here: 42.8 us
  waiting for transfers between devices  17 us (39%)
  starting transfers between devices  12.3 us (28%)
  Pallas kernels  11.1 us (26%)
  local copies, waits for them, and re-layouts  2.36 us (5%)
    pallas_call x5, Pallas kernels, call(): pl.pallas_call(kernel, name=name, out_shape=out_shape, in_specs=specs, ou...  11.1 us
    all_to_all x1, waiting for transfers between devices, body(): got = lax.all_to_all(send, 'seq', split_axis=0, concat_axis=0, tiled=True)  7.67 us
    all_to_all x1, starting transfers between devices, body(): got = lax.all_to_all(send, 'seq', split_axis=0, concat_axis=0, tiled=True)  7.3 us
    ppermute x1, waiting for transfers between devices, body(): far = lax.ppermute(fresh, 'seq', partner(2))  4.83 us
    all_to_all x1, waiting for transfers between devices, body(): hist = lax.all_to_all(back, 'seq', split_axis=0, concat_axis=0, tiled=True)  3.18 us
    all_to_all x1, starting transfers between devices, body(): hist = lax.all_to_all(back, 'seq', split_axis=0, concat_axis=0, tiled=True)  2.61 us
    ppermute x1, starting transfers between devices, body(): far = lax.ppermute(fresh, 'seq', partner(2))  1.7 us
    ppermute x2, waiting for transfers between devices, body(): lax.ppermute(x, 'seq', partner(1))  1.28 us
  transfers between devices with their start and end apart: 7, of which 4 were waited for; matrix products, arithmetic and copies ran while one was open for 6% of the time, Pallas kernels for 5%

profile of v12, /device:TPU:0, one launch (start us, length us, event | category | flops | bytes accessed | tf_op | source)
XLA Modules:
  0.0 42.8 jit_solution(3608825253230861825)
XLA Ops:
  0.0 0.0 copy-start
  0.0 0.0 copy-start.1
  0.0 2.0 %pack.1 = bf16[8,2,2,40,128]{4,3,2,1,0:T(8,128)(2,1)} custom-call(s32[3,1,14]{2,1,0:T(1,128)} %bitcast.8, bf16[8,1792]{1,0:T(8,128)(2,1)} %q_ref, bf16[8,256]{1,0:T(8,128)(2,1)} %k_hbm.1, bf16[8,256]{1,0:T(8,128)(2,1)} %v_hbm.1), custom_call_target="tpu_custom_call" | custom-call | tf_op jit(solution)/shard_map/pack/pallas_call | solution.py:241
  2.0 7.3 %all-to-all-start = ((bf16[32,40,128]{2,1,0:T(8,128)(2,1)}), bf16[32,40,128]{2,1,0:T(8,128)(2,1)S(1)}, u32[]{:S(2)}, u32[]{:S(2)}) async-start(bf16[32,40,128]{2,1,0:T(8,128)(2,1)} %bitcast.10), calls=%async_computation | async-start | bytes 655360 | tf_op jit(solution)/shard_map/all_to_all | solution.py:289
  9.3 1.2 %copy.8 = bf16[1024,256]{0,1:T(8,128)(2,1)S(1)} copy(bf16[1024,256]{1,0:T(8,128)(2,1)} %param.11) | data formatting | bytes 1048576 | tf_op jit(solution)/shard_map/optimization_barrier | solution.py:285
  10.7 0.3 collective-permute-start.1
  11.0 1.1 %constant_dynamic-slice_fusion = (bf16[1024,128]{1,0:T(8,128)(2,1)S(1)}, bf16[1024,128]{1,0:T(8,128)(2,1)S(1)}) fusion(bf16[1024,256]{1,0:T(8,128)(2,1)} %param.10, s32[]{:T(128)S(6)} %select_n.17, s32[]{:T(128)S(6)} %select_n.16), kind=kLoop, calls=%fused_computation.2 | loop fusion | bytes 1048584 | tf_op jit(solution)/shard_map/dynamic_slice | solution.py:294
  12.0 0.3 collective-permute-start
  12.4 0.0 collective-permute-done.1.vb_ref
  12.4 1.3 %collective-permute-done.kb_ref = bf16[1024,128]{1,0:T(8,128)(2,1)S(1)} collective-permute-done((bf16[1024,128]{1,0:T(8,128)(2,1)S(1)}, bf16[1024,128]{1,0:T(8,128)(2,1)S(1)}, u32[]{:S(2)}, u32[]{:S(2)}) %collective-permute-start) | collective-permute-done | bytes 262176 | tf_op jit(solution)/shard_map/ppermute | solution.py:298
  13.6 7.7 %all-to-all-done.q_ref = bf16[32,40,128]{2,1,0:T(8,128)(2,1)S(1)} async-done(((bf16[32,40,128]{2,1,0:T(8,128)(2,1)}), bf16[32,40,128]{2,1,0:T(8,128)(2,1)S(1)}, u32[]{:S(2)}, u32[]{:S(2)}) %all-to-all-start) | async-done | bytes 327712 | tf_op jit(solution)/shard_map/all_to_all | solution.py:289
  21.3 3.8 %attend.1 = (bf16[32,40,128]{2,1,0:T(8,128)(2,1)}, bf16[32,8,128]{2,1,0:T(8,128)(2,1)S(1)}) custom-call(bf16[32,40,128]{2,1,0:T(8,128)(2,1)S(1)} %all-to-all-done.q_ref, bf16[1024,128]{1,0:T(8,128)(2,1)S(1)} %get-tuple-element.40.ka_ref, bf16[128,1024]{1,0:T(8,128)(2,1)S(1)} %get-tuple-element.38.va_ref, bf16[1024,128]{1,0:T(8,128)(2,1)S(1)} %collective-permute-done.kb_ref, ...), custom_call_target="tpu_custom_call" | custom-call | flops 1073741824 | bytes 4194304 | tf_op jit(solution)/shard_map/attend/pallas_call | solution.py:241
  25.1 2.6 %all-to-all-start.1 = ((bf16[32,40,128]{2,1,0:T(8,128)(2,1)}), bf16[32,40,128]{2,1,0:T(8,128)(2,1)S(1)}, u32[]{:S(2)}, u32[]{:S(2)}) async-start(bf16[32,40,128]{2,1,0:T(8,128)(2,1)} %get-tuple-element.27), calls=%async_computation.1 | async-start | bytes 655360 | tf_op jit(solution)/shard_map/all_to_all | solution.py:320
  27.7 1.7 %collective-permute-start.3 = (bf16[32,8,128]{2,1,0:T(8,128)(2,1)S(1)}, bf16[32,8,128]{2,1,0:T(8,128)(2,1)S(1)}, u32[]{:S(2)}, u32[]{:S(2)}) collective-permute-start(bf16[32,8,128]{2,1,0:T(8,128)(2,1)S(1)} %get-tuple-element.32.kv_ref), channel_id=1, source_target_pairs={{0,2},{1,3},{2,0},{3,1},{4,6},{5,7},{6,4},{7,5},{8,10},{9,11},{10,... | collective-permute-start | bytes 196616 | tf_op jit(solution)/shard_map/ppermute | solution.py:337
  29.4 0.0 collective-permute-start.2
  29.4 4.8 %collective-permute-done.3.kv2_ref = bf16[32,8,128]{2,1,0:T(8,128)(2,1)S(1)} collective-permute-done((bf16[32,8,128]{2,1,0:T(8,128)(2,1)S(1)}, bf16[32,8,128]{2,1,0:T(8,128)(2,1)S(1)}, u32[]{:S(2)}, u32[]{:S(2)}) %collective-permute-start.3) | collective-permute-done | bytes 65568 | tf_op jit(solution)/shard_map/ppermute | solution.py:337
  34.3 0.0 collective-permute-start.4
  34.3 0.0 copy-done
  34.3 0.0 copy-done.1
  34.3 1.8 %masks.1 = (f32[2,56,512]{2,1,0:T(8,128)S(1)}, f32[2,56,128]{2,1,0:T(8,128)S(1)}, bf16[768,1792]{1,0:T(8,128)(2,1)S(1)}) custom-call(s32[3,1,14]{2,1,0:T(1,128)S(1)} %bitcast.9, bf16[8,1792]{1,0:T(8,128)(2,1)S(1)} %copy-done, bf16[1792,1792]{1,0:T(8,128)(2,1)} %w_hbm.1), custom_call_target="tpu_custom_call" | custom-call | tf_op jit(solution)/shard_map/masks/pallas_call | solution.py:241
  36.1 0.0 collective-permute-done.2.kv1_ref
  36.1 0.0 collective-permute-done.4.kv3_ref
  36.1 0.4 %fresh.1 = (f32[2,56,128]{2,1,0:T(8,128)S(1)}, f32[2,56,128]{2,1,0:T(8,128)S(1)}) custom-call(f32[2,56,128]{2,1,0:T(8,128)S(1)} %get-tuple-element.31.rows_ref, bf16[32,8,128]{2,1,0:T(8,128)(2,1)S(1)} %get-tuple-element.32.kv_ref, bf16[32,8,128]{2,1,0:T(8,128)(2,1)S(1)} %collective-permute-done.2.kv1_ref, ...), custom_call_target="tpu_custom_call" | custom-call | flops 29360128 | bytes 1048576 | tf_op jit(solution)/shard_map/fresh/pallas_call | solution.py:241
  36.5 3.2 %all-to-all-done.1 = bf16[32,40,128]{2,1,0:T(8,128)(2,1)S(1)} async-done(((bf16[32,40,128]{2,1,0:T(8,128)(2,1)}), bf16[32,40,128]{2,1,0:T(8,128)(2,1)S(1)}, u32[]{:S(2)}, u32[]{:S(2)}) %all-to-all-start.1) | async-done | bytes 327712 | tf_op jit(solution)/shard_map/all_to_all | solution.py:320
  39.7 3.1 %project.1 = bf16[8,1792]{1,0:T(8,128)(2,1)} custom-call(bf16[16,2,40,128]{3,2,1,0:T(8,128)(2,1)S(1)} %bitcast.7, f32[2,56,128]{2,1,0:T(8,128)S(1)} %get-tuple-element.33.out_ref, f32[2,56,128]{2,1,0:T(8,128)S(1)} %get-tuple-element.34.lse_ref, f32[2,56,512]{2,1,0:T(8,128)S(1)} %get-tuple-element.35.match_ref, ...), custom_call_target="tpu_custom_call" | custom-call | flops 51380224 | bytes 6422528 | tf_op jit(solution)/shard_map/project/pallas_call | solution.py:241
  (1 shorter events, 0.0 us)
Async XLA Ops:
  0.0 34.3 %copy-start = (bf16[8,1792]{1,0:T(8,128)(2,1)S(1)}, bf16[8,1792]{1,0:T(8,128)(2,1)}, u32[]{:S(2)}) copy-start(bf16[8,1792]{1,0:T(8,128)(2,1)} %q_ref) | copy-start | bytes 86020
  0.0 34.3 %copy-start.1 = (s32[1,14,3]{1,0,2:T(1,128)S(1)}, s32[1,14,3]{1,0,2:T(1,128)}, u32[]{:S(2)}) copy-start(s32[1,14,3]{1,0,2:T(1,128)} %param.12) | copy-start | bytes 508
  2.0 19.3 %all-to-all-start = ((bf16[32,40,128]{2,1,0:T(8,128)(2,1)}), bf16[32,40,128]{2,1,0:T(8,128)(2,1)S(1)}, u32[]{:S(2)}, u32[]{:S(2)}) async-start(bf16[32,40,128]{2,1,0:T(8,128)(2,1)} %bitcast.10), calls=%async_computation | async-start | bytes 655360 | tf_op jit(solution)/shard_map/all_to_all | solution.py:289
  10.7 1.7 %collective-permute-start.1 = (bf16[128,1024]{1,0:T(8,128)(2,1)S(1)}, bf16[128,1024]{1,0:T(8,128)(2,1)S(1)}, u32[]{:S(2)}, u32[]{:S(2)}) collective-permute-start(bf16[128,1024]{1,0:T(8,128)(2,1)S(1)} %get-tuple-element.37), channel_id=1, source_target_pairs={{0,1},{1,0},{2,3},{3,2},{4,5},{5,4},{6,7},{7,6},{8,9},{9,8},{10,11... | collective-permute-start | bytes 786440 | tf_op jit(solution)/shard_map/ppermute | solution.py:298
  12.0 1.6 %collective-permute-start = (bf16[1024,128]{1,0:T(8,128)(2,1)S(1)}, bf16[1024,128]{1,0:T(8,128)(2,1)S(1)}, u32[]{:S(2)}, u32[]{:S(2)}) collective-permute-start(bf16[1024,128]{1,0:T(8,128)(2,1)S(1)} %get-tuple-element.39), channel_id=1, source_target_pairs={{0,1},{1,0},{2,3},{3,2},{4,5},{5,4},{6,7},{7,6},{8,9},{9,8},{10,11... | collective-permute-start | bytes 786440 | tf_op jit(solution)/shard_map/ppermute | solution.py:298
  25.1 14.6 %all-to-all-start.1 = ((bf16[32,40,128]{2,1,0:T(8,128)(2,1)}), bf16[32,40,128]{2,1,0:T(8,128)(2,1)S(1)}, u32[]{:S(2)}, u32[]{:S(2)}) async-start(bf16[32,40,128]{2,1,0:T(8,128)(2,1)} %get-tuple-element.27), calls=%async_computation.1 | async-start | bytes 655360 | tf_op jit(solution)/shard_map/all_to_all | solution.py:320
  27.7 6.5 %collective-permute-start.3 = (bf16[32,8,128]{2,1,0:T(8,128)(2,1)S(1)}, bf16[32,8,128]{2,1,0:T(8,128)(2,1)S(1)}, u32[]{:S(2)}, u32[]{:S(2)}) collective-permute-start(bf16[32,8,128]{2,1,0:T(8,128)(2,1)S(1)} %get-tuple-element.32.kv_ref), channel_id=1, source_target_pairs={{0,2},{1,3},{2,0},{3,1},{4,6},{5,7},{6,4},{7,5},{8,10},{9,11},{10,... | collective-permute-start | bytes 196616 | tf_op jit(solution)/shard_map/ppermute | solution.py:337
  29.4 6.6 %collective-permute-start.2 = (bf16[32,8,128]{2,1,0:T(8,128)(2,1)S(1)}, bf16[32,8,128]{2,1,0:T(8,128)(2,1)S(1)}, u32[]{:S(2)}, u32[]{:S(2)}) collective-permute-start(bf16[32,8,128]{2,1,0:T(8,128)(2,1)S(1)} %get-tuple-element.32.kv_ref), channel_id=1, source_target_pairs={{0,1},{1,0},{2,3},{3,2},{4,5},{5,4},{6,7},{7,6},{8,9},{9,8},{10,11... | collective-permute-start | bytes 196616 | tf_op jit(solution)/shard_map/ppermute | solution.py:338
  34.3 1.8 %collective-permute-start.4 = (bf16[32,8,128]{2,1,0:T(8,128)(2,1)S(1)}, bf16[32,8,128]{2,1,0:T(8,128)(2,1)S(1)}, u32[]{:S(2)}, u32[]{:S(2)}) collective-permute-start(bf16[32,8,128]{2,1,0:T(8,128)(2,1)S(1)} %collective-permute-done.3.kv2_ref), channel_id=1, source_target_pairs={{0,1},{1,0},{2,3},{3,2},{4,5},{5,4},{6,7},{7,6},{8,9},{9,8},{10,11... | collective-permute-start | bytes 196616 | tf_op jit(solution)/shard_map/ppermute | solution.py:338

commit v13 on v10

--- a/solution.py
+++ b/solution.py
@@ -19,7 +19,12 @@
 LOG2E = math.log2(math.e)
 LANES = 128
 EARLY = 3
-STEP = 128
+STEP = 256
+
+
+def mirrored(index, count):
+    bits = count.bit_length() - 1
+    return sum(((index >> i) & 1) << (bits - 1 - i) for i in range(bits))
 
 
 def head_rows(q_ref, g):
@@ -48,11 +53,13 @@
     return copies
 
 
-def pack_kernel(capacity, chosen_hbm, q_hbm, k_hbm, v_hbm, send_hbm, chosen_ref, q_ref, k_ref, v_ref, send_ref, sems):
+def pack_kernel(chips, capacity, chosen_hbm, q_hbm, k_hbm, v_hbm, send_hbm, chosen_ref, q_ref, k_ref, v_ref, send_ref, sems):
     copies = fetch([(chosen_hbm, chosen_ref), (q_hbm, q_ref), (k_hbm, k_ref), (v_hbm, v_ref)], sems)
     tokens = q_ref.shape[0]
     per = capacity * tokens
-    key_blocks, chips = send_ref.shape[1:3]
+    devices = send_ref.shape[0]
+    key_blocks = devices // (chips * KVH)
+    half = devices // KVH
     lane = lax.broadcasted_iota(jnp.int32, (tokens, key_blocks * per), 1)
     block, slot, token = lane // per, lane % per // tokens, lane % tokens
     copies[0].wait()
@@ -73,9 +80,11 @@
         fresh = [k_ref[:, cols], v_ref[:, cols]]
         for b in range(key_blocks):
             for chip in range(chips):
-                send_ref[g, b, chip, :per, :] = slots[b * per : (b + 1) * per]
-                send_ref[g, b, chip, per:, :] = fresh[chip % 2]
-        sent.append(pltpu.make_async_copy(send_ref.at[g], send_hbm.at[:, :, g], sems.at[4 + g]))
+                to = mirrored((b * chips + chip) * KVH + g, devices)
+                send_ref[to, :per, :] = slots[b * per : (b + 1) * per]
+                send_ref[to, per:, :] = fresh[chip % 2]
+        done = pl.ds(g * half, half)
+        sent.append(pltpu.make_async_copy(send_ref.at[done], send_hbm.at[done], sems.at[4 + g]))
         sent[g].start()
     for copy in sent:
         copy.wait()
@@ -86,7 +95,8 @@
     tokens = q_ref.shape[0]
     per = capacity * tokens
     lane = lax.broadcasted_iota(jnp.int32, (tokens, match_ref.shape[2]), 1)
-    block, slot, token = lane // (per * chips), lane % per // tokens, lane % tokens
+    holder = mirrored(lane // per, match_ref.shape[2] // per)
+    block, slot, token = holder // chips, lane % per // tokens, lane % tokens
     for g in range(KVH):
         match_ref[g] = jnp.concatenate(slot_match(chosen_ref, g, block, slot, token), axis=0)
         rows_ref[g] = jnp.concatenate(head_rows(q_ref, g), axis=0)
@@ -152,7 +162,8 @@
     nt = (((1,), (1,)), ((), ()))
     column = lax.broadcasted_iota(jnp.int32, (tokens, sources * tokens), 1)
     query_pos = place * tokens + lax.broadcasted_iota(jnp.int32, column.shape, 0)
-    visible = (column <= query_pos) & (column // BLK == query_pos // BLK)
+    key_pos = mirrored(column // tokens, sources) * tokens + column % tokens
+    visible = (key_pos <= query_pos) & (key_pos // BLK == query_pos // BLK)
     visible = jnp.concatenate([visible.astype(jnp.int32)] * GROUP, axis=0) > 0
     ones = jnp.ones((sources * tokens, HD), jnp.bfloat16)
     here, near, far, both = [
@@ -185,7 +196,7 @@
         sems,
     )
     tokens = y_ref.shape[0]
-    holders = hist_ref.shape[0]
+    holders = hist_ref.shape[1]
     fold = LANES // per
     row = lax.broadcasted_iota(jnp.int32, (holders, LANES), 0)
     lane = lax.broadcasted_iota(jnp.int32, (holders, LANES), 1)
@@ -196,8 +207,8 @@
 
     heads = []
     for g in range(KVH):
-        outs = hist_ref[:, g, :per, :].reshape(holders * per, HD)
-        stats = jnp.sum(hist_ref[:, g, per:, :].astype(jnp.float32), axis=1)
+        outs = hist_ref[g, :, :per, :].reshape(holders * per, HD)
+        stats = jnp.sum(hist_ref[g, :, per:, :].astype(jnp.float32), axis=1)
         stats = jnp.where(row % fold == lane // per, stats, 0.0)
         lse = jnp.concatenate(
             [
@@ -264,9 +275,9 @@
         return [(i, i ^ bit) for i in range(devices)]
 
     send = call(
-        functools.partial(pack_kernel, capacity),
+        functools.partial(pack_kernel, chips, capacity),
         "pack",
-        jax.ShapeDtypeStruct((key_blocks, chips, KVH, per + tokens, HD), bf16),
+        jax.ShapeDtypeStruct((devices, per + tokens, HD), bf16),
         [HBM] * 4,
         picks, queries, stretch_keys, stretch_values,
         outs=ANY,
@@ -275,7 +286,7 @@
             pltpu.VMEM(queries.shape, bf16),
             pltpu.VMEM(stretch_keys.shape, bf16),
             pltpu.VMEM(stretch_values.shape, bf16),
-            pltpu.VMEM((KVH, key_blocks, chips, per + tokens, HD), bf16),
+            pltpu.VMEM((devices, per + tokens, HD), bf16),
             pltpu.SemaphoreType.DMA((4 + KVH,)),
         ],
         limit=60,
@@ -283,8 +294,12 @@
     send, cache_keys, cache_values, picks, queries = lax.optimization_barrier(
         (send, cache_keys, cache_values, picks, queries)
     )
-    send = send.reshape(devices, per + tokens, HD)
-    got = lax.all_to_all(send, "seq", split_axis=0, concat_axis=0, tiled=True)
+
+    def exchange(x):
+        ranks = [mirrored(i, devices) for i in range(devices)]
+        return lax.all_to_all(x, "seq", split_axis=0, concat_axis=0, axis_index_groups=[ranks], tiled=True)
+
+    got = exchange(send)
 
     core = lax.axis_index("seq") % KVH
 
@@ -314,7 +329,7 @@
         limit=32,
     )
     back, picks, queries, out_weight = lax.optimization_barrier((back, picks, queries, out_weight))
-    hist = lax.all_to_all(back, "seq", split_axis=0, concat_axis=0, tiled=True)
+    hist = exchange(back)
 
     ready = EARLY * KVH * HD
     match, query_rows, first = call(
@@ -348,7 +363,7 @@
         "project",
         jax.ShapeDtypeStruct((tokens, out_weight.shape[1]), bf16),
         [VMEM] * 5 + [HBM],
-        hist.reshape(holders, KVH, per + 8, HD), out, lse, match, first, out_weight,
+        hist.reshape(KVH, holders, per + 8, HD), out, lse, match, first, out_weight,
         scratch=[
             pltpu.VMEM((out_weight.shape[0] - ready, out_weight.shape[1]), bf16),
             pltpu.SemaphoreType.DMA((GROUP - EARLY,)),

time: 42.9 us -> 43.1 us (level)
    all_to_all x2, waiting for transfers between devices: 11.1 us -> 11.7 us  [exchange(): lax.all_to_all(x, 'seq', split_axis=0, concat_axis=0, axis_index_groups=[...]
where the time goes in v13:
time: 43.1 us; the launch traced here: 42.7 us
  waiting for transfers between devices  17.5 us (41%)
  starting transfers between devices  12.3 us (29%)
  Pallas kernels  10.7 us (25%)
  local copies, waits for them, and re-layouts  2.14 us (5%)
    all_to_all x2, waiting for transfers between devices, exchange(): lax.all_to_all(x, 'seq', split_axis=0, concat_axis=0, axis_index_groups=[...  11.7 us
    pallas_call x5, Pallas kernels, call(): pl.pallas_call(kernel, name=name, out_shape=out_shape, in_specs=specs, ou...  10.7 us
    all_to_all x2, starting transfers between devices, exchange(): lax.all_to_all(x, 'seq', split_axis=0, concat_axis=0, axis_index_groups=[...  9.91 us
    ppermute x1, waiting for transfers between devices, body(): far = lax.ppermute(fresh, 'seq', partner(2))  4.5 us
    dynamic_slice x2, local copies, waits for them, and re-layouts, halves(): lax.dynamic_slice_in_dim(x, head * HD, HD, axis=1)  2.13 us
    ppermute x1, starting transfers between devices, body(): far = lax.ppermute(fresh, 'seq', partner(2))  1.7 us
    ppermute x2, waiting for transfers between devices, body(): lax.ppermute(x, 'seq', partner(1))  1.28 us
  transfers between devices with their start and end apart: 7, of which 4 were waited for; matrix products, arithmetic and copies ran while one was open for 5% of the time, Pallas kernels for 5%

profile of v13, /device:TPU:0, one launch (start us, length us, event | category | flops | bytes accessed | tf_op | source)
XLA Modules:
  0.0 42.7 jit_solution(10639976246377054916)
XLA Ops:
  0.0 0.0 copy-start
  0.0 0.0 copy-start.1
  0.0 2.0 %pack.1 = bf16[32,40,128]{2,1,0:T(8,128)(2,1)} custom-call(s32[3,1,14]{2,1,0:T(1,128)} %bitcast.3, bf16[8,1792]{1,0:T(8,128)(2,1)} %q_ref, bf16[8,256]{1,0:T(8,128)(2,1)} %k_hbm.1, bf16[8,256]{1,0:T(8,128)(2,1)} %v_hbm.1), custom_call_target="tpu_custom_call" | custom-call | tf_op jit(solution)/shard_map/pack/pallas_call | solution.py:250
  2.0 7.3 %all-to-all-start = ((bf16[32,40,128]{2,1,0:T(8,128)(2,1)}), bf16[32,40,128]{2,1,0:T(8,128)(2,1)S(1)}, u32[]{:S(2)}, u32[]{:S(2)}) async-start(bf16[32,40,128]{2,1,0:T(8,128)(2,1)} %pack.1), calls=%async_computation | async-start | bytes 655360 | tf_op jit(solution)/shard_map/all_to_all | solution.py:300
  9.3 1.1 %constant_dynamic-slice_fusion.1 = (bf16[1024,128]{1,0:T(8,128)(2,1)S(1)}, bf16[1024,128]{1,0:T(8,128)(2,1)S(1)}) fusion(bf16[1024,256]{1,0:T(8,128)(2,1)} %param.10, s32[]{:T(128)S(6)} %select_n.17, s32[]{:T(128)S(6)} %select_n.16), kind=kLoop, calls=%fused_computation.1 | loop fusion | bytes 1048584 | tf_op jit(solution)/shard_map/dynamic_slice | solution.py:307
  10.4 0.3 collective-permute-start
  10.7 1.1 %constant_dynamic-slice_fusion = (bf16[1024,128]{1,0:T(8,128)(2,1)S(1)}, bf16[1024,128]{1,0:T(8,128)(2,1)S(1)}) fusion(bf16[1024,256]{1,0:T(8,128)(2,1)} %param.11, s32[]{:T(128)S(6)} %select_n.17, s32[]{:T(128)S(6)} %select_n.16), kind=kLoop, calls=%fused_computation | loop fusion | bytes 1048584 | tf_op jit(solution)/shard_map/dynamic_slice | solution.py:307
  11.8 0.3 collective-permute-start.1
  12.1 0.0 collective-permute-done.kb_ref
  12.1 1.3 %collective-permute-done.1.vb_ref = bf16[1024,128]{1,0:T(8,128)(2,1)S(1)} collective-permute-done((bf16[1024,128]{1,0:T(8,128)(2,1)S(1)}, bf16[1024,128]{1,0:T(8,128)(2,1)S(1)}, u32[]{:S(2)}, u32[]{:S(2)}) %collective-permute-start.1) | collective-permute-done | bytes 262176 | tf_op jit(solution)/shard_map/ppermute | solution.py:310
  13.4 8.1 %all-to-all-done.q_ref = bf16[32,40,128]{2,1,0:T(8,128)(2,1)S(1)} async-done(((bf16[32,40,128]{2,1,0:T(8,128)(2,1)}), bf16[32,40,128]{2,1,0:T(8,128)(2,1)S(1)}, u32[]{:S(2)}, u32[]{:S(2)}) %all-to-all-start) | async-done | bytes 327712 | tf_op jit(solution)/shard_map/all_to_all | solution.py:300
  21.5 3.3 %attend.1 = (bf16[32,40,128]{2,1,0:T(8,128)(2,1)}, bf16[32,8,128]{2,1,0:T(8,128)(2,1)S(1)}) custom-call(bf16[32,40,128]{2,1,0:T(8,128)(2,1)S(1)} %all-to-all-done.q_ref, bf16[1024,128]{1,0:T(8,128)(2,1)S(1)} %get-tuple-element.40.ka_ref, bf16[1024,128]{1,0:T(8,128)(2,1)S(1)} %get-tuple-element.38.va_ref, bf16[1024,128]{1,0:T(8,128)(2,1)S(1)} %collective-permute-done.kb_ref, ...), custom_call_target="tpu_custom_call" | custom-call | flops 1073741824 | bytes 4194304 | tf_op jit(solution)/shard_map/attend/pallas_call | solution.py:250
  24.8 2.6 %all-to-all-start.1 = ((bf16[32,40,128]{2,1,0:T(8,128)(2,1)}), bf16[32,40,128]{2,1,0:T(8,128)(2,1)S(1)}, u32[]{:S(2)}, u32[]{:S(2)}) async-start(bf16[32,40,128]{2,1,0:T(8,128)(2,1)} %get-tuple-element.27), calls=%async_computation.1 | async-start | bytes 655360 | tf_op jit(solution)/shard_map/all_to_all | solution.py:300
  27.4 1.7 %collective-permute-start.3 = (bf16[32,8,128]{2,1,0:T(8,128)(2,1)S(1)}, bf16[32,8,128]{2,1,0:T(8,128)(2,1)S(1)}, u32[]{:S(2)}, u32[]{:S(2)}) collective-permute-start(bf16[32,8,128]{2,1,0:T(8,128)(2,1)S(1)} %get-tuple-element.32.kv_ref), channel_id=1, source_target_pairs={{0,2},{1,3},{2,0},{3,1},{4,6},{5,7},{6,4},{7,5},{8,10},{9,11},{10,... | collective-permute-start | bytes 196616 | tf_op jit(solution)/shard_map/ppermute | solution.py:349
  29.1 0.0 collective-permute-start.2
  29.1 4.5 %collective-permute-done.3.kv2_ref = bf16[32,8,128]{2,1,0:T(8,128)(2,1)S(1)} collective-permute-done((bf16[32,8,128]{2,1,0:T(8,128)(2,1)S(1)}, bf16[32,8,128]{2,1,0:T(8,128)(2,1)S(1)}, u32[]{:S(2)}, u32[]{:S(2)}) %collective-permute-start.3) | collective-permute-done | bytes 65568 | tf_op jit(solution)/shard_map/ppermute | solution.py:349
  33.6 0.0 collective-permute-start.4
  33.6 0.0 copy-done
  33.6 0.0 copy-done.1
  33.6 1.8 %masks.1 = (f32[2,56,512]{2,1,0:T(8,128)S(1)}, f32[2,56,128]{2,1,0:T(8,128)S(1)}, bf16[768,1792]{1,0:T(8,128)(2,1)S(1)}) custom-call(s32[3,1,14]{2,1,0:T(1,128)S(1)} %bitcast.4, bf16[8,1792]{1,0:T(8,128)(2,1)S(1)} %copy-done, bf16[1792,1792]{1,0:T(8,128)(2,1)} %w_hbm.1), custom_call_target="tpu_custom_call" | custom-call | tf_op jit(solution)/shard_map/masks/pallas_call | solution.py:250
  35.4 0.0 collective-permute-done.2.kv1_ref
  35.4 0.0 collective-permute-done.4.kv3_ref
  35.5 0.4 %fresh.1 = (f32[2,56,128]{2,1,0:T(8,128)S(1)}, f32[2,56,128]{2,1,0:T(8,128)S(1)}) custom-call(f32[2,56,128]{2,1,0:T(8,128)S(1)} %get-tuple-element.31.rows_ref, bf16[32,8,128]{2,1,0:T(8,128)(2,1)S(1)} %get-tuple-element.32.kv_ref, bf16[32,8,128]{2,1,0:T(8,128)(2,1)S(1)} %collective-permute-done.2.kv1_ref, ...), custom_call_target="tpu_custom_call" | custom-call | flops 29360128 | bytes 1048576 | tf_op jit(solution)/shard_map/fresh/pallas_call | solution.py:250
  35.9 3.7 %all-to-all-done.1 = bf16[32,40,128]{2,1,0:T(8,128)(2,1)S(1)} async-done(((bf16[32,40,128]{2,1,0:T(8,128)(2,1)}), bf16[32,40,128]{2,1,0:T(8,128)(2,1)S(1)}, u32[]{:S(2)}, u32[]{:S(2)}) %all-to-all-start.1) | async-done | bytes 327712 | tf_op jit(solution)/shard_map/all_to_all | solution.py:300
  39.6 3.1 %project.1 = bf16[8,1792]{1,0:T(8,128)(2,1)} custom-call(bf16[2,16,40,128]{3,2,1,0:T(8,128)(2,1)S(1)} %bitcast.2, f32[2,56,128]{2,1,0:T(8,128)S(1)} %get-tuple-element.33.out_ref, f32[2,56,128]{2,1,0:T(8,128)S(1)} %get-tuple-element.34.lse_ref, f32[2,56,512]{2,1,0:T(8,128)S(1)} %get-tuple-element.35.match_ref, ...), custom_call_target="tpu_custom_call" | custom-call | flops 51380224 | bytes 6422528 | tf_op jit(solution)/shard_map/project/pallas_call | solution.py:250
Async XLA Ops:
  0.0 33.6 %copy-start = (bf16[8,1792]{1,0:T(8,128)(2,1)S(1)}, bf16[8,1792]{1,0:T(8,128)(2,1)}, u32[]{:S(2)}) copy-start(bf16[8,1792]{1,0:T(8,128)(2,1)} %q_ref) | copy-start | bytes 86020
  0.0 33.6 %copy-start.1 = (s32[1,14,3]{1,0,2:T(1,128)S(1)}, s32[1,14,3]{1,0,2:T(1,128)}, u32[]{:S(2)}) copy-start(s32[1,14,3]{1,0,2:T(1,128)} %param.12) | copy-start | bytes 508
  2.0 19.4 %all-to-all-start = ((bf16[32,40,128]{2,1,0:T(8,128)(2,1)}), bf16[32,40,128]{2,1,0:T(8,128)(2,1)S(1)}, u32[]{:S(2)}, u32[]{:S(2)}) async-start(bf16[32,40,128]{2,1,0:T(8,128)(2,1)} %pack.1), calls=%async_computation | async-start | bytes 655360 | tf_op jit(solution)/shard_map/all_to_all | solution.py:300
  10.4 1.7 %collective-permute-start = (bf16[1024,128]{1,0:T(8,128)(2,1)S(1)}, bf16[1024,128]{1,0:T(8,128)(2,1)S(1)}, u32[]{:S(2)}, u32[]{:S(2)}) collective-permute-start(bf16[1024,128]{1,0:T(8,128)(2,1)S(1)} %get-tuple-element.39), channel_id=1, source_target_pairs={{0,1},{1,0},{2,3},{3,2},{4,5},{5,4},{6,7},{7,6},{8,9},{9,8},{10,11... | collective-permute-start | bytes 786440 | tf_op jit(solution)/shard_map/ppermute | solution.py:310
  11.8 1.6 %collective-permute-start.1 = (bf16[1024,128]{1,0:T(8,128)(2,1)S(1)}, bf16[1024,128]{1,0:T(8,128)(2,1)S(1)}, u32[]{:S(2)}, u32[]{:S(2)}) collective-permute-start(bf16[1024,128]{1,0:T(8,128)(2,1)S(1)} %get-tuple-element.37), channel_id=1, source_target_pairs={{0,1},{1,0},{2,3},{3,2},{4,5},{5,4},{6,7},{7,6},{8,9},{9,8},{10,11... | collective-permute-start | bytes 786440 | tf_op jit(solution)/shard_map/ppermute | solution.py:310
  24.8 14.8 %all-to-all-start.1 = ((bf16[32,40,128]{2,1,0:T(8,128)(2,1)}), bf16[32,40,128]{2,1,0:T(8,128)(2,1)S(1)}, u32[]{:S(2)}, u32[]{:S(2)}) async-start(bf16[32,40,128]{2,1,0:T(8,128)(2,1)} %get-tuple-element.27), calls=%async_computation.1 | async-start | bytes 655360 | tf_op jit(solution)/shard_map/all_to_all | solution.py:300
  27.4 6.2 %collective-permute-start.3 = (bf16[32,8,128]{2,1,0:T(8,128)(2,1)S(1)}, bf16[32,8,128]{2,1,0:T(8,128)(2,1)S(1)}, u32[]{:S(2)}, u32[]{:S(2)}) collective-permute-start(bf16[32,8,128]{2,1,0:T(8,128)(2,1)S(1)} %get-tuple-element.32.kv_ref), channel_id=1, source_target_pairs={{0,2},{1,3},{2,0},{3,1},{4,6},{5,7},{6,4},{7,5},{8,10},{9,11},{10,... | collective-permute-start | bytes 196616 | tf_op jit(solution)/shard_map/ppermute | solution.py:349
  29.1 6.3 %collective-permute-start.2 = (bf16[32,8,128]{2,1,0:T(8,128)(2,1)S(1)}, bf16[32,8,128]{2,1,0:T(8,128)(2,1)S(1)}, u32[]{:S(2)}, u32[]{:S(2)}) collective-permute-start(bf16[32,8,128]{2,1,0:T(8,128)(2,1)S(1)} %get-tuple-element.32.kv_ref), channel_id=1, source_target_pairs={{0,1},{1,0},{2,3},{3,2},{4,5},{5,4},{6,7},{7,6},{8,9},{9,8},{10,11... | collective-permute-start | bytes 196616 | tf_op jit(solution)/shard_map/ppermute | solution.py:350
  33.6 1.8 %collective-permute-start.4 = (bf16[32,8,128]{2,1,0:T(8,128)(2,1)S(1)}, bf16[32,8,128]{2,1,0:T(8,128)(2,1)S(1)}, u32[]{:S(2)}, u32[]{:S(2)}) collective-permute-start(bf16[32,8,128]{2,1,0:T(8,128)(2,1)S(1)} %collective-permute-done.3.kv2_ref), channel_id=1, source_target_pairs={{0,1},{1,0},{2,3},{3,2},{4,5},{5,4},{6,7},{7,6},{8,9},{9,8},{10,11... | collective-permute-start | bytes 196616 | tf_op jit(solution)/shard_map/ppermute | solution.py:350

commit v14 on v10

--- a/solution.py
+++ b/solution.py
@@ -19,7 +19,7 @@
 LOG2E = math.log2(math.e)
 LANES = 128
 EARLY = 3
-STEP = 128
+STEP = 256
 
 
 def head_rows(q_ref, g):
@@ -48,11 +48,12 @@
     return copies
 
 
-def pack_kernel(capacity, chosen_hbm, q_hbm, k_hbm, v_hbm, send_hbm, chosen_ref, q_ref, k_ref, v_ref, send_ref, sems):
-    copies = fetch([(chosen_hbm, chosen_ref), (q_hbm, q_ref), (k_hbm, k_ref), (v_hbm, v_ref)], sems)
+def pack_kernel(capacity, chosen_hbm, q_hbm, send_hbm, chosen_ref, q_ref, send_ref, sems):
+    copies = fetch([(chosen_hbm, chosen_ref), (q_hbm, q_ref)], sems)
     tokens = q_ref.shape[0]
     per = capacity * tokens
-    key_blocks, chips = send_ref.shape[1:3]
+    key_blocks = send_ref.shape[1]
+    chips = send_hbm.shape[1]
     lane = lax.broadcasted_iota(jnp.int32, (tokens, key_blocks * per), 1)
     block, slot, token = lane // per, lane % per // tokens, lane % tokens
     copies[0].wait()
@@ -62,21 +63,16 @@
         ).T.astype(jnp.bfloat16)
         for g in range(KVH)
     ]
-    for copy in copies[1:]:
-        copy.wait()
+    copies[1].wait()
     sent = []
     for g in range(KVH):
         rows = head_rows(q_ref, g)
         rows = jnp.concatenate(rows + [jnp.zeros_like(rows[0])], axis=0).astype(jnp.bfloat16)
         slots = jnp.dot(spread[g], rows, preferred_element_type=jnp.float32).astype(jnp.bfloat16)
-        cols = slice(g * HD, (g + 1) * HD)
-        fresh = [k_ref[:, cols], v_ref[:, cols]]
-        for b in range(key_blocks):
-            for chip in range(chips):
-                send_ref[g, b, chip, :per, :] = slots[b * per : (b + 1) * per]
-                send_ref[g, b, chip, per:, :] = fresh[chip % 2]
-        sent.append(pltpu.make_async_copy(send_ref.at[g], send_hbm.at[:, :, g], sems.at[4 + g]))
-        sent[g].start()
+        send_ref[g] = slots.reshape(key_blocks, per, HD)
+        for chip in range(chips):
+            sent.append(pltpu.make_async_copy(send_ref.at[g], send_hbm.at[:, chip, g], sems.at[2 + len(sent)]))
+            sent[-1].start()
     for copy in sent:
         copy.wait()
 
@@ -94,8 +90,8 @@
         copy.wait()
 
 
-def attend_kernel(per, q_ref, ka_ref, va_ref, kb_ref, vb_ref, out_hbm, fresh_ref, out_ref, sems):
-    sources = q_ref.shape[0]
+def attend_kernel(q_ref, ka_ref, va_ref, kb_ref, vb_ref, out_hbm, out_ref, sems):
+    sources, per = q_ref.shape[:2]
     sent = []
     step = STEP // per
     scale = LOG2E * HD**-0.5
@@ -105,10 +101,9 @@
     diagonal = row == lane % per
     piece = lax.broadcasted_iota(jnp.int32, (8, LANES), 0)
     ones = jnp.ones(va_ref.shape, jnp.bfloat16)
-    fresh_ref[...] = q_ref[:, per:, :]
 
     def scores(first):
-        q = q_ref[first : first + step, :per, :].reshape(step * per, HD)
+        q = q_ref[first : first + step].reshape(step * per, HD)
         return [
             lax.dot_general(q, k_ref[...], nt, preferred_element_type=jnp.float32) for k_ref in (ka_ref, kb_ref)
         ]
@@ -263,28 +258,31 @@
     def partner(bit):
         return [(i, i ^ bit) for i in range(devices)]
 
+    def exchange(x):
+        return lax.all_to_all(x, "seq", split_axis=0, concat_axis=0, tiled=True)
+
     send = call(
         functools.partial(pack_kernel, capacity),
         "pack",
-        jax.ShapeDtypeStruct((key_blocks, chips, KVH, per + tokens, HD), bf16),
-        [HBM] * 4,
-        picks, queries, stretch_keys, stretch_values,
+        jax.ShapeDtypeStruct((key_blocks, chips, KVH, per, HD), bf16),
+        [HBM] * 2,
+        picks, queries,
         outs=ANY,
         scratch=[
             pltpu.VMEM(picks.shape, jnp.int32),
             pltpu.VMEM(queries.shape, bf16),
-            pltpu.VMEM(stretch_keys.shape, bf16),
-            pltpu.VMEM(stretch_values.shape, bf16),
-            pltpu.VMEM((KVH, key_blocks, chips, per + tokens, HD), bf16),
-            pltpu.SemaphoreType.DMA((4 + KVH,)),
+            pltpu.VMEM((KVH, key_blocks, per, HD), bf16),
+            pltpu.SemaphoreType.DMA((2 + KVH * chips,)),
         ],
         limit=60,
     )
-    send, cache_keys, cache_values, picks, queries = lax.optimization_barrier(
-        (send, cache_keys, cache_values, picks, queries)
-    )
-    send = send.reshape(devices, per + tokens, HD)
-    got = lax.all_to_all(send, "seq", split_axis=0, concat_axis=0, tiled=True)
+    send, cache_keys, cache_values, picks, queries, stretch_keys, stretch_values = lax.optimization_barrier(
+        (send, cache_keys, cache_values, picks, queries, stretch_keys, stretch_values)
+    )
+    got = exchange(send.reshape(devices, per, HD))
+    kinds = jnp.stack([stretch_keys, stretch_values]).reshape(2, tokens, KVH, HD).transpose(0, 2, 1, 3)
+    kinds = jnp.broadcast_to(kinds[None], (key_blocks, chips, KVH, tokens, HD))
+    fresh = exchange(kinds.reshape(devices, tokens, HD))
 
     core = lax.axis_index("seq") % KVH
 
@@ -295,26 +293,21 @@
     k_peer, v_peer = [lax.ppermute(x, "seq", partner(1)) for x in halves(1 - core)]
     holders = devices // KVH
     rows = devices * per
-    back, fresh = call(
-        functools.partial(attend_kernel, per),
+    back = call(
+        attend_kernel,
         "attend",
-        (
-            jax.ShapeDtypeStruct((devices, per + 8, HD), bf16),
-            jax.ShapeDtypeStruct((devices, tokens, HD), bf16),
-        ),
+        jax.ShapeDtypeStruct((devices, per + 8, HD), bf16),
         [VMEM] * 5,
         got, k_own, v_own, k_peer, v_peer,
-        outs=(ANY, VMEM),
+        outs=ANY,
         scratch=[
             pltpu.VMEM((devices, per + 8, HD), bf16),
             pltpu.SemaphoreType.DMA((rows // STEP,)),
         ],
-        flops=8 * rows * cache_rows * HD,
-        moved=4 << 20,
         limit=32,
     )
-    back, picks, queries, out_weight = lax.optimization_barrier((back, picks, queries, out_weight))
-    hist = lax.all_to_all(back, "seq", split_axis=0, concat_axis=0, tiled=True)
+    back, picks, queries, out_weight, fresh = lax.optimization_barrier((back, picks, queries, out_weight, fresh))
+    hist = exchange(back)
 
     ready = EARLY * KVH * HD
     match, query_rows, first = call(

time: 42.9 us -> 48.7 us (1.14)
  starting transfers between devices: 12.3 us -> 14.8 us
  local copies, waits for them, and re-layouts: 2.14 us -> 4.2 us
  other arithmetic: 0 us -> 0.71 us
  waiting for transfers between devices: 17.2 us -> 17.7 us
    all_to_all x2 -> x3, starting transfers between devices: 9.91 us -> 12.5 us  [exchange(): return lax.all_to_all(x, 'seq', split_axis=0, concat_axis=0, tiled=True)]
    all_to_all x2 -> x3, waiting for transfers between devices: 11.1 us -> 12.9 us  [exchange(): return lax.all_to_all(x, 'seq', split_axis=0, concat_axis=0, tiled=True)]
    unnamed x4, local copies, waits for them, and re-layouts: 0.01 us -> 1.43 us
    ppermute x2, waiting for transfers between devices: 1.28 us -> 0.01 us  [body(): lax.ppermute(x, 'seq', partner(1))]
    transpose x0 -> x1, other arithmetic: none -> 0.71 us  [body(): jnp.stack([stretch_keys, stretch_values]).reshape(2, tokens, KVH, HD)]
    broadcast_in_dim x0 -> x1, local copies, waits for them, and re-layouts: none -> 0.64 us  [body(): kinds = jnp.broadcast_to(kinds[None], (key_blocks, chips, KVH, tokens, HD))]
  transfers between devices with their start and end apart: 7 -> 8, of which waited for: 4 -> 4; matrix products, arithmetic and copies ran while one was open for 5% -> 7% of each run, Pallas kernels for 5% -> 12%
where the time goes in v14:
time: 48.7 us; the launch traced here: 48.1 us
  waiting for transfers between devices  17.7 us (36%)
  starting transfers between devices  14.8 us (30%)
  Pallas kernels  10.6 us (22%)
  local copies, waits for them, and re-layouts  4.2 us (9%)
  other arithmetic  0.71 us (1%)
    all_to_all x3, waiting for transfers between devices, exchange(): return lax.all_to_all(x, 'seq', split_axis=0, concat_axis=0, tiled=True)  12.9 us
    all_to_all x3, starting transfers between devices, exchange(): return lax.all_to_all(x, 'seq', split_axis=0, concat_axis=0, tiled=True)  12.5 us
    pallas_call x5, Pallas kernels, call(): pl.pallas_call(kernel, name=name, out_shape=out_shape, in_specs=specs, ou...  10.6 us
    ppermute x1, waiting for transfers between devices, body(): far = lax.ppermute(fresh, 'seq', partner(2))  4.83 us
    dynamic_slice x2, local copies, waits for them, and re-layouts, halves(): lax.dynamic_slice_in_dim(x, head * HD, HD, axis=1)  2.13 us
    ppermute x1, starting transfers between devices, body(): far = lax.ppermute(fresh, 'seq', partner(2))  1.7 us
    unnamed x4, local copies, waits for them, and re-layouts  1.43 us
  transfers between devices with their start and end apart: 8, of which 4 were waited for; matrix products, arithmetic and copies ran while one was open for 7% of the time, Pallas kernels for 12%

profile of v14, /device:TPU:0, one launch (start us, length us, event | category | flops | bytes accessed | tf_op | source)
XLA Modules:
  0.0 48.1 jit_solution(16659495118984620458)
XLA Ops:
  0.0 1.9 %pack.1 = bf16[8,2,2,32,128]{4,3,2,1,0:T(8,128)(2,1)} custom-call(s32[3,1,14]{2,1,0:T(1,128)} %bitcast.9, bf16[8,1792]{1,0:T(8,128)(2,1)} %q_ref), custom_call_target="tpu_custom_call" | custom-call | tf_op jit(solution)/shard_map/pack/pallas_call | solution.py:234
  1.9 7.3 %all-to-all-start = ((bf16[32,32,128]{2,1,0:T(8,128)(2,1)}), bf16[32,32,128]{2,1,0:T(8,128)(2,1)S(1)}, u32[]{:S(2)}, u32[]{:S(2)}) async-start(bf16[32,32,128]{2,1,0:T(8,128)(2,1)} %bitcast.11), calls=%async_computation | async-start | bytes 524288 | tf_op jit(solution)/shard_map/all_to_all | solution.py:262
  9.3 1.1 %constant_dynamic-slice_fusion.1 = (bf16[1024,128]{1,0:T(8,128)(2,1)S(1)}, bf16[1024,128]{1,0:T(8,128)(2,1)S(1)}) fusion(bf16[1024,256]{1,0:T(8,128)(2,1)} %param.10, s32[]{:T(128)S(6)} %select_n.17, s32[]{:T(128)S(6)} %select_n.16), kind=kLoop, calls=%fused_computation.2 | loop fusion | bytes 1048584 | tf_op jit(solution)/shard_map/dynamic_slice | solution.py:290
  10.3 0.3 collective-permute-start
  10.7 1.1 %constant_dynamic-slice_fusion = (bf16[1024,128]{1,0:T(8,128)(2,1)S(1)}, bf16[1024,128]{1,0:T(8,128)(2,1)S(1)}) fusion(bf16[1024,256]{1,0:T(8,128)(2,1)} %param.11, s32[]{:T(128)S(6)} %select_n.17, s32[]{:T(128)S(6)} %select_n.16), kind=kLoop, calls=%fused_computation.1 | loop fusion | bytes 1048584 | tf_op jit(solution)/shard_map/dynamic_slice | solution.py:290
  11.7 0.3 collective-permute-start.1
  12.0 0.7 %maximum_bitcast_fusion = bf16[2,2,8,128]{3,2,1,0:T(8,128)(2,1)S(1)} fusion(bf16[1,8,2,128]{3,1,2,0:T(8,128)(2,1)} %bitcast.12, bf16[1,8,2,128]{3,1,2,0:T(8,128)(2,1)} %bitcast.13), kind=kLoop, calls=%fused_computation | loop fusion | flops 4096 | bytes 16384 | tf_op jit(solution)/shard_map/transpose | solution.py:283
  12.7 7.1 %all-to-all-done.q_ref = bf16[32,32,128]{2,1,0:T(8,128)(2,1)S(1)} async-done(((bf16[32,32,128]{2,1,0:T(8,128)(2,1)}), bf16[32,32,128]{2,1,0:T(8,128)(2,1)S(1)}, u32[]{:S(2)}, u32[]{:S(2)}) %all-to-all-start) | async-done | bytes 262176 | tf_op jit(solution)/shard_map/all_to_all | solution.py:262
  19.8 0.6 %broadcast_in_dim.2 = bf16[8,2,2,8,128]{4,3,2,1,0:T(8,128)(2,1)} broadcast(bf16[2,2,8,128]{3,2,1,0:T(8,128)(2,1)S(1)} %maximum_bitcast_fusion), dimensions={1,2,3,4} | broadcast | bytes 73728 | tf_op jit(solution)/shard_map/broadcast_in_dim | solution.py:284
  20.5 2.6 %all-to-all-start.1 = ((bf16[32,8,128]{2,1,0:T(8,128)(2,1)}), bf16[32,8,128]{2,1,0:T(8,128)(2,1)S(1)}, u32[]{:S(2)}, u32[]{:S(2)}) async-start(bf16[32,8,128]{2,1,0:T(8,128)(2,1)} %bitcast.5), calls=%async_computation.1 | async-start | bytes 131072 | tf_op jit(solution)/shard_map/all_to_all | solution.py:262
  23.0 0.0 collective-permute-done.kb_ref
  23.1 0.0 collective-permute-done.1.vb_ref
  23.1 3.4 %attend.1 = bf16[32,40,128]{2,1,0:T(8,128)(2,1)} custom-call(bf16[32,32,128]{2,1,0:T(8,128)(2,1)S(1)} %all-to-all-done.q_ref, bf16[1024,128]{1,0:T(8,128)(2,1)S(1)} %get-tuple-element.42.ka_ref, bf16[1024,128]{1,0:T(8,128)(2,1)S(1)} %get-tuple-element.40.va_ref, bf16[1024,128]{1,0:T(8,128)(2,1)S(1)} %collective-permute-done.kb_ref, ...), custom_call_target="tpu_custom_call" | custom-call | tf_op jit(solution)/shard_map/attend/pallas_call | solution.py:234
  26.4 4.0 %all-to-all-done.1.kv_ref = bf16[32,8,128]{2,1,0:T(8,128)(2,1)S(1)} async-done(((bf16[32,8,128]{2,1,0:T(8,128)(2,1)}), bf16[32,8,128]{2,1,0:T(8,128)(2,1)S(1)}, u32[]{:S(2)}, u32[]{:S(2)}) %all-to-all-start.1) | async-done | bytes 65568 | tf_op jit(solution)/shard_map/all_to_all | solution.py:262
  30.5 2.6 %all-to-all-start.2 = ((bf16[32,40,128]{2,1,0:T(8,128)(2,1)}), bf16[32,40,128]{2,1,0:T(8,128)(2,1)S(1)}, u32[]{:S(2)}, u32[]{:S(2)}) async-start(bf16[32,40,128]{2,1,0:T(8,128)(2,1)} %attend.1), calls=%async_computation.2 | async-start | bytes 655360 | tf_op jit(solution)/shard_map/all_to_all | solution.py:262
  33.1 1.7 %collective-permute-start.3 = (bf16[32,8,128]{2,1,0:T(8,128)(2,1)S(1)}, bf16[32,8,128]{2,1,0:T(8,128)(2,1)S(1)}, u32[]{:S(2)}, u32[]{:S(2)}) collective-permute-start(bf16[32,8,128]{2,1,0:T(8,128)(2,1)S(1)} %all-to-all-done.1.kv_ref), channel_id=1, source_target_pairs={{0,2},{1,3},{2,0},{3,1},{4,6},{5,7},{6,4},{7,5},{8,10},{9,11},{10,... | collective-permute-start | bytes 196616 | tf_op jit(solution)/shard_map/ppermute | solution.py:327
  34.8 0.0 collective-permute-start.2
  34.8 4.8 %collective-permute-done.3.kv2_ref = bf16[32,8,128]{2,1,0:T(8,128)(2,1)S(1)} collective-permute-done((bf16[32,8,128]{2,1,0:T(8,128)(2,1)S(1)}, bf16[32,8,128]{2,1,0:T(8,128)(2,1)S(1)}, u32[]{:S(2)}, u32[]{:S(2)}) %collective-permute-start.3) | collective-permute-done | bytes 65568 | tf_op jit(solution)/shard_map/ppermute | solution.py:327
  39.6 0.0 collective-permute-start.4
  39.6 0.0 copy-start
  39.6 0.7 %copy-done = bf16[8,1792]{1,0:T(8,128)(2,1)S(1)} copy-done((bf16[8,1792]{1,0:T(8,128)(2,1)S(1)}, bf16[8,1792]{1,0:T(8,128)(2,1)}, u32[]{:S(2)}) %copy-start) | copy-done | bytes 28696
  40.3 0.0 copy-start.1
  40.3 0.7 %copy-done.1 = s32[1,14,3]{1,0,2:T(1,128)S(1)} copy-done((s32[1,14,3]{1,0,2:T(1,128)S(1)}, s32[1,14,3]{1,0,2:T(1,128)}, u32[]{:S(2)}) %copy-start.1) | copy-done | bytes 192
  41.0 1.8 %masks.1 = (f32[2,56,512]{2,1,0:T(8,128)S(1)}, f32[2,56,128]{2,1,0:T(8,128)S(1)}, bf16[768,1792]{1,0:T(8,128)(2,1)S(1)}) custom-call(s32[3,1,14]{2,1,0:T(1,128)S(1)} %bitcast.10, bf16[8,1792]{1,0:T(8,128)(2,1)S(1)} %copy-done, bf16[1792,1792]{1,0:T(8,128)(2,1)} %w_hbm.1), custom_call_target="tpu_custom_call" | custom-call | tf_op jit(solution)/shard_map/masks/pallas_call | solution.py:234
  42.8 0.0 collective-permute-done.2.kv1_ref
  42.8 0.0 collective-permute-done.4.kv3_ref
  42.8 0.4 fresh.1
  43.3 1.8 %all-to-all-done.2 = bf16[32,40,128]{2,1,0:T(8,128)(2,1)S(1)} async-done(((bf16[32,40,128]{2,1,0:T(8,128)(2,1)}), bf16[32,40,128]{2,1,0:T(8,128)(2,1)S(1)}, u32[]{:S(2)}, u32[]{:S(2)}) %all-to-all-start.2) | async-done | bytes 327712 | tf_op jit(solution)/shard_map/all_to_all | solution.py:262
  45.0 3.1 %project.1 = bf16[8,1792]{1,0:T(8,128)(2,1)} custom-call(bf16[16,2,40,128]{3,2,1,0:T(8,128)(2,1)S(1)} %bitcast.8, f32[2,56,128]{2,1,0:T(8,128)S(1)} %get-tuple-element.35.out_ref, f32[2,56,128]{2,1,0:T(8,128)S(1)} %get-tuple-element.36.lse_ref, f32[2,56,512]{2,1,0:T(8,128)S(1)} %get-tuple-element.37.match_ref, ...), custom_call_target="tpu_custom_call" | custom-call | flops 51380224 | bytes 6422528 | tf_op jit(solution)/shard_map/project/pallas_call | solution.py:234
Async XLA Ops:
  1.9 17.9 %all-to-all-start = ((bf16[32,32,128]{2,1,0:T(8,128)(2,1)}), bf16[32,32,128]{2,1,0:T(8,128)(2,1)S(1)}, u32[]{:S(2)}, u32[]{:S(2)}) async-start(bf16[32,32,128]{2,1,0:T(8,128)(2,1)} %bitcast.11), calls=%async_computation | async-start | bytes 524288 | tf_op jit(solution)/shard_map/all_to_all | solution.py:262
  10.3 12.7 %collective-permute-start = (bf16[1024,128]{1,0:T(8,128)(2,1)S(1)}, bf16[1024,128]{1,0:T(8,128)(2,1)S(1)}, u32[]{:S(2)}, u32[]{:S(2)}) collective-permute-start(bf16[1024,128]{1,0:T(8,128)(2,1)S(1)} %get-tuple-element.41), channel_id=1, source_target_pairs={{0,1},{1,0},{2,3},{3,2},{4,5},{5,4},{6,7},{7,6},{8,9},{9,8},{10,11... | collective-permute-start | bytes 786440 | tf_op jit(solution)/shard_map/ppermute | solution.py:293
  11.7 11.3 %collective-permute-start.1 = (bf16[1024,128]{1,0:T(8,128)(2,1)S(1)}, bf16[1024,128]{1,0:T(8,128)(2,1)S(1)}, u32[]{:S(2)}, u32[]{:S(2)}) collective-permute-start(bf16[1024,128]{1,0:T(8,128)(2,1)S(1)} %get-tuple-element.39), channel_id=1, source_target_pairs={{0,1},{1,0},{2,3},{3,2},{4,5},{5,4},{6,7},{7,6},{8,9},{9,8},{10,11... | collective-permute-start | bytes 786440 | tf_op jit(solution)/shard_map/ppermute | solution.py:293
  20.5 10.0 %all-to-all-start.1 = ((bf16[32,8,128]{2,1,0:T(8,128)(2,1)}), bf16[32,8,128]{2,1,0:T(8,128)(2,1)S(1)}, u32[]{:S(2)}, u32[]{:S(2)}) async-start(bf16[32,8,128]{2,1,0:T(8,128)(2,1)} %bitcast.5), calls=%async_computation.1 | async-start | bytes 131072 | tf_op jit(solution)/shard_map/all_to_all | solution.py:262
  30.5 14.6 %all-to-all-start.2 = ((bf16[32,40,128]{2,1,0:T(8,128)(2,1)}), bf16[32,40,128]{2,1,0:T(8,128)(2,1)S(1)}, u32[]{:S(2)}, u32[]{:S(2)}) async-start(bf16[32,40,128]{2,1,0:T(8,128)(2,1)} %attend.1), calls=%async_computation.2 | async-start | bytes 655360 | tf_op jit(solution)/shard_map/all_to_all | solution.py:262
  33.1 6.5 %collective-permute-start.3 = (bf16[32,8,128]{2,1,0:T(8,128)(2,1)S(1)}, bf16[32,8,128]{2,1,0:T(8,128)(2,1)S(1)}, u32[]{:S(2)}, u32[]{:S(2)}) collective-permute-start(bf16[32,8,128]{2,1,0:T(8,128)(2,1)S(1)} %all-to-all-done.1.kv_ref), channel_id=1, source_target_pairs={{0,2},{1,3},{2,0},{3,1},{4,6},{5,7},{6,4},{7,5},{8,10},{9,11},{10,... | collective-permute-start | bytes 196616 | tf_op jit(solution)/shard_map/ppermute | solution.py:327
  34.8 8.1 %collective-permute-start.2 = (bf16[32,8,128]{2,1,0:T(8,128)(2,1)S(1)}, bf16[32,8,128]{2,1,0:T(8,128)(2,1)S(1)}, u32[]{:S(2)}, u32[]{:S(2)}) collective-permute-start(bf16[32,8,128]{2,1,0:T(8,128)(2,1)S(1)} %all-to-all-done.1.kv_ref), channel_id=1, source_target_pairs={{0,1},{1,0},{2,3},{3,2},{4,5},{5,4},{6,7},{7,6},{8,9},{9,8},{10,11... | collective-permute-start | bytes 196616 | tf_op jit(solution)/shard_map/ppermute | solution.py:328
  39.6 3.2 %collective-permute-start.4 = (bf16[32,8,128]{2,1,0:T(8,128)(2,1)S(1)}, bf16[32,8,128]{2,1,0:T(8,128)(2,1)S(1)}, u32[]{:S(2)}, u32[]{:S(2)}) collective-permute-start(bf16[32,8,128]{2,1,0:T(8,128)(2,1)S(1)} %collective-permute-done.3.kv2_ref), channel_id=1, source_target_pairs={{0,1},{1,0},{2,3},{3,2},{4,5},{5,4},{6,7},{7,6},{8,9},{9,8},{10,11... | collective-permute-start | bytes 196616 | tf_op jit(solution)/shard_map/ppermute | solution.py:328
  39.6 0.7 %copy-start = (bf16[8,1792]{1,0:T(8,128)(2,1)S(1)}, bf16[8,1792]{1,0:T(8,128)(2,1)}, u32[]{:S(2)}) copy-start(bf16[8,1792]{1,0:T(8,128)(2,1)} %q_ref) | copy-start | bytes 86020
  40.3 0.7 %copy-start.1 = (s32[1,14,3]{1,0,2:T(1,128)S(1)}, s32[1,14,3]{1,0,2:T(1,128)}, u32[]{:S(2)}) copy-start(s32[1,14,3]{1,0,2:T(1,128)} %param.12) | copy-start | bytes 508

commit v15 on v10

--- a/solution.py
+++ b/solution.py
@@ -19,7 +19,7 @@
 LOG2E = math.log2(math.e)
 LANES = 128
 EARLY = 3
-STEP = 128
+STEP = 256
 
 
 def head_rows(q_ref, g):
@@ -103,7 +103,8 @@
     row = lax.broadcasted_iota(jnp.int32, (per, LANES), 0)
     lane = lax.broadcasted_iota(jnp.int32, (per, LANES), 1)
     diagonal = row == lane % per
-    piece = lax.broadcasted_iota(jnp.int32, (8, LANES), 0)
+    group = lax.broadcasted_iota(jnp.int32, (2, LANES), 1) // per
+    second = lax.broadcasted_iota(jnp.int32, (2, LANES), 0)
     ones = jnp.ones(va_ref.shape, jnp.bfloat16)
     fresh_ref[...] = q_ref[:, per:, :]
 
@@ -125,19 +126,19 @@
             wa, jnp.concatenate([va_ref[...], ones], axis=1), preferred_element_type=jnp.float32
         ) + jnp.dot(wb, jnp.concatenate([vb_ref[...], ones], axis=1), preferred_element_type=jnp.float32)
         total = both[:, HD:]
-        out = (both[:, :HD] / total).astype(jnp.bfloat16)
+        out = both[:, :HD] / total
         lse = top + jnp.log(total) * LOG2E
+        rows = []
         for s in range(step):
             part = slice(s * per, (s + 1) * per)
-            out_ref[first + s, :per, :] = out[part]
             flat = jnp.sum(jnp.where(diagonal, lse[part], 0.0), axis=0, keepdims=True)
             hi = flat.astype(jnp.bfloat16).astype(jnp.float32)
             mid = (flat - hi).astype(jnp.bfloat16).astype(jnp.float32)
             low = flat - hi - mid
-            out_ref[first + s, per:, :] = jnp.where(
-                piece == 0, hi, jnp.where(piece == 1, mid, jnp.where(piece == 2, low, 0.0))
-            ).astype(jnp.bfloat16)
-        done = pl.ds(first, step)
+            stats = jnp.where(group == 0, hi, jnp.where(group == 1, mid, jnp.where(group == 2, low, 0.0)))
+            rows = rows + [out[part], jnp.where(second == 0, stats, 0.0)]
+        done = pl.ds(first * (per + 2), step * (per + 2))
+        out_ref[done, :] = jnp.concatenate(rows, axis=0).astype(jnp.bfloat16)
         sent.append(pltpu.make_async_copy(out_ref.at[done], out_hbm.at[done], sems.at[first // step]))
         sent[-1].start()
     for copy in sent:
@@ -185,7 +186,9 @@
         sems,
     )
     tokens = y_ref.shape[0]
-    holders = hist_ref.shape[0]
+    holders = match_ref.shape[2] // per
+    stride = KVH * (per + 2)
+    hist = hist_ref[...].astype(jnp.float32)
     fold = LANES // per
     row = lax.broadcasted_iota(jnp.int32, (holders, LANES), 0)
     lane = lax.broadcasted_iota(jnp.int32, (holders, LANES), 1)
@@ -196,8 +199,13 @@
 
     heads = []
     for g in range(KVH):
-        outs = hist_ref[:, g, :per, :].reshape(holders * per, HD)
-        stats = jnp.sum(hist_ref[:, g, per:, :].astype(jnp.float32), axis=1)
+        starts = [m * stride + g * (per + 2) for m in range(holders)]
+        outs = jnp.concatenate([hist[i : i + per] for i in starts], axis=0).astype(jnp.bfloat16)
+        stats = jnp.concatenate([hist[i + per : i + per + 1] for i in starts], axis=0)
+        shift = LANES // 2
+        while shift >= per:
+            stats = stats + pltpu.roll(stats, shift, 1)
+            shift //= 2
         stats = jnp.where(row % fold == lane // per, stats, 0.0)
         lse = jnp.concatenate(
             [
@@ -299,14 +307,14 @@
         functools.partial(attend_kernel, per),
         "attend",
         (
-            jax.ShapeDtypeStruct((devices, per + 8, HD), bf16),
+            jax.ShapeDtypeStruct((devices * (per + 2), HD), bf16),
             jax.ShapeDtypeStruct((devices, tokens, HD), bf16),
         ),
         [VMEM] * 5,
         got, k_own, v_own, k_peer, v_peer,
         outs=(ANY, VMEM),
         scratch=[
-            pltpu.VMEM((devices, per + 8, HD), bf16),
+            pltpu.VMEM((devices * (per + 2), HD), bf16),
             pltpu.SemaphoreType.DMA((rows // STEP,)),
         ],
         flops=8 * rows * cache_rows * HD,
@@ -314,6 +322,7 @@
         limit=32,
     )
     back, picks, queries, out_weight = lax.optimization_barrier((back, picks, queries, out_weight))
+    back = back.reshape(devices, (per + 2) // 2, 2, HD)
     hist = lax.all_to_all(back, "seq", split_axis=0, concat_axis=0, tiled=True)
 
     ready = EARLY * KVH * HD
@@ -348,7 +357,7 @@
         "project",
         jax.ShapeDtypeStruct((tokens, out_weight.shape[1]), bf16),
         [VMEM] * 5 + [HBM],
-        hist.reshape(holders, KVH, per + 8, HD), out, lse, match, first, out_weight,
+        hist.reshape(devices * (per + 2), HD), out, lse, match, first, out_weight,
         scratch=[
             pltpu.VMEM((out_weight.shape[0] - ready, out_weight.shape[1]), bf16),
             pltpu.SemaphoreType.DMA((GROUP - EARLY,)),

time: 42.9 us -> 41.9 us (0.977)
  waiting for transfers between devices: 17.2 us -> 16.3 us
    ppermute x1, waiting for transfers between devices: 4.83 us -> 4.31 us  [body(): far = lax.ppermute(fresh, 'seq', partner(2))]
where the time goes in v15:
time: 41.9 us; the launch traced here: 41.5 us
  waiting for transfers between devices  16.3 us (39%)
  starting transfers between devices  12.3 us (29%)
  Pallas kernels  10.7 us (26%)
  local copies, waits for them, and re-layouts  2.14 us (5%)
    pallas_call x5, Pallas kernels, call(): pl.pallas_call(kernel, name=name, out_shape=out_shape, in_specs=specs, ou...  10.7 us
    all_to_all x1, waiting for transfers between devices, body(): got = lax.all_to_all(send, 'seq', split_axis=0, concat_axis=0, tiled=True)  7.91 us
    all_to_all x1, starting transfers between devices, body(): got = lax.all_to_all(send, 'seq', split_axis=0, concat_axis=0, tiled=True)  7.3 us
    ppermute x1, waiting for transfers between devices, body(): far = lax.ppermute(fresh, 'seq', partner(2))  4.31 us
    all_to_all x1, waiting for transfers between devices, body(): hist = lax.all_to_all(back, 'seq', split_axis=0, concat_axis=0, tiled=True)  2.8 us
    all_to_all x1, starting transfers between devices, body(): hist = lax.all_to_all(back, 'seq', split_axis=0, concat_axis=0, tiled=True)  2.6 us
    dynamic_slice x2, local copies, waits for them, and re-layouts, halves(): lax.dynamic_slice_in_dim(x, head * HD, HD, axis=1)  2.13 us
    ppermute x1, starting transfers between devices, body(): far = lax.ppermute(fresh, 'seq', partner(2))  1.7 us
  transfers between devices with their start and end apart: 7, of which 4 were waited for; matrix products, arithmetic and copies ran while one was open for 5% of the time, Pallas kernels for 5%

profile of v15, /device:TPU:0, one launch (start us, length us, event | category | flops | bytes accessed | tf_op | source)
XLA Modules:
  0.0 41.5 jit_solution(13053511965425777349)
XLA Ops:
  0.0 0.0 copy-start
  0.0 0.0 copy-start.1
  0.0 2.0 %pack.1 = bf16[8,2,2,40,128]{4,3,2,1,0:T(8,128)(2,1)} custom-call(s32[3,1,14]{2,1,0:T(1,128)} %bitcast.5, bf16[8,1792]{1,0:T(8,128)(2,1)} %q_ref, bf16[8,256]{1,0:T(8,128)(2,1)} %k_hbm.1, bf16[8,256]{1,0:T(8,128)(2,1)} %v_hbm.1), custom_call_target="tpu_custom_call" | custom-call | tf_op jit(solution)/shard_map/pack/pallas_call | solution.py:247
  2.0 7.3 %all-to-all-start = ((bf16[32,40,128]{2,1,0:T(8,128)(2,1)}), bf16[32,40,128]{2,1,0:T(8,128)(2,1)S(1)}, u32[]{:S(2)}, u32[]{:S(2)}) async-start(bf16[32,40,128]{2,1,0:T(8,128)(2,1)} %bitcast.7), calls=%async_computation | async-start | bytes 655360 | tf_op jit(solution)/shard_map/all_to_all | solution.py:295
  9.4 1.1 %constant_dynamic-slice_fusion.1 = (bf16[1024,128]{1,0:T(8,128)(2,1)S(1)}, bf16[1024,128]{1,0:T(8,128)(2,1)S(1)}) fusion(bf16[1024,256]{1,0:T(8,128)(2,1)} %param.10, s32[]{:T(128)S(6)} %select_n.17, s32[]{:T(128)S(6)} %select_n.16), kind=kLoop, calls=%fused_computation.1 | loop fusion | bytes 1048584 | tf_op jit(solution)/shard_map/dynamic_slice | solution.py:300
  10.4 0.3 collective-permute-start
  10.7 1.1 %constant_dynamic-slice_fusion = (bf16[1024,128]{1,0:T(8,128)(2,1)S(1)}, bf16[1024,128]{1,0:T(8,128)(2,1)S(1)}) fusion(bf16[1024,256]{1,0:T(8,128)(2,1)} %param.11, s32[]{:T(128)S(6)} %select_n.17, s32[]{:T(128)S(6)} %select_n.16), kind=kLoop, calls=%fused_computation | loop fusion | bytes 1048584 | tf_op jit(solution)/shard_map/dynamic_slice | solution.py:300
  11.8 0.3 collective-permute-start.1
  12.1 0.0 collective-permute-done.kb_ref
  12.1 1.3 %collective-permute-done.1.vb_ref = bf16[1024,128]{1,0:T(8,128)(2,1)S(1)} collective-permute-done((bf16[1024,128]{1,0:T(8,128)(2,1)S(1)}, bf16[1024,128]{1,0:T(8,128)(2,1)S(1)}, u32[]{:S(2)}, u32[]{:S(2)}) %collective-permute-start.1) | collective-permute-done | bytes 262176 | tf_op jit(solution)/shard_map/ppermute | solution.py:303
  13.4 7.9 %all-to-all-done.q_ref = bf16[32,40,128]{2,1,0:T(8,128)(2,1)S(1)} async-done(((bf16[32,40,128]{2,1,0:T(8,128)(2,1)}), bf16[32,40,128]{2,1,0:T(8,128)(2,1)S(1)}, u32[]{:S(2)}, u32[]{:S(2)}) %all-to-all-start) | async-done | bytes 327712 | tf_op jit(solution)/shard_map/all_to_all | solution.py:295
  21.3 3.4 %attend.1 = (bf16[1088,128]{1,0:T(8,128)(2,1)}, bf16[32,8,128]{2,1,0:T(8,128)(2,1)S(1)}) custom-call(bf16[32,40,128]{2,1,0:T(8,128)(2,1)S(1)} %all-to-all-done.q_ref, bf16[1024,128]{1,0:T(8,128)(2,1)S(1)} %get-tuple-element.40.ka_ref, bf16[1024,128]{1,0:T(8,128)(2,1)S(1)} %get-tuple-element.38.va_ref, bf16[1024,128]{1,0:T(8,128)(2,1)S(1)} %collective-permute-done.kb_ref, ...), custom_call_target="tpu_custom_call" | custom-call | flops 1073741824 | bytes 4194304 | tf_op jit(solution)/shard_map/attend/pallas_call | solution.py:247
  24.7 2.6 %all-to-all-start.1 = ((bf16[32,17,2,128]{3,2,1,0:T(2,128)(2,1)}), bf16[32,17,2,128]{3,2,1,0:T(2,128)(2,1)S(1)}, u32[]{:S(2)}, u32[]{:S(2)}) async-start(bf16[32,17,2,128]{3,2,1,0:T(2,128)(2,1)} %bitcast.2), calls=%async_computation.1 | async-start | bytes 557056 | tf_op jit(solution)/shard_map/all_to_all | solution.py:326
  27.3 1.7 %collective-permute-start.3 = (bf16[32,8,128]{2,1,0:T(8,128)(2,1)S(1)}, bf16[32,8,128]{2,1,0:T(8,128)(2,1)S(1)}, u32[]{:S(2)}, u32[]{:S(2)}) collective-permute-start(bf16[32,8,128]{2,1,0:T(8,128)(2,1)S(1)} %get-tuple-element.32.kv_ref), channel_id=1, source_target_pairs={{0,2},{1,3},{2,0},{3,1},{4,6},{5,7},{6,4},{7,5},{8,10},{9,11},{10,... | collective-permute-start | bytes 196616 | tf_op jit(solution)/shard_map/ppermute | solution.py:343
  29.0 0.0 collective-permute-start.2
  29.0 4.3 %collective-permute-done.3.kv2_ref = bf16[32,8,128]{2,1,0:T(8,128)(2,1)S(1)} collective-permute-done((bf16[32,8,128]{2,1,0:T(8,128)(2,1)S(1)}, bf16[32,8,128]{2,1,0:T(8,128)(2,1)S(1)}, u32[]{:S(2)}, u32[]{:S(2)}) %collective-permute-start.3) | collective-permute-done | bytes 65568 | tf_op jit(solution)/shard_map/ppermute | solution.py:343
  33.3 0.0 collective-permute-start.4
  33.3 0.0 copy-done
  33.3 0.0 copy-done.1
  33.3 1.8 %masks.1 = (f32[2,56,512]{2,1,0:T(8,128)S(1)}, f32[2,56,128]{2,1,0:T(8,128)S(1)}, bf16[768,1792]{1,0:T(8,128)(2,1)S(1)}) custom-call(s32[3,1,14]{2,1,0:T(1,128)S(1)} %bitcast.6, bf16[8,1792]{1,0:T(8,128)(2,1)S(1)} %copy-done, bf16[1792,1792]{1,0:T(8,128)(2,1)} %w_hbm.1), custom_call_target="tpu_custom_call" | custom-call | tf_op jit(solution)/shard_map/masks/pallas_call | solution.py:247
  35.1 0.0 collective-permute-done.2.kv1_ref
  35.1 0.0 collective-permute-done.4.kv3_ref
  35.1 0.4 %fresh.1 = (f32[2,56,128]{2,1,0:T(8,128)S(1)}, f32[2,56,128]{2,1,0:T(8,128)S(1)}) custom-call(f32[2,56,128]{2,1,0:T(8,128)S(1)} %get-tuple-element.31.rows_ref, bf16[32,8,128]{2,1,0:T(8,128)(2,1)S(1)} %get-tuple-element.32.kv_ref, bf16[32,8,128]{2,1,0:T(8,128)(2,1)S(1)} %collective-permute-done.2.kv1_ref, ...), custom_call_target="tpu_custom_call" | custom-call | flops 29360128 | bytes 1048576 | tf_op jit(solution)/shard_map/fresh/pallas_call | solution.py:247
  35.6 2.8 %all-to-all-done.1 = bf16[32,17,2,128]{3,2,1,0:T(2,128)(2,1)S(1)} async-done(((bf16[32,17,2,128]{3,2,1,0:T(2,128)(2,1)}), bf16[32,17,2,128]{3,2,1,0:T(2,128)(2,1)S(1)}, u32[]{:S(2)}, u32[]{:S(2)}) %all-to-all-start.1) | async-done | bytes 278560 | tf_op jit(solution)/shard_map/all_to_all | solution.py:326
  38.4 3.1 %project.1 = bf16[8,1792]{1,0:T(8,128)(2,1)} custom-call(bf16[1088,128]{1,0:T(8,128)(2,1)S(1)} %bitcast.4, f32[2,56,128]{2,1,0:T(8,128)S(1)} %get-tuple-element.33.out_ref, f32[2,56,128]{2,1,0:T(8,128)S(1)} %get-tuple-element.34.lse_ref, f32[2,56,512]{2,1,0:T(8,128)S(1)} %get-tuple-element.35.match_ref, bf16[768,1792]{1,0:T(8,128)(2,1)S(1)} %get-tuple-element.36.first_ref, ...), custom_call_target="tpu_custom_call" | custom-call | flops 51380224 | bytes 6422528 | tf_op jit(solution)/shard_map/project/pallas_call | solution.py:247
Async XLA Ops:
  0.0 33.3 %copy-start = (bf16[8,1792]{1,0:T(8,128)(2,1)S(1)}, bf16[8,1792]{1,0:T(8,128)(2,1)}, u32[]{:S(2)}) copy-start(bf16[8,1792]{1,0:T(8,128)(2,1)} %q_ref) | copy-start | bytes 86020
  0.0 33.3 %copy-start.1 = (s32[1,14,3]{1,0,2:T(1,128)S(1)}, s32[1,14,3]{1,0,2:T(1,128)}, u32[]{:S(2)}) copy-start(s32[1,14,3]{1,0,2:T(1,128)} %param.12) | copy-start | bytes 508
  2.0 19.3 %all-to-all-start = ((bf16[32,40,128]{2,1,0:T(8,128)(2,1)}), bf16[32,40,128]{2,1,0:T(8,128)(2,1)S(1)}, u32[]{:S(2)}, u32[]{:S(2)}) async-start(bf16[32,40,128]{2,1,0:T(8,128)(2,1)} %bitcast.7), calls=%async_computation | async-start | bytes 655360 | tf_op jit(solution)/shard_map/all_to_all | solution.py:295
  10.4 1.7 %collective-permute-start = (bf16[1024,128]{1,0:T(8,128)(2,1)S(1)}, bf16[1024,128]{1,0:T(8,128)(2,1)S(1)}, u32[]{:S(2)}, u32[]{:S(2)}) collective-permute-start(bf16[1024,128]{1,0:T(8,128)(2,1)S(1)} %get-tuple-element.39), channel_id=1, source_target_pairs={{0,1},{1,0},{2,3},{3,2},{4,5},{5,4},{6,7},{7,6},{8,9},{9,8},{10,11... | collective-permute-start | bytes 786440 | tf_op jit(solution)/shard_map/ppermute | solution.py:303
  11.8 1.6 %collective-permute-start.1 = (bf16[1024,128]{1,0:T(8,128)(2,1)S(1)}, bf16[1024,128]{1,0:T(8,128)(2,1)S(1)}, u32[]{:S(2)}, u32[]{:S(2)}) collective-permute-start(bf16[1024,128]{1,0:T(8,128)(2,1)S(1)} %get-tuple-element.37), channel_id=1, source_target_pairs={{0,1},{1,0},{2,3},{3,2},{4,5},{5,4},{6,7},{7,6},{8,9},{9,8},{10,11... | collective-permute-start | bytes 786440 | tf_op jit(solution)/shard_map/ppermute | solution.py:303
  24.7 13.7 %all-to-all-start.1 = ((bf16[32,17,2,128]{3,2,1,0:T(2,128)(2,1)}), bf16[32,17,2,128]{3,2,1,0:T(2,128)(2,1)S(1)}, u32[]{:S(2)}, u32[]{:S(2)}) async-start(bf16[32,17,2,128]{3,2,1,0:T(2,128)(2,1)} %bitcast.2), calls=%async_computation.1 | async-start | bytes 557056 | tf_op jit(solution)/shard_map/all_to_all | solution.py:326
  27.3 6.0 %collective-permute-start.3 = (bf16[32,8,128]{2,1,0:T(8,128)(2,1)S(1)}, bf16[32,8,128]{2,1,0:T(8,128)(2,1)S(1)}, u32[]{:S(2)}, u32[]{:S(2)}) collective-permute-start(bf16[32,8,128]{2,1,0:T(8,128)(2,1)S(1)} %get-tuple-element.32.kv_ref), channel_id=1, source_target_pairs={{0,2},{1,3},{2,0},{3,1},{4,6},{5,7},{6,4},{7,5},{8,10},{9,11},{10,... | collective-permute-start | bytes 196616 | tf_op jit(solution)/shard_map/ppermute | solution.py:343
  29.0 6.1 %collective-permute-start.2 = (bf16[32,8,128]{2,1,0:T(8,128)(2,1)S(1)}, bf16[32,8,128]{2,1,0:T(8,128)(2,1)S(1)}, u32[]{:S(2)}, u32[]{:S(2)}) collective-permute-start(bf16[32,8,128]{2,1,0:T(8,128)(2,1)S(1)} %get-tuple-element.32.kv_ref), channel_id=1, source_target_pairs={{0,1},{1,0},{2,3},{3,2},{4,5},{5,4},{6,7},{7,6},{8,9},{9,8},{10,11... | collective-permute-start | bytes 196616 | tf_op jit(solution)/shard_map/ppermute | solution.py:344
  33.3 1.8 %collective-permute-start.4 = (bf16[32,8,128]{2,1,0:T(8,128)(2,1)S(1)}, bf16[32,8,128]{2,1,0:T(8,128)(2,1)S(1)}, u32[]{:S(2)}, u32[]{:S(2)}) collective-permute-start(bf16[32,8,128]{2,1,0:T(8,128)(2,1)S(1)} %collective-permute-done.3.kv2_ref), channel_id=1, source_target_pairs={{0,1},{1,0},{2,3},{3,2},{4,5},{5,4},{6,7},{7,6},{8,9},{9,8},{10,11... | collective-permute-start | bytes 196616 | tf_op jit(solution)/shard_map/ppermute | solution.py:344

commit v16 on v15

--- a/solution.py
+++ b/solution.py
@@ -43,8 +43,8 @@
 
 def fetch(pairs, sems):
     copies = [pltpu.make_async_copy(src, dst, sems.at[i]) for i, (src, dst) in enumerate(pairs)]
-    for copy in copies:
-        copy.start()
+    for i, copy in enumerate(copies):
+        copy.start(priority=i % 2)
     return copies
 
 
@@ -82,7 +82,8 @@
 
 
 def masks_kernel(chips, capacity, chosen_ref, q_ref, w_hbm, match_ref, rows_ref, w_ref, sems):
-    copies = fetch([(w_hbm.at[: w_ref.shape[0]], w_ref)], sems)
+    half = w_ref.shape[0] // 2
+    copies = fetch([(w_hbm.at[pl.ds(i * half, half)], w_ref.at[pl.ds(i * half, half)]) for i in range(2)], sems)
     tokens = q_ref.shape[0]
     per = capacity * tokens
     lane = lax.broadcasted_iota(jnp.int32, (tokens, match_ref.shape[2]), 1)
@@ -108,23 +109,27 @@
     ones = jnp.ones(va_ref.shape, jnp.bfloat16)
     fresh_ref[...] = q_ref[:, per:, :]
 
-    def scores(first):
+    def scores(first, k_ref):
         q = q_ref[first : first + step, :per, :].reshape(step * per, HD)
-        return [
-            lax.dot_general(q, k_ref[...], nt, preferred_element_type=jnp.float32) for k_ref in (ka_ref, kb_ref)
-        ]
-
-    ahead = scores(0)
-    for first in range(0, sources, step):
-        sa, sb = ahead
-        if first + step < sources:
-            ahead = scores(first + step)
-        top = scale * jnp.maximum(jnp.max(sa, axis=1, keepdims=True), jnp.max(sb, axis=1, keepdims=True))
-        wa = jnp.exp2(sa * scale - top).astype(jnp.bfloat16)
-        wb = jnp.exp2(sb * scale - top).astype(jnp.bfloat16)
-        both = jnp.dot(
-            wa, jnp.concatenate([va_ref[...], ones], axis=1), preferred_element_type=jnp.float32
-        ) + jnp.dot(wb, jnp.concatenate([vb_ref[...], ones], axis=1), preferred_element_type=jnp.float32)
+        return lax.dot_general(q, k_ref[...], nt, preferred_element_type=jnp.float32)
+
+    sides = [(ka_ref, va_ref), (kb_ref, vb_ref)]
+    turns = [(first, side) for first in range(0, sources, step) for side in range(2)]
+    ahead = scores(0, ka_ref)
+    for turn, (first, side) in enumerate(turns):
+        s = ahead
+        if turn + 1 < len(turns):
+            ahead = scores(turns[turn + 1][0], sides[turns[turn + 1][1]][0])
+        most = scale * jnp.max(s, axis=1, keepdims=True)
+        w = jnp.exp2(s * scale - most).astype(jnp.bfloat16)
+        part_out = jnp.dot(
+            w, jnp.concatenate([sides[side][1][...], ones], axis=1), preferred_element_type=jnp.float32
+        )
+        if side == 0:
+            before, before_most = part_out, most
+            continue
+        top = jnp.maximum(before_most, most)
+        both = before * jnp.exp2(before_most - top) + part_out * jnp.exp2(most - top)
         total = both[:, HD:]
         out = both[:, :HD] / total
         lse = top + jnp.log(total) * LOG2E
@@ -336,7 +341,7 @@
         ),
         [VMEM, VMEM, HBM],
         picks, queries, out_weight,
-        scratch=[pltpu.SemaphoreType.DMA((1,))],
+        scratch=[pltpu.SemaphoreType.DMA((2,))],
         limit=50,
     )
 

time: 41.9 us -> 42.2 us (level)
  no operation moved by 1% of the time
where the time goes in v16:
time: 42.2 us; the launch traced here: 41.8 us
  waiting for transfers between devices  16.3 us (39%)
  starting transfers between devices  12.3 us (29%)
  Pallas kernels  10.9 us (26%)
  local copies, waits for them, and re-layouts  2.14 us (5%)
    pallas_call x5, Pallas kernels, call(): pl.pallas_call(kernel, name=name, out_shape=out_shape, in_specs=specs, ou...  10.9 us
    all_to_all x1, waiting for transfers between devices, body(): got = lax.all_to_all(send, 'seq', split_axis=0, concat_axis=0, tiled=True)  7.91 us
    all_to_all x1, starting transfers between devices, body(): got = lax.all_to_all(send, 'seq', split_axis=0, concat_axis=0, tiled=True)  7.3 us
    ppermute x1, waiting for transfers between devices, body(): far = lax.ppermute(fresh, 'seq', partner(2))  4.31 us
    all_to_all x1, waiting for transfers between devices, body(): hist = lax.all_to_all(back, 'seq', split_axis=0, concat_axis=0, tiled=True)  2.82 us
    all_to_all x1, starting transfers between devices, body(): hist = lax.all_to_all(back, 'seq', split_axis=0, concat_axis=0, tiled=True)  2.6 us
    dynamic_slice x2, local copies, waits for them, and re-layouts, halves(): lax.dynamic_slice_in_dim(x, head * HD, HD, axis=1)  2.13 us
    ppermute x1, starting transfers between devices, body(): far = lax.ppermute(fresh, 'seq', partner(2))  1.7 us
  transfers between devices with their start and end apart: 7, of which 4 were waited for; matrix products, arithmetic and copies ran while one was open for 5% of the time, Pallas kernels for 5%

profile of v16, /device:TPU:0, one launch (start us, length us, event | category | flops | bytes accessed | tf_op | source)
XLA Modules:
  0.0 41.8 jit_solution(17484419498609897836)
XLA Ops:
  0.0 0.0 copy-start
  0.0 0.0 copy-start.1
  0.0 2.0 %pack.1 = bf16[8,2,2,40,128]{4,3,2,1,0:T(8,128)(2,1)} custom-call(s32[3,1,14]{2,1,0:T(1,128)} %bitcast.5, bf16[8,1792]{1,0:T(8,128)(2,1)} %q_ref, bf16[8,256]{1,0:T(8,128)(2,1)} %k_hbm.1, bf16[8,256]{1,0:T(8,128)(2,1)} %v_hbm.1), custom_call_target="tpu_custom_call" | custom-call | tf_op jit(solution)/shard_map/pack/pallas_call | solution.py:252
  2.0 7.3 %all-to-all-start = ((bf16[32,40,128]{2,1,0:T(8,128)(2,1)}), bf16[32,40,128]{2,1,0:T(8,128)(2,1)S(1)}, u32[]{:S(2)}, u32[]{:S(2)}) async-start(bf16[32,40,128]{2,1,0:T(8,128)(2,1)} %bitcast.7), calls=%async_computation | async-start | bytes 655360 | tf_op jit(solution)/shard_map/all_to_all | solution.py:300
  9.4 1.1 %constant_dynamic-slice_fusion.1 = (bf16[1024,128]{1,0:T(8,128)(2,1)S(1)}, bf16[1024,128]{1,0:T(8,128)(2,1)S(1)}) fusion(bf16[1024,256]{1,0:T(8,128)(2,1)} %param.10, s32[]{:T(128)S(6)} %select_n.17, s32[]{:T(128)S(6)} %select_n.16), kind=kLoop, calls=%fused_computation.1 | loop fusion | bytes 1048584 | tf_op jit(solution)/shard_map/dynamic_slice | solution.py:305
  10.4 0.3 collective-permute-start
  10.7 1.1 %constant_dynamic-slice_fusion = (bf16[1024,128]{1,0:T(8,128)(2,1)S(1)}, bf16[1024,128]{1,0:T(8,128)(2,1)S(1)}) fusion(bf16[1024,256]{1,0:T(8,128)(2,1)} %param.11, s32[]{:T(128)S(6)} %select_n.17, s32[]{:T(128)S(6)} %select_n.16), kind=kLoop, calls=%fused_computation | loop fusion | bytes 1048584 | tf_op jit(solution)/shard_map/dynamic_slice | solution.py:305
  11.8 0.3 collective-permute-start.1
  12.1 0.0 collective-permute-done.kb_ref
  12.1 1.3 %collective-permute-done.1.vb_ref = bf16[1024,128]{1,0:T(8,128)(2,1)S(1)} collective-permute-done((bf16[1024,128]{1,0:T(8,128)(2,1)S(1)}, bf16[1024,128]{1,0:T(8,128)(2,1)S(1)}, u32[]{:S(2)}, u32[]{:S(2)}) %collective-permute-start.1) | collective-permute-done | bytes 262176 | tf_op jit(solution)/shard_map/ppermute | solution.py:308
  13.4 7.9 %all-to-all-done.q_ref = bf16[32,40,128]{2,1,0:T(8,128)(2,1)S(1)} async-done(((bf16[32,40,128]{2,1,0:T(8,128)(2,1)}), bf16[32,40,128]{2,1,0:T(8,128)(2,1)S(1)}, u32[]{:S(2)}, u32[]{:S(2)}) %all-to-all-start) | async-done | bytes 327712 | tf_op jit(solution)/shard_map/all_to_all | solution.py:300
  21.3 3.7 %attend.1 = (bf16[1088,128]{1,0:T(8,128)(2,1)}, bf16[32,8,128]{2,1,0:T(8,128)(2,1)S(1)}) custom-call(bf16[32,40,128]{2,1,0:T(8,128)(2,1)S(1)} %all-to-all-done.q_ref, bf16[1024,128]{1,0:T(8,128)(2,1)S(1)} %get-tuple-element.40.ka_ref, bf16[1024,128]{1,0:T(8,128)(2,1)S(1)} %get-tuple-element.38.va_ref, bf16[1024,128]{1,0:T(8,128)(2,1)S(1)} %collective-permute-done.kb_ref, ...), custom_call_target="tpu_custom_call" | custom-call | flops 1073741824 | bytes 4194304 | tf_op jit(solution)/shard_map/attend/pallas_call | solution.py:252
  25.0 2.6 %all-to-all-start.1 = ((bf16[32,17,2,128]{3,2,1,0:T(2,128)(2,1)}), bf16[32,17,2,128]{3,2,1,0:T(2,128)(2,1)S(1)}, u32[]{:S(2)}, u32[]{:S(2)}) async-start(bf16[32,17,2,128]{3,2,1,0:T(2,128)(2,1)} %bitcast.2), calls=%async_computation.1 | async-start | bytes 557056 | tf_op jit(solution)/shard_map/all_to_all | solution.py:331
  27.6 1.7 %collective-permute-start.3 = (bf16[32,8,128]{2,1,0:T(8,128)(2,1)S(1)}, bf16[32,8,128]{2,1,0:T(8,128)(2,1)S(1)}, u32[]{:S(2)}, u32[]{:S(2)}) collective-permute-start(bf16[32,8,128]{2,1,0:T(8,128)(2,1)S(1)} %get-tuple-element.32.kv_ref), channel_id=1, source_target_pairs={{0,2},{1,3},{2,0},{3,1},{4,6},{5,7},{6,4},{7,5},{8,10},{9,11},{10,... | collective-permute-start | bytes 196616 | tf_op jit(solution)/shard_map/ppermute | solution.py:348
  29.3 0.0 collective-permute-start.2
  29.3 4.3 %collective-permute-done.3.kv2_ref = bf16[32,8,128]{2,1,0:T(8,128)(2,1)S(1)} collective-permute-done((bf16[32,8,128]{2,1,0:T(8,128)(2,1)S(1)}, bf16[32,8,128]{2,1,0:T(8,128)(2,1)S(1)}, u32[]{:S(2)}, u32[]{:S(2)}) %collective-permute-start.3) | collective-permute-done | bytes 65568 | tf_op jit(solution)/shard_map/ppermute | solution.py:348
  33.6 0.0 collective-permute-start.4
  33.6 0.0 copy-done
  33.6 0.0 copy-done.1
  33.7 1.8 %masks.1 = (f32[2,56,512]{2,1,0:T(8,128)S(1)}, f32[2,56,128]{2,1,0:T(8,128)S(1)}, bf16[768,1792]{1,0:T(8,128)(2,1)S(1)}) custom-call(s32[3,1,14]{2,1,0:T(1,128)S(1)} %bitcast.6, bf16[8,1792]{1,0:T(8,128)(2,1)S(1)} %copy-done, bf16[1792,1792]{1,0:T(8,128)(2,1)} %w_hbm.1), custom_call_target="tpu_custom_call" | custom-call | tf_op jit(solution)/shard_map/masks/pallas_call | solution.py:252
  35.4 0.0 collective-permute-done.2.kv1_ref
  35.4 0.0 collective-permute-done.4.kv3_ref
  35.5 0.4 %fresh.1 = (f32[2,56,128]{2,1,0:T(8,128)S(1)}, f32[2,56,128]{2,1,0:T(8,128)S(1)}) custom-call(f32[2,56,128]{2,1,0:T(8,128)S(1)} %get-tuple-element.31.rows_ref, bf16[32,8,128]{2,1,0:T(8,128)(2,1)S(1)} %get-tuple-element.32.kv_ref, bf16[32,8,128]{2,1,0:T(8,128)(2,1)S(1)} %collective-permute-done.2.kv1_ref, ...), custom_call_target="tpu_custom_call" | custom-call | flops 29360128 | bytes 1048576 | tf_op jit(solution)/shard_map/fresh/pallas_call | solution.py:252
  35.9 2.8 %all-to-all-done.1 = bf16[32,17,2,128]{3,2,1,0:T(2,128)(2,1)S(1)} async-done(((bf16[32,17,2,128]{3,2,1,0:T(2,128)(2,1)}), bf16[32,17,2,128]{3,2,1,0:T(2,128)(2,1)S(1)}, u32[]{:S(2)}, u32[]{:S(2)}) %all-to-all-start.1) | async-done | bytes 278560 | tf_op jit(solution)/shard_map/all_to_all | solution.py:331
  38.7 3.0 %project.1 = bf16[8,1792]{1,0:T(8,128)(2,1)} custom-call(bf16[1088,128]{1,0:T(8,128)(2,1)S(1)} %bitcast.4, f32[2,56,128]{2,1,0:T(8,128)S(1)} %get-tuple-element.33.out_ref, f32[2,56,128]{2,1,0:T(8,128)S(1)} %get-tuple-element.34.lse_ref, f32[2,56,512]{2,1,0:T(8,128)S(1)} %get-tuple-element.35.match_ref, bf16[768,1792]{1,0:T(8,128)(2,1)S(1)} %get-tuple-element.36.first_ref, ...), custom_call_target="tpu_custom_call" | custom-call | flops 51380224 | bytes 6422528 | tf_op jit(solution)/shard_map/project/pallas_call | solution.py:252
Async XLA Ops:
  0.0 33.6 %copy-start = (bf16[8,1792]{1,0:T(8,128)(2,1)S(1)}, bf16[8,1792]{1,0:T(8,128)(2,1)}, u32[]{:S(2)}) copy-start(bf16[8,1792]{1,0:T(8,128)(2,1)} %q_ref) | copy-start | bytes 86020
  0.0 33.6 %copy-start.1 = (s32[1,14,3]{1,0,2:T(1,128)S(1)}, s32[1,14,3]{1,0,2:T(1,128)}, u32[]{:S(2)}) copy-start(s32[1,14,3]{1,0,2:T(1,128)} %param.12) | copy-start | bytes 508
  2.0 19.3 %all-to-all-start = ((bf16[32,40,128]{2,1,0:T(8,128)(2,1)}), bf16[32,40,128]{2,1,0:T(8,128)(2,1)S(1)}, u32[]{:S(2)}, u32[]{:S(2)}) async-start(bf16[32,40,128]{2,1,0:T(8,128)(2,1)} %bitcast.7), calls=%async_computation | async-start | bytes 655360 | tf_op jit(solution)/shard_map/all_to_all | solution.py:300
  10.4 1.7 %collective-permute-start = (bf16[1024,128]{1,0:T(8,128)(2,1)S(1)}, bf16[1024,128]{1,0:T(8,128)(2,1)S(1)}, u32[]{:S(2)}, u32[]{:S(2)}) collective-permute-start(bf16[1024,128]{1,0:T(8,128)(2,1)S(1)} %get-tuple-element.39), channel_id=1, source_target_pairs={{0,1},{1,0},{2,3},{3,2},{4,5},{5,4},{6,7},{7,6},{8,9},{9,8},{10,11... | collective-permute-start | bytes 786440 | tf_op jit(solution)/shard_map/ppermute | solution.py:308
  11.8 1.6 %collective-permute-start.1 = (bf16[1024,128]{1,0:T(8,128)(2,1)S(1)}, bf16[1024,128]{1,0:T(8,128)(2,1)S(1)}, u32[]{:S(2)}, u32[]{:S(2)}) collective-permute-start(bf16[1024,128]{1,0:T(8,128)(2,1)S(1)} %get-tuple-element.37), channel_id=1, source_target_pairs={{0,1},{1,0},{2,3},{3,2},{4,5},{5,4},{6,7},{7,6},{8,9},{9,8},{10,11... | collective-permute-start | bytes 786440 | tf_op jit(solution)/shard_map/ppermute | solution.py:308
  25.0 13.7 %all-to-all-start.1 = ((bf16[32,17,2,128]{3,2,1,0:T(2,128)(2,1)}), bf16[32,17,2,128]{3,2,1,0:T(2,128)(2,1)S(1)}, u32[]{:S(2)}, u32[]{:S(2)}) async-start(bf16[32,17,2,128]{3,2,1,0:T(2,128)(2,1)} %bitcast.2), calls=%async_computation.1 | async-start | bytes 557056 | tf_op jit(solution)/shard_map/all_to_all | solution.py:331
  27.6 6.0 %collective-permute-start.3 = (bf16[32,8,128]{2,1,0:T(8,128)(2,1)S(1)}, bf16[32,8,128]{2,1,0:T(8,128)(2,1)S(1)}, u32[]{:S(2)}, u32[]{:S(2)}) collective-permute-start(bf16[32,8,128]{2,1,0:T(8,128)(2,1)S(1)} %get-tuple-element.32.kv_ref), channel_id=1, source_target_pairs={{0,2},{1,3},{2,0},{3,1},{4,6},{5,7},{6,4},{7,5},{8,10},{9,11},{10,... | collective-permute-start | bytes 196616 | tf_op jit(solution)/shard_map/ppermute | solution.py:348
  29.3 6.1 %collective-permute-start.2 = (bf16[32,8,128]{2,1,0:T(8,128)(2,1)S(1)}, bf16[32,8,128]{2,1,0:T(8,128)(2,1)S(1)}, u32[]{:S(2)}, u32[]{:S(2)}) collective-permute-start(bf16[32,8,128]{2,1,0:T(8,128)(2,1)S(1)} %get-tuple-element.32.kv_ref), channel_id=1, source_target_pairs={{0,1},{1,0},{2,3},{3,2},{4,5},{5,4},{6,7},{7,6},{8,9},{9,8},{10,11... | collective-permute-start | bytes 196616 | tf_op jit(solution)/shard_map/ppermute | solution.py:349
  33.6 1.8 %collective-permute-start.4 = (bf16[32,8,128]{2,1,0:T(8,128)(2,1)S(1)}, bf16[32,8,128]{2,1,0:T(8,128)(2,1)S(1)}, u32[]{:S(2)}, u32[]{:S(2)}) collective-permute-start(bf16[32,8,128]{2,1,0:T(8,128)(2,1)S(1)} %collective-permute-done.3.kv2_ref), channel_id=1, source_target_pairs={{0,1},{1,0},{2,3},{3,2},{4,5},{5,4},{6,7},{7,6},{8,9},{9,8},{10,11... | collective-permute-start | bytes 196616 | tf_op jit(solution)/shard_map/ppermute | solution.py:349

commit v17 on v15

--- a/solution.py
+++ b/solution.py
@@ -109,9 +109,15 @@
     fresh_ref[...] = q_ref[:, per:, :]
 
     def scores(first):
-        q = q_ref[first : first + step, :per, :].reshape(step * per, HD)
+        q = q_ref[first : first + step, :per, :].reshape(step * per, HD).astype(jnp.float32) * scale
+        high = q.astype(jnp.bfloat16)
+        low = (q - high.astype(jnp.float32)).astype(jnp.bfloat16)
+        q = jnp.concatenate([high, low], axis=1)
         return [
-            lax.dot_general(q, k_ref[...], nt, preferred_element_type=jnp.float32) for k_ref in (ka_ref, kb_ref)
+            lax.dot_general(
+                q, jnp.concatenate([k_ref[...]] * 2, axis=1), nt, preferred_element_type=jnp.float32
+            )
+            for k_ref in (ka_ref, kb_ref)
         ]
 
     ahead = scores(0)
@@ -119,9 +125,9 @@
         sa, sb = ahead
         if first + step < sources:
             ahead = scores(first + step)
-        top = scale * jnp.maximum(jnp.max(sa, axis=1, keepdims=True), jnp.max(sb, axis=1, keepdims=True))
-        wa = jnp.exp2(sa * scale - top).astype(jnp.bfloat16)
-        wb = jnp.exp2(sb * scale - top).astype(jnp.bfloat16)
+        top = jnp.maximum(jnp.max(sa, axis=1, keepdims=True), jnp.max(sb, axis=1, keepdims=True))
+        wa = jnp.exp2(sa - top).astype(jnp.bfloat16)
+        wb = jnp.exp2(sb - top).astype(jnp.bfloat16)
         both = jnp.dot(
             wa, jnp.concatenate([va_ref[...], ones], axis=1), preferred_element_type=jnp.float32
         ) + jnp.dot(wb, jnp.concatenate([vb_ref[...], ones], axis=1), preferred_element_type=jnp.float32)

time: 41.9 us -> 41.9 us (level)
  no operation moved by 1% of the time
where the time goes in v17:
time: 41.9 us; the launch traced here: 41.5 us
  waiting for transfers between devices  16.3 us (39%)
  starting transfers between devices  12.3 us (29%)
  Pallas kernels  10.7 us (26%)
  local copies, waits for them, and re-layouts  2.14 us (5%)
    pallas_call x5, Pallas kernels, call(): pl.pallas_call(kernel, name=name, out_shape=out_shape, in_specs=specs, ou...  10.7 us
    all_to_all x1, waiting for transfers between devices, body(): got = lax.all_to_all(send, 'seq', split_axis=0, concat_axis=0, tiled=True)  7.91 us
    all_to_all x1, starting transfers between devices, body(): got = lax.all_to_all(send, 'seq', split_axis=0, concat_axis=0, tiled=True)  7.3 us
    ppermute x1, waiting for transfers between devices, body(): far = lax.ppermute(fresh, 'seq', partner(2))  4.31 us
    all_to_all x1, waiting for transfers between devices, body(): hist = lax.all_to_all(back, 'seq', split_axis=0, concat_axis=0, tiled=True)  2.8 us
    all_to_all x1, starting transfers between devices, body(): hist = lax.all_to_all(back, 'seq', split_axis=0, concat_axis=0, tiled=True)  2.6 us
    dynamic_slice x2, local copies, waits for them, and re-layouts, halves(): lax.dynamic_slice_in_dim(x, head * HD, HD, axis=1)  2.13 us
    ppermute x1, starting transfers between devices, body(): far = lax.ppermute(fresh, 'seq', partner(2))  1.7 us
  transfers between devices with their start and end apart: 7, of which 4 were waited for; matrix products, arithmetic and copies ran while one was open for 5% of the time, Pallas kernels for 5%

profile of v17, /device:TPU:0, one launch (start us, length us, event | category | flops | bytes accessed | tf_op | source)
XLA Modules:
  0.0 41.5 jit_solution(15229525156665858269)
XLA Ops:
  0.0 0.0 copy-start
  0.0 0.0 copy-start.1
  0.0 2.0 %pack.1 = bf16[8,2,2,40,128]{4,3,2,1,0:T(8,128)(2,1)} custom-call(s32[3,1,14]{2,1,0:T(1,128)} %bitcast.5, bf16[8,1792]{1,0:T(8,128)(2,1)} %q_ref, bf16[8,256]{1,0:T(8,128)(2,1)} %k_hbm.1, bf16[8,256]{1,0:T(8,128)(2,1)} %v_hbm.1), custom_call_target="tpu_custom_call" | custom-call | tf_op jit(solution)/shard_map/pack/pallas_call | solution.py:253
  2.0 7.3 %all-to-all-start = ((bf16[32,40,128]{2,1,0:T(8,128)(2,1)}), bf16[32,40,128]{2,1,0:T(8,128)(2,1)S(1)}, u32[]{:S(2)}, u32[]{:S(2)}) async-start(bf16[32,40,128]{2,1,0:T(8,128)(2,1)} %bitcast.7), calls=%async_computation | async-start | bytes 655360 | tf_op jit(solution)/shard_map/all_to_all | solution.py:301
  9.4 1.1 %constant_dynamic-slice_fusion.1 = (bf16[1024,128]{1,0:T(8,128)(2,1)S(1)}, bf16[1024,128]{1,0:T(8,128)(2,1)S(1)}) fusion(bf16[1024,256]{1,0:T(8,128)(2,1)} %param.10, s32[]{:T(128)S(6)} %select_n.17, s32[]{:T(128)S(6)} %select_n.16), kind=kLoop, calls=%fused_computation.1 | loop fusion | bytes 1048584 | tf_op jit(solution)/shard_map/dynamic_slice | solution.py:306
  10.4 0.3 collective-permute-start
  10.7 1.1 %constant_dynamic-slice_fusion = (bf16[1024,128]{1,0:T(8,128)(2,1)S(1)}, bf16[1024,128]{1,0:T(8,128)(2,1)S(1)}) fusion(bf16[1024,256]{1,0:T(8,128)(2,1)} %param.11, s32[]{:T(128)S(6)} %select_n.17, s32[]{:T(128)S(6)} %select_n.16), kind=kLoop, calls=%fused_computation | loop fusion | bytes 1048584 | tf_op jit(solution)/shard_map/dynamic_slice | solution.py:306
  11.8 0.3 collective-permute-start.1
  12.1 0.0 collective-permute-done.kb_ref
  12.1 1.3 %collective-permute-done.1.vb_ref = bf16[1024,128]{1,0:T(8,128)(2,1)S(1)} collective-permute-done((bf16[1024,128]{1,0:T(8,128)(2,1)S(1)}, bf16[1024,128]{1,0:T(8,128)(2,1)S(1)}, u32[]{:S(2)}, u32[]{:S(2)}) %collective-permute-start.1) | collective-permute-done | bytes 262176 | tf_op jit(solution)/shard_map/ppermute | solution.py:309
  13.4 7.9 %all-to-all-done.q_ref = bf16[32,40,128]{2,1,0:T(8,128)(2,1)S(1)} async-done(((bf16[32,40,128]{2,1,0:T(8,128)(2,1)}), bf16[32,40,128]{2,1,0:T(8,128)(2,1)S(1)}, u32[]{:S(2)}, u32[]{:S(2)}) %all-to-all-start) | async-done | bytes 327712 | tf_op jit(solution)/shard_map/all_to_all | solution.py:301
  21.3 3.4 %attend.1 = (bf16[1088,128]{1,0:T(8,128)(2,1)}, bf16[32,8,128]{2,1,0:T(8,128)(2,1)S(1)}) custom-call(bf16[32,40,128]{2,1,0:T(8,128)(2,1)S(1)} %all-to-all-done.q_ref, bf16[1024,128]{1,0:T(8,128)(2,1)S(1)} %get-tuple-element.40.ka_ref, bf16[1024,128]{1,0:T(8,128)(2,1)S(1)} %get-tuple-element.38.va_ref, bf16[1024,128]{1,0:T(8,128)(2,1)S(1)} %collective-permute-done.kb_ref, ...), custom_call_target="tpu_custom_call" | custom-call | flops 1073741824 | bytes 4194304 | tf_op jit(solution)/shard_map/attend/pallas_call | solution.py:253
  24.7 2.6 %all-to-all-start.1 = ((bf16[32,17,2,128]{3,2,1,0:T(2,128)(2,1)}), bf16[32,17,2,128]{3,2,1,0:T(2,128)(2,1)S(1)}, u32[]{:S(2)}, u32[]{:S(2)}) async-start(bf16[32,17,2,128]{3,2,1,0:T(2,128)(2,1)} %bitcast.2), calls=%async_computation.1 | async-start | bytes 557056 | tf_op jit(solution)/shard_map/all_to_all | solution.py:332
  27.3 1.7 %collective-permute-start.3 = (bf16[32,8,128]{2,1,0:T(8,128)(2,1)S(1)}, bf16[32,8,128]{2,1,0:T(8,128)(2,1)S(1)}, u32[]{:S(2)}, u32[]{:S(2)}) collective-permute-start(bf16[32,8,128]{2,1,0:T(8,128)(2,1)S(1)} %get-tuple-element.32.kv_ref), channel_id=1, source_target_pairs={{0,2},{1,3},{2,0},{3,1},{4,6},{5,7},{6,4},{7,5},{8,10},{9,11},{10,... | collective-permute-start | bytes 196616 | tf_op jit(solution)/shard_map/ppermute | solution.py:349
  29.0 0.0 collective-permute-start.2
  29.0 4.3 %collective-permute-done.3.kv2_ref = bf16[32,8,128]{2,1,0:T(8,128)(2,1)S(1)} collective-permute-done((bf16[32,8,128]{2,1,0:T(8,128)(2,1)S(1)}, bf16[32,8,128]{2,1,0:T(8,128)(2,1)S(1)}, u32[]{:S(2)}, u32[]{:S(2)}) %collective-permute-start.3) | collective-permute-done | bytes 65568 | tf_op jit(solution)/shard_map/ppermute | solution.py:349
  33.3 0.0 collective-permute-start.4
  33.3 0.0 copy-done
  33.3 0.0 copy-done.1
  33.4 1.8 %masks.1 = (f32[2,56,512]{2,1,0:T(8,128)S(1)}, f32[2,56,128]{2,1,0:T(8,128)S(1)}, bf16[768,1792]{1,0:T(8,128)(2,1)S(1)}) custom-call(s32[3,1,14]{2,1,0:T(1,128)S(1)} %bitcast.6, bf16[8,1792]{1,0:T(8,128)(2,1)S(1)} %copy-done, bf16[1792,1792]{1,0:T(8,128)(2,1)} %w_hbm.1), custom_call_target="tpu_custom_call" | custom-call | tf_op jit(solution)/shard_map/masks/pallas_call | solution.py:253
  35.1 0.0 collective-permute-done.2.kv1_ref
  35.2 0.0 collective-permute-done.4.kv3_ref
  35.2 0.4 %fresh.1 = (f32[2,56,128]{2,1,0:T(8,128)S(1)}, f32[2,56,128]{2,1,0:T(8,128)S(1)}) custom-call(f32[2,56,128]{2,1,0:T(8,128)S(1)} %get-tuple-element.31.rows_ref, bf16[32,8,128]{2,1,0:T(8,128)(2,1)S(1)} %get-tuple-element.32.kv_ref, bf16[32,8,128]{2,1,0:T(8,128)(2,1)S(1)} %collective-permute-done.2.kv1_ref, ...), custom_call_target="tpu_custom_call" | custom-call | flops 29360128 | bytes 1048576 | tf_op jit(solution)/shard_map/fresh/pallas_call | solution.py:253
  35.6 2.8 %all-to-all-done.1 = bf16[32,17,2,128]{3,2,1,0:T(2,128)(2,1)S(1)} async-done(((bf16[32,17,2,128]{3,2,1,0:T(2,128)(2,1)}), bf16[32,17,2,128]{3,2,1,0:T(2,128)(2,1)S(1)}, u32[]{:S(2)}, u32[]{:S(2)}) %all-to-all-start.1) | async-done | bytes 278560 | tf_op jit(solution)/shard_map/all_to_all | solution.py:332
  38.4 3.1 %project.1 = bf16[8,1792]{1,0:T(8,128)(2,1)} custom-call(bf16[1088,128]{1,0:T(8,128)(2,1)S(1)} %bitcast.4, f32[2,56,128]{2,1,0:T(8,128)S(1)} %get-tuple-element.33.out_ref, f32[2,56,128]{2,1,0:T(8,128)S(1)} %get-tuple-element.34.lse_ref, f32[2,56,512]{2,1,0:T(8,128)S(1)} %get-tuple-element.35.match_ref, bf16[768,1792]{1,0:T(8,128)(2,1)S(1)} %get-tuple-element.36.first_ref, ...), custom_call_target="tpu_custom_call" | custom-call | flops 51380224 | bytes 6422528 | tf_op jit(solution)/shard_map/project/pallas_call | solution.py:253
Async XLA Ops:
  0.0 33.3 %copy-start = (bf16[8,1792]{1,0:T(8,128)(2,1)S(1)}, bf16[8,1792]{1,0:T(8,128)(2,1)}, u32[]{:S(2)}) copy-start(bf16[8,1792]{1,0:T(8,128)(2,1)} %q_ref) | copy-start | bytes 86020
  0.0 33.3 %copy-start.1 = (s32[1,14,3]{1,0,2:T(1,128)S(1)}, s32[1,14,3]{1,0,2:T(1,128)}, u32[]{:S(2)}) copy-start(s32[1,14,3]{1,0,2:T(1,128)} %param.12) | copy-start | bytes 508
  2.0 19.3 %all-to-all-start = ((bf16[32,40,128]{2,1,0:T(8,128)(2,1)}), bf16[32,40,128]{2,1,0:T(8,128)(2,1)S(1)}, u32[]{:S(2)}, u32[]{:S(2)}) async-start(bf16[32,40,128]{2,1,0:T(8,128)(2,1)} %bitcast.7), calls=%async_computation | async-start | bytes 655360 | tf_op jit(solution)/shard_map/all_to_all | solution.py:301
  10.4 1.7 %collective-permute-start = (bf16[1024,128]{1,0:T(8,128)(2,1)S(1)}, bf16[1024,128]{1,0:T(8,128)(2,1)S(1)}, u32[]{:S(2)}, u32[]{:S(2)}) collective-permute-start(bf16[1024,128]{1,0:T(8,128)(2,1)S(1)} %get-tuple-element.39), channel_id=1, source_target_pairs={{0,1},{1,0},{2,3},{3,2},{4,5},{5,4},{6,7},{7,6},{8,9},{9,8},{10,11... | collective-permute-start | bytes 786440 | tf_op jit(solution)/shard_map/ppermute | solution.py:309
  11.8 1.6 %collective-permute-start.1 = (bf16[1024,128]{1,0:T(8,128)(2,1)S(1)}, bf16[1024,128]{1,0:T(8,128)(2,1)S(1)}, u32[]{:S(2)}, u32[]{:S(2)}) collective-permute-start(bf16[1024,128]{1,0:T(8,128)(2,1)S(1)} %get-tuple-element.37), channel_id=1, source_target_pairs={{0,1},{1,0},{2,3},{3,2},{4,5},{5,4},{6,7},{7,6},{8,9},{9,8},{10,11... | collective-permute-start | bytes 786440 | tf_op jit(solution)/shard_map/ppermute | solution.py:309
  24.7 13.7 %all-to-all-start.1 = ((bf16[32,17,2,128]{3,2,1,0:T(2,128)(2,1)}), bf16[32,17,2,128]{3,2,1,0:T(2,128)(2,1)S(1)}, u32[]{:S(2)}, u32[]{:S(2)}) async-start(bf16[32,17,2,128]{3,2,1,0:T(2,128)(2,1)} %bitcast.2), calls=%async_computation.1 | async-start | bytes 557056 | tf_op jit(solution)/shard_map/all_to_all | solution.py:332
  27.3 6.0 %collective-permute-start.3 = (bf16[32,8,128]{2,1,0:T(8,128)(2,1)S(1)}, bf16[32,8,128]{2,1,0:T(8,128)(2,1)S(1)}, u32[]{:S(2)}, u32[]{:S(2)}) collective-permute-start(bf16[32,8,128]{2,1,0:T(8,128)(2,1)S(1)} %get-tuple-element.32.kv_ref), channel_id=1, source_target_pairs={{0,2},{1,3},{2,0},{3,1},{4,6},{5,7},{6,4},{7,5},{8,10},{9,11},{10,... | collective-permute-start | bytes 196616 | tf_op jit(solution)/shard_map/ppermute | solution.py:349
  29.0 6.1 %collective-permute-start.2 = (bf16[32,8,128]{2,1,0:T(8,128)(2,1)S(1)}, bf16[32,8,128]{2,1,0:T(8,128)(2,1)S(1)}, u32[]{:S(2)}, u32[]{:S(2)}) collective-permute-start(bf16[32,8,128]{2,1,0:T(8,128)(2,1)S(1)} %get-tuple-element.32.kv_ref), channel_id=1, source_target_pairs={{0,1},{1,0},{2,3},{3,2},{4,5},{5,4},{6,7},{7,6},{8,9},{9,8},{10,11... | collective-permute-start | bytes 196616 | tf_op jit(solution)/shard_map/ppermute | solution.py:350
  33.3 1.8 %collective-permute-start.4 = (bf16[32,8,128]{2,1,0:T(8,128)(2,1)S(1)}, bf16[32,8,128]{2,1,0:T(8,128)(2,1)S(1)}, u32[]{:S(2)}, u32[]{:S(2)}) collective-permute-start(bf16[32,8,128]{2,1,0:T(8,128)(2,1)S(1)} %collective-permute-done.3.kv2_ref), channel_id=1, source_target_pairs={{0,1},{1,0},{2,3},{3,2},{4,5},{5,4},{6,7},{7,6},{8,9},{9,8},{10,11... | collective-permute-start | bytes 196616 | tf_op jit(solution)/shard_map/ppermute | solution.py:350

commit v18 on v15

--- a/solution.py
+++ b/solution.py
@@ -48,26 +48,46 @@
     return copies
 
 
+def slot_spread(chosen_ref, g, capacity, tokens, key_blocks):
+    lane = lax.broadcasted_iota(jnp.int32, (tokens, LANES), 1)
+    head = lane // tokens
+    same_token = (lane % tokens == lax.broadcasted_iota(jnp.int32, lane.shape, 0)) & (head < GROUP)
+    picks = [[chosen_ref[t, 0, g * GROUP + r] for r in range(GROUP)] for t in range(TOPK)]
+    places = []
+    for t in range(TOPK):
+        block = jnp.zeros(lane.shape, jnp.int32)
+        for r in range(GROUP):
+            block = jnp.where(head == r, picks[t][r], block)
+        rank = jnp.zeros(lane.shape, jnp.int32)
+        for r in range(GROUP - 1):
+            taken = block == picks[0][r]
+            for other in range(1, TOPK):
+                taken = taken | (block == picks[other][r])
+            rank = rank + jnp.where(taken & (head > r), 1, 0)
+        places.append(jnp.where(same_token, block * capacity + rank, -1))
+    rows = []
+    for place in range(key_blocks * capacity):
+        found = places[0] == place
+        for t in range(1, TOPK):
+            found = found | (places[t] == place)
+        rows.append(jnp.where(found, 1.0, 0.0))
+    return jnp.concatenate(rows, axis=0).astype(jnp.bfloat16)
+
+
 def pack_kernel(capacity, chosen_hbm, q_hbm, k_hbm, v_hbm, send_hbm, chosen_ref, q_ref, k_ref, v_ref, send_ref, sems):
     copies = fetch([(chosen_hbm, chosen_ref), (q_hbm, q_ref), (k_hbm, k_ref), (v_hbm, v_ref)], sems)
     tokens = q_ref.shape[0]
     per = capacity * tokens
     key_blocks, chips = send_ref.shape[1:3]
-    lane = lax.broadcasted_iota(jnp.int32, (tokens, key_blocks * per), 1)
-    block, slot, token = lane // per, lane % per // tokens, lane % tokens
     copies[0].wait()
-    spread = [
-        jnp.concatenate(
-            slot_match(chosen_ref, g, block, slot, token) + [jnp.zeros(lane.shape, jnp.float32)], axis=0
-        ).T.astype(jnp.bfloat16)
-        for g in range(KVH)
-    ]
+    spread = [slot_spread(chosen_ref, g, capacity, tokens, key_blocks) for g in range(KVH)]
     for copy in copies[1:]:
         copy.wait()
     sent = []
     for g in range(KVH):
         rows = head_rows(q_ref, g)
-        rows = jnp.concatenate(rows + [jnp.zeros_like(rows[0])], axis=0).astype(jnp.bfloat16)
+        rows = rows + [jnp.zeros_like(rows[0])] * (LANES // tokens - GROUP)
+        rows = jnp.concatenate(rows, axis=0).astype(jnp.bfloat16)
         slots = jnp.dot(spread[g], rows, preferred_element_type=jnp.float32).astype(jnp.bfloat16)
         cols = slice(g * HD, (g + 1) * HD)
         fresh = [k_ref[:, cols], v_ref[:, cols]]
@@ -120,8 +140,8 @@
         if first + step < sources:
             ahead = scores(first + step)
         top = scale * jnp.maximum(jnp.max(sa, axis=1, keepdims=True), jnp.max(sb, axis=1, keepdims=True))
-        wa = jnp.exp2(sa * scale - top).astype(jnp.bfloat16)
-        wb = jnp.exp2(sb * scale - top).astype(jnp.bfloat16)
+        wa = jnp.exp2((sa * scale - top).astype(jnp.bfloat16))
+        wb = jnp.exp2((sb * scale - top).astype(jnp.bfloat16))
         both = jnp.dot(
             wa, jnp.concatenate([va_ref[...], ones], axis=1), preferred_element_type=jnp.float32
         ) + jnp.dot(wb, jnp.concatenate([vb_ref[...], ones], axis=1), preferred_element_type=jnp.float32)
@@ -279,7 +299,7 @@
         picks, queries, stretch_keys, stretch_values,
         outs=ANY,
         scratch=[
-            pltpu.VMEM(picks.shape, jnp.int32),
+            pltpu.SMEM(picks.shape, jnp.int32),
             pltpu.VMEM(queries.shape, bf16),
             pltpu.VMEM(stretch_keys.shape, bf16),
             pltpu.VMEM(stretch_values.shape, bf16),

time: 41.9 us -> 42.1 us (level)
  no operation moved by 1% of the time
where the time goes in v18:
time: 42.1 us; the launch traced here: 41.7 us
  waiting for transfers between devices  16.3 us (39%)
  starting transfers between devices  12.3 us (29%)
  Pallas kernels  10.9 us (26%)
  local copies, waits for them, and re-layouts  2.14 us (5%)
    pallas_call x5, Pallas kernels, call(): pl.pallas_call(kernel, name=name, out_shape=out_shape, in_specs=specs, ou...  10.9 us
    all_to_all x1, waiting for transfers between devices, body(): got = lax.all_to_all(send, 'seq', split_axis=0, concat_axis=0, tiled=True)  7.91 us
    all_to_all x1, starting transfers between devices, body(): got = lax.all_to_all(send, 'seq', split_axis=0, concat_axis=0, tiled=True)  7.3 us
    ppermute x1, waiting for transfers between devices, body(): far = lax.ppermute(fresh, 'seq', partner(2))  4.31 us
    all_to_all x1, waiting for transfers between devices, body(): hist = lax.all_to_all(back, 'seq', split_axis=0, concat_axis=0, tiled=True)  2.8 us
    all_to_all x1, starting transfers between devices, body(): hist = lax.all_to_all(back, 'seq', split_axis=0, concat_axis=0, tiled=True)  2.6 us
    dynamic_slice x2, local copies, waits for them, and re-layouts, halves(): lax.dynamic_slice_in_dim(x, head * HD, HD, axis=1)  2.13 us
    ppermute x1, starting transfers between devices, body(): far = lax.ppermute(fresh, 'seq', partner(2))  1.7 us
  transfers between devices with their start and end apart: 7, of which 4 were waited for; matrix products, arithmetic and copies ran while one was open for 5% of the time, Pallas kernels for 5%

profile of v18, /device:TPU:0, one launch (start us, length us, event | category | flops | bytes accessed | tf_op | source)
XLA Modules:
  0.0 41.7 jit_solution(4712425421364707150)
XLA Ops:
  0.0 0.0 copy-start
  0.0 0.0 copy-start.1
  0.0 1.9 %pack.1 = bf16[8,2,2,40,128]{4,3,2,1,0:T(8,128)(2,1)} custom-call(s32[3,1,14]{2,1,0:T(1,128)} %bitcast.5, bf16[8,1792]{1,0:T(8,128)(2,1)} %q_ref, bf16[8,256]{1,0:T(8,128)(2,1)} %k_hbm.1, bf16[8,256]{1,0:T(8,128)(2,1)} %v_hbm.1), custom_call_target="tpu_custom_call" | custom-call | tf_op jit(solution)/shard_map/pack/pallas_call | solution.py:267
  1.9 7.3 %all-to-all-start = ((bf16[32,40,128]{2,1,0:T(8,128)(2,1)}), bf16[32,40,128]{2,1,0:T(8,128)(2,1)S(1)}, u32[]{:S(2)}, u32[]{:S(2)}) async-start(bf16[32,40,128]{2,1,0:T(8,128)(2,1)} %bitcast.7), calls=%async_computation | async-start | bytes 655360 | tf_op jit(solution)/shard_map/all_to_all | solution.py:315
  9.2 1.1 %constant_dynamic-slice_fusion.1 = (bf16[1024,128]{1,0:T(8,128)(2,1)S(1)}, bf16[1024,128]{1,0:T(8,128)(2,1)S(1)}) fusion(bf16[1024,256]{1,0:T(8,128)(2,1)} %param.10, s32[]{:T(128)S(6)} %select_n.17, s32[]{:T(128)S(6)} %select_n.16), kind=kLoop, calls=%fused_computation.1 | loop fusion | bytes 1048584 | tf_op jit(solution)/shard_map/dynamic_slice | solution.py:320
  10.3 0.3 collective-permute-start
  10.6 1.1 %constant_dynamic-slice_fusion = (bf16[1024,128]{1,0:T(8,128)(2,1)S(1)}, bf16[1024,128]{1,0:T(8,128)(2,1)S(1)}) fusion(bf16[1024,256]{1,0:T(8,128)(2,1)} %param.11, s32[]{:T(128)S(6)} %select_n.17, s32[]{:T(128)S(6)} %select_n.16), kind=kLoop, calls=%fused_computation | loop fusion | bytes 1048584 | tf_op jit(solution)/shard_map/dynamic_slice | solution.py:320
  11.7 0.3 collective-permute-start.1
  12.0 0.0 collective-permute-done.kb_ref
  12.0 1.3 %collective-permute-done.1.vb_ref = bf16[1024,128]{1,0:T(8,128)(2,1)S(1)} collective-permute-done((bf16[1024,128]{1,0:T(8,128)(2,1)S(1)}, bf16[1024,128]{1,0:T(8,128)(2,1)S(1)}, u32[]{:S(2)}, u32[]{:S(2)}) %collective-permute-start.1) | collective-permute-done | bytes 262176 | tf_op jit(solution)/shard_map/ppermute | solution.py:323
  13.3 7.9 %all-to-all-done.q_ref = bf16[32,40,128]{2,1,0:T(8,128)(2,1)S(1)} async-done(((bf16[32,40,128]{2,1,0:T(8,128)(2,1)}), bf16[32,40,128]{2,1,0:T(8,128)(2,1)S(1)}, u32[]{:S(2)}, u32[]{:S(2)}) %all-to-all-start) | async-done | bytes 327712 | tf_op jit(solution)/shard_map/all_to_all | solution.py:315
  21.2 3.7 %attend.1 = (bf16[1088,128]{1,0:T(8,128)(2,1)}, bf16[32,8,128]{2,1,0:T(8,128)(2,1)S(1)}) custom-call(bf16[32,40,128]{2,1,0:T(8,128)(2,1)S(1)} %all-to-all-done.q_ref, bf16[1024,128]{1,0:T(8,128)(2,1)S(1)} %get-tuple-element.40.ka_ref, bf16[1024,128]{1,0:T(8,128)(2,1)S(1)} %get-tuple-element.38.va_ref, bf16[1024,128]{1,0:T(8,128)(2,1)S(1)} %collective-permute-done.kb_ref, ...), custom_call_target="tpu_custom_call" | custom-call | flops 1073741824 | bytes 4194304 | tf_op jit(solution)/shard_map/attend/pallas_call | solution.py:267
  24.9 2.6 %all-to-all-start.1 = ((bf16[32,17,2,128]{3,2,1,0:T(2,128)(2,1)}), bf16[32,17,2,128]{3,2,1,0:T(2,128)(2,1)S(1)}, u32[]{:S(2)}, u32[]{:S(2)}) async-start(bf16[32,17,2,128]{3,2,1,0:T(2,128)(2,1)} %bitcast.2), calls=%async_computation.1 | async-start | bytes 557056 | tf_op jit(solution)/shard_map/all_to_all | solution.py:346
  27.6 1.7 %collective-permute-start.3 = (bf16[32,8,128]{2,1,0:T(8,128)(2,1)S(1)}, bf16[32,8,128]{2,1,0:T(8,128)(2,1)S(1)}, u32[]{:S(2)}, u32[]{:S(2)}) collective-permute-start(bf16[32,8,128]{2,1,0:T(8,128)(2,1)S(1)} %get-tuple-element.32.kv_ref), channel_id=1, source_target_pairs={{0,2},{1,3},{2,0},{3,1},{4,6},{5,7},{6,4},{7,5},{8,10},{9,11},{10,... | collective-permute-start | bytes 196616 | tf_op jit(solution)/shard_map/ppermute | solution.py:363
  29.3 0.0 collective-permute-start.2
  29.3 4.3 %collective-permute-done.3.kv2_ref = bf16[32,8,128]{2,1,0:T(8,128)(2,1)S(1)} collective-permute-done((bf16[32,8,128]{2,1,0:T(8,128)(2,1)S(1)}, bf16[32,8,128]{2,1,0:T(8,128)(2,1)S(1)}, u32[]{:S(2)}, u32[]{:S(2)}) %collective-permute-start.3) | collective-permute-done | bytes 65568 | tf_op jit(solution)/shard_map/ppermute | solution.py:363
  33.6 0.0 collective-permute-start.4
  33.6 0.0 copy-done
  33.6 0.0 copy-done.1
  33.6 1.8 %masks.1 = (f32[2,56,512]{2,1,0:T(8,128)S(1)}, f32[2,56,128]{2,1,0:T(8,128)S(1)}, bf16[768,1792]{1,0:T(8,128)(2,1)S(1)}) custom-call(s32[3,1,14]{2,1,0:T(1,128)S(1)} %bitcast.6, bf16[8,1792]{1,0:T(8,128)(2,1)S(1)} %copy-done, bf16[1792,1792]{1,0:T(8,128)(2,1)} %w_hbm.1), custom_call_target="tpu_custom_call" | custom-call | tf_op jit(solution)/shard_map/masks/pallas_call | solution.py:267
  35.4 0.0 collective-permute-done.2.kv1_ref
  35.4 0.0 collective-permute-done.4.kv3_ref
  35.4 0.4 %fresh.1 = (f32[2,56,128]{2,1,0:T(8,128)S(1)}, f32[2,56,128]{2,1,0:T(8,128)S(1)}) custom-call(f32[2,56,128]{2,1,0:T(8,128)S(1)} %get-tuple-element.31.rows_ref, bf16[32,8,128]{2,1,0:T(8,128)(2,1)S(1)} %get-tuple-element.32.kv_ref, bf16[32,8,128]{2,1,0:T(8,128)(2,1)S(1)} %collective-permute-done.2.kv1_ref, ...), custom_call_target="tpu_custom_call" | custom-call | flops 29360128 | bytes 1048576 | tf_op jit(solution)/shard_map/fresh/pallas_call | solution.py:267
  35.9 2.8 %all-to-all-done.1 = bf16[32,17,2,128]{3,2,1,0:T(2,128)(2,1)S(1)} async-done(((bf16[32,17,2,128]{3,2,1,0:T(2,128)(2,1)}), bf16[32,17,2,128]{3,2,1,0:T(2,128)(2,1)S(1)}, u32[]{:S(2)}, u32[]{:S(2)}) %all-to-all-start.1) | async-done | bytes 278560 | tf_op jit(solution)/shard_map/all_to_all | solution.py:346
  38.7 3.1 %project.1 = bf16[8,1792]{1,0:T(8,128)(2,1)} custom-call(bf16[1088,128]{1,0:T(8,128)(2,1)S(1)} %bitcast.4, f32[2,56,128]{2,1,0:T(8,128)S(1)} %get-tuple-element.33.out_ref, f32[2,56,128]{2,1,0:T(8,128)S(1)} %get-tuple-element.34.lse_ref, f32[2,56,512]{2,1,0:T(8,128)S(1)} %get-tuple-element.35.match_ref, bf16[768,1792]{1,0:T(8,128)(2,1)S(1)} %get-tuple-element.36.first_ref, ...), custom_call_target="tpu_custom_call" | custom-call | flops 51380224 | bytes 6422528 | tf_op jit(solution)/shard_map/project/pallas_call | solution.py:267
Async XLA Ops:
  0.0 33.6 %copy-start = (bf16[8,1792]{1,0:T(8,128)(2,1)S(1)}, bf16[8,1792]{1,0:T(8,128)(2,1)}, u32[]{:S(2)}) copy-start(bf16[8,1792]{1,0:T(8,128)(2,1)} %q_ref) | copy-start | bytes 86020
  0.0 33.6 %copy-start.1 = (s32[1,14,3]{1,0,2:T(1,128)S(1)}, s32[1,14,3]{1,0,2:T(1,128)}, u32[]{:S(2)}) copy-start(s32[1,14,3]{1,0,2:T(1,128)} %param.12) | copy-start | bytes 508
  1.9 19.3 %all-to-all-start = ((bf16[32,40,128]{2,1,0:T(8,128)(2,1)}), bf16[32,40,128]{2,1,0:T(8,128)(2,1)S(1)}, u32[]{:S(2)}, u32[]{:S(2)}) async-start(bf16[32,40,128]{2,1,0:T(8,128)(2,1)} %bitcast.7), calls=%async_computation | async-start | bytes 655360 | tf_op jit(solution)/shard_map/all_to_all | solution.py:315
  10.3 1.7 %collective-permute-start = (bf16[1024,128]{1,0:T(8,128)(2,1)S(1)}, bf16[1024,128]{1,0:T(8,128)(2,1)S(1)}, u32[]{:S(2)}, u32[]{:S(2)}) collective-permute-start(bf16[1024,128]{1,0:T(8,128)(2,1)S(1)} %get-tuple-element.39), channel_id=1, source_target_pairs={{0,1},{1,0},{2,3},{3,2},{4,5},{5,4},{6,7},{7,6},{8,9},{9,8},{10,11... | collective-permute-start | bytes 786440 | tf_op jit(solution)/shard_map/ppermute | solution.py:323
  11.7 1.6 %collective-permute-start.1 = (bf16[1024,128]{1,0:T(8,128)(2,1)S(1)}, bf16[1024,128]{1,0:T(8,128)(2,1)S(1)}, u32[]{:S(2)}, u32[]{:S(2)}) collective-permute-start(bf16[1024,128]{1,0:T(8,128)(2,1)S(1)} %get-tuple-element.37), channel_id=1, source_target_pairs={{0,1},{1,0},{2,3},{3,2},{4,5},{5,4},{6,7},{7,6},{8,9},{9,8},{10,11... | collective-permute-start | bytes 786440 | tf_op jit(solution)/shard_map/ppermute | solution.py:323
  24.9 13.7 %all-to-all-start.1 = ((bf16[32,17,2,128]{3,2,1,0:T(2,128)(2,1)}), bf16[32,17,2,128]{3,2,1,0:T(2,128)(2,1)S(1)}, u32[]{:S(2)}, u32[]{:S(2)}) async-start(bf16[32,17,2,128]{3,2,1,0:T(2,128)(2,1)} %bitcast.2), calls=%async_computation.1 | async-start | bytes 557056 | tf_op jit(solution)/shard_map/all_to_all | solution.py:346
  27.6 6.0 %collective-permute-start.3 = (bf16[32,8,128]{2,1,0:T(8,128)(2,1)S(1)}, bf16[32,8,128]{2,1,0:T(8,128)(2,1)S(1)}, u32[]{:S(2)}, u32[]{:S(2)}) collective-permute-start(bf16[32,8,128]{2,1,0:T(8,128)(2,1)S(1)} %get-tuple-element.32.kv_ref), channel_id=1, source_target_pairs={{0,2},{1,3},{2,0},{3,1},{4,6},{5,7},{6,4},{7,5},{8,10},{9,11},{10,... | collective-permute-start | bytes 196616 | tf_op jit(solution)/shard_map/ppermute | solution.py:363
  29.3 6.1 %collective-permute-start.2 = (bf16[32,8,128]{2,1,0:T(8,128)(2,1)S(1)}, bf16[32,8,128]{2,1,0:T(8,128)(2,1)S(1)}, u32[]{:S(2)}, u32[]{:S(2)}) collective-permute-start(bf16[32,8,128]{2,1,0:T(8,128)(2,1)S(1)} %get-tuple-element.32.kv_ref), channel_id=1, source_target_pairs={{0,1},{1,0},{2,3},{3,2},{4,5},{5,4},{6,7},{7,6},{8,9},{9,8},{10,11... | collective-permute-start | bytes 196616 | tf_op jit(solution)/shard_map/ppermute | solution.py:364
  33.6 1.8 %collective-permute-start.4 = (bf16[32,8,128]{2,1,0:T(8,128)(2,1)S(1)}, bf16[32,8,128]{2,1,0:T(8,128)(2,1)S(1)}, u32[]{:S(2)}, u32[]{:S(2)}) collective-permute-start(bf16[32,8,128]{2,1,0:T(8,128)(2,1)S(1)} %collective-permute-done.3.kv2_ref), channel_id=1, source_target_pairs={{0,1},{1,0},{2,3},{3,2},{4,5},{5,4},{6,7},{7,6},{8,9},{9,8},{10,11... | collective-permute-start | bytes 196616 | tf_op jit(solution)/shard_map/ppermute | solution.py:364

commit v19 on v18

--- a/solution.py
+++ b/solution.py
@@ -119,7 +119,6 @@
     sent = []
     step = STEP // per
     scale = LOG2E * HD**-0.5
-    nt = (((1,), (1,)), ((), ()))
     row = lax.broadcasted_iota(jnp.int32, (per, LANES), 0)
     lane = lax.broadcasted_iota(jnp.int32, (per, LANES), 1)
     diagonal = row == lane % per
@@ -130,9 +129,7 @@
 
     def scores(first):
         q = q_ref[first : first + step, :per, :].reshape(step * per, HD)
-        return [
-            lax.dot_general(q, k_ref[...], nt, preferred_element_type=jnp.float32) for k_ref in (ka_ref, kb_ref)
-        ]
+        return [jnp.dot(q, k_ref[...], preferred_element_type=jnp.float32) for k_ref in (ka_ref, kb_ref)]
 
     ahead = scores(0)
     for first in range(0, sources, step):
@@ -140,8 +137,8 @@
         if first + step < sources:
             ahead = scores(first + step)
         top = scale * jnp.maximum(jnp.max(sa, axis=1, keepdims=True), jnp.max(sb, axis=1, keepdims=True))
-        wa = jnp.exp2((sa * scale - top).astype(jnp.bfloat16))
-        wb = jnp.exp2((sb * scale - top).astype(jnp.bfloat16))
+        wa = jnp.exp2(sa * scale - top).astype(jnp.bfloat16)
+        wb = jnp.exp2(sb * scale - top).astype(jnp.bfloat16)
         both = jnp.dot(
             wa, jnp.concatenate([va_ref[...], ones], axis=1), preferred_element_type=jnp.float32
         ) + jnp.dot(wb, jnp.concatenate([vb_ref[...], ones], axis=1), preferred_element_type=jnp.float32)
@@ -317,7 +314,8 @@
     core = lax.axis_index("seq") % KVH
 
     def halves(head):
-        return [lax.dynamic_slice_in_dim(x, head * HD, HD, axis=1) for x in (cache_keys, cache_values)]
+        keys, values = [lax.dynamic_slice_in_dim(x, head * HD, HD, axis=1) for x in (cache_keys, cache_values)]
+        return keys.T, values
 
     k_own, v_own = halves(core)
     k_peer, v_peer = [lax.ppermute(x, "seq", partner(1)) for x in halves(1 - core)]

time: 42.1 us -> 41.8 us (level)
    optimization_barrier x0 -> x1, local copies, waits for them, and re-layouts: none -> 1.25 us  [body(): lax.optimization_barrier((send, cache_keys, cache_values, picks, queries))]
    dynamic_slice x2 -> x1, local copies, waits for them, and re-layouts: 2.13 us -> 1.06 us  [halves(): lax.dynamic_slice_in_dim(x, head * HD, HD, axis=1)]
  transfers between devices with their start and end apart: 7 -> 7, of which waited for: 4 -> 4; matrix products, arithmetic and copies ran while one was open for 5% -> 6% of each run, Pallas kernels for 5% -> 5%
where the time goes in v19:
time: 41.8 us; the launch traced here: 41.3 us
  waiting for transfers between devices  16.1 us (39%)
  starting transfers between devices  12.3 us (29%)
  Pallas kernels  10.5 us (25%)
  local copies, waits for them, and re-layouts  2.36 us (6%)
    pallas_call x5, Pallas kernels, call(): pl.pallas_call(kernel, name=name, out_shape=out_shape, in_specs=specs, ou...  10.5 us
    all_to_all x1, waiting for transfers between devices, body(): got = lax.all_to_all(send, 'seq', split_axis=0, concat_axis=0, tiled=True)  7.67 us
    all_to_all x1, starting transfers between devices, body(): got = lax.all_to_all(send, 'seq', split_axis=0, concat_axis=0, tiled=True)  7.3 us
    ppermute x1, waiting for transfers between devices, body(): far = lax.ppermute(fresh, 'seq', partner(2))  4.31 us
    all_to_all x1, waiting for transfers between devices, body(): hist = lax.all_to_all(back, 'seq', split_axis=0, concat_axis=0, tiled=True)  2.8 us
    all_to_all x1, starting transfers between devices, body(): hist = lax.all_to_all(back, 'seq', split_axis=0, concat_axis=0, tiled=True)  2.6 us
    ppermute x1, starting transfers between devices, body(): far = lax.ppermute(fresh, 'seq', partner(2))  1.7 us
    ppermute x2, waiting for transfers between devices, body(): lax.ppermute(x, 'seq', partner(1))  1.28 us
  transfers between devices with their start and end apart: 7, of which 4 were waited for; matrix products, arithmetic and copies ran while one was open for 6% of the time, Pallas kernels for 5%

profile of v19, /device:TPU:0, one launch (start us, length us, event | category | flops | bytes accessed | tf_op | source)
XLA Modules:
  0.0 41.3 jit_solution(1470189740944245550)
XLA Ops:
  0.0 0.0 copy-start
  0.0 0.0 copy-start.1
  0.0 1.9 %pack.1 = bf16[8,2,2,40,128]{4,3,2,1,0:T(8,128)(2,1)} custom-call(s32[3,1,14]{2,1,0:T(1,128)} %bitcast.9, bf16[8,1792]{1,0:T(8,128)(2,1)} %q_ref, bf16[8,256]{1,0:T(8,128)(2,1)} %k_hbm.1, bf16[8,256]{1,0:T(8,128)(2,1)} %v_hbm.1), custom_call_target="tpu_custom_call" | custom-call | tf_op jit(solution)/shard_map/pack/pallas_call | solution.py:264
  1.9 7.3 %all-to-all-start = ((bf16[32,40,128]{2,1,0:T(8,128)(2,1)}), bf16[32,40,128]{2,1,0:T(8,128)(2,1)S(1)}, u32[]{:S(2)}, u32[]{:S(2)}) async-start(bf16[32,40,128]{2,1,0:T(8,128)(2,1)} %bitcast.11), calls=%async_computation | async-start | bytes 655360 | tf_op jit(solution)/shard_map/all_to_all | solution.py:312
  9.2 1.2 %copy.8 = bf16[1024,256]{0,1:T(8,128)(2,1)S(1)} copy(bf16[1024,256]{1,0:T(8,128)(2,1)} %param.10) | data formatting | bytes 1048576 | tf_op jit(solution)/shard_map/optimization_barrier | solution.py:308
  10.5 0.3 collective-permute-start
  10.9 1.1 %constant_dynamic-slice_fusion = (bf16[1024,128]{1,0:T(8,128)(2,1)S(1)}, bf16[1024,128]{1,0:T(8,128)(2,1)S(1)}) fusion(bf16[1024,256]{1,0:T(8,128)(2,1)} %param.11, s32[]{:T(128)S(6)} %select_n.17, s32[]{:T(128)S(6)} %select_n.16), kind=kLoop, calls=%fused_computation.2 | loop fusion | bytes 1048584 | tf_op jit(solution)/shard_map/dynamic_slice | solution.py:317
  11.9 0.3 collective-permute-start.1
  12.3 0.0 collective-permute-done.kb_ref
  12.3 1.3 %collective-permute-done.1.vb_ref = bf16[1024,128]{1,0:T(8,128)(2,1)S(1)} collective-permute-done((bf16[1024,128]{1,0:T(8,128)(2,1)S(1)}, bf16[1024,128]{1,0:T(8,128)(2,1)S(1)}, u32[]{:S(2)}, u32[]{:S(2)}) %collective-permute-start.1) | collective-permute-done | bytes 262176 | tf_op jit(solution)/shard_map/ppermute | solution.py:321
  13.5 7.7 %all-to-all-done.q_ref = bf16[32,40,128]{2,1,0:T(8,128)(2,1)S(1)} async-done(((bf16[32,40,128]{2,1,0:T(8,128)(2,1)}), bf16[32,40,128]{2,1,0:T(8,128)(2,1)S(1)}, u32[]{:S(2)}, u32[]{:S(2)}) %all-to-all-start) | async-done | bytes 327712 | tf_op jit(solution)/shard_map/all_to_all | solution.py:312
  21.2 3.3 %attend.1 = (bf16[1088,128]{1,0:T(8,128)(2,1)}, bf16[32,8,128]{2,1,0:T(8,128)(2,1)S(1)}) custom-call(bf16[32,40,128]{2,1,0:T(8,128)(2,1)S(1)} %all-to-all-done.q_ref, bf16[128,1024]{1,0:T(8,128)(2,1)S(1)} %get-tuple-element.40.ka_ref, bf16[1024,128]{1,0:T(8,128)(2,1)S(1)} %get-tuple-element.38.va_ref, bf16[128,1024]{1,0:T(8,128)(2,1)S(1)} %collective-permute-done.kb_ref, ...), custom_call_target="tpu_custom_call" | custom-call | flops 1073741824 | bytes 4194304 | tf_op jit(solution)/shard_map/attend/pallas_call | solution.py:264
  24.6 2.6 %all-to-all-start.1 = ((bf16[32,17,2,128]{3,2,1,0:T(2,128)(2,1)}), bf16[32,17,2,128]{3,2,1,0:T(2,128)(2,1)S(1)}, u32[]{:S(2)}, u32[]{:S(2)}) async-start(bf16[32,17,2,128]{3,2,1,0:T(2,128)(2,1)} %bitcast.4), calls=%async_computation.1 | async-start | bytes 557056 | tf_op jit(solution)/shard_map/all_to_all | solution.py:344
  27.2 1.7 %collective-permute-start.3 = (bf16[32,8,128]{2,1,0:T(8,128)(2,1)S(1)}, bf16[32,8,128]{2,1,0:T(8,128)(2,1)S(1)}, u32[]{:S(2)}, u32[]{:S(2)}) collective-permute-start(bf16[32,8,128]{2,1,0:T(8,128)(2,1)S(1)} %get-tuple-element.32.kv_ref), channel_id=1, source_target_pairs={{0,2},{1,3},{2,0},{3,1},{4,6},{5,7},{6,4},{7,5},{8,10},{9,11},{10,... | collective-permute-start | bytes 196616 | tf_op jit(solution)/shard_map/ppermute | solution.py:361
  28.9 0.0 collective-permute-start.2
  28.9 4.3 %collective-permute-done.3.kv2_ref = bf16[32,8,128]{2,1,0:T(8,128)(2,1)S(1)} collective-permute-done((bf16[32,8,128]{2,1,0:T(8,128)(2,1)S(1)}, bf16[32,8,128]{2,1,0:T(8,128)(2,1)S(1)}, u32[]{:S(2)}, u32[]{:S(2)}) %collective-permute-start.3) | collective-permute-done | bytes 65568 | tf_op jit(solution)/shard_map/ppermute | solution.py:361
  33.2 0.0 collective-permute-start.4
  33.2 0.0 copy-done
  33.2 0.0 copy-done.1
  33.2 1.8 %masks.1 = (f32[2,56,512]{2,1,0:T(8,128)S(1)}, f32[2,56,128]{2,1,0:T(8,128)S(1)}, bf16[768,1792]{1,0:T(8,128)(2,1)S(1)}) custom-call(s32[3,1,14]{2,1,0:T(1,128)S(1)} %bitcast.10, bf16[8,1792]{1,0:T(8,128)(2,1)S(1)} %copy-done, bf16[1792,1792]{1,0:T(8,128)(2,1)} %w_hbm.1), custom_call_target="tpu_custom_call" | custom-call | tf_op jit(solution)/shard_map/masks/pallas_call | solution.py:264
  35.0 0.0 collective-permute-done.2.kv1_ref
  35.0 0.0 collective-permute-done.4.kv3_ref
  35.0 0.4 %fresh.1 = (f32[2,56,128]{2,1,0:T(8,128)S(1)}, f32[2,56,128]{2,1,0:T(8,128)S(1)}) custom-call(f32[2,56,128]{2,1,0:T(8,128)S(1)} %get-tuple-element.31.rows_ref, bf16[32,8,128]{2,1,0:T(8,128)(2,1)S(1)} %get-tuple-element.32.kv_ref, bf16[32,8,128]{2,1,0:T(8,128)(2,1)S(1)} %collective-permute-done.2.kv1_ref, ...), custom_call_target="tpu_custom_call" | custom-call | flops 29360128 | bytes 1048576 | tf_op jit(solution)/shard_map/fresh/pallas_call | solution.py:264
  35.5 2.8 %all-to-all-done.1 = bf16[32,17,2,128]{3,2,1,0:T(2,128)(2,1)S(1)} async-done(((bf16[32,17,2,128]{3,2,1,0:T(2,128)(2,1)}), bf16[32,17,2,128]{3,2,1,0:T(2,128)(2,1)S(1)}, u32[]{:S(2)}, u32[]{:S(2)}) %all-to-all-start.1) | async-done | bytes 278560 | tf_op jit(solution)/shard_map/all_to_all | solution.py:344
  38.3 3.1 %project.1 = bf16[8,1792]{1,0:T(8,128)(2,1)} custom-call(bf16[1088,128]{1,0:T(8,128)(2,1)S(1)} %bitcast.8, f32[2,56,128]{2,1,0:T(8,128)S(1)} %get-tuple-element.33.out_ref, f32[2,56,128]{2,1,0:T(8,128)S(1)} %get-tuple-element.34.lse_ref, f32[2,56,512]{2,1,0:T(8,128)S(1)} %get-tuple-element.35.match_ref, bf16[768,1792]{1,0:T(8,128)(2,1)S(1)} %get-tuple-element.36.first_ref, ...), custom_call_target="tpu_custom_call" | custom-call | flops 51380224 | bytes 6422528 | tf_op jit(solution)/shard_map/project/pallas_call | solution.py:264
  (1 shorter events, 0.0 us)
Async XLA Ops:
  0.0 33.2 %copy-start = (bf16[8,1792]{1,0:T(8,128)(2,1)S(1)}, bf16[8,1792]{1,0:T(8,128)(2,1)}, u32[]{:S(2)}) copy-start(bf16[8,1792]{1,0:T(8,128)(2,1)} %q_ref) | copy-start | bytes 86020
  0.0 33.2 %copy-start.1 = (s32[1,14,3]{1,0,2:T(1,128)S(1)}, s32[1,14,3]{1,0,2:T(1,128)}, u32[]{:S(2)}) copy-start(s32[1,14,3]{1,0,2:T(1,128)} %param.12) | copy-start | bytes 508
  1.9 19.3 %all-to-all-start = ((bf16[32,40,128]{2,1,0:T(8,128)(2,1)}), bf16[32,40,128]{2,1,0:T(8,128)(2,1)S(1)}, u32[]{:S(2)}, u32[]{:S(2)}) async-start(bf16[32,40,128]{2,1,0:T(8,128)(2,1)} %bitcast.11), calls=%async_computation | async-start | bytes 655360 | tf_op jit(solution)/shard_map/all_to_all | solution.py:312
  10.5 1.7 %collective-permute-start = (bf16[128,1024]{1,0:T(8,128)(2,1)S(1)}, bf16[128,1024]{1,0:T(8,128)(2,1)S(1)}, u32[]{:S(2)}, u32[]{:S(2)}) collective-permute-start(bf16[128,1024]{1,0:T(8,128)(2,1)S(1)} %get-tuple-element.39), channel_id=1, source_target_pairs={{0,1},{1,0},{2,3},{3,2},{4,5},{5,4},{6,7},{7,6},{8,9},{9,8},{10,11... | collective-permute-start | bytes 786440 | tf_op jit(solution)/shard_map/ppermute | solution.py:321
  11.9 1.6 %collective-permute-start.1 = (bf16[1024,128]{1,0:T(8,128)(2,1)S(1)}, bf16[1024,128]{1,0:T(8,128)(2,1)S(1)}, u32[]{:S(2)}, u32[]{:S(2)}) collective-permute-start(bf16[1024,128]{1,0:T(8,128)(2,1)S(1)} %get-tuple-element.37), channel_id=1, source_target_pairs={{0,1},{1,0},{2,3},{3,2},{4,5},{5,4},{6,7},{7,6},{8,9},{9,8},{10,11... | collective-permute-start | bytes 786440 | tf_op jit(solution)/shard_map/ppermute | solution.py:321
  24.6 13.7 %all-to-all-start.1 = ((bf16[32,17,2,128]{3,2,1,0:T(2,128)(2,1)}), bf16[32,17,2,128]{3,2,1,0:T(2,128)(2,1)S(1)}, u32[]{:S(2)}, u32[]{:S(2)}) async-start(bf16[32,17,2,128]{3,2,1,0:T(2,128)(2,1)} %bitcast.4), calls=%async_computation.1 | async-start | bytes 557056 | tf_op jit(solution)/shard_map/all_to_all | solution.py:344
  27.2 6.0 %collective-permute-start.3 = (bf16[32,8,128]{2,1,0:T(8,128)(2,1)S(1)}, bf16[32,8,128]{2,1,0:T(8,128)(2,1)S(1)}, u32[]{:S(2)}, u32[]{:S(2)}) collective-permute-start(bf16[32,8,128]{2,1,0:T(8,128)(2,1)S(1)} %get-tuple-element.32.kv_ref), channel_id=1, source_target_pairs={{0,2},{1,3},{2,0},{3,1},{4,6},{5,7},{6,4},{7,5},{8,10},{9,11},{10,... | collective-permute-start | bytes 196616 | tf_op jit(solution)/shard_map/ppermute | solution.py:361
  28.9 6.1 %collective-permute-start.2 = (bf16[32,8,128]{2,1,0:T(8,128)(2,1)S(1)}, bf16[32,8,128]{2,1,0:T(8,128)(2,1)S(1)}, u32[]{:S(2)}, u32[]{:S(2)}) collective-permute-start(bf16[32,8,128]{2,1,0:T(8,128)(2,1)S(1)} %get-tuple-element.32.kv_ref), channel_id=1, source_target_pairs={{0,1},{1,0},{2,3},{3,2},{4,5},{5,4},{6,7},{7,6},{8,9},{9,8},{10,11... | collective-permute-start | bytes 196616 | tf_op jit(solution)/shard_map/ppermute | solution.py:362
  33.2 1.8 %collective-permute-start.4 = (bf16[32,8,128]{2,1,0:T(8,128)(2,1)S(1)}, bf16[32,8,128]{2,1,0:T(8,128)(2,1)S(1)}, u32[]{:S(2)}, u32[]{:S(2)}) collective-permute-start(bf16[32,8,128]{2,1,0:T(8,128)(2,1)S(1)} %collective-permute-done.3.kv2_ref), channel_id=1, source_target_pairs={{0,1},{1,0},{2,3},{3,2},{4,5},{5,4},{6,7},{7,6},{8,9},{9,8},{10,11... | collective-permute-start | bytes 196616 | tf_op jit(solution)/shard_map/ppermute | solution.py:362

commit v20 on v19

--- a/solution.py
+++ b/solution.py
@@ -93,9 +93,10 @@
         fresh = [k_ref[:, cols], v_ref[:, cols]]
         for b in range(key_blocks):
             for chip in range(chips):
-                send_ref[g, b, chip, :per, :] = slots[b * per : (b + 1) * per]
-                send_ref[g, b, chip, per:, :] = fresh[chip % 2]
-        sent.append(pltpu.make_async_copy(send_ref.at[g], send_hbm.at[:, :, g], sems.at[4 + g]))
+                to = (g, key_blocks - 1 - b, chips - 1 - chip)
+                send_ref[(*to, slice(0, per))] = slots[b * per : (b + 1) * per]
+                send_ref[(*to, slice(per, None))] = fresh[chip % 2]
+        sent.append(pltpu.make_async_copy(send_ref.at[g], send_hbm.at[:, :, KVH - 1 - g], sems.at[4 + g]))
         sent[g].start()
     for copy in sent:
         copy.wait()
@@ -170,7 +171,8 @@
     nt = (((1,), (1,)), ((), ()))
     column = lax.broadcasted_iota(jnp.int32, (tokens, sources * tokens), 1)
     query_pos = place * tokens + lax.broadcasted_iota(jnp.int32, column.shape, 0)
-    visible = (column <= query_pos) & (column // BLK == query_pos // BLK)
+    key_pos = (sources - 1 - column // tokens) * tokens + column % tokens
+    visible = (key_pos <= query_pos) & (key_pos // BLK == query_pos // BLK)
     visible = jnp.concatenate([visible.astype(jnp.int32)] * GROUP, axis=0) > 0
     ones = jnp.ones((sources * tokens, HD), jnp.bfloat16)
     here, near, far, both = [
@@ -204,7 +206,6 @@
     )
     tokens = y_ref.shape[0]
     holders = match_ref.shape[2] // per
-    stride = KVH * (per + 2)
     hist = hist_ref[...].astype(jnp.float32)
     fold = LANES // per
     row = lax.broadcasted_iota(jnp.int32, (holders, LANES), 0)
@@ -216,7 +217,7 @@
 
     heads = []
     for g in range(KVH):
-        starts = [m * stride + g * (per + 2) for m in range(holders)]
+        starts = [(KVH * (holders - m) - 1 - g) * (per + 2) for m in range(holders)]
         outs = jnp.concatenate([hist[i : i + per] for i in starts], axis=0).astype(jnp.bfloat16)
         stats = jnp.concatenate([hist[i + per : i + per + 1] for i in starts], axis=0)
         shift = LANES // 2
@@ -308,8 +309,12 @@
     send, cache_keys, cache_values, picks, queries = lax.optimization_barrier(
         (send, cache_keys, cache_values, picks, queries)
     )
-    send = send.reshape(devices, per + tokens, HD)
-    got = lax.all_to_all(send, "seq", split_axis=0, concat_axis=0, tiled=True)
+
+    def exchange(x):
+        ranks = [list(range(devices))[::-1]]
+        return lax.all_to_all(x, "seq", split_axis=0, concat_axis=0, axis_index_groups=ranks, tiled=True)
+
+    got = exchange(send.reshape(devices, per + tokens, HD))
 
     core = lax.axis_index("seq") % KVH
 
@@ -340,8 +345,7 @@
         limit=32,
     )
     back, picks, queries, out_weight = lax.optimization_barrier((back, picks, queries, out_weight))
-    back = back.reshape(devices, (per + 2) // 2, 2, HD)
-    hist = lax.all_to_all(back, "seq", split_axis=0, concat_axis=0, tiled=True)
+    hist = exchange(back.reshape(devices, (per + 2) // 2, 2, HD))
 
     ready = EARLY * KVH * HD
     match, query_rows, first = call(

time: 41.8 us -> 41.2 us (0.986)
  the two profiles are of different devices: /device:TPU:0 before, /device:TPU:1 now
where the time goes in v20:
time: 41.2 us; the launch traced here: 40.8 us
  waiting for transfers between devices  14.8 us (36%)
  starting transfers between devices  13.1 us (32%)
  Pallas kernels  10.4 us (25%)
  local copies, waits for them, and re-layouts  2.36 us (6%)
    pallas_call x5, Pallas kernels, call(): pl.pallas_call(kernel, name=name, out_shape=out_shape, in_specs=specs, ou...  10.4 us
    all_to_all x2, waiting for transfers between devices, exchange(): lax.all_to_all(x, 'seq', split_axis=0, concat_axis=0, axis_index_groups=r...  10.2 us
    all_to_all x2, starting transfers between devices, exchange(): lax.all_to_all(x, 'seq', split_axis=0, concat_axis=0, axis_index_groups=r...  9.45 us
    ppermute x1, waiting for transfers between devices, body(): far = lax.ppermute(fresh, 'seq', partner(2))  3.25 us
    ppermute x2, starting transfers between devices, body(): near, both = [lax.ppermute(x, 'seq', partner(1)) for x in (fresh, far)]  1.6 us
    ppermute x1, starting transfers between devices, body(): far = lax.ppermute(fresh, 'seq', partner(2))  1.44 us
    ppermute x2, waiting for transfers between devices, body(): lax.ppermute(x, 'seq', partner(1))  1.28 us
    optimization_barrier x1, local copies, waits for them, and re-layouts, body(): lax.optimization_barrier((send, cache_keys, cache_values, picks, queries))  1.25 us
  transfers between devices with their start and end apart: 7, of which 4 were waited for; matrix products, arithmetic and copies ran while one was open for 6% of the time, Pallas kernels for 5%

profile of v20, /device:TPU:1, one launch (start us, length us, event | category | flops | bytes accessed | tf_op | source)
XLA Modules:
  0.0 40.8 jit_solution(15082369893793847606)
XLA Ops:
  0.0 0.0 copy-start
  0.0 0.0 copy-start.1
  0.0 1.9 %pack.1 = bf16[8,2,2,40,128]{4,3,2,1,0:T(8,128)(2,1)} custom-call(s32[3,1,14]{2,1,0:T(1,128)} %bitcast.9, bf16[8,1792]{1,0:T(8,128)(2,1)} %q_ref, bf16[8,256]{1,0:T(8,128)(2,1)} %k_hbm.1, bf16[8,256]{1,0:T(8,128)(2,1)} %v_hbm.1), custom_call_target="tpu_custom_call" | custom-call | tf_op jit(solution)/shard_map/pack/pallas_call | solution.py:265
  1.9 7.1 %all-to-all-start = ((bf16[32,40,128]{2,1,0:T(8,128)(2,1)}), bf16[32,40,128]{2,1,0:T(8,128)(2,1)S(1)}, u32[]{:S(2)}, u32[]{:S(2)}) async-start(bf16[32,40,128]{2,1,0:T(8,128)(2,1)} %bitcast.11), calls=%async_computation | async-start | bytes 655360 | tf_op jit(solution)/shard_map/all_to_all | solution.py:315
  9.0 1.2 %copy.8 = bf16[1024,256]{0,1:T(8,128)(2,1)S(1)} copy(bf16[1024,256]{1,0:T(8,128)(2,1)} %param.10) | data formatting | bytes 1048576 | tf_op jit(solution)/shard_map/optimization_barrier | solution.py:309
  10.3 0.3 collective-permute-start
  10.7 1.1 %constant_dynamic-slice_fusion = (bf16[1024,128]{1,0:T(8,128)(2,1)S(1)}, bf16[1024,128]{1,0:T(8,128)(2,1)S(1)}) fusion(bf16[1024,256]{1,0:T(8,128)(2,1)} %param.11, s32[]{:T(128)S(6)} %select_n.17, s32[]{:T(128)S(6)} %select_n.16), kind=kLoop, calls=%fused_computation.2 | loop fusion | bytes 1048584 | tf_op jit(solution)/shard_map/dynamic_slice | solution.py:322
  11.7 0.3 collective-permute-start.1
  12.0 0.0 collective-permute-done.kb_ref
  12.0 1.3 %collective-permute-done.1.vb_ref = bf16[1024,128]{1,0:T(8,128)(2,1)S(1)} collective-permute-done((bf16[1024,128]{1,0:T(8,128)(2,1)S(1)}, bf16[1024,128]{1,0:T(8,128)(2,1)S(1)}, u32[]{:S(2)}, u32[]{:S(2)}) %collective-permute-start.1) | collective-permute-done | bytes 262176 | tf_op jit(solution)/shard_map/ppermute | solution.py:326
  13.3 7.8 %all-to-all-done.q_ref = bf16[32,40,128]{2,1,0:T(8,128)(2,1)S(1)} async-done(((bf16[32,40,128]{2,1,0:T(8,128)(2,1)}), bf16[32,40,128]{2,1,0:T(8,128)(2,1)S(1)}, u32[]{:S(2)}, u32[]{:S(2)}) %all-to-all-start) | async-done | bytes 327712 | tf_op jit(solution)/shard_map/all_to_all | solution.py:315
  21.1 3.3 %attend.1 = (bf16[1088,128]{1,0:T(8,128)(2,1)}, bf16[32,8,128]{2,1,0:T(8,128)(2,1)S(1)}) custom-call(bf16[32,40,128]{2,1,0:T(8,128)(2,1)S(1)} %all-to-all-done.q_ref, bf16[128,1024]{1,0:T(8,128)(2,1)S(1)} %get-tuple-element.40.ka_ref, bf16[1024,128]{1,0:T(8,128)(2,1)S(1)} %get-tuple-element.38.va_ref, bf16[128,1024]{1,0:T(8,128)(2,1)S(1)} %collective-permute-done.kb_ref, ...), custom_call_target="tpu_custom_call" | custom-call | flops 1073741824 | bytes 4194304 | tf_op jit(solution)/shard_map/attend/pallas_call | solution.py:265
  24.4 2.4 %all-to-all-start.1 = ((bf16[32,17,2,128]{3,2,1,0:T(2,128)(2,1)}), bf16[32,17,2,128]{3,2,1,0:T(2,128)(2,1)S(1)}, u32[]{:S(2)}, u32[]{:S(2)}) async-start(bf16[32,17,2,128]{3,2,1,0:T(2,128)(2,1)} %bitcast.4), calls=%async_computation.1 | async-start | bytes 557056 | tf_op jit(solution)/shard_map/all_to_all | solution.py:315
  26.8 1.4 %collective-permute-start.3 = (bf16[32,8,128]{2,1,0:T(8,128)(2,1)S(1)}, bf16[32,8,128]{2,1,0:T(8,128)(2,1)S(1)}, u32[]{:S(2)}, u32[]{:S(2)}) collective-permute-start(bf16[32,8,128]{2,1,0:T(8,128)(2,1)S(1)} %get-tuple-element.32.kv_ref), channel_id=1, source_target_pairs={{0,2},{1,3},{2,0},{3,1},{4,6},{5,7},{6,4},{7,5},{8,10},{9,11},{10,... | collective-permute-start | bytes 196616 | tf_op jit(solution)/shard_map/ppermute | solution.py:365
  28.2 0.6 %collective-permute-start.2 = (bf16[32,8,128]{2,1,0:T(8,128)(2,1)S(1)}, bf16[32,8,128]{2,1,0:T(8,128)(2,1)S(1)}, u32[]{:S(2)}, u32[]{:S(2)}) collective-permute-start(bf16[32,8,128]{2,1,0:T(8,128)(2,1)S(1)} %get-tuple-element.32.kv_ref), channel_id=1, source_target_pairs={{0,1},{1,0},{2,3},{3,2},{4,5},{5,4},{6,7},{7,6},{8,9},{9,8},{10,11... | collective-permute-start | bytes 196616 | tf_op jit(solution)/shard_map/ppermute | solution.py:366
  28.9 3.2 %collective-permute-done.3.kv2_ref = bf16[32,8,128]{2,1,0:T(8,128)(2,1)S(1)} collective-permute-done((bf16[32,8,128]{2,1,0:T(8,128)(2,1)S(1)}, bf16[32,8,128]{2,1,0:T(8,128)(2,1)S(1)}, u32[]{:S(2)}, u32[]{:S(2)}) %collective-permute-start.3) | collective-permute-done | bytes 65568 | tf_op jit(solution)/shard_map/ppermute | solution.py:365
  32.1 1.0 %collective-permute-start.4 = (bf16[32,8,128]{2,1,0:T(8,128)(2,1)S(1)}, bf16[32,8,128]{2,1,0:T(8,128)(2,1)S(1)}, u32[]{:S(2)}, u32[]{:S(2)}) collective-permute-start(bf16[32,8,128]{2,1,0:T(8,128)(2,1)S(1)} %collective-permute-done.3.kv2_ref), channel_id=1, source_target_pairs={{0,1},{1,0},{2,3},{3,2},{4,5},{5,4},{6,7},{7,6},{8,9},{9,8},{10,11... | collective-permute-start | bytes 196616 | tf_op jit(solution)/shard_map/ppermute | solution.py:366
  33.1 0.0 copy-done
  33.1 0.0 copy-done.1
  33.1 1.8 %masks.1 = (f32[2,56,512]{2,1,0:T(8,128)S(1)}, f32[2,56,128]{2,1,0:T(8,128)S(1)}, bf16[768,1792]{1,0:T(8,128)(2,1)S(1)}) custom-call(s32[3,1,14]{2,1,0:T(1,128)S(1)} %bitcast.10, bf16[8,1792]{1,0:T(8,128)(2,1)S(1)} %copy-done, bf16[1792,1792]{1,0:T(8,128)(2,1)} %w_hbm.1), custom_call_target="tpu_custom_call" | custom-call | tf_op jit(solution)/shard_map/masks/pallas_call | solution.py:265
  34.9 0.0 collective-permute-done.2.kv1_ref
  34.9 0.0 collective-permute-done.4.kv3_ref
  34.9 0.4 %fresh.1 = (f32[2,56,128]{2,1,0:T(8,128)S(1)}, f32[2,56,128]{2,1,0:T(8,128)S(1)}) custom-call(f32[2,56,128]{2,1,0:T(8,128)S(1)} %get-tuple-element.31.rows_ref, bf16[32,8,128]{2,1,0:T(8,128)(2,1)S(1)} %get-tuple-element.32.kv_ref, bf16[32,8,128]{2,1,0:T(8,128)(2,1)S(1)} %collective-permute-done.2.kv1_ref, ...), custom_call_target="tpu_custom_call" | custom-call | flops 29360128 | bytes 1048576 | tf_op jit(solution)/shard_map/fresh/pallas_call | solution.py:265
  35.4 2.5 %all-to-all-done.1 = bf16[32,17,2,128]{3,2,1,0:T(2,128)(2,1)S(1)} async-done(((bf16[32,17,2,128]{3,2,1,0:T(2,128)(2,1)}), bf16[32,17,2,128]{3,2,1,0:T(2,128)(2,1)S(1)}, u32[]{:S(2)}, u32[]{:S(2)}) %all-to-all-start.1) | async-done | bytes 278560 | tf_op jit(solution)/shard_map/all_to_all | solution.py:315
  37.8 3.0 %project.1 = bf16[8,1792]{1,0:T(8,128)(2,1)} custom-call(bf16[1088,128]{1,0:T(8,128)(2,1)S(1)} %bitcast.8, f32[2,56,128]{2,1,0:T(8,128)S(1)} %get-tuple-element.33.out_ref, f32[2,56,128]{2,1,0:T(8,128)S(1)} %get-tuple-element.34.lse_ref, f32[2,56,512]{2,1,0:T(8,128)S(1)} %get-tuple-element.35.match_ref, bf16[768,1792]{1,0:T(8,128)(2,1)S(1)} %get-tuple-element.36.first_ref, ...), custom_call_target="tpu_custom_call" | custom-call | flops 51380224 | bytes 6422528 | tf_op jit(solution)/shard_map/project/pallas_call | solution.py:265
  (1 shorter events, 0.0 us)
Async XLA Ops:
  0.0 33.1 %copy-start = (bf16[8,1792]{1,0:T(8,128)(2,1)S(1)}, bf16[8,1792]{1,0:T(8,128)(2,1)}, u32[]{:S(2)}) copy-start(bf16[8,1792]{1,0:T(8,128)(2,1)} %q_ref) | copy-start | bytes 86020
  0.0 33.1 %copy-start.1 = (s32[1,14,3]{1,0,2:T(1,128)S(1)}, s32[1,14,3]{1,0,2:T(1,128)}, u32[]{:S(2)}) copy-start(s32[1,14,3]{1,0,2:T(1,128)} %param.12) | copy-start | bytes 508
  1.9 19.2 %all-to-all-start = ((bf16[32,40,128]{2,1,0:T(8,128)(2,1)}), bf16[32,40,128]{2,1,0:T(8,128)(2,1)S(1)}, u32[]{:S(2)}, u32[]{:S(2)}) async-start(bf16[32,40,128]{2,1,0:T(8,128)(2,1)} %bitcast.11), calls=%async_computation | async-start | bytes 655360 | tf_op jit(solution)/shard_map/all_to_all | solution.py:315
  10.3 1.7 %collective-permute-start = (bf16[128,1024]{1,0:T(8,128)(2,1)S(1)}, bf16[128,1024]{1,0:T(8,128)(2,1)S(1)}, u32[]{:S(2)}, u32[]{:S(2)}) collective-permute-start(bf16[128,1024]{1,0:T(8,128)(2,1)S(1)} %get-tuple-element.39), channel_id=1, source_target_pairs={{0,1},{1,0},{2,3},{3,2},{4,5},{5,4},{6,7},{7,6},{8,9},{9,8},{10,11... | collective-permute-start | bytes 786440 | tf_op jit(solution)/shard_map/ppermute | solution.py:326
  11.7 1.6 %collective-permute-start.1 = (bf16[1024,128]{1,0:T(8,128)(2,1)S(1)}, bf16[1024,128]{1,0:T(8,128)(2,1)S(1)}, u32[]{:S(2)}, u32[]{:S(2)}) collective-permute-start(bf16[1024,128]{1,0:T(8,128)(2,1)S(1)} %get-tuple-element.37), channel_id=1, source_target_pairs={{0,1},{1,0},{2,3},{3,2},{4,5},{5,4},{6,7},{7,6},{8,9},{9,8},{10,11... | collective-permute-start | bytes 786440 | tf_op jit(solution)/shard_map/ppermute | solution.py:326
  24.4 13.4 %all-to-all-start.1 = ((bf16[32,17,2,128]{3,2,1,0:T(2,128)(2,1)}), bf16[32,17,2,128]{3,2,1,0:T(2,128)(2,1)S(1)}, u32[]{:S(2)}, u32[]{:S(2)}) async-start(bf16[32,17,2,128]{3,2,1,0:T(2,128)(2,1)} %bitcast.4), calls=%async_computation.1 | async-start | bytes 557056 | tf_op jit(solution)/shard_map/all_to_all | solution.py:315
  26.8 5.3 %collective-permute-start.3 = (bf16[32,8,128]{2,1,0:T(8,128)(2,1)S(1)}, bf16[32,8,128]{2,1,0:T(8,128)(2,1)S(1)}, u32[]{:S(2)}, u32[]{:S(2)}) collective-permute-start(bf16[32,8,128]{2,1,0:T(8,128)(2,1)S(1)} %get-tuple-element.32.kv_ref), channel_id=1, source_target_pairs={{0,2},{1,3},{2,0},{3,1},{4,6},{5,7},{6,4},{7,5},{8,10},{9,11},{10,... | collective-permute-start | bytes 196616 | tf_op jit(solution)/shard_map/ppermute | solution.py:365
  28.2 6.7 %collective-permute-start.2 = (bf16[32,8,128]{2,1,0:T(8,128)(2,1)S(1)}, bf16[32,8,128]{2,1,0:T(8,128)(2,1)S(1)}, u32[]{:S(2)}, u32[]{:S(2)}) collective-permute-start(bf16[32,8,128]{2,1,0:T(8,128)(2,1)S(1)} %get-tuple-element.32.kv_ref), channel_id=1, source_target_pairs={{0,1},{1,0},{2,3},{3,2},{4,5},{5,4},{6,7},{7,6},{8,9},{9,8},{10,11... | collective-permute-start | bytes 196616 | tf_op jit(solution)/shard_map/ppermute | solution.py:366
  32.1 2.8 %collective-permute-start.4 = (bf16[32,8,128]{2,1,0:T(8,128)(2,1)S(1)}, bf16[32,8,128]{2,1,0:T(8,128)(2,1)S(1)}, u32[]{:S(2)}, u32[]{:S(2)}) collective-permute-start(bf16[32,8,128]{2,1,0:T(8,128)(2,1)S(1)} %collective-permute-done.3.kv2_ref), channel_id=1, source_target_pairs={{0,1},{1,0},{2,3},{3,2},{4,5},{5,4},{6,7},{7,6},{8,9},{9,8},{10,11... | collective-permute-start | bytes 196616 | tf_op jit(solution)/shard_map/ppermute | solution.py:366

commit v21 on v20

--- a/solution.py
+++ b/solution.py
@@ -117,26 +117,29 @@
 
 def attend_kernel(per, q_ref, ka_ref, va_ref, kb_ref, vb_ref, out_hbm, fresh_ref, out_ref, sems):
     sources = q_ref.shape[0]
-    sent = []
     step = STEP // per
     scale = LOG2E * HD**-0.5
     row = lax.broadcasted_iota(jnp.int32, (per, LANES), 0)
     lane = lax.broadcasted_iota(jnp.int32, (per, LANES), 1)
     diagonal = row == lane % per
-    group = lax.broadcasted_iota(jnp.int32, (2, LANES), 1) // per
-    second = lax.broadcasted_iota(jnp.int32, (2, LANES), 0)
     ones = jnp.ones(va_ref.shape, jnp.bfloat16)
+    empty = jnp.zeros((1, LANES), jnp.float32)
     fresh_ref[...] = q_ref[:, per:, :]
 
-    def scores(first):
-        q = q_ref[first : first + step, :per, :].reshape(step * per, HD)
+    half = step // 2
+    turns = [(first, step) for first in range(step, sources - step, step)]
+    turns = [(0, half), (half, half)] + turns + [(sources - step, half), (sources - half, half)]
+
+    def scores(first, count):
+        q = q_ref[first : first + count, :per, :].reshape(count * per, HD)
         return [jnp.dot(q, k_ref[...], preferred_element_type=jnp.float32) for k_ref in (ka_ref, kb_ref)]
 
-    ahead = scores(0)
-    for first in range(0, sources, step):
+    ahead = scores(*turns[0])
+    sent, rows = [], []
+    for turn, (first, count) in enumerate(turns):
         sa, sb = ahead
-        if first + step < sources:
-            ahead = scores(first + step)
+        if turn + 1 < len(turns):
+            ahead = scores(*turns[turn + 1])
         top = scale * jnp.maximum(jnp.max(sa, axis=1, keepdims=True), jnp.max(sb, axis=1, keepdims=True))
         wa = jnp.exp2(sa * scale - top).astype(jnp.bfloat16)
         wb = jnp.exp2(sb * scale - top).astype(jnp.bfloat16)
@@ -145,20 +148,21 @@
         ) + jnp.dot(wb, jnp.concatenate([vb_ref[...], ones], axis=1), preferred_element_type=jnp.float32)
         total = both[:, HD:]
         out = both[:, :HD] / total
-        lse = top + jnp.log(total) * LOG2E
-        rows = []
-        for s in range(step):
-            part = slice(s * per, (s + 1) * per)
-            flat = jnp.sum(jnp.where(diagonal, lse[part], 0.0), axis=0, keepdims=True)
-            hi = flat.astype(jnp.bfloat16).astype(jnp.float32)
-            mid = (flat - hi).astype(jnp.bfloat16).astype(jnp.float32)
-            low = flat - hi - mid
-            stats = jnp.where(group == 0, hi, jnp.where(group == 1, mid, jnp.where(group == 2, low, 0.0)))
-            rows = rows + [out[part], jnp.where(second == 0, stats, 0.0)]
-        done = pl.ds(first * (per + 2), step * (per + 2))
-        out_ref[done, :] = jnp.concatenate(rows, axis=0).astype(jnp.bfloat16)
-        sent.append(pltpu.make_async_copy(out_ref.at[done], out_hbm.at[done], sems.at[first // step]))
-        sent[-1].start()
+        lse = (top + jnp.log(total) * LOG2E).reshape(count, per, LANES)
+        flat = jnp.sum(jnp.where(diagonal[None], lse, 0.0), axis=1)
+        hi = flat.astype(jnp.bfloat16).astype(jnp.float32)
+        mid = (flat - hi).astype(jnp.bfloat16).astype(jnp.float32)
+        low = flat - hi - mid
+        group = lax.broadcasted_iota(jnp.int32, flat.shape, 1) // per
+        stats = jnp.where(group == 0, hi, jnp.where(group == 1, mid, jnp.where(group == 2, low, 0.0)))
+        for s in range(count):
+            rows = rows + [out[s * per : (s + 1) * per], stats[s : s + 1], empty]
+        if len(rows) == 3 * step:
+            done = pl.ds((first + count - step) * (per + 2), step * (per + 2))
+            out_ref[done, :] = jnp.concatenate(rows, axis=0).astype(jnp.bfloat16)
+            sent.append(pltpu.make_async_copy(out_ref.at[done], out_hbm.at[done], sems.at[len(sent)]))
+            sent[-1].start()
+            rows = []
     for copy in sent:
         copy.wait()
 

time: 41.2 us -> 41.4 us (level)
  no operation moved by 1% of the time
where the time goes in v21:
time: 41.4 us; the launch traced here: 40.9 us
  waiting for transfers between devices  14.8 us (36%)
  starting transfers between devices  13.1 us (32%)
  Pallas kernels  10.6 us (26%)
  local copies, waits for them, and re-layouts  2.36 us (6%)
    pallas_call x5, Pallas kernels, call(): pl.pallas_call(kernel, name=name, out_shape=out_shape, in_specs=specs, ou...  10.6 us
    all_to_all x2, waiting for transfers between devices, exchange(): lax.all_to_all(x, 'seq', split_axis=0, concat_axis=0, axis_index_groups=r...  10.2 us
    all_to_all x2, starting transfers between devices, exchange(): lax.all_to_all(x, 'seq', split_axis=0, concat_axis=0, axis_index_groups=r...  9.46 us
    ppermute x1, waiting for transfers between devices, body(): far = lax.ppermute(fresh, 'seq', partner(2))  3.25 us
    ppermute x2, starting transfers between devices, body(): near, both = [lax.ppermute(x, 'seq', partner(1)) for x in (fresh, far)]  1.6 us
    ppermute x1, starting transfers between devices, body(): far = lax.ppermute(fresh, 'seq', partner(2))  1.44 us
    ppermute x2, waiting for transfers between devices, body(): lax.ppermute(x, 'seq', partner(1))  1.28 us
    optimization_barrier x1, local copies, waits for them, and re-layouts, body(): lax.optimization_barrier((send, cache_keys, cache_values, picks, queries))  1.25 us
  transfers between devices with their start and end apart: 7, of which 4 were waited for; matrix products, arithmetic and copies ran while one was open for 6% of the time, Pallas kernels for 5%

profile of v21, /device:TPU:1, one launch (start us, length us, event | category | flops | bytes accessed | tf_op | source)
XLA Modules:
  0.0 40.9 jit_solution(14377381074999320837)
XLA Ops:
  0.0 0.0 copy-start
  0.0 0.0 copy-start.1
  0.0 1.9 %pack.1 = bf16[8,2,2,40,128]{4,3,2,1,0:T(8,128)(2,1)} custom-call(s32[3,1,14]{2,1,0:T(1,128)} %bitcast.9, bf16[8,1792]{1,0:T(8,128)(2,1)} %q_ref, bf16[8,256]{1,0:T(8,128)(2,1)} %k_hbm.1, bf16[8,256]{1,0:T(8,128)(2,1)} %v_hbm.1), custom_call_target="tpu_custom_call" | custom-call | tf_op jit(solution)/shard_map/pack/pallas_call | solution.py:269
  1.9 7.1 %all-to-all-start = ((bf16[32,40,128]{2,1,0:T(8,128)(2,1)}), bf16[32,40,128]{2,1,0:T(8,128)(2,1)S(1)}, u32[]{:S(2)}, u32[]{:S(2)}) async-start(bf16[32,40,128]{2,1,0:T(8,128)(2,1)} %bitcast.11), calls=%async_computation | async-start | bytes 655360 | tf_op jit(solution)/shard_map/all_to_all | solution.py:319
  9.0 1.2 %copy.8 = bf16[1024,256]{0,1:T(8,128)(2,1)S(1)} copy(bf16[1024,256]{1,0:T(8,128)(2,1)} %param.10) | data formatting | bytes 1048576 | tf_op jit(solution)/shard_map/optimization_barrier | solution.py:313
  10.3 0.3 collective-permute-start
  10.7 1.1 %constant_dynamic-slice_fusion = (bf16[1024,128]{1,0:T(8,128)(2,1)S(1)}, bf16[1024,128]{1,0:T(8,128)(2,1)S(1)}) fusion(bf16[1024,256]{1,0:T(8,128)(2,1)} %param.11, s32[]{:T(128)S(6)} %select_n.17, s32[]{:T(128)S(6)} %select_n.16), kind=kLoop, calls=%fused_computation.2 | loop fusion | bytes 1048584 | tf_op jit(solution)/shard_map/dynamic_slice | solution.py:326
  11.7 0.3 collective-permute-start.1
  12.0 0.0 collective-permute-done.kb_ref
  12.0 1.3 %collective-permute-done.1.vb_ref = bf16[1024,128]{1,0:T(8,128)(2,1)S(1)} collective-permute-done((bf16[1024,128]{1,0:T(8,128)(2,1)S(1)}, bf16[1024,128]{1,0:T(8,128)(2,1)S(1)}, u32[]{:S(2)}, u32[]{:S(2)}) %collective-permute-start.1) | collective-permute-done | bytes 262176 | tf_op jit(solution)/shard_map/ppermute | solution.py:330
  13.3 7.8 %all-to-all-done.q_ref = bf16[32,40,128]{2,1,0:T(8,128)(2,1)S(1)} async-done(((bf16[32,40,128]{2,1,0:T(8,128)(2,1)}), bf16[32,40,128]{2,1,0:T(8,128)(2,1)S(1)}, u32[]{:S(2)}, u32[]{:S(2)}) %all-to-all-start) | async-done | bytes 327712 | tf_op jit(solution)/shard_map/all_to_all | solution.py:319
  21.1 3.5 %attend.1 = (bf16[1088,128]{1,0:T(8,128)(2,1)}, bf16[32,8,128]{2,1,0:T(8,128)(2,1)S(1)}) custom-call(bf16[32,40,128]{2,1,0:T(8,128)(2,1)S(1)} %all-to-all-done.q_ref, bf16[128,1024]{1,0:T(8,128)(2,1)S(1)} %get-tuple-element.40.ka_ref, bf16[1024,128]{1,0:T(8,128)(2,1)S(1)} %get-tuple-element.38.va_ref, bf16[128,1024]{1,0:T(8,128)(2,1)S(1)} %collective-permute-done.kb_ref, ...), custom_call_target="tpu_custom_call" | custom-call | flops 1073741824 | bytes 4194304 | tf_op jit(solution)/shard_map/attend/pallas_call | solution.py:269
  24.6 2.4 %all-to-all-start.1 = ((bf16[32,17,2,128]{3,2,1,0:T(2,128)(2,1)}), bf16[32,17,2,128]{3,2,1,0:T(2,128)(2,1)S(1)}, u32[]{:S(2)}, u32[]{:S(2)}) async-start(bf16[32,17,2,128]{3,2,1,0:T(2,128)(2,1)} %bitcast.4), calls=%async_computation.1 | async-start | bytes 557056 | tf_op jit(solution)/shard_map/all_to_all | solution.py:319
  26.9 1.4 %collective-permute-start.3 = (bf16[32,8,128]{2,1,0:T(8,128)(2,1)S(1)}, bf16[32,8,128]{2,1,0:T(8,128)(2,1)S(1)}, u32[]{:S(2)}, u32[]{:S(2)}) collective-permute-start(bf16[32,8,128]{2,1,0:T(8,128)(2,1)S(1)} %get-tuple-element.32.kv_ref), channel_id=1, source_target_pairs={{0,2},{1,3},{2,0},{3,1},{4,6},{5,7},{6,4},{7,5},{8,10},{9,11},{10,... | collective-permute-start | bytes 196616 | tf_op jit(solution)/shard_map/ppermute | solution.py:369
  28.4 0.6 %collective-permute-start.2 = (bf16[32,8,128]{2,1,0:T(8,128)(2,1)S(1)}, bf16[32,8,128]{2,1,0:T(8,128)(2,1)S(1)}, u32[]{:S(2)}, u32[]{:S(2)}) collective-permute-start(bf16[32,8,128]{2,1,0:T(8,128)(2,1)S(1)} %get-tuple-element.32.kv_ref), channel_id=1, source_target_pairs={{0,1},{1,0},{2,3},{3,2},{4,5},{5,4},{6,7},{7,6},{8,9},{9,8},{10,11... | collective-permute-start | bytes 196616 | tf_op jit(solution)/shard_map/ppermute | solution.py:370
  29.0 3.2 %collective-permute-done.3.kv2_ref = bf16[32,8,128]{2,1,0:T(8,128)(2,1)S(1)} collective-permute-done((bf16[32,8,128]{2,1,0:T(8,128)(2,1)S(1)}, bf16[32,8,128]{2,1,0:T(8,128)(2,1)S(1)}, u32[]{:S(2)}, u32[]{:S(2)}) %collective-permute-start.3) | collective-permute-done | bytes 65568 | tf_op jit(solution)/shard_map/ppermute | solution.py:369
  32.3 1.0 %collective-permute-start.4 = (bf16[32,8,128]{2,1,0:T(8,128)(2,1)S(1)}, bf16[32,8,128]{2,1,0:T(8,128)(2,1)S(1)}, u32[]{:S(2)}, u32[]{:S(2)}) collective-permute-start(bf16[32,8,128]{2,1,0:T(8,128)(2,1)S(1)} %collective-permute-done.3.kv2_ref), channel_id=1, source_target_pairs={{0,1},{1,0},{2,3},{3,2},{4,5},{5,4},{6,7},{7,6},{8,9},{9,8},{10,11... | collective-permute-start | bytes 196616 | tf_op jit(solution)/shard_map/ppermute | solution.py:370
  33.2 0.0 copy-done
  33.2 0.0 copy-done.1
  33.2 1.8 %masks.1 = (f32[2,56,512]{2,1,0:T(8,128)S(1)}, f32[2,56,128]{2,1,0:T(8,128)S(1)}, bf16[768,1792]{1,0:T(8,128)(2,1)S(1)}) custom-call(s32[3,1,14]{2,1,0:T(1,128)S(1)} %bitcast.10, bf16[8,1792]{1,0:T(8,128)(2,1)S(1)} %copy-done, bf16[1792,1792]{1,0:T(8,128)(2,1)} %w_hbm.1), custom_call_target="tpu_custom_call" | custom-call | tf_op jit(solution)/shard_map/masks/pallas_call | solution.py:269
  35.0 0.0 collective-permute-done.2.kv1_ref
  35.0 0.0 collective-permute-done.4.kv3_ref
  35.0 0.4 %fresh.1 = (f32[2,56,128]{2,1,0:T(8,128)S(1)}, f32[2,56,128]{2,1,0:T(8,128)S(1)}) custom-call(f32[2,56,128]{2,1,0:T(8,128)S(1)} %get-tuple-element.31.rows_ref, bf16[32,8,128]{2,1,0:T(8,128)(2,1)S(1)} %get-tuple-element.32.kv_ref, bf16[32,8,128]{2,1,0:T(8,128)(2,1)S(1)} %collective-permute-done.2.kv1_ref, ...), custom_call_target="tpu_custom_call" | custom-call | flops 29360128 | bytes 1048576 | tf_op jit(solution)/shard_map/fresh/pallas_call | solution.py:269
  35.5 2.5 %all-to-all-done.1 = bf16[32,17,2,128]{3,2,1,0:T(2,128)(2,1)S(1)} async-done(((bf16[32,17,2,128]{3,2,1,0:T(2,128)(2,1)}), bf16[32,17,2,128]{3,2,1,0:T(2,128)(2,1)S(1)}, u32[]{:S(2)}, u32[]{:S(2)}) %all-to-all-start.1) | async-done | bytes 278560 | tf_op jit(solution)/shard_map/all_to_all | solution.py:319
  38.0 3.0 %project.1 = bf16[8,1792]{1,0:T(8,128)(2,1)} custom-call(bf16[1088,128]{1,0:T(8,128)(2,1)S(1)} %bitcast.8, f32[2,56,128]{2,1,0:T(8,128)S(1)} %get-tuple-element.33.out_ref, f32[2,56,128]{2,1,0:T(8,128)S(1)} %get-tuple-element.34.lse_ref, f32[2,56,512]{2,1,0:T(8,128)S(1)} %get-tuple-element.35.match_ref, bf16[768,1792]{1,0:T(8,128)(2,1)S(1)} %get-tuple-element.36.first_ref, ...), custom_call_target="tpu_custom_call" | custom-call | flops 51380224 | bytes 6422528 | tf_op jit(solution)/shard_map/project/pallas_call | solution.py:269
  (1 shorter events, 0.0 us)
Async XLA Ops:
  0.0 33.2 %copy-start = (bf16[8,1792]{1,0:T(8,128)(2,1)S(1)}, bf16[8,1792]{1,0:T(8,128)(2,1)}, u32[]{:S(2)}) copy-start(bf16[8,1792]{1,0:T(8,128)(2,1)} %q_ref) | copy-start | bytes 86020
  0.0 33.2 %copy-start.1 = (s32[1,14,3]{1,0,2:T(1,128)S(1)}, s32[1,14,3]{1,0,2:T(1,128)}, u32[]{:S(2)}) copy-start(s32[1,14,3]{1,0,2:T(1,128)} %param.12) | copy-start | bytes 508
  1.9 19.2 %all-to-all-start = ((bf16[32,40,128]{2,1,0:T(8,128)(2,1)}), bf16[32,40,128]{2,1,0:T(8,128)(2,1)S(1)}, u32[]{:S(2)}, u32[]{:S(2)}) async-start(bf16[32,40,128]{2,1,0:T(8,128)(2,1)} %bitcast.11), calls=%async_computation | async-start | bytes 655360 | tf_op jit(solution)/shard_map/all_to_all | solution.py:319
  10.3 1.7 %collective-permute-start = (bf16[128,1024]{1,0:T(8,128)(2,1)S(1)}, bf16[128,1024]{1,0:T(8,128)(2,1)S(1)}, u32[]{:S(2)}, u32[]{:S(2)}) collective-permute-start(bf16[128,1024]{1,0:T(8,128)(2,1)S(1)} %get-tuple-element.39), channel_id=1, source_target_pairs={{0,1},{1,0},{2,3},{3,2},{4,5},{5,4},{6,7},{7,6},{8,9},{9,8},{10,11... | collective-permute-start | bytes 786440 | tf_op jit(solution)/shard_map/ppermute | solution.py:330
  11.7 1.6 %collective-permute-start.1 = (bf16[1024,128]{1,0:T(8,128)(2,1)S(1)}, bf16[1024,128]{1,0:T(8,128)(2,1)S(1)}, u32[]{:S(2)}, u32[]{:S(2)}) collective-permute-start(bf16[1024,128]{1,0:T(8,128)(2,1)S(1)} %get-tuple-element.37), channel_id=1, source_target_pairs={{0,1},{1,0},{2,3},{3,2},{4,5},{5,4},{6,7},{7,6},{8,9},{9,8},{10,11... | collective-permute-start | bytes 786440 | tf_op jit(solution)/shard_map/ppermute | solution.py:330
  24.6 13.4 %all-to-all-start.1 = ((bf16[32,17,2,128]{3,2,1,0:T(2,128)(2,1)}), bf16[32,17,2,128]{3,2,1,0:T(2,128)(2,1)S(1)}, u32[]{:S(2)}, u32[]{:S(2)}) async-start(bf16[32,17,2,128]{3,2,1,0:T(2,128)(2,1)} %bitcast.4), calls=%async_computation.1 | async-start | bytes 557056 | tf_op jit(solution)/shard_map/all_to_all | solution.py:319
  26.9 5.3 %collective-permute-start.3 = (bf16[32,8,128]{2,1,0:T(8,128)(2,1)S(1)}, bf16[32,8,128]{2,1,0:T(8,128)(2,1)S(1)}, u32[]{:S(2)}, u32[]{:S(2)}) collective-permute-start(bf16[32,8,128]{2,1,0:T(8,128)(2,1)S(1)} %get-tuple-element.32.kv_ref), channel_id=1, source_target_pairs={{0,2},{1,3},{2,0},{3,1},{4,6},{5,7},{6,4},{7,5},{8,10},{9,11},{10,... | collective-permute-start | bytes 196616 | tf_op jit(solution)/shard_map/ppermute | solution.py:369
  28.4 6.7 %collective-permute-start.2 = (bf16[32,8,128]{2,1,0:T(8,128)(2,1)S(1)}, bf16[32,8,128]{2,1,0:T(8,128)(2,1)S(1)}, u32[]{:S(2)}, u32[]{:S(2)}) collective-permute-start(bf16[32,8,128]{2,1,0:T(8,128)(2,1)S(1)} %get-tuple-element.32.kv_ref), channel_id=1, source_target_pairs={{0,1},{1,0},{2,3},{3,2},{4,5},{5,4},{6,7},{7,6},{8,9},{9,8},{10,11... | collective-permute-start | bytes 196616 | tf_op jit(solution)/shard_map/ppermute | solution.py:370
  32.3 2.8 %collective-permute-start.4 = (bf16[32,8,128]{2,1,0:T(8,128)(2,1)S(1)}, bf16[32,8,128]{2,1,0:T(8,128)(2,1)S(1)}, u32[]{:S(2)}, u32[]{:S(2)}) collective-permute-start(bf16[32,8,128]{2,1,0:T(8,128)(2,1)S(1)} %collective-permute-done.3.kv2_ref), channel_id=1, source_target_pairs={{0,1},{1,0},{2,3},{3,2},{4,5},{5,4},{6,7},{7,6},{8,9},{9,8},{10,11... | collective-permute-start | bytes 196616 | tf_op jit(solution)/shard_map/ppermute | solution.py:370

commit v22 on v20

--- a/solution.py
+++ b/solution.py
@@ -115,7 +115,7 @@
         copy.wait()
 
 
-def attend_kernel(per, q_ref, ka_ref, va_ref, kb_ref, vb_ref, out_hbm, fresh_ref, out_ref, sems):
+def attend_kernel(per, q_ref, k_ref, v_ref, out_hbm, fresh_ref, out_ref, sems):
     sources = q_ref.shape[0]
     sent = []
     step = STEP // per
@@ -125,24 +125,23 @@
     diagonal = row == lane % per
     group = lax.broadcasted_iota(jnp.int32, (2, LANES), 1) // per
     second = lax.broadcasted_iota(jnp.int32, (2, LANES), 0)
-    ones = jnp.ones(va_ref.shape, jnp.bfloat16)
+    ones = jnp.ones(v_ref.shape, jnp.bfloat16)
     fresh_ref[...] = q_ref[:, per:, :]
 
     def scores(first):
         q = q_ref[first : first + step, :per, :].reshape(step * per, HD)
-        return [jnp.dot(q, k_ref[...], preferred_element_type=jnp.float32) for k_ref in (ka_ref, kb_ref)]
+        return jnp.dot(q, k_ref[...], preferred_element_type=jnp.float32)
 
     ahead = scores(0)
     for first in range(0, sources, step):
-        sa, sb = ahead
+        score = ahead
         if first + step < sources:
             ahead = scores(first + step)
-        top = scale * jnp.maximum(jnp.max(sa, axis=1, keepdims=True), jnp.max(sb, axis=1, keepdims=True))
-        wa = jnp.exp2(sa * scale - top).astype(jnp.bfloat16)
-        wb = jnp.exp2(sb * scale - top).astype(jnp.bfloat16)
+        top = scale * jnp.max(score, axis=1, keepdims=True)
+        weights = jnp.exp2(score * scale - top).astype(jnp.bfloat16)
         both = jnp.dot(
-            wa, jnp.concatenate([va_ref[...], ones], axis=1), preferred_element_type=jnp.float32
-        ) + jnp.dot(wb, jnp.concatenate([vb_ref[...], ones], axis=1), preferred_element_type=jnp.float32)
+            weights, jnp.concatenate([v_ref[...], ones], axis=1), preferred_element_type=jnp.float32
+        )
         total = both[:, HD:]
         out = both[:, :HD] / total
         lse = top + jnp.log(total) * LOG2E
@@ -333,8 +332,10 @@
             jax.ShapeDtypeStruct((devices * (per + 2), HD), bf16),
             jax.ShapeDtypeStruct((devices, tokens, HD), bf16),
         ),
-        [VMEM] * 5,
-        got, k_own, v_own, k_peer, v_peer,
+        [VMEM] * 3,
+        got,
+        jnp.concatenate([k_own, k_peer], axis=1),
+        jnp.concatenate([v_own, v_peer], axis=0),
         outs=(ANY, VMEM),
         scratch=[
             pltpu.VMEM((devices * (per + 2), HD), bf16),

time: 41.2 us -> 43 us (1.044)
  waiting for transfers between devices: 14.8 us -> 16.3 us
    all_to_all x2, waiting for transfers between devices: 10.2 us -> 11.8 us  [exchange(): lax.all_to_all(x, 'seq', split_axis=0, concat_axis=0, axis_index_groups=r...]
  transfers between devices with their start and end apart: 7 -> 7, of which waited for: 4 -> 4; matrix products, arithmetic and copies ran while one was open for 6% -> 3% of each run, Pallas kernels for 5% -> 5%
where the time goes in v22:
time: 43 us; the launch traced here: 42.5 us
  waiting for transfers between devices  16.3 us (38%)
  starting transfers between devices  13 us (30%)
  Pallas kernels  10.7 us (25%)
  local copies, waits for them, and re-layouts  2.37 us (6%)
    all_to_all x2, waiting for transfers between devices, exchange(): lax.all_to_all(x, 'seq', split_axis=0, concat_axis=0, axis_index_groups=r...  11.8 us
    pallas_call x5, Pallas kernels, call(): pl.pallas_call(kernel, name=name, out_shape=out_shape, in_specs=specs, ou...  10.7 us
    all_to_all x2, starting transfers between devices, exchange(): lax.all_to_all(x, 'seq', split_axis=0, concat_axis=0, axis_index_groups=r...  9.5 us
    ppermute x1, waiting for transfers between devices, body(): far = lax.ppermute(fresh, 'seq', partner(2))  3.25 us
    ppermute x2, starting transfers between devices, body(): near, both = [lax.ppermute(x, 'seq', partner(1)) for x in (fresh, far)]  1.6 us
    ppermute x1, starting transfers between devices, body(): far = lax.ppermute(fresh, 'seq', partner(2))  1.44 us
    optimization_barrier x1, local copies, waits for them, and re-layouts, body(): lax.optimization_barrier((send, cache_keys, cache_values, picks, queries))  1.25 us
    ppermute x2, waiting for transfers between devices, body(): lax.ppermute(x, 'seq', partner(1))  1.24 us
  transfers between devices with their start and end apart: 7, of which 4 were waited for; matrix products, arithmetic and copies ran while one was open for 3% of the time, Pallas kernels for 5%

profile of v22, /device:TPU:1, one launch (start us, length us, event | category | flops | bytes accessed | tf_op | source)
XLA Modules:
  0.0 42.5 jit_solution(7774067810527687802)
XLA Ops:
  0.0 0.0 copy-start
  0.0 0.0 copy-start.1
  0.0 1.9 %pack.1 = bf16[8,2,2,40,128]{4,3,2,1,0:T(8,128)(2,1)} custom-call(s32[3,1,14]{2,1,0:T(1,128)} %bitcast.9, bf16[8,1792]{1,0:T(8,128)(2,1)} %q_ref, bf16[8,256]{1,0:T(8,128)(2,1)} %k_hbm.1, bf16[8,256]{1,0:T(8,128)(2,1)} %v_hbm.1), custom_call_target="tpu_custom_call" | custom-call | tf_op jit(solution)/shard_map/pack/pallas_call | solution.py:264
  1.9 1.2 %copy.8 = bf16[1024,256]{0,1:T(8,128)(2,1)S(1)} copy(bf16[1024,256]{1,0:T(8,128)(2,1)} %param.10) | data formatting | bytes 1048576 | tf_op jit(solution)/shard_map/optimization_barrier | solution.py:308
  3.2 0.1 collective-permute-start
  3.3 7.2 %all-to-all-start = ((bf16[32,40,128]{2,1,0:T(8,128)(2,1)}), bf16[32,40,128]{2,1,0:T(8,128)(2,1)S(1)}, u32[]{:S(2)}, u32[]{:S(2)}) async-start(bf16[32,40,128]{2,1,0:T(8,128)(2,1)} %bitcast.11), calls=%async_computation | async-start | bytes 655360 | tf_op jit(solution)/shard_map/all_to_all | solution.py:314
  10.5 1.1 %constant_dynamic-slice_fusion.1 = (bf16[1024,128]{1,0:T(8,128)(2,1)S(1)}, bf16[1024,128]{1,0:T(8,128)(2,1)S(1)}) fusion(bf16[1024,256]{1,0:T(8,128)(2,1)} %param.11, s32[]{:T(128)S(6)} %select_n.16, s32[]{:T(128)S(6)} %select_n.17), kind=kLoop, calls=%fused_computation.5 | loop fusion | bytes 1048584 | tf_op jit(solution)/shard_map/dynamic_slice | solution.py:321
  11.6 0.3 collective-permute-start.1
  11.9 0.0 collective-permute-done
  11.9 1.2 %collective-permute-done.1 = bf16[1024,128]{1,0:T(8,128)(2,1)S(1)} collective-permute-done((bf16[1024,128]{1,0:T(8,128)(2,1)S(1)}, bf16[1024,128]{1,0:T(8,128)(2,1)S(1)}, u32[]{:S(2)}, u32[]{:S(2)}) %collective-permute-start.1) | collective-permute-done | bytes 262176 | tf_op jit(solution)/shard_map/ppermute | solution.py:325
  13.2 9.4 %all-to-all-done.q_ref = bf16[32,40,128]{2,1,0:T(8,128)(2,1)S(1)} async-done(((bf16[32,40,128]{2,1,0:T(8,128)(2,1)}), bf16[32,40,128]{2,1,0:T(8,128)(2,1)S(1)}, u32[]{:S(2)}, u32[]{:S(2)}) %all-to-all-start) | async-done | bytes 327712 | tf_op jit(solution)/shard_map/all_to_all | solution.py:314
  22.6 3.6 %attend.1 = (bf16[1088,128]{1,0:T(8,128)(2,1)}, bf16[32,8,128]{2,1,0:T(8,128)(2,1)S(1)}) custom-call(bf16[32,40,128]{2,1,0:T(8,128)(2,1)S(1)} %all-to-all-done.q_ref, bf16[128,2048]{1,0:T(8,128)(2,1)S(1)} %pad_maximum_fusion.k_ref, bf16[2048,128]{1,0:T(8,128)(2,1)S(1)} %pad_maximum_fusion.1.v_ref), custom_call_target="tpu_custom_call" | custom-call | flops 1073741824 | bytes 4194304 | tf_op jit(solution)/shard_map/attend/pallas_call | solution.py:264
  26.2 2.4 %all-to-all-start.1 = ((bf16[32,17,2,128]{3,2,1,0:T(2,128)(2,1)}), bf16[32,17,2,128]{3,2,1,0:T(2,128)(2,1)S(1)}, u32[]{:S(2)}, u32[]{:S(2)}) async-start(bf16[32,17,2,128]{3,2,1,0:T(2,128)(2,1)} %bitcast.4), calls=%async_computation.1 | async-start | bytes 557056 | tf_op jit(solution)/shard_map/all_to_all | solution.py:314
  28.5 1.4 %collective-permute-start.3 = (bf16[32,8,128]{2,1,0:T(8,128)(2,1)S(1)}, bf16[32,8,128]{2,1,0:T(8,128)(2,1)S(1)}, u32[]{:S(2)}, u32[]{:S(2)}) collective-permute-start(bf16[32,8,128]{2,1,0:T(8,128)(2,1)S(1)} %get-tuple-element.32.kv_ref), channel_id=1, source_target_pairs={{0,2},{1,3},{2,0},{3,1},{4,6},{5,7},{6,4},{7,5},{8,10},{9,11},{10,... | collective-permute-start | bytes 196616 | tf_op jit(solution)/shard_map/ppermute | solution.py:366
  30.0 0.6 %collective-permute-start.2 = (bf16[32,8,128]{2,1,0:T(8,128)(2,1)S(1)}, bf16[32,8,128]{2,1,0:T(8,128)(2,1)S(1)}, u32[]{:S(2)}, u32[]{:S(2)}) collective-permute-start(bf16[32,8,128]{2,1,0:T(8,128)(2,1)S(1)} %get-tuple-element.32.kv_ref), channel_id=1, source_target_pairs={{0,1},{1,0},{2,3},{3,2},{4,5},{5,4},{6,7},{7,6},{8,9},{9,8},{10,11... | collective-permute-start | bytes 196616 | tf_op jit(solution)/shard_map/ppermute | solution.py:367
  30.6 3.2 %collective-permute-done.3.kv2_ref = bf16[32,8,128]{2,1,0:T(8,128)(2,1)S(1)} collective-permute-done((bf16[32,8,128]{2,1,0:T(8,128)(2,1)S(1)}, bf16[32,8,128]{2,1,0:T(8,128)(2,1)S(1)}, u32[]{:S(2)}, u32[]{:S(2)}) %collective-permute-start.3) | collective-permute-done | bytes 65568 | tf_op jit(solution)/shard_map/ppermute | solution.py:366
  33.8 1.0 %collective-permute-start.4 = (bf16[32,8,128]{2,1,0:T(8,128)(2,1)S(1)}, bf16[32,8,128]{2,1,0:T(8,128)(2,1)S(1)}, u32[]{:S(2)}, u32[]{:S(2)}) collective-permute-start(bf16[32,8,128]{2,1,0:T(8,128)(2,1)S(1)} %collective-permute-done.3.kv2_ref), channel_id=1, source_target_pairs={{0,1},{1,0},{2,3},{3,2},{4,5},{5,4},{6,7},{7,6},{8,9},{9,8},{10,11... | collective-permute-start | bytes 196616 | tf_op jit(solution)/shard_map/ppermute | solution.py:367
  34.8 0.0 copy-done
  34.8 0.0 copy-done.1
  34.8 1.8 %masks.1 = (f32[2,56,512]{2,1,0:T(8,128)S(1)}, f32[2,56,128]{2,1,0:T(8,128)S(1)}, bf16[768,1792]{1,0:T(8,128)(2,1)S(1)}) custom-call(s32[3,1,14]{2,1,0:T(1,128)S(1)} %bitcast.10, bf16[8,1792]{1,0:T(8,128)(2,1)S(1)} %copy-done, bf16[1792,1792]{1,0:T(8,128)(2,1)} %w_hbm.1), custom_call_target="tpu_custom_call" | custom-call | tf_op jit(solution)/shard_map/masks/pallas_call | solution.py:264
  36.6 0.0 collective-permute-done.2.kv1_ref
  36.6 0.0 collective-permute-done.4.kv3_ref
  36.6 0.4 %fresh.1 = (f32[2,56,128]{2,1,0:T(8,128)S(1)}, f32[2,56,128]{2,1,0:T(8,128)S(1)}) custom-call(f32[2,56,128]{2,1,0:T(8,128)S(1)} %get-tuple-element.31.rows_ref, bf16[32,8,128]{2,1,0:T(8,128)(2,1)S(1)} %get-tuple-element.32.kv_ref, bf16[32,8,128]{2,1,0:T(8,128)(2,1)S(1)} %collective-permute-done.2.kv1_ref, ...), custom_call_target="tpu_custom_call" | custom-call | flops 29360128 | bytes 1048576 | tf_op jit(solution)/shard_map/fresh/pallas_call | solution.py:264
  37.1 2.5 %all-to-all-done.1 = bf16[32,17,2,128]{3,2,1,0:T(2,128)(2,1)S(1)} async-done(((bf16[32,17,2,128]{3,2,1,0:T(2,128)(2,1)}), bf16[32,17,2,128]{3,2,1,0:T(2,128)(2,1)S(1)}, u32[]{:S(2)}, u32[]{:S(2)}) %all-to-all-start.1) | async-done | bytes 278560 | tf_op jit(solution)/shard_map/all_to_all | solution.py:314
  39.5 3.0 %project.1 = bf16[8,1792]{1,0:T(8,128)(2,1)} custom-call(bf16[1088,128]{1,0:T(8,128)(2,1)S(1)} %bitcast.8, f32[2,56,128]{2,1,0:T(8,128)S(1)} %get-tuple-element.33.out_ref, f32[2,56,128]{2,1,0:T(8,128)S(1)} %get-tuple-element.34.lse_ref, f32[2,56,512]{2,1,0:T(8,128)S(1)} %get-tuple-element.35.match_ref, bf16[768,1792]{1,0:T(8,128)(2,1)S(1)} %get-tuple-element.36.first_ref, ...), custom_call_target="tpu_custom_call" | custom-call | flops 51380224 | bytes 6422528 | tf_op jit(solution)/shard_map/project/pallas_call | solution.py:264
  (3 shorter events, 0.1 us)
Async XLA Ops:
  0.0 34.8 %copy-start = (bf16[8,1792]{1,0:T(8,128)(2,1)S(1)}, bf16[8,1792]{1,0:T(8,128)(2,1)}, u32[]{:S(2)}) copy-start(bf16[8,1792]{1,0:T(8,128)(2,1)} %q_ref) | copy-start | bytes 86020
  0.0 34.8 %copy-start.1 = (s32[1,14,3]{1,0,2:T(1,128)S(1)}, s32[1,14,3]{1,0,2:T(1,128)}, u32[]{:S(2)}) copy-start(s32[1,14,3]{1,0,2:T(1,128)} %param.12) | copy-start | bytes 508
  3.2 8.7 %collective-permute-start = (bf16[128,1024]{1,0:T(8,128)(2,1)S(1)}, bf16[128,1024]{1,0:T(8,128)(2,1)S(1)}, u32[]{:S(2)}, u32[]{:S(2)}) collective-permute-start(bf16[128,1024]{1,0:T(8,128)(2,1)S(1)} %get-tuple-element.40), channel_id=1, source_target_pairs={{0,1},{1,0},{2,3},{3,2},{4,5},{5,4},{6,7},{7,6},{8,9},{9,8},{10,11... | collective-permute-start | bytes 786440 | tf_op jit(solution)/shard_map/ppermute | solution.py:325
  3.3 19.2 %all-to-all-start = ((bf16[32,40,128]{2,1,0:T(8,128)(2,1)}), bf16[32,40,128]{2,1,0:T(8,128)(2,1)S(1)}, u32[]{:S(2)}, u32[]{:S(2)}) async-start(bf16[32,40,128]{2,1,0:T(8,128)(2,1)} %bitcast.11), calls=%async_computation | async-start | bytes 655360 | tf_op jit(solution)/shard_map/all_to_all | solution.py:314
  11.6 1.6 %collective-permute-start.1 = (bf16[1024,128]{1,0:T(8,128)(2,1)S(1)}, bf16[1024,128]{1,0:T(8,128)(2,1)S(1)}, u32[]{:S(2)}, u32[]{:S(2)}) collective-permute-start(bf16[1024,128]{1,0:T(8,128)(2,1)S(1)} %get-tuple-element.38), channel_id=1, source_target_pairs={{0,1},{1,0},{2,3},{3,2},{4,5},{5,4},{6,7},{7,6},{8,9},{9,8},{10,11... | collective-permute-start | bytes 786440 | tf_op jit(solution)/shard_map/ppermute | solution.py:325
  26.2 13.4 %all-to-all-start.1 = ((bf16[32,17,2,128]{3,2,1,0:T(2,128)(2,1)}), bf16[32,17,2,128]{3,2,1,0:T(2,128)(2,1)S(1)}, u32[]{:S(2)}, u32[]{:S(2)}) async-start(bf16[32,17,2,128]{3,2,1,0:T(2,128)(2,1)} %bitcast.4), calls=%async_computation.1 | async-start | bytes 557056 | tf_op jit(solution)/shard_map/all_to_all | solution.py:314
  28.5 5.3 %collective-permute-start.3 = (bf16[32,8,128]{2,1,0:T(8,128)(2,1)S(1)}, bf16[32,8,128]{2,1,0:T(8,128)(2,1)S(1)}, u32[]{:S(2)}, u32[]{:S(2)}) collective-permute-start(bf16[32,8,128]{2,1,0:T(8,128)(2,1)S(1)} %get-tuple-element.32.kv_ref), channel_id=1, source_target_pairs={{0,2},{1,3},{2,0},{3,1},{4,6},{5,7},{6,4},{7,5},{8,10},{9,11},{10,... | collective-permute-start | bytes 196616 | tf_op jit(solution)/shard_map/ppermute | solution.py:366
  30.0 6.7 %collective-permute-start.2 = (bf16[32,8,128]{2,1,0:T(8,128)(2,1)S(1)}, bf16[32,8,128]{2,1,0:T(8,128)(2,1)S(1)}, u32[]{:S(2)}, u32[]{:S(2)}) collective-permute-start(bf16[32,8,128]{2,1,0:T(8,128)(2,1)S(1)} %get-tuple-element.32.kv_ref), channel_id=1, source_target_pairs={{0,1},{1,0},{2,3},{3,2},{4,5},{5,4},{6,7},{7,6},{8,9},{9,8},{10,11... | collective-permute-start | bytes 196616 | tf_op jit(solution)/shard_map/ppermute | solution.py:367
  33.8 2.8 %collective-permute-start.4 = (bf16[32,8,128]{2,1,0:T(8,128)(2,1)S(1)}, bf16[32,8,128]{2,1,0:T(8,128)(2,1)S(1)}, u32[]{:S(2)}, u32[]{:S(2)}) collective-permute-start(bf16[32,8,128]{2,1,0:T(8,128)(2,1)S(1)} %collective-permute-done.3.kv2_ref), channel_id=1, source_target_pairs={{0,1},{1,0},{2,3},{3,2},{4,5},{5,4},{6,7},{7,6},{8,9},{9,8},{10,11... | collective-permute-start | bytes 196616 | tf_op jit(solution)/shard_map/ppermute | solution.py:367

commit v23 on v20

--- a/solution.py
+++ b/solution.py
@@ -117,7 +117,6 @@
 
 def attend_kernel(per, q_ref, ka_ref, va_ref, kb_ref, vb_ref, out_hbm, fresh_ref, out_ref, sems):
     sources = q_ref.shape[0]
-    sent = []
     step = STEP // per
     scale = LOG2E * HD**-0.5
     row = lax.broadcasted_iota(jnp.int32, (per, LANES), 0)
@@ -132,14 +131,9 @@
         q = q_ref[first : first + step, :per, :].reshape(step * per, HD)
         return [jnp.dot(q, k_ref[...], preferred_element_type=jnp.float32) for k_ref in (ka_ref, kb_ref)]
 
-    ahead = scores(0)
-    for first in range(0, sources, step):
-        sa, sb = ahead
-        if first + step < sources:
-            ahead = scores(first + step)
-        top = scale * jnp.maximum(jnp.max(sa, axis=1, keepdims=True), jnp.max(sb, axis=1, keepdims=True))
-        wa = jnp.exp2(sa * scale - top).astype(jnp.bfloat16)
-        wb = jnp.exp2(sb * scale - top).astype(jnp.bfloat16)
+    sent = []
+
+    def finish(first, wa, wb, top):
         both = jnp.dot(
             wa, jnp.concatenate([va_ref[...], ones], axis=1), preferred_element_type=jnp.float32
         ) + jnp.dot(wb, jnp.concatenate([vb_ref[...], ones], axis=1), preferred_element_type=jnp.float32)
@@ -159,6 +153,19 @@
         out_ref[done, :] = jnp.concatenate(rows, axis=0).astype(jnp.bfloat16)
         sent.append(pltpu.make_async_copy(out_ref.at[done], out_hbm.at[done], sems.at[first // step]))
         sent[-1].start()
+
+    ahead, behind = scores(0), None
+    for first in range(0, sources, step):
+        sa, sb = ahead
+        if first + step < sources:
+            ahead = scores(first + step)
+        if behind is not None:
+            finish(*behind)
+        top = scale * jnp.maximum(jnp.max(sa, axis=1, keepdims=True), jnp.max(sb, axis=1, keepdims=True))
+        wa = jnp.exp2(sa * scale - top).astype(jnp.bfloat16)
+        wb = jnp.exp2(sb * scale - top).astype(jnp.bfloat16)
+        behind = (first, wa, wb, top)
+    finish(*behind)
     for copy in sent:
         copy.wait()
 

time: 41.2 us -> 41.3 us (level)
  no operation moved by 1% of the time
where the time goes in v23:
time: 41.3 us; the launch traced here: 40.9 us
  waiting for transfers between devices  14.8 us (36%)
  starting transfers between devices  13.1 us (32%)
  Pallas kernels  10.5 us (25%)
  local copies, waits for them, and re-layouts  2.36 us (6%)
    pallas_call x5, Pallas kernels, call(): pl.pallas_call(kernel, name=name, out_shape=out_shape, in_specs=specs, ou...  10.5 us
    all_to_all x2, waiting for transfers between devices, exchange(): lax.all_to_all(x, 'seq', split_axis=0, concat_axis=0, axis_index_groups=r...  10.2 us
    all_to_all x2, starting transfers between devices, exchange(): lax.all_to_all(x, 'seq', split_axis=0, concat_axis=0, axis_index_groups=r...  9.46 us
    ppermute x1, waiting for transfers between devices, body(): far = lax.ppermute(fresh, 'seq', partner(2))  3.25 us
    ppermute x2, starting transfers between devices, body(): near, both = [lax.ppermute(x, 'seq', partner(1)) for x in (fresh, far)]  1.6 us
    ppermute x1, starting transfers between devices, body(): far = lax.ppermute(fresh, 'seq', partner(2))  1.45 us
    ppermute x2, waiting for transfers between devices, body(): lax.ppermute(x, 'seq', partner(1))  1.28 us
    optimization_barrier x1, local copies, waits for them, and re-layouts, body(): lax.optimization_barrier((send, cache_keys, cache_values, picks, queries))  1.25 us
  transfers between devices with their start and end apart: 7, of which 4 were waited for; matrix products, arithmetic and copies ran while one was open for 6% of the time, Pallas kernels for 5%

profile of v23, /device:TPU:1, one launch (start us, length us, event | category | flops | bytes accessed | tf_op | source)
XLA Modules:
  0.0 40.9 jit_solution(5185080340598006815)
XLA Ops:
  0.0 0.0 copy-start
  0.0 0.0 copy-start.1
  0.0 1.9 %pack.1 = bf16[8,2,2,40,128]{4,3,2,1,0:T(8,128)(2,1)} custom-call(s32[3,1,14]{2,1,0:T(1,128)} %bitcast.9, bf16[8,1792]{1,0:T(8,128)(2,1)} %q_ref, bf16[8,256]{1,0:T(8,128)(2,1)} %k_hbm.1, bf16[8,256]{1,0:T(8,128)(2,1)} %v_hbm.1), custom_call_target="tpu_custom_call" | custom-call | tf_op jit(solution)/shard_map/pack/pallas_call | solution.py:272
  1.9 7.1 %all-to-all-start = ((bf16[32,40,128]{2,1,0:T(8,128)(2,1)}), bf16[32,40,128]{2,1,0:T(8,128)(2,1)S(1)}, u32[]{:S(2)}, u32[]{:S(2)}) async-start(bf16[32,40,128]{2,1,0:T(8,128)(2,1)} %bitcast.11), calls=%async_computation | async-start | bytes 655360 | tf_op jit(solution)/shard_map/all_to_all | solution.py:322
  9.0 1.2 %copy.8 = bf16[1024,256]{0,1:T(8,128)(2,1)S(1)} copy(bf16[1024,256]{1,0:T(8,128)(2,1)} %param.10) | data formatting | bytes 1048576 | tf_op jit(solution)/shard_map/optimization_barrier | solution.py:316
  10.3 0.3 collective-permute-start
  10.7 1.1 %constant_dynamic-slice_fusion = (bf16[1024,128]{1,0:T(8,128)(2,1)S(1)}, bf16[1024,128]{1,0:T(8,128)(2,1)S(1)}) fusion(bf16[1024,256]{1,0:T(8,128)(2,1)} %param.11, s32[]{:T(128)S(6)} %select_n.17, s32[]{:T(128)S(6)} %select_n.16), kind=kLoop, calls=%fused_computation.2 | loop fusion | bytes 1048584 | tf_op jit(solution)/shard_map/dynamic_slice | solution.py:329
  11.7 0.3 collective-permute-start.1
  12.0 0.0 collective-permute-done.kb_ref
  12.0 1.3 %collective-permute-done.1.vb_ref = bf16[1024,128]{1,0:T(8,128)(2,1)S(1)} collective-permute-done((bf16[1024,128]{1,0:T(8,128)(2,1)S(1)}, bf16[1024,128]{1,0:T(8,128)(2,1)S(1)}, u32[]{:S(2)}, u32[]{:S(2)}) %collective-permute-start.1) | collective-permute-done | bytes 262176 | tf_op jit(solution)/shard_map/ppermute | solution.py:333
  13.3 7.8 %all-to-all-done.q_ref = bf16[32,40,128]{2,1,0:T(8,128)(2,1)S(1)} async-done(((bf16[32,40,128]{2,1,0:T(8,128)(2,1)}), bf16[32,40,128]{2,1,0:T(8,128)(2,1)S(1)}, u32[]{:S(2)}, u32[]{:S(2)}) %all-to-all-start) | async-done | bytes 327712 | tf_op jit(solution)/shard_map/all_to_all | solution.py:322
  21.1 3.4 %attend.1 = (bf16[1088,128]{1,0:T(8,128)(2,1)}, bf16[32,8,128]{2,1,0:T(8,128)(2,1)S(1)}) custom-call(bf16[32,40,128]{2,1,0:T(8,128)(2,1)S(1)} %all-to-all-done.q_ref, bf16[128,1024]{1,0:T(8,128)(2,1)S(1)} %get-tuple-element.40.ka_ref, bf16[1024,128]{1,0:T(8,128)(2,1)S(1)} %get-tuple-element.38.va_ref, bf16[128,1024]{1,0:T(8,128)(2,1)S(1)} %collective-permute-done.kb_ref, ...), custom_call_target="tpu_custom_call" | custom-call | flops 1073741824 | bytes 4194304 | tf_op jit(solution)/shard_map/attend/pallas_call | solution.py:272
  24.5 2.4 %all-to-all-start.1 = ((bf16[32,17,2,128]{3,2,1,0:T(2,128)(2,1)}), bf16[32,17,2,128]{3,2,1,0:T(2,128)(2,1)S(1)}, u32[]{:S(2)}, u32[]{:S(2)}) async-start(bf16[32,17,2,128]{3,2,1,0:T(2,128)(2,1)} %bitcast.4), calls=%async_computation.1 | async-start | bytes 557056 | tf_op jit(solution)/shard_map/all_to_all | solution.py:322
  26.8 1.4 %collective-permute-start.3 = (bf16[32,8,128]{2,1,0:T(8,128)(2,1)S(1)}, bf16[32,8,128]{2,1,0:T(8,128)(2,1)S(1)}, u32[]{:S(2)}, u32[]{:S(2)}) collective-permute-start(bf16[32,8,128]{2,1,0:T(8,128)(2,1)S(1)} %get-tuple-element.32.kv_ref), channel_id=1, source_target_pairs={{0,2},{1,3},{2,0},{3,1},{4,6},{5,7},{6,4},{7,5},{8,10},{9,11},{10,... | collective-permute-start | bytes 196616 | tf_op jit(solution)/shard_map/ppermute | solution.py:372
  28.3 0.6 %collective-permute-start.2 = (bf16[32,8,128]{2,1,0:T(8,128)(2,1)S(1)}, bf16[32,8,128]{2,1,0:T(8,128)(2,1)S(1)}, u32[]{:S(2)}, u32[]{:S(2)}) collective-permute-start(bf16[32,8,128]{2,1,0:T(8,128)(2,1)S(1)} %get-tuple-element.32.kv_ref), channel_id=1, source_target_pairs={{0,1},{1,0},{2,3},{3,2},{4,5},{5,4},{6,7},{7,6},{8,9},{9,8},{10,11... | collective-permute-start | bytes 196616 | tf_op jit(solution)/shard_map/ppermute | solution.py:373
  28.9 3.2 %collective-permute-done.3.kv2_ref = bf16[32,8,128]{2,1,0:T(8,128)(2,1)S(1)} collective-permute-done((bf16[32,8,128]{2,1,0:T(8,128)(2,1)S(1)}, bf16[32,8,128]{2,1,0:T(8,128)(2,1)S(1)}, u32[]{:S(2)}, u32[]{:S(2)}) %collective-permute-start.3) | collective-permute-done | bytes 65568 | tf_op jit(solution)/shard_map/ppermute | solution.py:372
  32.2 1.0 %collective-permute-start.4 = (bf16[32,8,128]{2,1,0:T(8,128)(2,1)S(1)}, bf16[32,8,128]{2,1,0:T(8,128)(2,1)S(1)}, u32[]{:S(2)}, u32[]{:S(2)}) collective-permute-start(bf16[32,8,128]{2,1,0:T(8,128)(2,1)S(1)} %collective-permute-done.3.kv2_ref), channel_id=1, source_target_pairs={{0,1},{1,0},{2,3},{3,2},{4,5},{5,4},{6,7},{7,6},{8,9},{9,8},{10,11... | collective-permute-start | bytes 196616 | tf_op jit(solution)/shard_map/ppermute | solution.py:373
  33.1 0.0 copy-done
  33.1 0.0 copy-done.1
  33.1 1.8 %masks.1 = (f32[2,56,512]{2,1,0:T(8,128)S(1)}, f32[2,56,128]{2,1,0:T(8,128)S(1)}, bf16[768,1792]{1,0:T(8,128)(2,1)S(1)}) custom-call(s32[3,1,14]{2,1,0:T(1,128)S(1)} %bitcast.10, bf16[8,1792]{1,0:T(8,128)(2,1)S(1)} %copy-done, bf16[1792,1792]{1,0:T(8,128)(2,1)} %w_hbm.1), custom_call_target="tpu_custom_call" | custom-call | tf_op jit(solution)/shard_map/masks/pallas_call | solution.py:272
  34.9 0.0 collective-permute-done.2.kv1_ref
  34.9 0.0 collective-permute-done.4.kv3_ref
  34.9 0.4 %fresh.1 = (f32[2,56,128]{2,1,0:T(8,128)S(1)}, f32[2,56,128]{2,1,0:T(8,128)S(1)}) custom-call(f32[2,56,128]{2,1,0:T(8,128)S(1)} %get-tuple-element.31.rows_ref, bf16[32,8,128]{2,1,0:T(8,128)(2,1)S(1)} %get-tuple-element.32.kv_ref, bf16[32,8,128]{2,1,0:T(8,128)(2,1)S(1)} %collective-permute-done.2.kv1_ref, ...), custom_call_target="tpu_custom_call" | custom-call | flops 29360128 | bytes 1048576 | tf_op jit(solution)/shard_map/fresh/pallas_call | solution.py:272
  35.4 2.5 %all-to-all-done.1 = bf16[32,17,2,128]{3,2,1,0:T(2,128)(2,1)S(1)} async-done(((bf16[32,17,2,128]{3,2,1,0:T(2,128)(2,1)}), bf16[32,17,2,128]{3,2,1,0:T(2,128)(2,1)S(1)}, u32[]{:S(2)}, u32[]{:S(2)}) %all-to-all-start.1) | async-done | bytes 278560 | tf_op jit(solution)/shard_map/all_to_all | solution.py:322
  37.9 3.0 %project.1 = bf16[8,1792]{1,0:T(8,128)(2,1)} custom-call(bf16[1088,128]{1,0:T(8,128)(2,1)S(1)} %bitcast.8, f32[2,56,128]{2,1,0:T(8,128)S(1)} %get-tuple-element.33.out_ref, f32[2,56,128]{2,1,0:T(8,128)S(1)} %get-tuple-element.34.lse_ref, f32[2,56,512]{2,1,0:T(8,128)S(1)} %get-tuple-element.35.match_ref, bf16[768,1792]{1,0:T(8,128)(2,1)S(1)} %get-tuple-element.36.first_ref, ...), custom_call_target="tpu_custom_call" | custom-call | flops 51380224 | bytes 6422528 | tf_op jit(solution)/shard_map/project/pallas_call | solution.py:272
  (1 shorter events, 0.0 us)
Async XLA Ops:
  0.0 33.1 %copy-start = (bf16[8,1792]{1,0:T(8,128)(2,1)S(1)}, bf16[8,1792]{1,0:T(8,128)(2,1)}, u32[]{:S(2)}) copy-start(bf16[8,1792]{1,0:T(8,128)(2,1)} %q_ref) | copy-start | bytes 86020
  0.0 33.1 %copy-start.1 = (s32[1,14,3]{1,0,2:T(1,128)S(1)}, s32[1,14,3]{1,0,2:T(1,128)}, u32[]{:S(2)}) copy-start(s32[1,14,3]{1,0,2:T(1,128)} %param.12) | copy-start | bytes 508
  1.9 19.2 %all-to-all-start = ((bf16[32,40,128]{2,1,0:T(8,128)(2,1)}), bf16[32,40,128]{2,1,0:T(8,128)(2,1)S(1)}, u32[]{:S(2)}, u32[]{:S(2)}) async-start(bf16[32,40,128]{2,1,0:T(8,128)(2,1)} %bitcast.11), calls=%async_computation | async-start | bytes 655360 | tf_op jit(solution)/shard_map/all_to_all | solution.py:322
  10.3 1.7 %collective-permute-start = (bf16[128,1024]{1,0:T(8,128)(2,1)S(1)}, bf16[128,1024]{1,0:T(8,128)(2,1)S(1)}, u32[]{:S(2)}, u32[]{:S(2)}) collective-permute-start(bf16[128,1024]{1,0:T(8,128)(2,1)S(1)} %get-tuple-element.39), channel_id=1, source_target_pairs={{0,1},{1,0},{2,3},{3,2},{4,5},{5,4},{6,7},{7,6},{8,9},{9,8},{10,11... | collective-permute-start | bytes 786440 | tf_op jit(solution)/shard_map/ppermute | solution.py:333
  11.7 1.6 %collective-permute-start.1 = (bf16[1024,128]{1,0:T(8,128)(2,1)S(1)}, bf16[1024,128]{1,0:T(8,128)(2,1)S(1)}, u32[]{:S(2)}, u32[]{:S(2)}) collective-permute-start(bf16[1024,128]{1,0:T(8,128)(2,1)S(1)} %get-tuple-element.37), channel_id=1, source_target_pairs={{0,1},{1,0},{2,3},{3,2},{4,5},{5,4},{6,7},{7,6},{8,9},{9,8},{10,11... | collective-permute-start | bytes 786440 | tf_op jit(solution)/shard_map/ppermute | solution.py:333
  24.5 13.4 %all-to-all-start.1 = ((bf16[32,17,2,128]{3,2,1,0:T(2,128)(2,1)}), bf16[32,17,2,128]{3,2,1,0:T(2,128)(2,1)S(1)}, u32[]{:S(2)}, u32[]{:S(2)}) async-start(bf16[32,17,2,128]{3,2,1,0:T(2,128)(2,1)} %bitcast.4), calls=%async_computation.1 | async-start | bytes 557056 | tf_op jit(solution)/shard_map/all_to_all | solution.py:322
  26.8 5.3 %collective-permute-start.3 = (bf16[32,8,128]{2,1,0:T(8,128)(2,1)S(1)}, bf16[32,8,128]{2,1,0:T(8,128)(2,1)S(1)}, u32[]{:S(2)}, u32[]{:S(2)}) collective-permute-start(bf16[32,8,128]{2,1,0:T(8,128)(2,1)S(1)} %get-tuple-element.32.kv_ref), channel_id=1, source_target_pairs={{0,2},{1,3},{2,0},{3,1},{4,6},{5,7},{6,4},{7,5},{8,10},{9,11},{10,... | collective-permute-start | bytes 196616 | tf_op jit(solution)/shard_map/ppermute | solution.py:372
  28.3 6.7 %collective-permute-start.2 = (bf16[32,8,128]{2,1,0:T(8,128)(2,1)S(1)}, bf16[32,8,128]{2,1,0:T(8,128)(2,1)S(1)}, u32[]{:S(2)}, u32[]{:S(2)}) collective-permute-start(bf16[32,8,128]{2,1,0:T(8,128)(2,1)S(1)} %get-tuple-element.32.kv_ref), channel_id=1, source_target_pairs={{0,1},{1,0},{2,3},{3,2},{4,5},{5,4},{6,7},{7,6},{8,9},{9,8},{10,11... | collective-permute-start | bytes 196616 | tf_op jit(solution)/shard_map/ppermute | solution.py:373
  32.2 2.8 %collective-permute-start.4 = (bf16[32,8,128]{2,1,0:T(8,128)(2,1)S(1)}, bf16[32,8,128]{2,1,0:T(8,128)(2,1)S(1)}, u32[]{:S(2)}, u32[]{:S(2)}) collective-permute-start(bf16[32,8,128]{2,1,0:T(8,128)(2,1)S(1)} %collective-permute-done.3.kv2_ref), channel_id=1, source_target_pairs={{0,1},{1,0},{2,3},{3,2},{4,5},{5,4},{6,7},{7,6},{8,9},{9,8},{10,11... | collective-permute-start | bytes 196616 | tf_op jit(solution)/shard_map/ppermute | solution.py:373

commit v24 on v20

--- a/solution.py
+++ b/solution.py
@@ -125,7 +125,7 @@
     diagonal = row == lane % per
     group = lax.broadcasted_iota(jnp.int32, (2, LANES), 1) // per
     second = lax.broadcasted_iota(jnp.int32, (2, LANES), 0)
-    ones = jnp.ones(va_ref.shape, jnp.bfloat16)
+    ones = jnp.ones((2 * LANES, LANES), jnp.bfloat16)
     fresh_ref[...] = q_ref[:, per:, :]
 
     def scores(first):
@@ -138,13 +138,16 @@
         if first + step < sources:
             ahead = scores(first + step)
         top = scale * jnp.maximum(jnp.max(sa, axis=1, keepdims=True), jnp.max(sb, axis=1, keepdims=True))
-        wa = jnp.exp2(sa * scale - top).astype(jnp.bfloat16)
-        wb = jnp.exp2(sb * scale - top).astype(jnp.bfloat16)
+        wa = jnp.exp2(sa * scale - top)
+        wb = jnp.exp2(sb * scale - top)
+        lanes = sum(w[:, i : i + LANES] for w in (wa, wb) for i in range(0, w.shape[1], LANES))
+        high = lanes.astype(jnp.bfloat16)
+        low = (lanes - high.astype(jnp.float32)).astype(jnp.bfloat16)
+        total = jnp.dot(jnp.concatenate([high, low], axis=1), ones, preferred_element_type=jnp.float32)
         both = jnp.dot(
-            wa, jnp.concatenate([va_ref[...], ones], axis=1), preferred_element_type=jnp.float32
-        ) + jnp.dot(wb, jnp.concatenate([vb_ref[...], ones], axis=1), preferred_element_type=jnp.float32)
-        total = both[:, HD:]
-        out = both[:, :HD] / total
+            wa.astype(jnp.bfloat16), va_ref[...], preferred_element_type=jnp.float32
+        ) + jnp.dot(wb.astype(jnp.bfloat16), vb_ref[...], preferred_element_type=jnp.float32)
+        out = both / total
         lse = top + jnp.log(total) * LOG2E
         rows = []
         for s in range(step):

time: 41.2 us -> 41.9 us (1.017)
  Pallas kernels: 10.4 us -> 11.1 us
    pallas_call x5, Pallas kernels: 10.4 us -> 11.1 us  [call(): pl.pallas_call(kernel, name=name, out_shape=out_shape, in_specs=specs, ou...]
where the time goes in v24:
time: 41.9 us; the launch traced here: 41.5 us
  waiting for transfers between devices  14.8 us (35%)
  starting transfers between devices  13.1 us (31%)
  Pallas kernels  11.1 us (26%)
  local copies, waits for them, and re-layouts  2.36 us (6%)
    pallas_call x5, Pallas kernels, call(): pl.pallas_call(kernel, name=name, out_shape=out_shape, in_specs=specs, ou...  11.1 us
    all_to_all x2, waiting for transfers between devices, exchange(): lax.all_to_all(x, 'seq', split_axis=0, concat_axis=0, axis_index_groups=r...  10.2 us
    all_to_all x2, starting transfers between devices, exchange(): lax.all_to_all(x, 'seq', split_axis=0, concat_axis=0, axis_index_groups=r...  9.45 us
    ppermute x1, waiting for transfers between devices, body(): far = lax.ppermute(fresh, 'seq', partner(2))  3.25 us
    ppermute x2, starting transfers between devices, body(): near, both = [lax.ppermute(x, 'seq', partner(1)) for x in (fresh, far)]  1.6 us
    ppermute x1, starting transfers between devices, body(): far = lax.ppermute(fresh, 'seq', partner(2))  1.44 us
    ppermute x2, waiting for transfers between devices, body(): lax.ppermute(x, 'seq', partner(1))  1.28 us
    optimization_barrier x1, local copies, waits for them, and re-layouts, body(): lax.optimization_barrier((send, cache_keys, cache_values, picks, queries))  1.25 us
  transfers between devices with their start and end apart: 7, of which 4 were waited for; matrix products, arithmetic and copies ran while one was open for 6% of the time, Pallas kernels for 5%

profile of v24, /device:TPU:1, one launch (start us, length us, event | category | flops | bytes accessed | tf_op | source)
XLA Modules:
  0.0 41.5 jit_solution(6631775839967249177)
XLA Ops:
  0.0 0.0 copy-start
  0.0 0.0 copy-start.1
  0.0 1.9 %pack.1 = bf16[8,2,2,40,128]{4,3,2,1,0:T(8,128)(2,1)} custom-call(s32[3,1,14]{2,1,0:T(1,128)} %bitcast.9, bf16[8,1792]{1,0:T(8,128)(2,1)} %q_ref, bf16[8,256]{1,0:T(8,128)(2,1)} %k_hbm.1, bf16[8,256]{1,0:T(8,128)(2,1)} %v_hbm.1), custom_call_target="tpu_custom_call" | custom-call | tf_op jit(solution)/shard_map/pack/pallas_call | solution.py:268
  1.9 7.1 %all-to-all-start = ((bf16[32,40,128]{2,1,0:T(8,128)(2,1)}), bf16[32,40,128]{2,1,0:T(8,128)(2,1)S(1)}, u32[]{:S(2)}, u32[]{:S(2)}) async-start(bf16[32,40,128]{2,1,0:T(8,128)(2,1)} %bitcast.11), calls=%async_computation | async-start | bytes 655360 | tf_op jit(solution)/shard_map/all_to_all | solution.py:318
  9.0 1.2 %copy.8 = bf16[1024,256]{0,1:T(8,128)(2,1)S(1)} copy(bf16[1024,256]{1,0:T(8,128)(2,1)} %param.10) | data formatting | bytes 1048576 | tf_op jit(solution)/shard_map/optimization_barrier | solution.py:312
  10.3 0.3 collective-permute-start
  10.7 1.1 %constant_dynamic-slice_fusion = (bf16[1024,128]{1,0:T(8,128)(2,1)S(1)}, bf16[1024,128]{1,0:T(8,128)(2,1)S(1)}) fusion(bf16[1024,256]{1,0:T(8,128)(2,1)} %param.11, s32[]{:T(128)S(6)} %select_n.17, s32[]{:T(128)S(6)} %select_n.16), kind=kLoop, calls=%fused_computation.2 | loop fusion | bytes 1048584 | tf_op jit(solution)/shard_map/dynamic_slice | solution.py:325
  11.7 0.3 collective-permute-start.1
  12.0 0.0 collective-permute-done.kb_ref
  12.0 1.3 %collective-permute-done.1.vb_ref = bf16[1024,128]{1,0:T(8,128)(2,1)S(1)} collective-permute-done((bf16[1024,128]{1,0:T(8,128)(2,1)S(1)}, bf16[1024,128]{1,0:T(8,128)(2,1)S(1)}, u32[]{:S(2)}, u32[]{:S(2)}) %collective-permute-start.1) | collective-permute-done | bytes 262176 | tf_op jit(solution)/shard_map/ppermute | solution.py:329
  13.3 7.8 %all-to-all-done.q_ref = bf16[32,40,128]{2,1,0:T(8,128)(2,1)S(1)} async-done(((bf16[32,40,128]{2,1,0:T(8,128)(2,1)}), bf16[32,40,128]{2,1,0:T(8,128)(2,1)S(1)}, u32[]{:S(2)}, u32[]{:S(2)}) %all-to-all-start) | async-done | bytes 327712 | tf_op jit(solution)/shard_map/all_to_all | solution.py:318
  21.1 4.0 %attend.1 = (bf16[1088,128]{1,0:T(8,128)(2,1)}, bf16[32,8,128]{2,1,0:T(8,128)(2,1)S(1)}) custom-call(bf16[32,40,128]{2,1,0:T(8,128)(2,1)S(1)} %all-to-all-done.q_ref, bf16[128,1024]{1,0:T(8,128)(2,1)S(1)} %get-tuple-element.40.ka_ref, bf16[1024,128]{1,0:T(8,128)(2,1)S(1)} %get-tuple-element.38.va_ref, bf16[128,1024]{1,0:T(8,128)(2,1)S(1)} %collective-permute-done.kb_ref, ...), custom_call_target="tpu_custom_call" | custom-call | flops 1073741824 | bytes 4194304 | tf_op jit(solution)/shard_map/attend/pallas_call | solution.py:268
  25.1 2.4 %all-to-all-start.1 = ((bf16[32,17,2,128]{3,2,1,0:T(2,128)(2,1)}), bf16[32,17,2,128]{3,2,1,0:T(2,128)(2,1)S(1)}, u32[]{:S(2)}, u32[]{:S(2)}) async-start(bf16[32,17,2,128]{3,2,1,0:T(2,128)(2,1)} %bitcast.4), calls=%async_computation.1 | async-start | bytes 557056 | tf_op jit(solution)/shard_map/all_to_all | solution.py:318
  27.5 1.4 %collective-permute-start.3 = (bf16[32,8,128]{2,1,0:T(8,128)(2,1)S(1)}, bf16[32,8,128]{2,1,0:T(8,128)(2,1)S(1)}, u32[]{:S(2)}, u32[]{:S(2)}) collective-permute-start(bf16[32,8,128]{2,1,0:T(8,128)(2,1)S(1)} %get-tuple-element.32.kv_ref), channel_id=1, source_target_pairs={{0,2},{1,3},{2,0},{3,1},{4,6},{5,7},{6,4},{7,5},{8,10},{9,11},{10,... | collective-permute-start | bytes 196616 | tf_op jit(solution)/shard_map/ppermute | solution.py:368
  28.9 0.6 %collective-permute-start.2 = (bf16[32,8,128]{2,1,0:T(8,128)(2,1)S(1)}, bf16[32,8,128]{2,1,0:T(8,128)(2,1)S(1)}, u32[]{:S(2)}, u32[]{:S(2)}) collective-permute-start(bf16[32,8,128]{2,1,0:T(8,128)(2,1)S(1)} %get-tuple-element.32.kv_ref), channel_id=1, source_target_pairs={{0,1},{1,0},{2,3},{3,2},{4,5},{5,4},{6,7},{7,6},{8,9},{9,8},{10,11... | collective-permute-start | bytes 196616 | tf_op jit(solution)/shard_map/ppermute | solution.py:369
  29.5 3.2 %collective-permute-done.3.kv2_ref = bf16[32,8,128]{2,1,0:T(8,128)(2,1)S(1)} collective-permute-done((bf16[32,8,128]{2,1,0:T(8,128)(2,1)S(1)}, bf16[32,8,128]{2,1,0:T(8,128)(2,1)S(1)}, u32[]{:S(2)}, u32[]{:S(2)}) %collective-permute-start.3) | collective-permute-done | bytes 65568 | tf_op jit(solution)/shard_map/ppermute | solution.py:368
  32.8 1.0 %collective-permute-start.4 = (bf16[32,8,128]{2,1,0:T(8,128)(2,1)S(1)}, bf16[32,8,128]{2,1,0:T(8,128)(2,1)S(1)}, u32[]{:S(2)}, u32[]{:S(2)}) collective-permute-start(bf16[32,8,128]{2,1,0:T(8,128)(2,1)S(1)} %collective-permute-done.3.kv2_ref), channel_id=1, source_target_pairs={{0,1},{1,0},{2,3},{3,2},{4,5},{5,4},{6,7},{7,6},{8,9},{9,8},{10,11... | collective-permute-start | bytes 196616 | tf_op jit(solution)/shard_map/ppermute | solution.py:369
  33.8 0.0 copy-done
  33.8 0.0 copy-done.1
  33.8 1.8 %masks.1 = (f32[2,56,512]{2,1,0:T(8,128)S(1)}, f32[2,56,128]{2,1,0:T(8,128)S(1)}, bf16[768,1792]{1,0:T(8,128)(2,1)S(1)}) custom-call(s32[3,1,14]{2,1,0:T(1,128)S(1)} %bitcast.10, bf16[8,1792]{1,0:T(8,128)(2,1)S(1)} %copy-done, bf16[1792,1792]{1,0:T(8,128)(2,1)} %w_hbm.1), custom_call_target="tpu_custom_call" | custom-call | tf_op jit(solution)/shard_map/masks/pallas_call | solution.py:268
  35.6 0.0 collective-permute-done.2.kv1_ref
  35.6 0.0 collective-permute-done.4.kv3_ref
  35.6 0.4 %fresh.1 = (f32[2,56,128]{2,1,0:T(8,128)S(1)}, f32[2,56,128]{2,1,0:T(8,128)S(1)}) custom-call(f32[2,56,128]{2,1,0:T(8,128)S(1)} %get-tuple-element.31.rows_ref, bf16[32,8,128]{2,1,0:T(8,128)(2,1)S(1)} %get-tuple-element.32.kv_ref, bf16[32,8,128]{2,1,0:T(8,128)(2,1)S(1)} %collective-permute-done.2.kv1_ref, ...), custom_call_target="tpu_custom_call" | custom-call | flops 29360128 | bytes 1048576 | tf_op jit(solution)/shard_map/fresh/pallas_call | solution.py:268
  36.0 2.5 %all-to-all-done.1 = bf16[32,17,2,128]{3,2,1,0:T(2,128)(2,1)S(1)} async-done(((bf16[32,17,2,128]{3,2,1,0:T(2,128)(2,1)}), bf16[32,17,2,128]{3,2,1,0:T(2,128)(2,1)S(1)}, u32[]{:S(2)}, u32[]{:S(2)}) %all-to-all-start.1) | async-done | bytes 278560 | tf_op jit(solution)/shard_map/all_to_all | solution.py:318
  38.5 3.0 %project.1 = bf16[8,1792]{1,0:T(8,128)(2,1)} custom-call(bf16[1088,128]{1,0:T(8,128)(2,1)S(1)} %bitcast.8, f32[2,56,128]{2,1,0:T(8,128)S(1)} %get-tuple-element.33.out_ref, f32[2,56,128]{2,1,0:T(8,128)S(1)} %get-tuple-element.34.lse_ref, f32[2,56,512]{2,1,0:T(8,128)S(1)} %get-tuple-element.35.match_ref, bf16[768,1792]{1,0:T(8,128)(2,1)S(1)} %get-tuple-element.36.first_ref, ...), custom_call_target="tpu_custom_call" | custom-call | flops 51380224 | bytes 6422528 | tf_op jit(solution)/shard_map/project/pallas_call | solution.py:268
  (1 shorter events, 0.0 us)
Async XLA Ops:
  0.0 33.8 %copy-start = (bf16[8,1792]{1,0:T(8,128)(2,1)S(1)}, bf16[8,1792]{1,0:T(8,128)(2,1)}, u32[]{:S(2)}) copy-start(bf16[8,1792]{1,0:T(8,128)(2,1)} %q_ref) | copy-start | bytes 86020
  0.0 33.8 %copy-start.1 = (s32[1,14,3]{1,0,2:T(1,128)S(1)}, s32[1,14,3]{1,0,2:T(1,128)}, u32[]{:S(2)}) copy-start(s32[1,14,3]{1,0,2:T(1,128)} %param.12) | copy-start | bytes 508
  1.9 19.2 %all-to-all-start = ((bf16[32,40,128]{2,1,0:T(8,128)(2,1)}), bf16[32,40,128]{2,1,0:T(8,128)(2,1)S(1)}, u32[]{:S(2)}, u32[]{:S(2)}) async-start(bf16[32,40,128]{2,1,0:T(8,128)(2,1)} %bitcast.11), calls=%async_computation | async-start | bytes 655360 | tf_op jit(solution)/shard_map/all_to_all | solution.py:318
  10.3 1.7 %collective-permute-start = (bf16[128,1024]{1,0:T(8,128)(2,1)S(1)}, bf16[128,1024]{1,0:T(8,128)(2,1)S(1)}, u32[]{:S(2)}, u32[]{:S(2)}) collective-permute-start(bf16[128,1024]{1,0:T(8,128)(2,1)S(1)} %get-tuple-element.39), channel_id=1, source_target_pairs={{0,1},{1,0},{2,3},{3,2},{4,5},{5,4},{6,7},{7,6},{8,9},{9,8},{10,11... | collective-permute-start | bytes 786440 | tf_op jit(solution)/shard_map/ppermute | solution.py:329
  11.7 1.6 %collective-permute-start.1 = (bf16[1024,128]{1,0:T(8,128)(2,1)S(1)}, bf16[1024,128]{1,0:T(8,128)(2,1)S(1)}, u32[]{:S(2)}, u32[]{:S(2)}) collective-permute-start(bf16[1024,128]{1,0:T(8,128)(2,1)S(1)} %get-tuple-element.37), channel_id=1, source_target_pairs={{0,1},{1,0},{2,3},{3,2},{4,5},{5,4},{6,7},{7,6},{8,9},{9,8},{10,11... | collective-permute-start | bytes 786440 | tf_op jit(solution)/shard_map/ppermute | solution.py:329
  25.1 13.4 %all-to-all-start.1 = ((bf16[32,17,2,128]{3,2,1,0:T(2,128)(2,1)}), bf16[32,17,2,128]{3,2,1,0:T(2,128)(2,1)S(1)}, u32[]{:S(2)}, u32[]{:S(2)}) async-start(bf16[32,17,2,128]{3,2,1,0:T(2,128)(2,1)} %bitcast.4), calls=%async_computation.1 | async-start | bytes 557056 | tf_op jit(solution)/shard_map/all_to_all | solution.py:318
  27.5 5.3 %collective-permute-start.3 = (bf16[32,8,128]{2,1,0:T(8,128)(2,1)S(1)}, bf16[32,8,128]{2,1,0:T(8,128)(2,1)S(1)}, u32[]{:S(2)}, u32[]{:S(2)}) collective-permute-start(bf16[32,8,128]{2,1,0:T(8,128)(2,1)S(1)} %get-tuple-element.32.kv_ref), channel_id=1, source_target_pairs={{0,2},{1,3},{2,0},{3,1},{4,6},{5,7},{6,4},{7,5},{8,10},{9,11},{10,... | collective-permute-start | bytes 196616 | tf_op jit(solution)/shard_map/ppermute | solution.py:368
  28.9 6.7 %collective-permute-start.2 = (bf16[32,8,128]{2,1,0:T(8,128)(2,1)S(1)}, bf16[32,8,128]{2,1,0:T(8,128)(2,1)S(1)}, u32[]{:S(2)}, u32[]{:S(2)}) collective-permute-start(bf16[32,8,128]{2,1,0:T(8,128)(2,1)S(1)} %get-tuple-element.32.kv_ref), channel_id=1, source_target_pairs={{0,1},{1,0},{2,3},{3,2},{4,5},{5,4},{6,7},{7,6},{8,9},{9,8},{10,11... | collective-permute-start | bytes 196616 | tf_op jit(solution)/shard_map/ppermute | solution.py:369
  32.8 2.8 %collective-permute-start.4 = (bf16[32,8,128]{2,1,0:T(8,128)(2,1)S(1)}, bf16[32,8,128]{2,1,0:T(8,128)(2,1)S(1)}, u32[]{:S(2)}, u32[]{:S(2)}) collective-permute-start(bf16[32,8,128]{2,1,0:T(8,128)(2,1)S(1)} %collective-permute-done.3.kv2_ref), channel_id=1, source_target_pairs={{0,1},{1,0},{2,3},{3,2},{4,5},{5,4},{6,7},{7,6},{8,9},{9,8},{10,11... | collective-permute-start | bytes 196616 | tf_op jit(solution)/shard_map/ppermute | solution.py:369

commit v25 on v20

--- a/solution.py
+++ b/solution.py
@@ -128,16 +128,19 @@
     ones = jnp.ones(va_ref.shape, jnp.bfloat16)
     fresh_ref[...] = q_ref[:, per:, :]
 
-    def scores(first):
-        q = q_ref[first : first + step, :per, :].reshape(step * per, HD)
+    def scores(first, count):
+        q = q_ref[first : first + count, :per, :].reshape(count * per, HD)
         return [jnp.dot(q, k_ref[...], preferred_element_type=jnp.float32) for k_ref in (ka_ref, kb_ref)]
 
-    ahead = scores(0)
+    wide = 2 * step
+    tops = []
+    for first in range(0, sources, wide):
+        most = [jnp.max(s, axis=1, keepdims=True) for s in scores(first, wide)]
+        tops.append(scale * jnp.maximum(*most))
     for first in range(0, sources, step):
-        sa, sb = ahead
-        if first + step < sources:
-            ahead = scores(first + step)
-        top = scale * jnp.maximum(jnp.max(sa, axis=1, keepdims=True), jnp.max(sb, axis=1, keepdims=True))
+        begin = first % wide * per
+        top = tops[first // wide][begin : begin + step * per]
+        sa, sb = scores(first, step)
         wa = jnp.exp2(sa * scale - top).astype(jnp.bfloat16)
         wb = jnp.exp2(sb * scale - top).astype(jnp.bfloat16)
         both = jnp.dot(

time: 41.2 us -> 42.5 us (1.032)
  Pallas kernels: 10.4 us -> 11.7 us
    pallas_call x5, Pallas kernels: 10.4 us -> 11.7 us  [call(): pl.pallas_call(kernel, name=name, out_shape=out_shape, in_specs=specs, ou...]
where the time goes in v25:
time: 42.5 us; the launch traced here: 42.1 us
  waiting for transfers between devices  14.8 us (35%)
  starting transfers between devices  13.1 us (31%)
  Pallas kernels  11.7 us (28%)
  local copies, waits for them, and re-layouts  2.36 us (6%)
    pallas_call x5, Pallas kernels, call(): pl.pallas_call(kernel, name=name, out_shape=out_shape, in_specs=specs, ou...  11.7 us
    all_to_all x2, waiting for transfers between devices, exchange(): lax.all_to_all(x, 'seq', split_axis=0, concat_axis=0, axis_index_groups=r...  10.2 us
    all_to_all x2, starting transfers between devices, exchange(): lax.all_to_all(x, 'seq', split_axis=0, concat_axis=0, axis_index_groups=r...  9.45 us
    ppermute x1, waiting for transfers between devices, body(): far = lax.ppermute(fresh, 'seq', partner(2))  3.25 us
    ppermute x2, starting transfers between devices, body(): near, both = [lax.ppermute(x, 'seq', partner(1)) for x in (fresh, far)]  1.6 us
    ppermute x1, starting transfers between devices, body(): far = lax.ppermute(fresh, 'seq', partner(2))  1.44 us
    ppermute x2, waiting for transfers between devices, body(): lax.ppermute(x, 'seq', partner(1))  1.28 us
    optimization_barrier x1, local copies, waits for them, and re-layouts, body(): lax.optimization_barrier((send, cache_keys, cache_values, picks, queries))  1.25 us
  transfers between devices with their start and end apart: 7, of which 4 were waited for; matrix products, arithmetic and copies ran while one was open for 6% of the time, Pallas kernels for 5%

profile of v25, /device:TPU:1, one launch (start us, length us, event | category | flops | bytes accessed | tf_op | source)
XLA Modules:
  0.0 42.1 jit_solution(13551208662852879630)
XLA Ops:
  0.0 0.0 copy-start
  0.0 0.0 copy-start.1
  0.0 1.9 %pack.1 = bf16[8,2,2,40,128]{4,3,2,1,0:T(8,128)(2,1)} custom-call(s32[3,1,14]{2,1,0:T(1,128)} %bitcast.9, bf16[8,1792]{1,0:T(8,128)(2,1)} %q_ref, bf16[8,256]{1,0:T(8,128)(2,1)} %k_hbm.1, bf16[8,256]{1,0:T(8,128)(2,1)} %v_hbm.1), custom_call_target="tpu_custom_call" | custom-call | tf_op jit(solution)/shard_map/pack/pallas_call | solution.py:268
  1.9 7.1 %all-to-all-start = ((bf16[32,40,128]{2,1,0:T(8,128)(2,1)}), bf16[32,40,128]{2,1,0:T(8,128)(2,1)S(1)}, u32[]{:S(2)}, u32[]{:S(2)}) async-start(bf16[32,40,128]{2,1,0:T(8,128)(2,1)} %bitcast.11), calls=%async_computation | async-start | bytes 655360 | tf_op jit(solution)/shard_map/all_to_all | solution.py:318
  9.0 1.2 %copy.8 = bf16[1024,256]{0,1:T(8,128)(2,1)S(1)} copy(bf16[1024,256]{1,0:T(8,128)(2,1)} %param.10) | data formatting | bytes 1048576 | tf_op jit(solution)/shard_map/optimization_barrier | solution.py:312
  10.3 0.3 collective-permute-start
  10.7 1.1 %constant_dynamic-slice_fusion = (bf16[1024,128]{1,0:T(8,128)(2,1)S(1)}, bf16[1024,128]{1,0:T(8,128)(2,1)S(1)}) fusion(bf16[1024,256]{1,0:T(8,128)(2,1)} %param.11, s32[]{:T(128)S(6)} %select_n.17, s32[]{:T(128)S(6)} %select_n.16), kind=kLoop, calls=%fused_computation.2 | loop fusion | bytes 1048584 | tf_op jit(solution)/shard_map/dynamic_slice | solution.py:325
  11.7 0.3 collective-permute-start.1
  12.0 0.0 collective-permute-done.kb_ref
  12.0 1.3 %collective-permute-done.1.vb_ref = bf16[1024,128]{1,0:T(8,128)(2,1)S(1)} collective-permute-done((bf16[1024,128]{1,0:T(8,128)(2,1)S(1)}, bf16[1024,128]{1,0:T(8,128)(2,1)S(1)}, u32[]{:S(2)}, u32[]{:S(2)}) %collective-permute-start.1) | collective-permute-done | bytes 262176 | tf_op jit(solution)/shard_map/ppermute | solution.py:329
  13.3 7.8 %all-to-all-done.q_ref = bf16[32,40,128]{2,1,0:T(8,128)(2,1)S(1)} async-done(((bf16[32,40,128]{2,1,0:T(8,128)(2,1)}), bf16[32,40,128]{2,1,0:T(8,128)(2,1)S(1)}, u32[]{:S(2)}, u32[]{:S(2)}) %all-to-all-start) | async-done | bytes 327712 | tf_op jit(solution)/shard_map/all_to_all | solution.py:318
  21.1 4.6 %attend.1 = (bf16[1088,128]{1,0:T(8,128)(2,1)}, bf16[32,8,128]{2,1,0:T(8,128)(2,1)S(1)}) custom-call(bf16[32,40,128]{2,1,0:T(8,128)(2,1)S(1)} %all-to-all-done.q_ref, bf16[128,1024]{1,0:T(8,128)(2,1)S(1)} %get-tuple-element.40.ka_ref, bf16[1024,128]{1,0:T(8,128)(2,1)S(1)} %get-tuple-element.38.va_ref, bf16[128,1024]{1,0:T(8,128)(2,1)S(1)} %collective-permute-done.kb_ref, ...), custom_call_target="tpu_custom_call" | custom-call | flops 1073741824 | bytes 4194304 | tf_op jit(solution)/shard_map/attend/pallas_call | solution.py:268
  25.7 2.3 %all-to-all-start.1 = ((bf16[32,17,2,128]{3,2,1,0:T(2,128)(2,1)}), bf16[32,17,2,128]{3,2,1,0:T(2,128)(2,1)S(1)}, u32[]{:S(2)}, u32[]{:S(2)}) async-start(bf16[32,17,2,128]{3,2,1,0:T(2,128)(2,1)} %bitcast.4), calls=%async_computation.1 | async-start | bytes 557056 | tf_op jit(solution)/shard_map/all_to_all | solution.py:318
  28.1 1.4 %collective-permute-start.3 = (bf16[32,8,128]{2,1,0:T(8,128)(2,1)S(1)}, bf16[32,8,128]{2,1,0:T(8,128)(2,1)S(1)}, u32[]{:S(2)}, u32[]{:S(2)}) collective-permute-start(bf16[32,8,128]{2,1,0:T(8,128)(2,1)S(1)} %get-tuple-element.32.kv_ref), channel_id=1, source_target_pairs={{0,2},{1,3},{2,0},{3,1},{4,6},{5,7},{6,4},{7,5},{8,10},{9,11},{10,... | collective-permute-start | bytes 196616 | tf_op jit(solution)/shard_map/ppermute | solution.py:368
  29.5 0.6 %collective-permute-start.2 = (bf16[32,8,128]{2,1,0:T(8,128)(2,1)S(1)}, bf16[32,8,128]{2,1,0:T(8,128)(2,1)S(1)}, u32[]{:S(2)}, u32[]{:S(2)}) collective-permute-start(bf16[32,8,128]{2,1,0:T(8,128)(2,1)S(1)} %get-tuple-element.32.kv_ref), channel_id=1, source_target_pairs={{0,1},{1,0},{2,3},{3,2},{4,5},{5,4},{6,7},{7,6},{8,9},{9,8},{10,11... | collective-permute-start | bytes 196616 | tf_op jit(solution)/shard_map/ppermute | solution.py:369
  30.2 3.2 %collective-permute-done.3.kv2_ref = bf16[32,8,128]{2,1,0:T(8,128)(2,1)S(1)} collective-permute-done((bf16[32,8,128]{2,1,0:T(8,128)(2,1)S(1)}, bf16[32,8,128]{2,1,0:T(8,128)(2,1)S(1)}, u32[]{:S(2)}, u32[]{:S(2)}) %collective-permute-start.3) | collective-permute-done | bytes 65568 | tf_op jit(solution)/shard_map/ppermute | solution.py:368
  33.4 1.0 %collective-permute-start.4 = (bf16[32,8,128]{2,1,0:T(8,128)(2,1)S(1)}, bf16[32,8,128]{2,1,0:T(8,128)(2,1)S(1)}, u32[]{:S(2)}, u32[]{:S(2)}) collective-permute-start(bf16[32,8,128]{2,1,0:T(8,128)(2,1)S(1)} %collective-permute-done.3.kv2_ref), channel_id=1, source_target_pairs={{0,1},{1,0},{2,3},{3,2},{4,5},{5,4},{6,7},{7,6},{8,9},{9,8},{10,11... | collective-permute-start | bytes 196616 | tf_op jit(solution)/shard_map/ppermute | solution.py:369
  34.4 0.0 copy-done
  34.4 0.0 copy-done.1
  34.4 1.8 %masks.1 = (f32[2,56,512]{2,1,0:T(8,128)S(1)}, f32[2,56,128]{2,1,0:T(8,128)S(1)}, bf16[768,1792]{1,0:T(8,128)(2,1)S(1)}) custom-call(s32[3,1,14]{2,1,0:T(1,128)S(1)} %bitcast.10, bf16[8,1792]{1,0:T(8,128)(2,1)S(1)} %copy-done, bf16[1792,1792]{1,0:T(8,128)(2,1)} %w_hbm.1), custom_call_target="tpu_custom_call" | custom-call | tf_op jit(solution)/shard_map/masks/pallas_call | solution.py:268
  36.2 0.0 collective-permute-done.2.kv1_ref
  36.2 0.0 collective-permute-done.4.kv3_ref
  36.2 0.4 %fresh.1 = (f32[2,56,128]{2,1,0:T(8,128)S(1)}, f32[2,56,128]{2,1,0:T(8,128)S(1)}) custom-call(f32[2,56,128]{2,1,0:T(8,128)S(1)} %get-tuple-element.31.rows_ref, bf16[32,8,128]{2,1,0:T(8,128)(2,1)S(1)} %get-tuple-element.32.kv_ref, bf16[32,8,128]{2,1,0:T(8,128)(2,1)S(1)} %collective-permute-done.2.kv1_ref, ...), custom_call_target="tpu_custom_call" | custom-call | flops 29360128 | bytes 1048576 | tf_op jit(solution)/shard_map/fresh/pallas_call | solution.py:268
  36.6 2.5 %all-to-all-done.1 = bf16[32,17,2,128]{3,2,1,0:T(2,128)(2,1)S(1)} async-done(((bf16[32,17,2,128]{3,2,1,0:T(2,128)(2,1)}), bf16[32,17,2,128]{3,2,1,0:T(2,128)(2,1)S(1)}, u32[]{:S(2)}, u32[]{:S(2)}) %all-to-all-start.1) | async-done | bytes 278560 | tf_op jit(solution)/shard_map/all_to_all | solution.py:318
  39.1 3.0 %project.1 = bf16[8,1792]{1,0:T(8,128)(2,1)} custom-call(bf16[1088,128]{1,0:T(8,128)(2,1)S(1)} %bitcast.8, f32[2,56,128]{2,1,0:T(8,128)S(1)} %get-tuple-element.33.out_ref, f32[2,56,128]{2,1,0:T(8,128)S(1)} %get-tuple-element.34.lse_ref, f32[2,56,512]{2,1,0:T(8,128)S(1)} %get-tuple-element.35.match_ref, bf16[768,1792]{1,0:T(8,128)(2,1)S(1)} %get-tuple-element.36.first_ref, ...), custom_call_target="tpu_custom_call" | custom-call | flops 51380224 | bytes 6422528 | tf_op jit(solution)/shard_map/project/pallas_call | solution.py:268
  (1 shorter events, 0.0 us)
Async XLA Ops:
  0.0 34.4 %copy-start = (bf16[8,1792]{1,0:T(8,128)(2,1)S(1)}, bf16[8,1792]{1,0:T(8,128)(2,1)}, u32[]{:S(2)}) copy-start(bf16[8,1792]{1,0:T(8,128)(2,1)} %q_ref) | copy-start | bytes 86020
  0.0 34.4 %copy-start.1 = (s32[1,14,3]{1,0,2:T(1,128)S(1)}, s32[1,14,3]{1,0,2:T(1,128)}, u32[]{:S(2)}) copy-start(s32[1,14,3]{1,0,2:T(1,128)} %param.12) | copy-start | bytes 508
  1.9 19.2 %all-to-all-start = ((bf16[32,40,128]{2,1,0:T(8,128)(2,1)}), bf16[32,40,128]{2,1,0:T(8,128)(2,1)S(1)}, u32[]{:S(2)}, u32[]{:S(2)}) async-start(bf16[32,40,128]{2,1,0:T(8,128)(2,1)} %bitcast.11), calls=%async_computation | async-start | bytes 655360 | tf_op jit(solution)/shard_map/all_to_all | solution.py:318
  10.3 1.7 %collective-permute-start = (bf16[128,1024]{1,0:T(8,128)(2,1)S(1)}, bf16[128,1024]{1,0:T(8,128)(2,1)S(1)}, u32[]{:S(2)}, u32[]{:S(2)}) collective-permute-start(bf16[128,1024]{1,0:T(8,128)(2,1)S(1)} %get-tuple-element.39), channel_id=1, source_target_pairs={{0,1},{1,0},{2,3},{3,2},{4,5},{5,4},{6,7},{7,6},{8,9},{9,8},{10,11... | collective-permute-start | bytes 786440 | tf_op jit(solution)/shard_map/ppermute | solution.py:329
  11.7 1.6 %collective-permute-start.1 = (bf16[1024,128]{1,0:T(8,128)(2,1)S(1)}, bf16[1024,128]{1,0:T(8,128)(2,1)S(1)}, u32[]{:S(2)}, u32[]{:S(2)}) collective-permute-start(bf16[1024,128]{1,0:T(8,128)(2,1)S(1)} %get-tuple-element.37), channel_id=1, source_target_pairs={{0,1},{1,0},{2,3},{3,2},{4,5},{5,4},{6,7},{7,6},{8,9},{9,8},{10,11... | collective-permute-start | bytes 786440 | tf_op jit(solution)/shard_map/ppermute | solution.py:329
  25.7 13.4 %all-to-all-start.1 = ((bf16[32,17,2,128]{3,2,1,0:T(2,128)(2,1)}), bf16[32,17,2,128]{3,2,1,0:T(2,128)(2,1)S(1)}, u32[]{:S(2)}, u32[]{:S(2)}) async-start(bf16[32,17,2,128]{3,2,1,0:T(2,128)(2,1)} %bitcast.4), calls=%async_computation.1 | async-start | bytes 557056 | tf_op jit(solution)/shard_map/all_to_all | solution.py:318
  28.1 5.3 %collective-permute-start.3 = (bf16[32,8,128]{2,1,0:T(8,128)(2,1)S(1)}, bf16[32,8,128]{2,1,0:T(8,128)(2,1)S(1)}, u32[]{:S(2)}, u32[]{:S(2)}) collective-permute-start(bf16[32,8,128]{2,1,0:T(8,128)(2,1)S(1)} %get-tuple-element.32.kv_ref), channel_id=1, source_target_pairs={{0,2},{1,3},{2,0},{3,1},{4,6},{5,7},{6,4},{7,5},{8,10},{9,11},{10,... | collective-permute-start | bytes 196616 | tf_op jit(solution)/shard_map/ppermute | solution.py:368
  29.5 6.7 %collective-permute-start.2 = (bf16[32,8,128]{2,1,0:T(8,128)(2,1)S(1)}, bf16[32,8,128]{2,1,0:T(8,128)(2,1)S(1)}, u32[]{:S(2)}, u32[]{:S(2)}) collective-permute-start(bf16[32,8,128]{2,1,0:T(8,128)(2,1)S(1)} %get-tuple-element.32.kv_ref), channel_id=1, source_target_pairs={{0,1},{1,0},{2,3},{3,2},{4,5},{5,4},{6,7},{7,6},{8,9},{9,8},{10,11... | collective-permute-start | bytes 196616 | tf_op jit(solution)/shard_map/ppermute | solution.py:369
  33.4 2.8 %collective-permute-start.4 = (bf16[32,8,128]{2,1,0:T(8,128)(2,1)S(1)}, bf16[32,8,128]{2,1,0:T(8,128)(2,1)S(1)}, u32[]{:S(2)}, u32[]{:S(2)}) collective-permute-start(bf16[32,8,128]{2,1,0:T(8,128)(2,1)S(1)} %collective-permute-done.3.kv2_ref), channel_id=1, source_target_pairs={{0,1},{1,0},{2,3},{3,2},{4,5},{5,4},{6,7},{7,6},{8,9},{9,8},{10,11... | collective-permute-start | bytes 196616 | tf_op jit(solution)/shard_map/ppermute | solution.py:369

commit v26 on v20

--- a/solution.py
+++ b/solution.py
@@ -96,7 +96,7 @@
                 to = (g, key_blocks - 1 - b, chips - 1 - chip)
                 send_ref[(*to, slice(0, per))] = slots[b * per : (b + 1) * per]
                 send_ref[(*to, slice(per, None))] = fresh[chip % 2]
-        sent.append(pltpu.make_async_copy(send_ref.at[g], send_hbm.at[:, :, KVH - 1 - g], sems.at[4 + g]))
+        sent.append(pltpu.make_async_copy(send_ref.at[g], send_hbm.at[KVH - 1 - g], sems.at[4 + g]))
         sent[g].start()
     for copy in sent:
         copy.wait()
@@ -171,7 +171,10 @@
     nt = (((1,), (1,)), ((), ()))
     column = lax.broadcasted_iota(jnp.int32, (tokens, sources * tokens), 1)
     query_pos = place * tokens + lax.broadcasted_iota(jnp.int32, column.shape, 0)
-    key_pos = (sources - 1 - column // tokens) * tokens + column % tokens
+    rank = column // tokens
+    half = sources // KVH
+    source = (half - 1 - rank % half) * KVH + KVH - 1 - rank // half
+    key_pos = source * tokens + column % tokens
     visible = (key_pos <= query_pos) & (key_pos // BLK == query_pos // BLK)
     visible = jnp.concatenate([visible.astype(jnp.int32)] * GROUP, axis=0) > 0
     ones = jnp.ones((sources * tokens, HD), jnp.bfloat16)
@@ -217,7 +220,7 @@
 
     heads = []
     for g in range(KVH):
-        starts = [(KVH * (holders - m) - 1 - g) * (per + 2) for m in range(holders)]
+        starts = [((KVH - g) * holders - 1 - m) * (per + 2) for m in range(holders)]
         outs = jnp.concatenate([hist[i : i + per] for i in starts], axis=0).astype(jnp.bfloat16)
         stats = jnp.concatenate([hist[i + per : i + per + 1] for i in starts], axis=0)
         shift = LANES // 2
@@ -292,7 +295,7 @@
     send = call(
         functools.partial(pack_kernel, capacity),
         "pack",
-        jax.ShapeDtypeStruct((key_blocks, chips, KVH, per + tokens, HD), bf16),
+        jax.ShapeDtypeStruct((KVH, key_blocks, chips, per + tokens, HD), bf16),
         [HBM] * 4,
         picks, queries, stretch_keys, stretch_values,
         outs=ANY,
@@ -311,8 +314,8 @@
     )
 
     def exchange(x):
-        ranks = [list(range(devices))[::-1]]
-        return lax.all_to_all(x, "seq", split_axis=0, concat_axis=0, axis_index_groups=ranks, tiled=True)
+        ranks = [i for g in range(KVH) for i in range(g, devices, KVH)][::-1]
+        return lax.all_to_all(x, "seq", split_axis=0, concat_axis=0, axis_index_groups=[ranks], tiled=True)
 
     got = exchange(send.reshape(devices, per + tokens, HD))
 

time: 41.2 us -> 40.8 us (level)
  the two profiles are of different devices: /device:TPU:1 before, /device:TPU:0 now
where the time goes in v26:
time: 40.8 us; the launch traced here: 40.4 us
  waiting for transfers between devices  13.7 us (34%)
  starting transfers between devices  13.2 us (32%)
  Pallas kernels  10.9 us (27%)
  local copies, waits for them, and re-layouts  2.36 us (6%)
    pallas_call x5, Pallas kernels, call(): pl.pallas_call(kernel, name=name, out_shape=out_shape, in_specs=specs, ou...  10.9 us
    all_to_all x2, starting transfers between devices, exchange(): lax.all_to_all(x, 'seq', split_axis=0, concat_axis=0, axis_index_groups=[...  10.8 us
    all_to_all x2, waiting for transfers between devices, exchange(): lax.all_to_all(x, 'seq', split_axis=0, concat_axis=0, axis_index_groups=[...  7.91 us
    ppermute x1, waiting for transfers between devices, body(): far = lax.ppermute(fresh, 'seq', partner(2))  4.52 us
    ppermute x1, starting transfers between devices, body(): far = lax.ppermute(fresh, 'seq', partner(2))  1.83 us
    ppermute x2, waiting for transfers between devices, body(): lax.ppermute(x, 'seq', partner(1))  1.28 us
    optimization_barrier x1, local copies, waits for them, and re-layouts, body(): lax.optimization_barrier((send, cache_keys, cache_values, picks, queries))  1.25 us
    dynamic_slice x1, local copies, waits for them, and re-layouts, halves(): lax.dynamic_slice_in_dim(x, head * HD, HD, axis=1)  1.06 us
  transfers between devices with their start and end apart: 7, of which 4 were waited for; matrix products, arithmetic and copies ran while one was open for 6% of the time, Pallas kernels for 6%

profile of v26, /device:TPU:0, one launch (start us, length us, event | category | flops | bytes accessed | tf_op | source)
XLA Modules:
  0.0 40.4 jit_solution(898015602226749802)
XLA Ops:
  0.0 0.0 copy-start
  0.0 0.0 copy-start.1
  0.0 1.9 %pack.1 = bf16[2,8,2,40,128]{4,3,2,1,0:T(8,128)(2,1)} custom-call(s32[3,1,14]{2,1,0:T(1,128)} %bitcast.9, bf16[8,1792]{1,0:T(8,128)(2,1)} %q_ref, bf16[8,256]{1,0:T(8,128)(2,1)} %k_hbm.1, bf16[8,256]{1,0:T(8,128)(2,1)} %v_hbm.1), custom_call_target="tpu_custom_call" | custom-call | tf_op jit(solution)/shard_map/pack/pallas_call | solution.py:268
  1.9 7.3 %all-to-all-start = ((bf16[32,40,128]{2,1,0:T(8,128)(2,1)}), bf16[32,40,128]{2,1,0:T(8,128)(2,1)S(1)}, u32[]{:S(2)}, u32[]{:S(2)}) async-start(bf16[32,40,128]{2,1,0:T(8,128)(2,1)} %bitcast.11), calls=%async_computation | async-start | bytes 655360 | tf_op jit(solution)/shard_map/all_to_all | solution.py:318
  9.2 1.2 %copy.8 = bf16[1024,256]{0,1:T(8,128)(2,1)S(1)} copy(bf16[1024,256]{1,0:T(8,128)(2,1)} %param.10) | data formatting | bytes 1048576 | tf_op jit(solution)/shard_map/optimization_barrier | solution.py:312
  10.5 0.3 collective-permute-start
  10.8 1.1 %constant_dynamic-slice_fusion = (bf16[1024,128]{1,0:T(8,128)(2,1)S(1)}, bf16[1024,128]{1,0:T(8,128)(2,1)S(1)}) fusion(bf16[1024,256]{1,0:T(8,128)(2,1)} %param.11, s32[]{:T(128)S(6)} %select_n.17, s32[]{:T(128)S(6)} %select_n.16), kind=kLoop, calls=%fused_computation.2 | loop fusion | bytes 1048584 | tf_op jit(solution)/shard_map/dynamic_slice | solution.py:325
  11.9 0.3 collective-permute-start.1
  12.2 0.0 collective-permute-done.kb_ref
  12.2 1.3 %collective-permute-done.1.vb_ref = bf16[1024,128]{1,0:T(8,128)(2,1)S(1)} collective-permute-done((bf16[1024,128]{1,0:T(8,128)(2,1)S(1)}, bf16[1024,128]{1,0:T(8,128)(2,1)S(1)}, u32[]{:S(2)}, u32[]{:S(2)}) %collective-permute-start.1) | collective-permute-done | bytes 262176 | tf_op jit(solution)/shard_map/ppermute | solution.py:329
  13.5 6.5 %all-to-all-done.q_ref = bf16[32,40,128]{2,1,0:T(8,128)(2,1)S(1)} async-done(((bf16[32,40,128]{2,1,0:T(8,128)(2,1)}), bf16[32,40,128]{2,1,0:T(8,128)(2,1)S(1)}, u32[]{:S(2)}, u32[]{:S(2)}) %all-to-all-start) | async-done | bytes 327712 | tf_op jit(solution)/shard_map/all_to_all | solution.py:318
  20.1 3.3 %attend.1 = (bf16[1088,128]{1,0:T(8,128)(2,1)}, bf16[32,8,128]{2,1,0:T(8,128)(2,1)S(1)}) custom-call(bf16[32,40,128]{2,1,0:T(8,128)(2,1)S(1)} %all-to-all-done.q_ref, bf16[128,1024]{1,0:T(8,128)(2,1)S(1)} %get-tuple-element.40.ka_ref, bf16[1024,128]{1,0:T(8,128)(2,1)S(1)} %get-tuple-element.38.va_ref, bf16[128,1024]{1,0:T(8,128)(2,1)S(1)} %collective-permute-done.kb_ref, ...), custom_call_target="tpu_custom_call" | custom-call | flops 1073741824 | bytes 4194304 | tf_op jit(solution)/shard_map/attend/pallas_call | solution.py:268
  23.4 3.5 %all-to-all-start.1 = ((bf16[32,17,2,128]{3,2,1,0:T(2,128)(2,1)}), bf16[32,17,2,128]{3,2,1,0:T(2,128)(2,1)S(1)}, u32[]{:S(2)}, u32[]{:S(2)}) async-start(bf16[32,17,2,128]{3,2,1,0:T(2,128)(2,1)} %bitcast.4), calls=%async_computation.1 | async-start | bytes 557056 | tf_op jit(solution)/shard_map/all_to_all | solution.py:318
  26.9 1.8 %collective-permute-start.3 = (bf16[32,8,128]{2,1,0:T(8,128)(2,1)S(1)}, bf16[32,8,128]{2,1,0:T(8,128)(2,1)S(1)}, u32[]{:S(2)}, u32[]{:S(2)}) collective-permute-start(bf16[32,8,128]{2,1,0:T(8,128)(2,1)S(1)} %get-tuple-element.32.kv_ref), channel_id=1, source_target_pairs={{0,2},{1,3},{2,0},{3,1},{4,6},{5,7},{6,4},{7,5},{8,10},{9,11},{10,... | collective-permute-start | bytes 196616 | tf_op jit(solution)/shard_map/ppermute | solution.py:368
  28.7 0.0 collective-permute-start.2
  28.7 4.5 %collective-permute-done.3.kv2_ref = bf16[32,8,128]{2,1,0:T(8,128)(2,1)S(1)} collective-permute-done((bf16[32,8,128]{2,1,0:T(8,128)(2,1)S(1)}, bf16[32,8,128]{2,1,0:T(8,128)(2,1)S(1)}, u32[]{:S(2)}, u32[]{:S(2)}) %collective-permute-start.3) | collective-permute-done | bytes 65568 | tf_op jit(solution)/shard_map/ppermute | solution.py:368
  33.2 0.0 collective-permute-start.4
  33.2 0.0 copy-done
  33.2 0.0 copy-done.1
  33.2 1.8 %masks.1 = (f32[2,56,512]{2,1,0:T(8,128)S(1)}, f32[2,56,128]{2,1,0:T(8,128)S(1)}, bf16[768,1792]{1,0:T(8,128)(2,1)S(1)}) custom-call(s32[3,1,14]{2,1,0:T(1,128)S(1)} %bitcast.10, bf16[8,1792]{1,0:T(8,128)(2,1)S(1)} %copy-done, bf16[1792,1792]{1,0:T(8,128)(2,1)} %w_hbm.1), custom_call_target="tpu_custom_call" | custom-call | tf_op jit(solution)/shard_map/masks/pallas_call | solution.py:268
  35.0 0.0 collective-permute-done.2.kv1_ref
  35.1 0.0 collective-permute-done.4.kv3_ref
  35.1 0.4 %fresh.1 = (f32[2,56,128]{2,1,0:T(8,128)S(1)}, f32[2,56,128]{2,1,0:T(8,128)S(1)}) custom-call(f32[2,56,128]{2,1,0:T(8,128)S(1)} %get-tuple-element.31.rows_ref, bf16[32,8,128]{2,1,0:T(8,128)(2,1)S(1)} %get-tuple-element.32.kv_ref, bf16[32,8,128]{2,1,0:T(8,128)(2,1)S(1)} %collective-permute-done.2.kv1_ref, ...), custom_call_target="tpu_custom_call" | custom-call | flops 29360128 | bytes 1048576 | tf_op jit(solution)/shard_map/fresh/pallas_call | solution.py:268
  35.5 1.4 %all-to-all-done.1 = bf16[32,17,2,128]{3,2,1,0:T(2,128)(2,1)S(1)} async-done(((bf16[32,17,2,128]{3,2,1,0:T(2,128)(2,1)}), bf16[32,17,2,128]{3,2,1,0:T(2,128)(2,1)S(1)}, u32[]{:S(2)}, u32[]{:S(2)}) %all-to-all-start.1) | async-done | bytes 278560 | tf_op jit(solution)/shard_map/all_to_all | solution.py:318
  36.9 3.5 %project.1 = bf16[8,1792]{1,0:T(8,128)(2,1)} custom-call(bf16[1088,128]{1,0:T(8,128)(2,1)S(1)} %bitcast.8, f32[2,56,128]{2,1,0:T(8,128)S(1)} %get-tuple-element.33.out_ref, f32[2,56,128]{2,1,0:T(8,128)S(1)} %get-tuple-element.34.lse_ref, f32[2,56,512]{2,1,0:T(8,128)S(1)} %get-tuple-element.35.match_ref, bf16[768,1792]{1,0:T(8,128)(2,1)S(1)} %get-tuple-element.36.first_ref, ...), custom_call_target="tpu_custom_call" | custom-call | flops 51380224 | bytes 6422528 | tf_op jit(solution)/shard_map/project/pallas_call | solution.py:268
  (1 shorter events, 0.0 us)
Async XLA Ops:
  0.0 33.2 %copy-start = (bf16[8,1792]{1,0:T(8,128)(2,1)S(1)}, bf16[8,1792]{1,0:T(8,128)(2,1)}, u32[]{:S(2)}) copy-start(bf16[8,1792]{1,0:T(8,128)(2,1)} %q_ref) | copy-start | bytes 86020
  0.0 33.2 %copy-start.1 = (s32[1,14,3]{1,0,2:T(1,128)S(1)}, s32[1,14,3]{1,0,2:T(1,128)}, u32[]{:S(2)}) copy-start(s32[1,14,3]{1,0,2:T(1,128)} %param.12) | copy-start | bytes 508
  1.9 18.2 %all-to-all-start = ((bf16[32,40,128]{2,1,0:T(8,128)(2,1)}), bf16[32,40,128]{2,1,0:T(8,128)(2,1)S(1)}, u32[]{:S(2)}, u32[]{:S(2)}) async-start(bf16[32,40,128]{2,1,0:T(8,128)(2,1)} %bitcast.11), calls=%async_computation | async-start | bytes 655360 | tf_op jit(solution)/shard_map/all_to_all | solution.py:318
  10.5 1.7 %collective-permute-start = (bf16[128,1024]{1,0:T(8,128)(2,1)S(1)}, bf16[128,1024]{1,0:T(8,128)(2,1)S(1)}, u32[]{:S(2)}, u32[]{:S(2)}) collective-permute-start(bf16[128,1024]{1,0:T(8,128)(2,1)S(1)} %get-tuple-element.39), channel_id=1, source_target_pairs={{0,1},{1,0},{2,3},{3,2},{4,5},{5,4},{6,7},{7,6},{8,9},{9,8},{10,11... | collective-permute-start | bytes 786440 | tf_op jit(solution)/shard_map/ppermute | solution.py:329
  11.9 1.6 %collective-permute-start.1 = (bf16[1024,128]{1,0:T(8,128)(2,1)S(1)}, bf16[1024,128]{1,0:T(8,128)(2,1)S(1)}, u32[]{:S(2)}, u32[]{:S(2)}) collective-permute-start(bf16[1024,128]{1,0:T(8,128)(2,1)S(1)} %get-tuple-element.37), channel_id=1, source_target_pairs={{0,1},{1,0},{2,3},{3,2},{4,5},{5,4},{6,7},{7,6},{8,9},{9,8},{10,11... | collective-permute-start | bytes 786440 | tf_op jit(solution)/shard_map/ppermute | solution.py:329
  23.4 13.5 %all-to-all-start.1 = ((bf16[32,17,2,128]{3,2,1,0:T(2,128)(2,1)}), bf16[32,17,2,128]{3,2,1,0:T(2,128)(2,1)S(1)}, u32[]{:S(2)}, u32[]{:S(2)}) async-start(bf16[32,17,2,128]{3,2,1,0:T(2,128)(2,1)} %bitcast.4), calls=%async_computation.1 | async-start | bytes 557056 | tf_op jit(solution)/shard_map/all_to_all | solution.py:318
  26.9 6.4 %collective-permute-start.3 = (bf16[32,8,128]{2,1,0:T(8,128)(2,1)S(1)}, bf16[32,8,128]{2,1,0:T(8,128)(2,1)S(1)}, u32[]{:S(2)}, u32[]{:S(2)}) collective-permute-start(bf16[32,8,128]{2,1,0:T(8,128)(2,1)S(1)} %get-tuple-element.32.kv_ref), channel_id=1, source_target_pairs={{0,2},{1,3},{2,0},{3,1},{4,6},{5,7},{6,4},{7,5},{8,10},{9,11},{10,... | collective-permute-start | bytes 196616 | tf_op jit(solution)/shard_map/ppermute | solution.py:368
  28.7 6.3 %collective-permute-start.2 = (bf16[32,8,128]{2,1,0:T(8,128)(2,1)S(1)}, bf16[32,8,128]{2,1,0:T(8,128)(2,1)S(1)}, u32[]{:S(2)}, u32[]{:S(2)}) collective-permute-start(bf16[32,8,128]{2,1,0:T(8,128)(2,1)S(1)} %get-tuple-element.32.kv_ref), channel_id=1, source_target_pairs={{0,1},{1,0},{2,3},{3,2},{4,5},{5,4},{6,7},{7,6},{8,9},{9,8},{10,11... | collective-permute-start | bytes 196616 | tf_op jit(solution)/shard_map/ppermute | solution.py:369
  33.2 1.8 %collective-permute-start.4 = (bf16[32,8,128]{2,1,0:T(8,128)(2,1)S(1)}, bf16[32,8,128]{2,1,0:T(8,128)(2,1)S(1)}, u32[]{:S(2)}, u32[]{:S(2)}) collective-permute-start(bf16[32,8,128]{2,1,0:T(8,128)(2,1)S(1)} %collective-permute-done.3.kv2_ref), channel_id=1, source_target_pairs={{0,1},{1,0},{2,3},{3,2},{4,5},{5,4},{6,7},{7,6},{8,9},{9,8},{10,11... | collective-permute-start | bytes 196616 | tf_op jit(solution)/shard_map/ppermute | solution.py:369

commit v27 on v26

--- a/solution.py
+++ b/solution.py
@@ -107,7 +107,10 @@
     tokens = q_ref.shape[0]
     per = capacity * tokens
     lane = lax.broadcasted_iota(jnp.int32, (tokens, match_ref.shape[2]), 1)
-    block, slot, token = lane // (per * chips), lane % per // tokens, lane % tokens
+    holders = match_ref.shape[2] // (per + 2)
+    rank = sum((lane >= i * (per + 2)).astype(jnp.int32) for i in range(1, holders))
+    place = lane - rank * (per + 2)
+    block, slot, token = (holders - 1 - rank) // chips, place // tokens, place % tokens
     for g in range(KVH):
         match_ref[g] = jnp.concatenate(slot_match(chosen_ref, g, block, slot, token), axis=0)
         rows_ref[g] = jnp.concatenate(head_rows(q_ref, g), axis=0)
@@ -208,11 +211,15 @@
         sems,
     )
     tokens = y_ref.shape[0]
-    holders = match_ref.shape[2] // per
-    hist = hist_ref[...].astype(jnp.float32)
-    fold = LANES // per
-    row = lax.broadcasted_iota(jnp.int32, (holders, LANES), 0)
+    stride = per + 2
+    count = match_ref.shape[2]
+    holders = count // stride
+    picked = lax.broadcasted_iota(jnp.int32, (holders, count), 1) - per == stride * lax.broadcasted_iota(
+        jnp.int32, (holders, count), 0
+    )
+    picked = jnp.where(picked, 1.0, 0.0).astype(jnp.bfloat16)
     lane = lax.broadcasted_iota(jnp.int32, (holders, LANES), 1)
+    begin = stride * lax.broadcasted_iota(jnp.int32, (holders, LANES), 0)
 
     def times(heads, weights):
         lhs = jnp.concatenate(heads, axis=1).astype(jnp.bfloat16)
@@ -220,21 +227,18 @@
 
     heads = []
     for g in range(KVH):
-        starts = [((KVH - g) * holders - 1 - m) * (per + 2) for m in range(holders)]
-        outs = jnp.concatenate([hist[i : i + per] for i in starts], axis=0).astype(jnp.bfloat16)
-        stats = jnp.concatenate([hist[i + per : i + per + 1] for i in starts], axis=0)
+        outs = hist_ref[(KVH - 1 - g) * count : (KVH - g) * count, :]
+        stats = jnp.dot(picked, outs, preferred_element_type=jnp.float32)
         shift = LANES // 2
         while shift >= per:
             stats = stats + pltpu.roll(stats, shift, 1)
             shift //= 2
-        stats = jnp.where(row % fold == lane // per, stats, 0.0)
-        lse = jnp.concatenate(
-            [
-                jnp.sum(jnp.where(row // fold == m, stats, 0.0), axis=0, keepdims=True)
-                for m in range(holders // fold)
-            ],
-            axis=1,
-        )
+        stats = pltpu.roll(stats, 0, 1, stride=2, stride_axis=0)
+        tiles = []
+        for first in range(0, count, LANES):
+            inside = (lane + first >= begin) & (lane + first < begin + stride)
+            tiles.append(jnp.sum(jnp.where(inside, stats, 0.0), axis=0, keepdims=True))
+        lse = jnp.concatenate(tiles, axis=1)[:, :count]
         match = match_ref[g] > 0.5
         lse = jnp.where(match, lse, LOW_SCORE)
         own = lse_ref[g]
@@ -355,7 +359,7 @@
         functools.partial(masks_kernel, chips, capacity),
         "masks",
         (
-            jax.ShapeDtypeStruct((KVH, GROUP * tokens, holders * per), f32),
+            jax.ShapeDtypeStruct((KVH, GROUP * tokens, holders * (per + 2)), f32),
             jax.ShapeDtypeStruct((KVH, GROUP * tokens, HD), f32),
             jax.ShapeDtypeStruct((ready, out_weight.shape[1]), bf16),
         ),

time: 40.8 us -> 41.3 us (1.012)
  Pallas kernels: 10.9 us -> 11.4 us
    pallas_call x5, Pallas kernels: 10.9 us -> 11.4 us  [call(): pl.pallas_call(kernel, name=name, out_shape=out_shape, in_specs=specs, ou...]
  transfers between devices with their start and end apart: 7 -> 7, of which waited for: 4 -> 4; matrix products, arithmetic and copies ran while one was open for 6% -> 6% of each run, Pallas kernels for 6% -> 5%
where the time goes in v27:
time: 41.3 us; the launch traced here: 40.8 us
  waiting for transfers between devices  13.7 us (33%)
  starting transfers between devices  13.2 us (32%)
  Pallas kernels  11.4 us (28%)
  local copies, waits for them, and re-layouts  2.36 us (6%)
    pallas_call x5, Pallas kernels, call(): pl.pallas_call(kernel, name=name, out_shape=out_shape, in_specs=specs, ou...  11.4 us
    all_to_all x2, starting transfers between devices, exchange(): lax.all_to_all(x, 'seq', split_axis=0, concat_axis=0, axis_index_groups=[...  10.8 us
    all_to_all x2, waiting for transfers between devices, exchange(): lax.all_to_all(x, 'seq', split_axis=0, concat_axis=0, axis_index_groups=[...  7.91 us
    ppermute x1, waiting for transfers between devices, body(): far = lax.ppermute(fresh, 'seq', partner(2))  4.52 us
    ppermute x1, starting transfers between devices, body(): far = lax.ppermute(fresh, 'seq', partner(2))  1.83 us
    ppermute x2, waiting for transfers between devices, body(): lax.ppermute(x, 'seq', partner(1))  1.28 us
    optimization_barrier x1, local copies, waits for them, and re-layouts, body(): lax.optimization_barrier((send, cache_keys, cache_values, picks, queries))  1.25 us
    dynamic_slice x1, local copies, waits for them, and re-layouts, halves(): lax.dynamic_slice_in_dim(x, head * HD, HD, axis=1)  1.06 us
  transfers between devices with their start and end apart: 7, of which 4 were waited for; matrix products, arithmetic and copies ran while one was open for 6% of the time, Pallas kernels for 5%

profile of v27, /device:TPU:0, one launch (start us, length us, event | category | flops | bytes accessed | tf_op | source)
XLA Modules:
  0.0 40.8 jit_solution(17138309600055977389)
XLA Ops:
  0.0 0.0 copy-start
  0.0 0.0 copy-start.1
  0.0 1.9 %pack.1 = bf16[2,8,2,40,128]{4,3,2,1,0:T(8,128)(2,1)} custom-call(s32[3,1,14]{2,1,0:T(1,128)} %bitcast.9, bf16[8,1792]{1,0:T(8,128)(2,1)} %q_ref, bf16[8,256]{1,0:T(8,128)(2,1)} %k_hbm.1, bf16[8,256]{1,0:T(8,128)(2,1)} %v_hbm.1), custom_call_target="tpu_custom_call" | custom-call | tf_op jit(solution)/shard_map/pack/pallas_call | solution.py:272
  1.9 7.3 %all-to-all-start = ((bf16[32,40,128]{2,1,0:T(8,128)(2,1)}), bf16[32,40,128]{2,1,0:T(8,128)(2,1)S(1)}, u32[]{:S(2)}, u32[]{:S(2)}) async-start(bf16[32,40,128]{2,1,0:T(8,128)(2,1)} %bitcast.11), calls=%async_computation | async-start | bytes 655360 | tf_op jit(solution)/shard_map/all_to_all | solution.py:322
  9.2 1.2 %copy.8 = bf16[1024,256]{0,1:T(8,128)(2,1)S(1)} copy(bf16[1024,256]{1,0:T(8,128)(2,1)} %param.10) | data formatting | bytes 1048576 | tf_op jit(solution)/shard_map/optimization_barrier | solution.py:316
  10.5 0.3 collective-permute-start
  10.8 1.1 %constant_dynamic-slice_fusion = (bf16[1024,128]{1,0:T(8,128)(2,1)S(1)}, bf16[1024,128]{1,0:T(8,128)(2,1)S(1)}) fusion(bf16[1024,256]{1,0:T(8,128)(2,1)} %param.11, s32[]{:T(128)S(6)} %select_n.17, s32[]{:T(128)S(6)} %select_n.16), kind=kLoop, calls=%fused_computation.2 | loop fusion | bytes 1048584 | tf_op jit(solution)/shard_map/dynamic_slice | solution.py:329
  11.9 0.3 collective-permute-start.1
  12.2 0.0 collective-permute-done.kb_ref
  12.2 1.3 %collective-permute-done.1.vb_ref = bf16[1024,128]{1,0:T(8,128)(2,1)S(1)} collective-permute-done((bf16[1024,128]{1,0:T(8,128)(2,1)S(1)}, bf16[1024,128]{1,0:T(8,128)(2,1)S(1)}, u32[]{:S(2)}, u32[]{:S(2)}) %collective-permute-start.1) | collective-permute-done | bytes 262176 | tf_op jit(solution)/shard_map/ppermute | solution.py:333
  13.5 6.5 %all-to-all-done.q_ref = bf16[32,40,128]{2,1,0:T(8,128)(2,1)S(1)} async-done(((bf16[32,40,128]{2,1,0:T(8,128)(2,1)}), bf16[32,40,128]{2,1,0:T(8,128)(2,1)S(1)}, u32[]{:S(2)}, u32[]{:S(2)}) %all-to-all-start) | async-done | bytes 327712 | tf_op jit(solution)/shard_map/all_to_all | solution.py:322
  20.1 3.3 %attend.1 = (bf16[1088,128]{1,0:T(8,128)(2,1)}, bf16[32,8,128]{2,1,0:T(8,128)(2,1)S(1)}) custom-call(bf16[32,40,128]{2,1,0:T(8,128)(2,1)S(1)} %all-to-all-done.q_ref, bf16[128,1024]{1,0:T(8,128)(2,1)S(1)} %get-tuple-element.40.ka_ref, bf16[1024,128]{1,0:T(8,128)(2,1)S(1)} %get-tuple-element.38.va_ref, bf16[128,1024]{1,0:T(8,128)(2,1)S(1)} %collective-permute-done.kb_ref, ...), custom_call_target="tpu_custom_call" | custom-call | flops 1073741824 | bytes 4194304 | tf_op jit(solution)/shard_map/attend/pallas_call | solution.py:272
  23.4 3.5 %all-to-all-start.1 = ((bf16[32,17,2,128]{3,2,1,0:T(2,128)(2,1)}), bf16[32,17,2,128]{3,2,1,0:T(2,128)(2,1)S(1)}, u32[]{:S(2)}, u32[]{:S(2)}) async-start(bf16[32,17,2,128]{3,2,1,0:T(2,128)(2,1)} %bitcast.4), calls=%async_computation.1 | async-start | bytes 557056 | tf_op jit(solution)/shard_map/all_to_all | solution.py:322
  26.9 1.8 %collective-permute-start.3 = (bf16[32,8,128]{2,1,0:T(8,128)(2,1)S(1)}, bf16[32,8,128]{2,1,0:T(8,128)(2,1)S(1)}, u32[]{:S(2)}, u32[]{:S(2)}) collective-permute-start(bf16[32,8,128]{2,1,0:T(8,128)(2,1)S(1)} %get-tuple-element.32.kv_ref), channel_id=1, source_target_pairs={{0,2},{1,3},{2,0},{3,1},{4,6},{5,7},{6,4},{7,5},{8,10},{9,11},{10,... | collective-permute-start | bytes 196616 | tf_op jit(solution)/shard_map/ppermute | solution.py:372
  28.7 0.0 collective-permute-start.2
  28.7 4.5 %collective-permute-done.3.kv2_ref = bf16[32,8,128]{2,1,0:T(8,128)(2,1)S(1)} collective-permute-done((bf16[32,8,128]{2,1,0:T(8,128)(2,1)S(1)}, bf16[32,8,128]{2,1,0:T(8,128)(2,1)S(1)}, u32[]{:S(2)}, u32[]{:S(2)}) %collective-permute-start.3) | collective-permute-done | bytes 65568 | tf_op jit(solution)/shard_map/ppermute | solution.py:372
  33.2 0.0 collective-permute-start.4
  33.2 0.0 copy-done
  33.2 0.0 copy-done.1
  33.2 1.8 %masks.1 = (f32[2,56,544]{2,1,0:T(8,128)S(1)}, f32[2,56,128]{2,1,0:T(8,128)S(1)}, bf16[768,1792]{1,0:T(8,128)(2,1)S(1)}) custom-call(s32[3,1,14]{2,1,0:T(1,128)S(1)} %bitcast.10, bf16[8,1792]{1,0:T(8,128)(2,1)S(1)} %copy-done, bf16[1792,1792]{1,0:T(8,128)(2,1)} %w_hbm.1), custom_call_target="tpu_custom_call" | custom-call | tf_op jit(solution)/shard_map/masks/pallas_call | solution.py:272
  35.0 0.0 collective-permute-done.2.kv1_ref
  35.1 0.0 collective-permute-done.4.kv3_ref
  35.1 0.4 %fresh.1 = (f32[2,56,128]{2,1,0:T(8,128)S(1)}, f32[2,56,128]{2,1,0:T(8,128)S(1)}) custom-call(f32[2,56,128]{2,1,0:T(8,128)S(1)} %get-tuple-element.31.rows_ref, bf16[32,8,128]{2,1,0:T(8,128)(2,1)S(1)} %get-tuple-element.32.kv_ref, bf16[32,8,128]{2,1,0:T(8,128)(2,1)S(1)} %collective-permute-done.2.kv1_ref, ...), custom_call_target="tpu_custom_call" | custom-call | flops 29360128 | bytes 1048576 | tf_op jit(solution)/shard_map/fresh/pallas_call | solution.py:272
  35.5 1.4 %all-to-all-done.1 = bf16[32,17,2,128]{3,2,1,0:T(2,128)(2,1)S(1)} async-done(((bf16[32,17,2,128]{3,2,1,0:T(2,128)(2,1)}), bf16[32,17,2,128]{3,2,1,0:T(2,128)(2,1)S(1)}, u32[]{:S(2)}, u32[]{:S(2)}) %all-to-all-start.1) | async-done | bytes 278560 | tf_op jit(solution)/shard_map/all_to_all | solution.py:322
  36.9 4.0 %project.1 = bf16[8,1792]{1,0:T(8,128)(2,1)} custom-call(bf16[1088,128]{1,0:T(8,128)(2,1)S(1)} %bitcast.8, f32[2,56,128]{2,1,0:T(8,128)S(1)} %get-tuple-element.33.out_ref, f32[2,56,128]{2,1,0:T(8,128)S(1)} %get-tuple-element.34.lse_ref, f32[2,56,544]{2,1,0:T(8,128)S(1)} %get-tuple-element.35.match_ref, bf16[768,1792]{1,0:T(8,128)(2,1)S(1)} %get-tuple-element.36.first_ref, ...), custom_call_target="tpu_custom_call" | custom-call | flops 51380224 | bytes 6422528 | tf_op jit(solution)/shard_map/project/pallas_call | solution.py:272
  (1 shorter events, 0.0 us)
Async XLA Ops:
  0.0 33.2 %copy-start = (bf16[8,1792]{1,0:T(8,128)(2,1)S(1)}, bf16[8,1792]{1,0:T(8,128)(2,1)}, u32[]{:S(2)}) copy-start(bf16[8,1792]{1,0:T(8,128)(2,1)} %q_ref) | copy-start | bytes 86020
  0.0 33.2 %copy-start.1 = (s32[1,14,3]{1,0,2:T(1,128)S(1)}, s32[1,14,3]{1,0,2:T(1,128)}, u32[]{:S(2)}) copy-start(s32[1,14,3]{1,0,2:T(1,128)} %param.12) | copy-start | bytes 508
  1.9 18.2 %all-to-all-start = ((bf16[32,40,128]{2,1,0:T(8,128)(2,1)}), bf16[32,40,128]{2,1,0:T(8,128)(2,1)S(1)}, u32[]{:S(2)}, u32[]{:S(2)}) async-start(bf16[32,40,128]{2,1,0:T(8,128)(2,1)} %bitcast.11), calls=%async_computation | async-start | bytes 655360 | tf_op jit(solution)/shard_map/all_to_all | solution.py:322
  10.5 1.7 %collective-permute-start = (bf16[128,1024]{1,0:T(8,128)(2,1)S(1)}, bf16[128,1024]{1,0:T(8,128)(2,1)S(1)}, u32[]{:S(2)}, u32[]{:S(2)}) collective-permute-start(bf16[128,1024]{1,0:T(8,128)(2,1)S(1)} %get-tuple-element.39), channel_id=1, source_target_pairs={{0,1},{1,0},{2,3},{3,2},{4,5},{5,4},{6,7},{7,6},{8,9},{9,8},{10,11... | collective-permute-start | bytes 786440 | tf_op jit(solution)/shard_map/ppermute | solution.py:333
  11.9 1.6 %collective-permute-start.1 = (bf16[1024,128]{1,0:T(8,128)(2,1)S(1)}, bf16[1024,128]{1,0:T(8,128)(2,1)S(1)}, u32[]{:S(2)}, u32[]{:S(2)}) collective-permute-start(bf16[1024,128]{1,0:T(8,128)(2,1)S(1)} %get-tuple-element.37), channel_id=1, source_target_pairs={{0,1},{1,0},{2,3},{3,2},{4,5},{5,4},{6,7},{7,6},{8,9},{9,8},{10,11... | collective-permute-start | bytes 786440 | tf_op jit(solution)/shard_map/ppermute | solution.py:333
  23.4 13.5 %all-to-all-start.1 = ((bf16[32,17,2,128]{3,2,1,0:T(2,128)(2,1)}), bf16[32,17,2,128]{3,2,1,0:T(2,128)(2,1)S(1)}, u32[]{:S(2)}, u32[]{:S(2)}) async-start(bf16[32,17,2,128]{3,2,1,0:T(2,128)(2,1)} %bitcast.4), calls=%async_computation.1 | async-start | bytes 557056 | tf_op jit(solution)/shard_map/all_to_all | solution.py:322
  26.9 6.4 %collective-permute-start.3 = (bf16[32,8,128]{2,1,0:T(8,128)(2,1)S(1)}, bf16[32,8,128]{2,1,0:T(8,128)(2,1)S(1)}, u32[]{:S(2)}, u32[]{:S(2)}) collective-permute-start(bf16[32,8,128]{2,1,0:T(8,128)(2,1)S(1)} %get-tuple-element.32.kv_ref), channel_id=1, source_target_pairs={{0,2},{1,3},{2,0},{3,1},{4,6},{5,7},{6,4},{7,5},{8,10},{9,11},{10,... | collective-permute-start | bytes 196616 | tf_op jit(solution)/shard_map/ppermute | solution.py:372
  28.7 6.3 %collective-permute-start.2 = (bf16[32,8,128]{2,1,0:T(8,128)(2,1)S(1)}, bf16[32,8,128]{2,1,0:T(8,128)(2,1)S(1)}, u32[]{:S(2)}, u32[]{:S(2)}) collective-permute-start(bf16[32,8,128]{2,1,0:T(8,128)(2,1)S(1)} %get-tuple-element.32.kv_ref), channel_id=1, source_target_pairs={{0,1},{1,0},{2,3},{3,2},{4,5},{5,4},{6,7},{7,6},{8,9},{9,8},{10,11... | collective-permute-start | bytes 196616 | tf_op jit(solution)/shard_map/ppermute | solution.py:373
  33.2 1.8 %collective-permute-start.4 = (bf16[32,8,128]{2,1,0:T(8,128)(2,1)S(1)}, bf16[32,8,128]{2,1,0:T(8,128)(2,1)S(1)}, u32[]{:S(2)}, u32[]{:S(2)}) collective-permute-start(bf16[32,8,128]{2,1,0:T(8,128)(2,1)S(1)} %collective-permute-done.3.kv2_ref), channel_id=1, source_target_pairs={{0,1},{1,0},{2,3},{3,2},{4,5},{5,4},{6,7},{7,6},{8,9},{9,8},{10,11... | collective-permute-start | bytes 196616 | tf_op jit(solution)/shard_map/ppermute | solution.py:373

commit v28 on v26

--- a/solution.py
+++ b/solution.py
@@ -197,7 +197,7 @@
         lse_ref[g] = top + jnp.log(total) * LOG2E
 
 
-def project_kernel(per, hist_ref, out_ref, lse_ref, match_ref, first_ref, w_hbm, y_ref, w_ref, sems):
+def project_kernel(per, hist_ref, out_ref, lse_ref, match_ref, first_ref, w_hbm, y_ref, w_ref, rows_ref, sems):
     depth = KVH * HD
     ready = first_ref.shape[0] // depth
     copies = fetch(
@@ -209,7 +209,7 @@
     )
     tokens = y_ref.shape[0]
     holders = match_ref.shape[2] // per
-    hist = hist_ref[...].astype(jnp.float32)
+    rows_ref[...] = hist_ref[...].astype(jnp.float32)
     fold = LANES // per
     row = lax.broadcasted_iota(jnp.int32, (holders, LANES), 0)
     lane = lax.broadcasted_iota(jnp.int32, (holders, LANES), 1)
@@ -221,8 +221,8 @@
     heads = []
     for g in range(KVH):
         starts = [((KVH - g) * holders - 1 - m) * (per + 2) for m in range(holders)]
-        outs = jnp.concatenate([hist[i : i + per] for i in starts], axis=0).astype(jnp.bfloat16)
-        stats = jnp.concatenate([hist[i + per : i + per + 1] for i in starts], axis=0)
+        outs = jnp.concatenate([rows_ref[i : i + per, :] for i in starts], axis=0).astype(jnp.bfloat16)
+        stats = jnp.concatenate([rows_ref[i + per : i + per + 1, :] for i in starts], axis=0)
         shift = LANES // 2
         while shift >= per:
             stats = stats + pltpu.roll(stats, shift, 1)
@@ -385,6 +385,7 @@
         hist.reshape(devices * (per + 2), HD), out, lse, match, first, out_weight,
         scratch=[
             pltpu.VMEM((out_weight.shape[0] - ready, out_weight.shape[1]), bf16),
+            pltpu.VMEM((devices * (per + 2), HD), f32),
             pltpu.SemaphoreType.DMA((GROUP - EARLY,)),
         ],
         flops=2 * tokens * out_weight.size,

time: 40.8 us -> 40.4 us (level)
    pallas_call x5, Pallas kernels: 10.9 us -> 10.5 us  [call(): pl.pallas_call(kernel, name=name, out_shape=out_shape, in_specs=specs, ou...]
where the time goes in v28:
time: 40.4 us; the launch traced here: 39.9 us
  waiting for transfers between devices  13.7 us (34%)
  starting transfers between devices  13.2 us (33%)
  Pallas kernels  10.5 us (26%)
  local copies, waits for them, and re-layouts  2.36 us (6%)
    all_to_all x2, starting transfers between devices, exchange(): lax.all_to_all(x, 'seq', split_axis=0, concat_axis=0, axis_index_groups=[...  10.8 us
    pallas_call x5, Pallas kernels, call(): pl.pallas_call(kernel, name=name, out_shape=out_shape, in_specs=specs, ou...  10.5 us
    all_to_all x2, waiting for transfers between devices, exchange(): lax.all_to_all(x, 'seq', split_axis=0, concat_axis=0, axis_index_groups=[...  7.91 us
    ppermute x1, waiting for transfers between devices, body(): far = lax.ppermute(fresh, 'seq', partner(2))  4.52 us
    ppermute x1, starting transfers between devices, body(): far = lax.ppermute(fresh, 'seq', partner(2))  1.83 us
    ppermute x2, waiting for transfers between devices, body(): lax.ppermute(x, 'seq', partner(1))  1.28 us
    optimization_barrier x1, local copies, waits for them, and re-layouts, body(): lax.optimization_barrier((send, cache_keys, cache_values, picks, queries))  1.25 us
    dynamic_slice x1, local copies, waits for them, and re-layouts, halves(): lax.dynamic_slice_in_dim(x, head * HD, HD, axis=1)  1.06 us
  transfers between devices with their start and end apart: 7, of which 4 were waited for; matrix products, arithmetic and copies ran while one was open for 6% of the time, Pallas kernels for 6%

profile of v28, /device:TPU:0, one launch (start us, length us, event | category | flops | bytes accessed | tf_op | source)
XLA Modules:
  0.0 39.9 jit_solution(10551972499337856681)
XLA Ops:
  0.0 0.0 copy-start
  0.0 0.0 copy-start.1
  0.0 1.9 %pack.1 = bf16[2,8,2,40,128]{4,3,2,1,0:T(8,128)(2,1)} custom-call(s32[3,1,14]{2,1,0:T(1,128)} %bitcast.9, bf16[8,1792]{1,0:T(8,128)(2,1)} %q_ref, bf16[8,256]{1,0:T(8,128)(2,1)} %k_hbm.1, bf16[8,256]{1,0:T(8,128)(2,1)} %v_hbm.1), custom_call_target="tpu_custom_call" | custom-call | tf_op jit(solution)/shard_map/pack/pallas_call | solution.py:268
  1.9 7.3 %all-to-all-start = ((bf16[32,40,128]{2,1,0:T(8,128)(2,1)}), bf16[32,40,128]{2,1,0:T(8,128)(2,1)S(1)}, u32[]{:S(2)}, u32[]{:S(2)}) async-start(bf16[32,40,128]{2,1,0:T(8,128)(2,1)} %bitcast.11), calls=%async_computation | async-start | bytes 655360 | tf_op jit(solution)/shard_map/all_to_all | solution.py:318
  9.2 1.2 %copy.8 = bf16[1024,256]{0,1:T(8,128)(2,1)S(1)} copy(bf16[1024,256]{1,0:T(8,128)(2,1)} %param.10) | data formatting | bytes 1048576 | tf_op jit(solution)/shard_map/optimization_barrier | solution.py:312
  10.5 0.3 collective-permute-start
  10.8 1.1 %constant_dynamic-slice_fusion = (bf16[1024,128]{1,0:T(8,128)(2,1)S(1)}, bf16[1024,128]{1,0:T(8,128)(2,1)S(1)}) fusion(bf16[1024,256]{1,0:T(8,128)(2,1)} %param.11, s32[]{:T(128)S(6)} %select_n.17, s32[]{:T(128)S(6)} %select_n.16), kind=kLoop, calls=%fused_computation.2 | loop fusion | bytes 1048584 | tf_op jit(solution)/shard_map/dynamic_slice | solution.py:325
  11.9 0.3 collective-permute-start.1
  12.2 0.0 collective-permute-done.kb_ref
  12.2 1.3 %collective-permute-done.1.vb_ref = bf16[1024,128]{1,0:T(8,128)(2,1)S(1)} collective-permute-done((bf16[1024,128]{1,0:T(8,128)(2,1)S(1)}, bf16[1024,128]{1,0:T(8,128)(2,1)S(1)}, u32[]{:S(2)}, u32[]{:S(2)}) %collective-permute-start.1) | collective-permute-done | bytes 262176 | tf_op jit(solution)/shard_map/ppermute | solution.py:329
  13.5 6.5 %all-to-all-done.q_ref = bf16[32,40,128]{2,1,0:T(8,128)(2,1)S(1)} async-done(((bf16[32,40,128]{2,1,0:T(8,128)(2,1)}), bf16[32,40,128]{2,1,0:T(8,128)(2,1)S(1)}, u32[]{:S(2)}, u32[]{:S(2)}) %all-to-all-start) | async-done | bytes 327712 | tf_op jit(solution)/shard_map/all_to_all | solution.py:318
  20.1 3.3 %attend.1 = (bf16[1088,128]{1,0:T(8,128)(2,1)}, bf16[32,8,128]{2,1,0:T(8,128)(2,1)S(1)}) custom-call(bf16[32,40,128]{2,1,0:T(8,128)(2,1)S(1)} %all-to-all-done.q_ref, bf16[128,1024]{1,0:T(8,128)(2,1)S(1)} %get-tuple-element.40.ka_ref, bf16[1024,128]{1,0:T(8,128)(2,1)S(1)} %get-tuple-element.38.va_ref, bf16[128,1024]{1,0:T(8,128)(2,1)S(1)} %collective-permute-done.kb_ref, ...), custom_call_target="tpu_custom_call" | custom-call | flops 1073741824 | bytes 4194304 | tf_op jit(solution)/shard_map/attend/pallas_call | solution.py:268
  23.4 3.5 %all-to-all-start.1 = ((bf16[32,17,2,128]{3,2,1,0:T(2,128)(2,1)}), bf16[32,17,2,128]{3,2,1,0:T(2,128)(2,1)S(1)}, u32[]{:S(2)}, u32[]{:S(2)}) async-start(bf16[32,17,2,128]{3,2,1,0:T(2,128)(2,1)} %bitcast.4), calls=%async_computation.1 | async-start | bytes 557056 | tf_op jit(solution)/shard_map/all_to_all | solution.py:318
  26.9 1.8 %collective-permute-start.3 = (bf16[32,8,128]{2,1,0:T(8,128)(2,1)S(1)}, bf16[32,8,128]{2,1,0:T(8,128)(2,1)S(1)}, u32[]{:S(2)}, u32[]{:S(2)}) collective-permute-start(bf16[32,8,128]{2,1,0:T(8,128)(2,1)S(1)} %get-tuple-element.32.kv_ref), channel_id=1, source_target_pairs={{0,2},{1,3},{2,0},{3,1},{4,6},{5,7},{6,4},{7,5},{8,10},{9,11},{10,... | collective-permute-start | bytes 196616 | tf_op jit(solution)/shard_map/ppermute | solution.py:368
  28.7 0.0 collective-permute-start.2
  28.7 4.5 %collective-permute-done.3.kv2_ref = bf16[32,8,128]{2,1,0:T(8,128)(2,1)S(1)} collective-permute-done((bf16[32,8,128]{2,1,0:T(8,128)(2,1)S(1)}, bf16[32,8,128]{2,1,0:T(8,128)(2,1)S(1)}, u32[]{:S(2)}, u32[]{:S(2)}) %collective-permute-start.3) | collective-permute-done | bytes 65568 | tf_op jit(solution)/shard_map/ppermute | solution.py:368
  33.2 0.0 collective-permute-start.4
  33.2 0.0 copy-done
  33.2 0.0 copy-done.1
  33.2 1.8 %masks.1 = (f32[2,56,512]{2,1,0:T(8,128)S(1)}, f32[2,56,128]{2,1,0:T(8,128)S(1)}, bf16[768,1792]{1,0:T(8,128)(2,1)S(1)}) custom-call(s32[3,1,14]{2,1,0:T(1,128)S(1)} %bitcast.10, bf16[8,1792]{1,0:T(8,128)(2,1)S(1)} %copy-done, bf16[1792,1792]{1,0:T(8,128)(2,1)} %w_hbm.1), custom_call_target="tpu_custom_call" | custom-call | tf_op jit(solution)/shard_map/masks/pallas_call | solution.py:268
  35.0 0.0 collective-permute-done.2.kv1_ref
  35.1 0.0 collective-permute-done.4.kv3_ref
  35.1 0.4 %fresh.1 = (f32[2,56,128]{2,1,0:T(8,128)S(1)}, f32[2,56,128]{2,1,0:T(8,128)S(1)}) custom-call(f32[2,56,128]{2,1,0:T(8,128)S(1)} %get-tuple-element.31.rows_ref, bf16[32,8,128]{2,1,0:T(8,128)(2,1)S(1)} %get-tuple-element.32.kv_ref, bf16[32,8,128]{2,1,0:T(8,128)(2,1)S(1)} %collective-permute-done.2.kv1_ref, ...), custom_call_target="tpu_custom_call" | custom-call | flops 29360128 | bytes 1048576 | tf_op jit(solution)/shard_map/fresh/pallas_call | solution.py:268
  35.5 1.4 %all-to-all-done.1 = bf16[32,17,2,128]{3,2,1,0:T(2,128)(2,1)S(1)} async-done(((bf16[32,17,2,128]{3,2,1,0:T(2,128)(2,1)}), bf16[32,17,2,128]{3,2,1,0:T(2,128)(2,1)S(1)}, u32[]{:S(2)}, u32[]{:S(2)}) %all-to-all-start.1) | async-done | bytes 278560 | tf_op jit(solution)/shard_map/all_to_all | solution.py:318
  36.9 3.0 %project.1 = bf16[8,1792]{1,0:T(8,128)(2,1)} custom-call(bf16[1088,128]{1,0:T(8,128)(2,1)S(1)} %bitcast.8, f32[2,56,128]{2,1,0:T(8,128)S(1)} %get-tuple-element.33.out_ref, f32[2,56,128]{2,1,0:T(8,128)S(1)} %get-tuple-element.34.lse_ref, f32[2,56,512]{2,1,0:T(8,128)S(1)} %get-tuple-element.35.match_ref, bf16[768,1792]{1,0:T(8,128)(2,1)S(1)} %get-tuple-element.36.first_ref, ...), custom_call_target="tpu_custom_call" | custom-call | flops 51380224 | bytes 6422528 | tf_op jit(solution)/shard_map/project/pallas_call | solution.py:268
  (1 shorter events, 0.0 us)
Async XLA Ops:
  0.0 33.2 %copy-start = (bf16[8,1792]{1,0:T(8,128)(2,1)S(1)}, bf16[8,1792]{1,0:T(8,128)(2,1)}, u32[]{:S(2)}) copy-start(bf16[8,1792]{1,0:T(8,128)(2,1)} %q_ref) | copy-start | bytes 86020
  0.0 33.2 %copy-start.1 = (s32[1,14,3]{1,0,2:T(1,128)S(1)}, s32[1,14,3]{1,0,2:T(1,128)}, u32[]{:S(2)}) copy-start(s32[1,14,3]{1,0,2:T(1,128)} %param.12) | copy-start | bytes 508
  1.9 18.2 %all-to-all-start = ((bf16[32,40,128]{2,1,0:T(8,128)(2,1)}), bf16[32,40,128]{2,1,0:T(8,128)(2,1)S(1)}, u32[]{:S(2)}, u32[]{:S(2)}) async-start(bf16[32,40,128]{2,1,0:T(8,128)(2,1)} %bitcast.11), calls=%async_computation | async-start | bytes 655360 | tf_op jit(solution)/shard_map/all_to_all | solution.py:318
  10.5 1.7 %collective-permute-start = (bf16[128,1024]{1,0:T(8,128)(2,1)S(1)}, bf16[128,1024]{1,0:T(8,128)(2,1)S(1)}, u32[]{:S(2)}, u32[]{:S(2)}) collective-permute-start(bf16[128,1024]{1,0:T(8,128)(2,1)S(1)} %get-tuple-element.39), channel_id=1, source_target_pairs={{0,1},{1,0},{2,3},{3,2},{4,5},{5,4},{6,7},{7,6},{8,9},{9,8},{10,11... | collective-permute-start | bytes 786440 | tf_op jit(solution)/shard_map/ppermute | solution.py:329
  11.9 1.6 %collective-permute-start.1 = (bf16[1024,128]{1,0:T(8,128)(2,1)S(1)}, bf16[1024,128]{1,0:T(8,128)(2,1)S(1)}, u32[]{:S(2)}, u32[]{:S(2)}) collective-permute-start(bf16[1024,128]{1,0:T(8,128)(2,1)S(1)} %get-tuple-element.37), channel_id=1, source_target_pairs={{0,1},{1,0},{2,3},{3,2},{4,5},{5,4},{6,7},{7,6},{8,9},{9,8},{10,11... | collective-permute-start | bytes 786440 | tf_op jit(solution)/shard_map/ppermute | solution.py:329
  23.4 13.5 %all-to-all-start.1 = ((bf16[32,17,2,128]{3,2,1,0:T(2,128)(2,1)}), bf16[32,17,2,128]{3,2,1,0:T(2,128)(2,1)S(1)}, u32[]{:S(2)}, u32[]{:S(2)}) async-start(bf16[32,17,2,128]{3,2,1,0:T(2,128)(2,1)} %bitcast.4), calls=%async_computation.1 | async-start | bytes 557056 | tf_op jit(solution)/shard_map/all_to_all | solution.py:318
  26.9 6.4 %collective-permute-start.3 = (bf16[32,8,128]{2,1,0:T(8,128)(2,1)S(1)}, bf16[32,8,128]{2,1,0:T(8,128)(2,1)S(1)}, u32[]{:S(2)}, u32[]{:S(2)}) collective-permute-start(bf16[32,8,128]{2,1,0:T(8,128)(2,1)S(1)} %get-tuple-element.32.kv_ref), channel_id=1, source_target_pairs={{0,2},{1,3},{2,0},{3,1},{4,6},{5,7},{6,4},{7,5},{8,10},{9,11},{10,... | collective-permute-start | bytes 196616 | tf_op jit(solution)/shard_map/ppermute | solution.py:368
  28.7 6.3 %collective-permute-start.2 = (bf16[32,8,128]{2,1,0:T(8,128)(2,1)S(1)}, bf16[32,8,128]{2,1,0:T(8,128)(2,1)S(1)}, u32[]{:S(2)}, u32[]{:S(2)}) collective-permute-start(bf16[32,8,128]{2,1,0:T(8,128)(2,1)S(1)} %get-tuple-element.32.kv_ref), channel_id=1, source_target_pairs={{0,1},{1,0},{2,3},{3,2},{4,5},{5,4},{6,7},{7,6},{8,9},{9,8},{10,11... | collective-permute-start | bytes 196616 | tf_op jit(solution)/shard_map/ppermute | solution.py:369
  33.2 1.8 %collective-permute-start.4 = (bf16[32,8,128]{2,1,0:T(8,128)(2,1)S(1)}, bf16[32,8,128]{2,1,0:T(8,128)(2,1)S(1)}, u32[]{:S(2)}, u32[]{:S(2)}) collective-permute-start(bf16[32,8,128]{2,1,0:T(8,128)(2,1)S(1)} %collective-permute-done.3.kv2_ref), channel_id=1, source_target_pairs={{0,1},{1,0},{2,3},{3,2},{4,5},{5,4},{6,7},{7,6},{8,9},{9,8},{10,11... | collective-permute-start | bytes 196616 | tf_op jit(solution)/shard_map/ppermute | solution.py:369

commit v29 on v28

--- a/solution.py
+++ b/solution.py
@@ -115,7 +115,7 @@
         copy.wait()
 
 
-def attend_kernel(per, q_ref, ka_ref, va_ref, kb_ref, vb_ref, out_hbm, fresh_ref, out_ref, sems):
+def attend_kernel(per, q_ref, ka_ref, va_ref, kb_ref, vb_ref, out_hbm, fresh_ref, out_ref, rows_ref, sems):
     sources = q_ref.shape[0]
     sent = []
     step = STEP // per
@@ -146,7 +146,6 @@
         total = both[:, HD:]
         out = both[:, :HD] / total
         lse = top + jnp.log(total) * LOG2E
-        rows = []
         for s in range(step):
             part = slice(s * per, (s + 1) * per)
             flat = jnp.sum(jnp.where(diagonal, lse[part], 0.0), axis=0, keepdims=True)
@@ -154,9 +153,11 @@
             mid = (flat - hi).astype(jnp.bfloat16).astype(jnp.float32)
             low = flat - hi - mid
             stats = jnp.where(group == 0, hi, jnp.where(group == 1, mid, jnp.where(group == 2, low, 0.0)))
-            rows = rows + [out[part], jnp.where(second == 0, stats, 0.0)]
+            begin = (first + s) * (per + 2)
+            rows_ref[begin : begin + per, :] = out[part]
+            rows_ref[begin + per : begin + per + 2, :] = jnp.where(second == 0, stats, 0.0)
         done = pl.ds(first * (per + 2), step * (per + 2))
-        out_ref[done, :] = jnp.concatenate(rows, axis=0).astype(jnp.bfloat16)
+        out_ref[done, :] = rows_ref[done, :].astype(jnp.bfloat16)
         sent.append(pltpu.make_async_copy(out_ref.at[done], out_hbm.at[done], sems.at[first // step]))
         sent[-1].start()
     for copy in sent:
@@ -341,6 +342,7 @@
         outs=(ANY, VMEM),
         scratch=[
             pltpu.VMEM((devices * (per + 2), HD), bf16),
+            pltpu.VMEM((devices * (per + 2), HD), f32),
             pltpu.SemaphoreType.DMA((rows // STEP,)),
         ],
         flops=8 * rows * cache_rows * HD,

time: 40.4 us -> 40.4 us (level)
  no operation moved by 1% of the time
where the time goes in v29:
time: 40.4 us; the launch traced here: 39.9 us
  waiting for transfers between devices  13.7 us (34%)
  starting transfers between devices  13.2 us (33%)
  Pallas kernels  10.5 us (26%)
  local copies, waits for them, and re-layouts  2.36 us (6%)
    all_to_all x2, starting transfers between devices, exchange(): lax.all_to_all(x, 'seq', split_axis=0, concat_axis=0, axis_index_groups=[...  10.8 us
    pallas_call x5, Pallas kernels, call(): pl.pallas_call(kernel, name=name, out_shape=out_shape, in_specs=specs, ou...  10.5 us
    all_to_all x2, waiting for transfers between devices, exchange(): lax.all_to_all(x, 'seq', split_axis=0, concat_axis=0, axis_index_groups=[...  7.91 us
    ppermute x1, waiting for transfers between devices, body(): far = lax.ppermute(fresh, 'seq', partner(2))  4.52 us
    ppermute x1, starting transfers between devices, body(): far = lax.ppermute(fresh, 'seq', partner(2))  1.83 us
    ppermute x2, waiting for transfers between devices, body(): lax.ppermute(x, 'seq', partner(1))  1.28 us
    optimization_barrier x1, local copies, waits for them, and re-layouts, body(): lax.optimization_barrier((send, cache_keys, cache_values, picks, queries))  1.25 us
    dynamic_slice x1, local copies, waits for them, and re-layouts, halves(): lax.dynamic_slice_in_dim(x, head * HD, HD, axis=1)  1.06 us
  transfers between devices with their start and end apart: 7, of which 4 were waited for; matrix products, arithmetic and copies ran while one was open for 6% of the time, Pallas kernels for 6%

profile of v29, /device:TPU:0, one launch (start us, length us, event | category | flops | bytes accessed | tf_op | source)
XLA Modules:
  0.0 39.9 jit_solution(16355041077923851299)
XLA Ops:
  0.0 0.0 copy-start
  0.0 0.0 copy-start.1
  0.0 1.9 %pack.1 = bf16[2,8,2,40,128]{4,3,2,1,0:T(8,128)(2,1)} custom-call(s32[3,1,14]{2,1,0:T(1,128)} %bitcast.9, bf16[8,1792]{1,0:T(8,128)(2,1)} %q_ref, bf16[8,256]{1,0:T(8,128)(2,1)} %k_hbm.1, bf16[8,256]{1,0:T(8,128)(2,1)} %v_hbm.1), custom_call_target="tpu_custom_call" | custom-call | tf_op jit(solution)/shard_map/pack/pallas_call | solution.py:269
  1.9 7.3 %all-to-all-start = ((bf16[32,40,128]{2,1,0:T(8,128)(2,1)}), bf16[32,40,128]{2,1,0:T(8,128)(2,1)S(1)}, u32[]{:S(2)}, u32[]{:S(2)}) async-start(bf16[32,40,128]{2,1,0:T(8,128)(2,1)} %bitcast.11), calls=%async_computation | async-start | bytes 655360 | tf_op jit(solution)/shard_map/all_to_all | solution.py:319
  9.2 1.2 %copy.8 = bf16[1024,256]{0,1:T(8,128)(2,1)S(1)} copy(bf16[1024,256]{1,0:T(8,128)(2,1)} %param.10) | data formatting | bytes 1048576 | tf_op jit(solution)/shard_map/optimization_barrier | solution.py:313
  10.5 0.3 collective-permute-start
  10.8 1.1 %constant_dynamic-slice_fusion = (bf16[1024,128]{1,0:T(8,128)(2,1)S(1)}, bf16[1024,128]{1,0:T(8,128)(2,1)S(1)}) fusion(bf16[1024,256]{1,0:T(8,128)(2,1)} %param.11, s32[]{:T(128)S(6)} %select_n.17, s32[]{:T(128)S(6)} %select_n.16), kind=kLoop, calls=%fused_computation.2 | loop fusion | bytes 1048584 | tf_op jit(solution)/shard_map/dynamic_slice | solution.py:326
  11.9 0.3 collective-permute-start.1
  12.2 0.0 collective-permute-done.kb_ref
  12.2 1.3 %collective-permute-done.1.vb_ref = bf16[1024,128]{1,0:T(8,128)(2,1)S(1)} collective-permute-done((bf16[1024,128]{1,0:T(8,128)(2,1)S(1)}, bf16[1024,128]{1,0:T(8,128)(2,1)S(1)}, u32[]{:S(2)}, u32[]{:S(2)}) %collective-permute-start.1) | collective-permute-done | bytes 262176 | tf_op jit(solution)/shard_map/ppermute | solution.py:330
  13.5 6.5 %all-to-all-done.q_ref = bf16[32,40,128]{2,1,0:T(8,128)(2,1)S(1)} async-done(((bf16[32,40,128]{2,1,0:T(8,128)(2,1)}), bf16[32,40,128]{2,1,0:T(8,128)(2,1)S(1)}, u32[]{:S(2)}, u32[]{:S(2)}) %all-to-all-start) | async-done | bytes 327712 | tf_op jit(solution)/shard_map/all_to_all | solution.py:319
  20.1 3.4 %attend.1 = (bf16[1088,128]{1,0:T(8,128)(2,1)}, bf16[32,8,128]{2,1,0:T(8,128)(2,1)S(1)}) custom-call(bf16[32,40,128]{2,1,0:T(8,128)(2,1)S(1)} %all-to-all-done.q_ref, bf16[128,1024]{1,0:T(8,128)(2,1)S(1)} %get-tuple-element.40.ka_ref, bf16[1024,128]{1,0:T(8,128)(2,1)S(1)} %get-tuple-element.38.va_ref, bf16[128,1024]{1,0:T(8,128)(2,1)S(1)} %collective-permute-done.kb_ref, ...), custom_call_target="tpu_custom_call" | custom-call | flops 1073741824 | bytes 4194304 | tf_op jit(solution)/shard_map/attend/pallas_call | solution.py:269
  23.4 3.5 %all-to-all-start.1 = ((bf16[32,17,2,128]{3,2,1,0:T(2,128)(2,1)}), bf16[32,17,2,128]{3,2,1,0:T(2,128)(2,1)S(1)}, u32[]{:S(2)}, u32[]{:S(2)}) async-start(bf16[32,17,2,128]{3,2,1,0:T(2,128)(2,1)} %bitcast.4), calls=%async_computation.1 | async-start | bytes 557056 | tf_op jit(solution)/shard_map/all_to_all | solution.py:319
  26.9 1.8 %collective-permute-start.3 = (bf16[32,8,128]{2,1,0:T(8,128)(2,1)S(1)}, bf16[32,8,128]{2,1,0:T(8,128)(2,1)S(1)}, u32[]{:S(2)}, u32[]{:S(2)}) collective-permute-start(bf16[32,8,128]{2,1,0:T(8,128)(2,1)S(1)} %get-tuple-element.32.kv_ref), channel_id=1, source_target_pairs={{0,2},{1,3},{2,0},{3,1},{4,6},{5,7},{6,4},{7,5},{8,10},{9,11},{10,... | collective-permute-start | bytes 196616 | tf_op jit(solution)/shard_map/ppermute | solution.py:370
  28.7 0.0 collective-permute-start.2
  28.7 4.5 %collective-permute-done.3.kv2_ref = bf16[32,8,128]{2,1,0:T(8,128)(2,1)S(1)} collective-permute-done((bf16[32,8,128]{2,1,0:T(8,128)(2,1)S(1)}, bf16[32,8,128]{2,1,0:T(8,128)(2,1)S(1)}, u32[]{:S(2)}, u32[]{:S(2)}) %collective-permute-start.3) | collective-permute-done | bytes 65568 | tf_op jit(solution)/shard_map/ppermute | solution.py:370
  33.3 0.0 collective-permute-start.4
  33.3 0.0 copy-done
  33.3 0.0 copy-done.1
  33.3 1.8 %masks.1 = (f32[2,56,512]{2,1,0:T(8,128)S(1)}, f32[2,56,128]{2,1,0:T(8,128)S(1)}, bf16[768,1792]{1,0:T(8,128)(2,1)S(1)}) custom-call(s32[3,1,14]{2,1,0:T(1,128)S(1)} %bitcast.10, bf16[8,1792]{1,0:T(8,128)(2,1)S(1)} %copy-done, bf16[1792,1792]{1,0:T(8,128)(2,1)} %w_hbm.1), custom_call_target="tpu_custom_call" | custom-call | tf_op jit(solution)/shard_map/masks/pallas_call | solution.py:269
  35.1 0.0 collective-permute-done.2.kv1_ref
  35.1 0.0 collective-permute-done.4.kv3_ref
  35.1 0.4 %fresh.1 = (f32[2,56,128]{2,1,0:T(8,128)S(1)}, f32[2,56,128]{2,1,0:T(8,128)S(1)}) custom-call(f32[2,56,128]{2,1,0:T(8,128)S(1)} %get-tuple-element.31.rows_ref, bf16[32,8,128]{2,1,0:T(8,128)(2,1)S(1)} %get-tuple-element.32.kv_ref, bf16[32,8,128]{2,1,0:T(8,128)(2,1)S(1)} %collective-permute-done.2.kv1_ref, ...), custom_call_target="tpu_custom_call" | custom-call | flops 29360128 | bytes 1048576 | tf_op jit(solution)/shard_map/fresh/pallas_call | solution.py:269
  35.5 1.4 %all-to-all-done.1 = bf16[32,17,2,128]{3,2,1,0:T(2,128)(2,1)S(1)} async-done(((bf16[32,17,2,128]{3,2,1,0:T(2,128)(2,1)}), bf16[32,17,2,128]{3,2,1,0:T(2,128)(2,1)S(1)}, u32[]{:S(2)}, u32[]{:S(2)}) %all-to-all-start.1) | async-done | bytes 278560 | tf_op jit(solution)/shard_map/all_to_all | solution.py:319
  36.9 3.0 %project.1 = bf16[8,1792]{1,0:T(8,128)(2,1)} custom-call(bf16[1088,128]{1,0:T(8,128)(2,1)S(1)} %bitcast.8, f32[2,56,128]{2,1,0:T(8,128)S(1)} %get-tuple-element.33.out_ref, f32[2,56,128]{2,1,0:T(8,128)S(1)} %get-tuple-element.34.lse_ref, f32[2,56,512]{2,1,0:T(8,128)S(1)} %get-tuple-element.35.match_ref, bf16[768,1792]{1,0:T(8,128)(2,1)S(1)} %get-tuple-element.36.first_ref, ...), custom_call_target="tpu_custom_call" | custom-call | flops 51380224 | bytes 6422528 | tf_op jit(solution)/shard_map/project/pallas_call | solution.py:269
  (1 shorter events, 0.0 us)
Async XLA Ops:
  0.0 33.3 %copy-start = (bf16[8,1792]{1,0:T(8,128)(2,1)S(1)}, bf16[8,1792]{1,0:T(8,128)(2,1)}, u32[]{:S(2)}) copy-start(bf16[8,1792]{1,0:T(8,128)(2,1)} %q_ref) | copy-start | bytes 86020
  0.0 33.3 %copy-start.1 = (s32[1,14,3]{1,0,2:T(1,128)S(1)}, s32[1,14,3]{1,0,2:T(1,128)}, u32[]{:S(2)}) copy-start(s32[1,14,3]{1,0,2:T(1,128)} %param.12) | copy-start | bytes 508
  1.9 18.2 %all-to-all-start = ((bf16[32,40,128]{2,1,0:T(8,128)(2,1)}), bf16[32,40,128]{2,1,0:T(8,128)(2,1)S(1)}, u32[]{:S(2)}, u32[]{:S(2)}) async-start(bf16[32,40,128]{2,1,0:T(8,128)(2,1)} %bitcast.11), calls=%async_computation | async-start | bytes 655360 | tf_op jit(solution)/shard_map/all_to_all | solution.py:319
  10.5 1.7 %collective-permute-start = (bf16[128,1024]{1,0:T(8,128)(2,1)S(1)}, bf16[128,1024]{1,0:T(8,128)(2,1)S(1)}, u32[]{:S(2)}, u32[]{:S(2)}) collective-permute-start(bf16[128,1024]{1,0:T(8,128)(2,1)S(1)} %get-tuple-element.39), channel_id=1, source_target_pairs={{0,1},{1,0},{2,3},{3,2},{4,5},{5,4},{6,7},{7,6},{8,9},{9,8},{10,11... | collective-permute-start | bytes 786440 | tf_op jit(solution)/shard_map/ppermute | solution.py:330
  11.9 1.6 %collective-permute-start.1 = (bf16[1024,128]{1,0:T(8,128)(2,1)S(1)}, bf16[1024,128]{1,0:T(8,128)(2,1)S(1)}, u32[]{:S(2)}, u32[]{:S(2)}) collective-permute-start(bf16[1024,128]{1,0:T(8,128)(2,1)S(1)} %get-tuple-element.37), channel_id=1, source_target_pairs={{0,1},{1,0},{2,3},{3,2},{4,5},{5,4},{6,7},{7,6},{8,9},{9,8},{10,11... | collective-permute-start | bytes 786440 | tf_op jit(solution)/shard_map/ppermute | solution.py:330
  23.4 13.5 %all-to-all-start.1 = ((bf16[32,17,2,128]{3,2,1,0:T(2,128)(2,1)}), bf16[32,17,2,128]{3,2,1,0:T(2,128)(2,1)S(1)}, u32[]{:S(2)}, u32[]{:S(2)}) async-start(bf16[32,17,2,128]{3,2,1,0:T(2,128)(2,1)} %bitcast.4), calls=%async_computation.1 | async-start | bytes 557056 | tf_op jit(solution)/shard_map/all_to_all | solution.py:319
  26.9 6.4 %collective-permute-start.3 = (bf16[32,8,128]{2,1,0:T(8,128)(2,1)S(1)}, bf16[32,8,128]{2,1,0:T(8,128)(2,1)S(1)}, u32[]{:S(2)}, u32[]{:S(2)}) collective-permute-start(bf16[32,8,128]{2,1,0:T(8,128)(2,1)S(1)} %get-tuple-element.32.kv_ref), channel_id=1, source_target_pairs={{0,2},{1,3},{2,0},{3,1},{4,6},{5,7},{6,4},{7,5},{8,10},{9,11},{10,... | collective-permute-start | bytes 196616 | tf_op jit(solution)/shard_map/ppermute | solution.py:370
  28.7 6.3 %collective-permute-start.2 = (bf16[32,8,128]{2,1,0:T(8,128)(2,1)S(1)}, bf16[32,8,128]{2,1,0:T(8,128)(2,1)S(1)}, u32[]{:S(2)}, u32[]{:S(2)}) collective-permute-start(bf16[32,8,128]{2,1,0:T(8,128)(2,1)S(1)} %get-tuple-element.32.kv_ref), channel_id=1, source_target_pairs={{0,1},{1,0},{2,3},{3,2},{4,5},{5,4},{6,7},{7,6},{8,9},{9,8},{10,11... | collective-permute-start | bytes 196616 | tf_op jit(solution)/shard_map/ppermute | solution.py:371
  33.3 1.8 %collective-permute-start.4 = (bf16[32,8,128]{2,1,0:T(8,128)(2,1)S(1)}, bf16[32,8,128]{2,1,0:T(8,128)(2,1)S(1)}, u32[]{:S(2)}, u32[]{:S(2)}) collective-permute-start(bf16[32,8,128]{2,1,0:T(8,128)(2,1)S(1)} %collective-permute-done.3.kv2_ref), channel_id=1, source_target_pairs={{0,1},{1,0},{2,3},{3,2},{4,5},{5,4},{6,7},{7,6},{8,9},{9,8},{10,11... | collective-permute-start | bytes 196616 | tf_op jit(solution)/shard_map/ppermute | solution.py:371

commit v30 on v28

--- a/solution.py
+++ b/solution.py
@@ -19,6 +19,7 @@
 LOG2E = math.log2(math.e)
 LANES = 128
 EARLY = 3
+WIDE = 4
 STEP = 256
 
 
@@ -198,11 +199,11 @@
 
 
 def project_kernel(per, hist_ref, out_ref, lse_ref, match_ref, first_ref, w_hbm, y_ref, w_ref, rows_ref, sems):
-    depth = KVH * HD
-    ready = first_ref.shape[0] // depth
+    depth = WIDE * HD
+    ready = first_ref.shape[0] // HD
     copies = fetch(
         [
-            (w_hbm.at[pl.ds((ready + i) * depth, depth)], w_ref.at[pl.ds(i * depth, depth)])
+            (w_hbm.at[pl.ds(ready * HD + i * depth, depth)], w_ref.at[pl.ds(i * depth, depth)])
             for i in range(w_ref.shape[0] // depth)
         ],
         sems,
@@ -251,10 +252,10 @@
         att = num / (jnp.sum(w, axis=1, keepdims=True) + own_w)
         heads = heads + [att[r * tokens : (r + 1) * tokens] for r in range(GROUP)]
         if g == 0:
-            y = times(heads[: ready * KVH], first_ref[...])
+            y = times(heads[:ready], first_ref[...])
     for i, copy in enumerate(copies):
         copy.wait()
-        y = y + times(heads[(ready + i) * KVH : (ready + i + 1) * KVH], w_ref[i * depth : (i + 1) * depth, :])
+        y = y + times(heads[ready + i * WIDE : ready + (i + 1) * WIDE], w_ref[i * depth : (i + 1) * depth, :])
     y_ref[...] = y.astype(jnp.bfloat16)
 
 
@@ -386,7 +387,7 @@
         scratch=[
             pltpu.VMEM((out_weight.shape[0] - ready, out_weight.shape[1]), bf16),
             pltpu.VMEM((devices * (per + 2), HD), f32),
-            pltpu.SemaphoreType.DMA((GROUP - EARLY,)),
+            pltpu.SemaphoreType.DMA(((GROUP - EARLY) * KVH // WIDE,)),
         ],
         flops=2 * tokens * out_weight.size,
         moved=out_weight.size * 2,

time: 40.4 us -> 40.5 us (level)
  no operation moved by 1% of the time
where the time goes in v30:
time: 40.5 us; the launch traced here: 40 us
  waiting for transfers between devices  13.7 us (34%)
  starting transfers between devices  13.2 us (33%)
  Pallas kernels  10.6 us (26%)
  local copies, waits for them, and re-layouts  2.36 us (6%)
    all_to_all x2, starting transfers between devices, exchange(): lax.all_to_all(x, 'seq', split_axis=0, concat_axis=0, axis_index_groups=[...  10.8 us
    pallas_call x5, Pallas kernels, call(): pl.pallas_call(kernel, name=name, out_shape=out_shape, in_specs=specs, ou...  10.6 us
    all_to_all x2, waiting for transfers between devices, exchange(): lax.all_to_all(x, 'seq', split_axis=0, concat_axis=0, axis_index_groups=[...  7.91 us
    ppermute x1, waiting for transfers between devices, body(): far = lax.ppermute(fresh, 'seq', partner(2))  4.52 us
    ppermute x1, starting transfers between devices, body(): far = lax.ppermute(fresh, 'seq', partner(2))  1.83 us
    ppermute x2, waiting for transfers between devices, body(): lax.ppermute(x, 'seq', partner(1))  1.28 us
    optimization_barrier x1, local copies, waits for them, and re-layouts, body(): lax.optimization_barrier((send, cache_keys, cache_values, picks, queries))  1.25 us
    dynamic_slice x1, local copies, waits for them, and re-layouts, halves(): lax.dynamic_slice_in_dim(x, head * HD, HD, axis=1)  1.06 us
  transfers between devices with their start and end apart: 7, of which 4 were waited for; matrix products, arithmetic and copies ran while one was open for 6% of the time, Pallas kernels for 6%

profile of v30, /device:TPU:0, one launch (start us, length us, event | category | flops | bytes accessed | tf_op | source)
XLA Modules:
  0.0 40.0 jit_solution(13992297049640260095)
XLA Ops:
  0.0 0.0 copy-start
  0.0 0.0 copy-start.1
  0.0 1.9 %pack.1 = bf16[2,8,2,40,128]{4,3,2,1,0:T(8,128)(2,1)} custom-call(s32[3,1,14]{2,1,0:T(1,128)} %bitcast.9, bf16[8,1792]{1,0:T(8,128)(2,1)} %q_ref, bf16[8,256]{1,0:T(8,128)(2,1)} %k_hbm.1, bf16[8,256]{1,0:T(8,128)(2,1)} %v_hbm.1), custom_call_target="tpu_custom_call" | custom-call | tf_op jit(solution)/shard_map/pack/pallas_call | solution.py:269
  1.9 7.3 %all-to-all-start = ((bf16[32,40,128]{2,1,0:T(8,128)(2,1)}), bf16[32,40,128]{2,1,0:T(8,128)(2,1)S(1)}, u32[]{:S(2)}, u32[]{:S(2)}) async-start(bf16[32,40,128]{2,1,0:T(8,128)(2,1)} %bitcast.11), calls=%async_computation | async-start | bytes 655360 | tf_op jit(solution)/shard_map/all_to_all | solution.py:319
  9.2 1.2 %copy.8 = bf16[1024,256]{0,1:T(8,128)(2,1)S(1)} copy(bf16[1024,256]{1,0:T(8,128)(2,1)} %param.10) | data formatting | bytes 1048576 | tf_op jit(solution)/shard_map/optimization_barrier | solution.py:313
  10.5 0.3 collective-permute-start
  10.8 1.1 %constant_dynamic-slice_fusion = (bf16[1024,128]{1,0:T(8,128)(2,1)S(1)}, bf16[1024,128]{1,0:T(8,128)(2,1)S(1)}) fusion(bf16[1024,256]{1,0:T(8,128)(2,1)} %param.11, s32[]{:T(128)S(6)} %select_n.17, s32[]{:T(128)S(6)} %select_n.16), kind=kLoop, calls=%fused_computation.2 | loop fusion | bytes 1048584 | tf_op jit(solution)/shard_map/dynamic_slice | solution.py:326
  11.9 0.3 collective-permute-start.1
  12.2 0.0 collective-permute-done.kb_ref
  12.2 1.3 %collective-permute-done.1.vb_ref = bf16[1024,128]{1,0:T(8,128)(2,1)S(1)} collective-permute-done((bf16[1024,128]{1,0:T(8,128)(2,1)S(1)}, bf16[1024,128]{1,0:T(8,128)(2,1)S(1)}, u32[]{:S(2)}, u32[]{:S(2)}) %collective-permute-start.1) | collective-permute-done | bytes 262176 | tf_op jit(solution)/shard_map/ppermute | solution.py:330
  13.5 6.5 %all-to-all-done.q_ref = bf16[32,40,128]{2,1,0:T(8,128)(2,1)S(1)} async-done(((bf16[32,40,128]{2,1,0:T(8,128)(2,1)}), bf16[32,40,128]{2,1,0:T(8,128)(2,1)S(1)}, u32[]{:S(2)}, u32[]{:S(2)}) %all-to-all-start) | async-done | bytes 327712 | tf_op jit(solution)/shard_map/all_to_all | solution.py:319
  20.1 3.3 %attend.1 = (bf16[1088,128]{1,0:T(8,128)(2,1)}, bf16[32,8,128]{2,1,0:T(8,128)(2,1)S(1)}) custom-call(bf16[32,40,128]{2,1,0:T(8,128)(2,1)S(1)} %all-to-all-done.q_ref, bf16[128,1024]{1,0:T(8,128)(2,1)S(1)} %get-tuple-element.40.ka_ref, bf16[1024,128]{1,0:T(8,128)(2,1)S(1)} %get-tuple-element.38.va_ref, bf16[128,1024]{1,0:T(8,128)(2,1)S(1)} %collective-permute-done.kb_ref, ...), custom_call_target="tpu_custom_call" | custom-call | flops 1073741824 | bytes 4194304 | tf_op jit(solution)/shard_map/attend/pallas_call | solution.py:269
  23.4 3.5 %all-to-all-start.1 = ((bf16[32,17,2,128]{3,2,1,0:T(2,128)(2,1)}), bf16[32,17,2,128]{3,2,1,0:T(2,128)(2,1)S(1)}, u32[]{:S(2)}, u32[]{:S(2)}) async-start(bf16[32,17,2,128]{3,2,1,0:T(2,128)(2,1)} %bitcast.4), calls=%async_computation.1 | async-start | bytes 557056 | tf_op jit(solution)/shard_map/all_to_all | solution.py:319
  26.9 1.8 %collective-permute-start.3 = (bf16[32,8,128]{2,1,0:T(8,128)(2,1)S(1)}, bf16[32,8,128]{2,1,0:T(8,128)(2,1)S(1)}, u32[]{:S(2)}, u32[]{:S(2)}) collective-permute-start(bf16[32,8,128]{2,1,0:T(8,128)(2,1)S(1)} %get-tuple-element.32.kv_ref), channel_id=1, source_target_pairs={{0,2},{1,3},{2,0},{3,1},{4,6},{5,7},{6,4},{7,5},{8,10},{9,11},{10,... | collective-permute-start | bytes 196616 | tf_op jit(solution)/shard_map/ppermute | solution.py:369
  28.7 0.0 collective-permute-start.2
  28.7 4.5 %collective-permute-done.3.kv2_ref = bf16[32,8,128]{2,1,0:T(8,128)(2,1)S(1)} collective-permute-done((bf16[32,8,128]{2,1,0:T(8,128)(2,1)S(1)}, bf16[32,8,128]{2,1,0:T(8,128)(2,1)S(1)}, u32[]{:S(2)}, u32[]{:S(2)}) %collective-permute-start.3) | collective-permute-done | bytes 65568 | tf_op jit(solution)/shard_map/ppermute | solution.py:369
  33.2 0.0 collective-permute-start.4
  33.2 0.0 copy-done
  33.2 0.0 copy-done.1
  33.2 1.8 %masks.1 = (f32[2,56,512]{2,1,0:T(8,128)S(1)}, f32[2,56,128]{2,1,0:T(8,128)S(1)}, bf16[768,1792]{1,0:T(8,128)(2,1)S(1)}) custom-call(s32[3,1,14]{2,1,0:T(1,128)S(1)} %bitcast.10, bf16[8,1792]{1,0:T(8,128)(2,1)S(1)} %copy-done, bf16[1792,1792]{1,0:T(8,128)(2,1)} %w_hbm.1), custom_call_target="tpu_custom_call" | custom-call | tf_op jit(solution)/shard_map/masks/pallas_call | solution.py:269
  35.0 0.0 collective-permute-done.2.kv1_ref
  35.1 0.0 collective-permute-done.4.kv3_ref
  35.1 0.4 %fresh.1 = (f32[2,56,128]{2,1,0:T(8,128)S(1)}, f32[2,56,128]{2,1,0:T(8,128)S(1)}) custom-call(f32[2,56,128]{2,1,0:T(8,128)S(1)} %get-tuple-element.31.rows_ref, bf16[32,8,128]{2,1,0:T(8,128)(2,1)S(1)} %get-tuple-element.32.kv_ref, bf16[32,8,128]{2,1,0:T(8,128)(2,1)S(1)} %collective-permute-done.2.kv1_ref, ...), custom_call_target="tpu_custom_call" | custom-call | flops 29360128 | bytes 1048576 | tf_op jit(solution)/shard_map/fresh/pallas_call | solution.py:269
  35.5 1.4 %all-to-all-done.1 = bf16[32,17,2,128]{3,2,1,0:T(2,128)(2,1)S(1)} async-done(((bf16[32,17,2,128]{3,2,1,0:T(2,128)(2,1)}), bf16[32,17,2,128]{3,2,1,0:T(2,128)(2,1)S(1)}, u32[]{:S(2)}, u32[]{:S(2)}) %all-to-all-start.1) | async-done | bytes 278560 | tf_op jit(solution)/shard_map/all_to_all | solution.py:319
  36.9 3.2 %project.1 = bf16[8,1792]{1,0:T(8,128)(2,1)} custom-call(bf16[1088,128]{1,0:T(8,128)(2,1)S(1)} %bitcast.8, f32[2,56,128]{2,1,0:T(8,128)S(1)} %get-tuple-element.33.out_ref, f32[2,56,128]{2,1,0:T(8,128)S(1)} %get-tuple-element.34.lse_ref, f32[2,56,512]{2,1,0:T(8,128)S(1)} %get-tuple-element.35.match_ref, bf16[768,1792]{1,0:T(8,128)(2,1)S(1)} %get-tuple-element.36.first_ref, ...), custom_call_target="tpu_custom_call" | custom-call | flops 51380224 | bytes 6422528 | tf_op jit(solution)/shard_map/project/pallas_call | solution.py:269
  (1 shorter events, 0.0 us)
Async XLA Ops:
  0.0 33.2 %copy-start = (bf16[8,1792]{1,0:T(8,128)(2,1)S(1)}, bf16[8,1792]{1,0:T(8,128)(2,1)}, u32[]{:S(2)}) copy-start(bf16[8,1792]{1,0:T(8,128)(2,1)} %q_ref) | copy-start | bytes 86020
  0.0 33.2 %copy-start.1 = (s32[1,14,3]{1,0,2:T(1,128)S(1)}, s32[1,14,3]{1,0,2:T(1,128)}, u32[]{:S(2)}) copy-start(s32[1,14,3]{1,0,2:T(1,128)} %param.12) | copy-start | bytes 508
  1.9 18.2 %all-to-all-start = ((bf16[32,40,128]{2,1,0:T(8,128)(2,1)}), bf16[32,40,128]{2,1,0:T(8,128)(2,1)S(1)}, u32[]{:S(2)}, u32[]{:S(2)}) async-start(bf16[32,40,128]{2,1,0:T(8,128)(2,1)} %bitcast.11), calls=%async_computation | async-start | bytes 655360 | tf_op jit(solution)/shard_map/all_to_all | solution.py:319
  10.5 1.7 %collective-permute-start = (bf16[128,1024]{1,0:T(8,128)(2,1)S(1)}, bf16[128,1024]{1,0:T(8,128)(2,1)S(1)}, u32[]{:S(2)}, u32[]{:S(2)}) collective-permute-start(bf16[128,1024]{1,0:T(8,128)(2,1)S(1)} %get-tuple-element.39), channel_id=1, source_target_pairs={{0,1},{1,0},{2,3},{3,2},{4,5},{5,4},{6,7},{7,6},{8,9},{9,8},{10,11... | collective-permute-start | bytes 786440 | tf_op jit(solution)/shard_map/ppermute | solution.py:330
  11.9 1.6 %collective-permute-start.1 = (bf16[1024,128]{1,0:T(8,128)(2,1)S(1)}, bf16[1024,128]{1,0:T(8,128)(2,1)S(1)}, u32[]{:S(2)}, u32[]{:S(2)}) collective-permute-start(bf16[1024,128]{1,0:T(8,128)(2,1)S(1)} %get-tuple-element.37), channel_id=1, source_target_pairs={{0,1},{1,0},{2,3},{3,2},{4,5},{5,4},{6,7},{7,6},{8,9},{9,8},{10,11... | collective-permute-start | bytes 786440 | tf_op jit(solution)/shard_map/ppermute | solution.py:330
  23.4 13.5 %all-to-all-start.1 = ((bf16[32,17,2,128]{3,2,1,0:T(2,128)(2,1)}), bf16[32,17,2,128]{3,2,1,0:T(2,128)(2,1)S(1)}, u32[]{:S(2)}, u32[]{:S(2)}) async-start(bf16[32,17,2,128]{3,2,1,0:T(2,128)(2,1)} %bitcast.4), calls=%async_computation.1 | async-start | bytes 557056 | tf_op jit(solution)/shard_map/all_to_all | solution.py:319
  26.9 6.4 %collective-permute-start.3 = (bf16[32,8,128]{2,1,0:T(8,128)(2,1)S(1)}, bf16[32,8,128]{2,1,0:T(8,128)(2,1)S(1)}, u32[]{:S(2)}, u32[]{:S(2)}) collective-permute-start(bf16[32,8,128]{2,1,0:T(8,128)(2,1)S(1)} %get-tuple-element.32.kv_ref), channel_id=1, source_target_pairs={{0,2},{1,3},{2,0},{3,1},{4,6},{5,7},{6,4},{7,5},{8,10},{9,11},{10,... | collective-permute-start | bytes 196616 | tf_op jit(solution)/shard_map/ppermute | solution.py:369
  28.7 6.3 %collective-permute-start.2 = (bf16[32,8,128]{2,1,0:T(8,128)(2,1)S(1)}, bf16[32,8,128]{2,1,0:T(8,128)(2,1)S(1)}, u32[]{:S(2)}, u32[]{:S(2)}) collective-permute-start(bf16[32,8,128]{2,1,0:T(8,128)(2,1)S(1)} %get-tuple-element.32.kv_ref), channel_id=1, source_target_pairs={{0,1},{1,0},{2,3},{3,2},{4,5},{5,4},{6,7},{7,6},{8,9},{9,8},{10,11... | collective-permute-start | bytes 196616 | tf_op jit(solution)/shard_map/ppermute | solution.py:370
  33.2 1.8 %collective-permute-start.4 = (bf16[32,8,128]{2,1,0:T(8,128)(2,1)S(1)}, bf16[32,8,128]{2,1,0:T(8,128)(2,1)S(1)}, u32[]{:S(2)}, u32[]{:S(2)}) collective-permute-start(bf16[32,8,128]{2,1,0:T(8,128)(2,1)S(1)} %collective-permute-done.3.kv2_ref), channel_id=1, source_target_pairs={{0,1},{1,0},{2,3},{3,2},{4,5},{5,4},{6,7},{7,6},{8,9},{9,8},{10,11... | collective-permute-start | bytes 196616 | tf_op jit(solution)/shard_map/ppermute | solution.py:370
